TPU v7x, 32 devices: a whole 2x2x4 slice. The times are simulated.
32 devices in a mesh: ch: 16 (over z, y, core), fq: 2 (over x).
Axes of the slice: x: 2, y: 2, z: 4, core: 2. Of those that a mesh axis runs over, the one named last changes fastest.
Arguments:
- spectra: bfloat16 [2, 48, 128, 2048], P(None, None, 'fq', 'ch')
- band_ids: int32 [128], P('fq'), may hold values from 0 to 7, as said below
Outputs:
- coherence: float32 [2, 4, 8, 2048, 128], P(None, None, 'fq', 'ch')
Inputs may be any that keep to these rules, and one draw needn't show every extreme that they name: band_ids never falls, every band has at least one bin, and the bins of the g-th run of 64 bins belong only to bands g * 4 to (g + 1) * 4 - 1.
All inputs are finite; a program needn't handle non-finite values.
Results may differ from a plain program's by a relative error of at most 0.004.
Values may be sent and summed in bfloat16 or wider, within the bound.
No kernel may reach another device: no remote copies, remote signals or barrier semaphores. Data moves between devices by JAX's collectives and lax.ppermute only.
A program may use at most 64 MiB of HBM per device.

v0:
```python
import functools

import jax
import jax.numpy as jnp
from jax import lax
from jax.experimental import pallas as pl
from jax.experimental.pallas import tpu as pltpu
from jax.sharding import PartitionSpec as P

BANDS = 8
ROUNDS = 4
SMOOTH = 4
EPS = 1e-06

GROUP = 16
CHUNKS = 6
VMEM_LIMIT = 24 * 1024 * 1024


def vmem():
    return pl.BlockSpec(memory_space=pltpu.VMEM)


def smem():
    return pl.BlockSpec(memory_space=pltpu.SMEM)


def params():
    return pltpu.CompilerParams(vmem_limit_bytes=VMEM_LIMIT)


def power_kernel(x_ref, power_ref):
    rows = x_ref.shape[0]

    def step(i, total):
        value = x_ref[i].astype(jnp.float32)
        return total + value * value

    total = lax.fori_loop(0, rows, step, jnp.zeros(power_ref.shape, jnp.float32), unroll=8)
    power_ref[...] = total / (rows // 2)


def left_kernel(where_ref, x_ref, power_ref, halo_ref, scale_ref, left_ref, padded):
    fq, bin_total = where_ref[0], where_ref[1]
    rows, width, channels = x_ref.shape
    padded[...] = jnp.zeros_like(padded)
    padded[8 : 8 + width, :] = power_ref[...]

    @pl.when(fq > 0)
    def _():
        padded[8 - SMOOTH : 8, :] = halo_ref[...]

    @pl.when(fq == 0)
    def _():
        padded[8 + width : 8 + width + SMOOTH, :] = halo_ref[...]

    total = padded[8 - SMOOTH : 8 - SMOOTH + width, :]
    for offset in range(1, 2 * SMOOTH + 1):
        total = total + padded[8 - SMOOTH + offset : 8 - SMOOTH + offset + width, :]
    bins = fq * width + lax.broadcasted_iota(jnp.int32, (width, channels), 0)
    counts = jnp.minimum(bins + SMOOTH, bin_total - 1) - jnp.maximum(bins - SMOOTH, 0) + 1
    scale_ref[...] = lax.rsqrt(total / counts.astype(jnp.float32) + EPS)

    span = 16 * GROUP
    pieces = rows // 16
    for group in range(width // GROUP):
        bins_here = slice(group * GROUP, (group + 1) * GROUP)
        scale = scale_ref[bins_here, :]
        for piece in range(pieces):
            raw = x_ref[piece * 16 : (piece + 1) * 16, bins_here, :].astype(jnp.float32)
            white = (raw * scale[None]).reshape(span, channels)
            turned = white.T
            here = slice(piece * span, (piece + 1) * span)
            left_ref[group, :channels, here] = turned.astype(jnp.bfloat16)
            if piece < pieces // 2:
                there = slice((piece + pieces // 2) * span, (piece + pieces // 2 + 1) * span)
                left_ref[group, channels:, there] = (-turned).astype(jnp.bfloat16)
            else:
                there = slice((piece - pieces // 2) * span, (piece - pieces // 2 + 1) * span)
                left_ref[group, channels:, there] = turned.astype(jnp.bfloat16)


def cross_kernel(
    start, first, last, where_ref, norm_ref, left_ref, bands_ref, scales_ref, *refs
):
    rights = refs[:ROUNDS]
    out_ref = refs[-1]
    if first:
        out_ref[...] = jnp.zeros_like(out_ref)
    else:
        out_ref[...] = refs[ROUNDS][...]
    rows, width, channels = rights[0].shape
    span = rows * GROUP
    core = where_ref[0]
    rounds = (2 - 2 * core, 2 * core, 1, 3)
    for group in range(width // GROUP):
        bins_here = slice(group * GROUP, (group + 1) * GROUP)
        left = left_ref[group, :, start * GROUP : (start + rows) * GROUP]

        def one_band(band, carry):
            inside = bands_ref[bins_here, :] == band
            columns = []
            for index, right in enumerate(rights):
                scale = jnp.where(inside, scales_ref[index, bins_here, :], 0.0)
                raw = right[:, bins_here, :].astype(jnp.float32)
                columns.append((raw * scale[None]).astype(jnp.bfloat16).reshape(span, channels))
            product = jnp.dot(
                left, jnp.concatenate(columns, axis=1), preferred_element_type=jnp.float32
            )
            for index, turn in enumerate(rounds):
                lanes = slice(index * channels, (index + 1) * channels)
                out_ref[0, turn, band] += product[:channels, lanes]
                out_ref[1, turn, band] += product[channels:, lanes]
            return carry

        lax.fori_loop(where_ref[1 + 2 * group], where_ref[2 + 2 * group] + 1, one_band, 0)
    if last:
        for band in range(out_ref.shape[2]):
            out_ref[:, :, band] = out_ref[:, :, band] / norm_ref[band]


def shards(spectra, band_ids):
    parts, windows, width, channels = spectra.shape
    rows = parts * windows
    count = lax.axis_size("ch")
    fq_count = lax.axis_size("fq")
    index = lax.axis_index("ch")
    fq = lax.axis_index("fq")
    core = index % 2
    odd_chip = (index // 2) % 2

    ahead = [(i, (i + 4) % count) for i in range(count)]
    beside = [(i, i ^ 2) for i in range(count)]
    mate = [(i, i ^ 1) for i in range(count)]

    own = spectra.reshape(rows, width, channels)
    size = rows // CHUNKS

    def spread(value):
        two = lax.ppermute(value, "ch", ahead)
        one = lax.ppermute(jnp.where(odd_chip == 1, two, value), "ch", beside)
        mixed = lax.ppermute(jnp.where(core == 0, value, two), "ch", mate)
        other = lax.ppermute(one, "ch", mate)
        return mixed, other, one, two

    chunks = [spread(own[k * size : (k + 1) * size]) for k in range(CHUNKS)]

    power = pl.pallas_call(
        power_kernel,
        out_shape=jax.ShapeDtypeStruct((width, channels), jnp.float32),
        in_specs=[vmem()],
        out_specs=vmem(),
        compiler_params=params(),
        name="power",
    )(own)
    edge = jnp.where(fq == 0, power[width - SMOOTH :], power[:SMOOTH])
    halo = lax.ppermute(edge, "fq", [(0, 1), (1, 0)])
    groups = width // GROUP
    place = jnp.stack([fq, width * fq_count]).astype(jnp.int32)
    scale, left = pl.pallas_call(
        left_kernel,
        out_shape=(
            jax.ShapeDtypeStruct((width, channels), jnp.float32),
            jax.ShapeDtypeStruct((groups, 2 * channels, rows * GROUP), jnp.bfloat16),
        ),
        in_specs=[smem(), vmem(), vmem(), vmem()],
        out_specs=(vmem(), vmem()),
        scratch_shapes=[pltpu.VMEM((width + 16, channels), jnp.float32)],
        compiler_params=params(),
        name="left",
    )(place, own, power, halo)
    scales = jnp.stack(spread(scale))

    band_width = BANDS // fq_count
    local_band = band_ids - fq * band_width
    onehot = (local_band[:, None] == jnp.arange(band_width, dtype=jnp.int32)[None, :]).astype(
        jnp.float32
    )
    norms = jnp.sqrt(windows * jnp.sum(onehot, axis=0))
    bands = jnp.broadcast_to(local_band[:, None], (width, channels))
    ends = jnp.stack([local_band[0::GROUP], local_band[GROUP - 1 :: GROUP]], axis=1)
    where = jnp.concatenate([core[None], ends.reshape(-1)]).astype(jnp.int32)

    shape = jax.ShapeDtypeStruct((2, ROUNDS, band_width, channels, channels), jnp.float32)
    total = None
    for k, rights in enumerate(chunks):
        first, last = k == 0, k == CHUNKS - 1
        operands = [where, norms, left, bands, scales, *rights]
        if not first:
            operands.append(total)
        total = pl.pallas_call(
            functools.partial(cross_kernel, k * size, first, last),
            out_shape=shape,
            in_specs=[smem(), smem()] + [vmem()] * (len(operands) - 2),
            out_specs=vmem(),
            input_output_aliases={} if first else {len(operands) - 1: 0},
            compiler_params=params(),
            name="cross",
        )(*operands)
    return total


def solution(mesh):
    placed = (P(None, None, "fq", "ch"), P("fq"))
    return jax.shard_map(
        shards,
        mesh=mesh,
        in_specs=placed,
        out_specs=P(None, None, "fq", "ch", None),
        check_vma=False,
    )
```

profile of v0, /device:TPU:1, one launch (start us, length us, event | category | flops | bytes accessed | tf_op | source)
XLA Modules:
  0.0 116.9 jit_solution(8332458377899396635)
XLA Ops:
  0.0 1.7 %slice.47 = bf16[16,64,128]{2,1,0:T(8,128)(2,1)} slice(bf16[96,64,128]{2,1,0:T(8,128)(2,1)} %bitcast.9), slice={[0:16], [0:64], [0:128]} | slice | bytes 524288 | tf_op jit(solution)/shard_map/slice | solution.py:146
  1.7 2.1 %collective-permute-start.25 = (bf16[16,64,128]{2,1,0:T(8,128)(2,1)}, bf16[16,64,128]{2,1,0:T(8,128)(2,1)S(1)}, u32[]{:S(2)}, u32[]{:S(2)}) collective-permute-start(bf16[16,64,128]{2,1,0:T(8,128)(2,1)} %slice.47), channel_id=1, source_target_pairs={{0,8},{2,10},{4,12},{6,14},{8,16},{10,18},{12,20},{14,22},{16,24},... | collective-permute-start | bytes 786440 | tf_op jit(solution)/shard_map/ppermute | solution.py:140
  3.8 1.4 %copy-done = bf16[2,48,64,128]{3,2,1,0:T(8,128)(2,1)S(1)} copy-done((bf16[2,48,64,128]{3,2,1,0:T(8,128)(2,1)S(1)}, bf16[2,48,64,128]{3,2,1,0:T(8,128)(2,1)}, u32[]{:S(2)}) %copy-start) | copy-done | bytes 1572888
  5.2 0.3 power.1.power_ref
  5.6 1.3 %collective-permute-start = (f32[4,128]{1,0:T(4,128)S(1)}, f32[4,128]{1,0:T(4,128)S(1)}, u32[]{:S(2)}, u32[]{:S(2)}) collective-permute-start(f32[4,128]{1,0:T(4,128)S(1)} %slice_select_fusion), channel_id=1, source_target_pairs={{0,1},{1,0},{2,3},{3,2},{4,5},{5,4},{6,7},{7,6},{8,9},{9,8},{10,11... | collective-permute-start | bytes 6152 | tf_op jit(solution)/shard_map/ppermute | solution.py:157
  6.8 0.1 pad_add_fusion.2.where_ref
  6.9 1.4 %collective-permute-done.halo_ref = f32[4,128]{1,0:T(4,128)S(1)} collective-permute-done((f32[4,128]{1,0:T(4,128)S(1)}, f32[4,128]{1,0:T(4,128)S(1)}, u32[]{:S(2)}, u32[]{:S(2)}) %collective-permute-start) | collective-permute-done | bytes 2080 | tf_op jit(solution)/shard_map/ppermute | solution.py:157
  8.4 1.4 %copy-done.1 = bf16[2,48,64,128]{3,2,1,0:T(8,128)(2,1)S(1)} copy-done((bf16[2,48,64,128]{3,2,1,0:T(8,128)(2,1)S(1)}, bf16[2,48,64,128]{3,2,1,0:T(8,128)(2,1)}, u32[]{:S(2)}) %copy-start.1) | copy-done | bytes 1572888
  9.8 1.2 %left.1 = (f32[64,128]{1,0:T(8,128)S(1)}, bf16[4,256,1536]{2,1,0:T(8,128)(2,1)S(1)}) custom-call(s32[2]{0:T(128)S(1)} %pad_add_fusion.2.where_ref, bf16[96,64,128]{2,1,0:T(8,128)(2,1)S(1)} %bitcast.11, f32[64,128]{1,0:T(8,128)S(1)} %power.1.power_ref, f32[4,128]{1,0:T(4,128)S(1)} %collective-permute-done.halo_ref), custom_call_target="tpu_custom_call" | custom-call | tf_op jit(solution)/shard_map/left/pallas_call | solution.py:160
  11.0 1.3 %collective-permute-start.1 = (f32[64,128]{1,0:T(8,128)S(1)}, f32[64,128]{1,0:T(8,128)S(1)}, u32[]{:S(2)}, u32[]{:S(2)}) collective-permute-start(f32[64,128]{1,0:T(8,128)S(1)} %get-tuple-element.8), channel_id=1, source_target_pairs={{0,8},{2,10},{4,12},{6,14},{8,16},{10,18},{12,20},{14,22},{16,24},... | collective-permute-start | bytes 98312 | tf_op jit(solution)/shard_map/ppermute | solution.py:140
  12.4 0.1 broadcast_select_fusion
  12.5 1.3 %collective-permute-start.27 = (bf16[16,64,128]{2,1,0:T(8,128)(2,1)S(1)}, bf16[16,64,128]{2,1,0:T(8,128)(2,1)S(1)}, u32[]{:S(2)}, u32[]{:S(2)}) collective-permute-start(bf16[16,64,128]{2,1,0:T(8,128)(2,1)S(1)} %get-tuple-element.9), channel_id=1, source_target_pairs={{0,4},{2,6},{4,0},{6,2},{8,12},{10,14},{12,8},{14,10},{16,20},{18,... | collective-permute-start | bytes 786440 | tf_op jit(solution)/shard_map/ppermute | solution.py:141
  13.8 1.8 %collective-permute-done.1 = f32[64,128]{1,0:T(8,128)S(1)} collective-permute-done((f32[64,128]{1,0:T(8,128)S(1)}, f32[64,128]{1,0:T(8,128)S(1)}, u32[]{:S(2)}, u32[]{:S(2)}) %collective-permute-start.1) | collective-permute-done | bytes 32800 | tf_op jit(solution)/shard_map/ppermute | solution.py:140
  15.6 1.3 %collective-permute-start.3 = (f32[64,128]{1,0:T(8,128)S(1)}, f32[64,128]{1,0:T(8,128)S(1)}, u32[]{:S(2)}, u32[]{:S(2)}) collective-permute-start(f32[64,128]{1,0:T(8,128)S(1)} %get-tuple-element.35), channel_id=1, source_target_pairs={{0,4},{2,6},{4,0},{6,2},{8,12},{10,14},{12,8},{14,10},{16,20},{18,... | collective-permute-start | bytes 98312 | tf_op jit(solution)/shard_map/ppermute | solution.py:141
  17.0 0.0 collective-permute-start.13
  17.0 0.8 collective-permute-start.17
  17.8 0.0 collective-permute-start.21
  17.8 1.3 %collective-permute-done.3 = f32[64,128]{1,0:T(8,128)S(1)} collective-permute-done((f32[64,128]{1,0:T(8,128)S(1)}, f32[64,128]{1,0:T(8,128)S(1)}, u32[]{:S(2)}, u32[]{:S(2)}) %collective-permute-start.3) | collective-permute-done | bytes 32800 | tf_op jit(solution)/shard_map/ppermute | solution.py:141
  19.1 1.7 %collective-permute-start.5 = (bf16[16,64,128]{2,1,0:T(8,128)(2,1)S(1)}, bf16[16,64,128]{2,1,0:T(8,128)(2,1)S(1)}, u32[]{:S(2)}, u32[]{:S(2)}) collective-permute-start(bf16[16,64,128]{2,1,0:T(8,128)(2,1)S(1)} %get-tuple-element.25), channel_id=1, source_target_pairs={{0,8},{2,10},{4,12},{6,14},{8,16},{10,18},{12,20},{14,22},{16,24},... | collective-permute-start | bytes 786440 | tf_op jit(solution)/shard_map/ppermute | solution.py:140
  20.8 0.0 collective-permute-done.27.refs_2_
  20.8 0.1 collective-permute-start.9
  20.9 3.1 %collective-permute-done.13.refs_3_ = bf16[16,64,128]{2,1,0:T(8,128)(2,1)S(1)} collective-permute-done((bf16[16,64,128]{2,1,0:T(8,128)(2,1)S(1)}, bf16[16,64,128]{2,1,0:T(8,128)(2,1)S(1)}, u32[]{:S(2)}, u32[]{:S(2)}) %collective-permute-start.13) | collective-permute-done | bytes 262176 | tf_op jit(solution)/shard_map/ppermute | solution.py:140
  24.0 7.3 %collective-permute-start.2 = (f32[64,128]{1,0:T(8,128)S(1)}, f32[64,128]{1,0:T(8,128)S(1)}, u32[]{:S(2)}, u32[]{:S(2)}) collective-permute-start(f32[64,128]{1,0:T(8,128)S(1)} %get-tuple-element.34), channel_id=1, source_target_pairs={{0,2},{2,0},{4,6},{6,4},{8,10},{10,8},{12,14},{14,12},{16,18},{18,... | collective-permute-start | bytes 98312 | tf_op jit(solution)/shard_map/ppermute | solution.py:142
  31.2 5.6 %collective-permute-start.4 = (f32[64,128]{1,0:T(8,128)S(1)}, f32[64,128]{1,0:T(8,128)S(1)}, u32[]{:S(2)}, u32[]{:S(2)}) collective-permute-start(f32[64,128]{1,0:T(8,128)S(1)} %collective-permute-done.3), channel_id=1, source_target_pairs={{0,2},{2,0},{4,6},{6,4},{8,10},{10,8},{12,14},{14,12},{16,18},{18,... | collective-permute-start | bytes 98312 | tf_op jit(solution)/shard_map/ppermute | solution.py:143
  36.9 0.0 collective-permute-done.21.refs_3_
  36.9 5.6 %collective-permute-start.26 = (bf16[16,64,128]{2,1,0:T(8,128)(2,1)S(1)}, bf16[16,64,128]{2,1,0:T(8,128)(2,1)S(1)}, u32[]{:S(2)}, u32[]{:S(2)}) collective-permute-start(bf16[16,64,128]{2,1,0:T(8,128)(2,1)S(1)} %get-tuple-element.10), channel_id=1, source_target_pairs={{0,2},{2,0},{4,6},{6,4},{8,10},{10,8},{12,14},{14,12},{16,18},{18,... | collective-permute-start | bytes 786440 | tf_op jit(solution)/shard_map/ppermute | solution.py:142
  42.5 0.0 collective-permute-done.5.refs_3_
  42.5 4.7 %collective-permute-start.28 = (bf16[16,64,128]{2,1,0:T(8,128)(2,1)S(1)}, bf16[16,64,128]{2,1,0:T(8,128)(2,1)S(1)}, u32[]{:S(2)}, u32[]{:S(2)}) collective-permute-start(bf16[16,64,128]{2,1,0:T(8,128)(2,1)S(1)} %collective-permute-done.27.refs_2_), channel_id=1, source_target_pairs={{0,2},{2,0},{4,6},{6,4},{8,10},{10,8},{12,14},{14,12},{16,18},{18,... | collective-permute-start | bytes 786440 | tf_op jit(solution)/shard_map/ppermute | solution.py:143
  47.1 0.0 collective-permute-done.9.refs_3_
  47.1 1.6 %broadcast_select_fusion.1 = (bf16[16,64,128]{2,1,0:T(8,128)(2,1)}, bf16[16,64,128]{2,1,0:T(8,128)(2,1)}, bf16[16,64,128]{2,1,0:T(8,128)(2,1)}, bf16[16,64,128]{...) fusion(bf16[16,64,128]{2,1,0:T(8,128)(2,1)S(1)} %collective-per, ...), kind=kLoop, calls=%fused_computation.1 | loop fusion | flops 1310720 | bytes 5242882 | tf_op jit(solution)/shard_map/jit(_where)/select_n | solution.py:141
  48.8 0.3 collective-permute-start.23
  49.1 3.1 %collective-permute-start.22 = (bf16[16,64,128]{2,1,0:T(8,128)(2,1)}, bf16[16,64,128]{2,1,0:T(8,128)(2,1)}, u32[]{:S(2)}, u32[]{:S(2)}) collective-permute-start(bf16[16,64,128]{2,1,0:T(8,128)(2,1)} %get-tuple-element.12), channel_id=1, source_target_pairs={{0,2},{2,0},{4,6},{6,4},{8,10},{10,8},{12,14},{14,12},{16,18},{18,... | collective-permute-start | bytes 786440 | tf_op jit(solution)/shard_map/ppermute | solution.py:142
  52.1 1.2 %collective-permute-start.19 = (bf16[16,64,128]{2,1,0:T(8,128)(2,1)}, bf16[16,64,128]{2,1,0:T(8,128)(2,1)}, u32[]{:S(2)}, u32[]{:S(2)}) collective-permute-start(bf16[16,64,128]{2,1,0:T(8,128)(2,1)} %get-tuple-element.31), channel_id=1, source_target_pairs={{0,4},{2,6},{4,0},{6,2},{8,12},{10,14},{12,8},{14,10},{16,20},{18,... | collective-permute-start | bytes 786440 | tf_op jit(solution)/shard_map/ppermute | solution.py:141
  53.4 0.7 copy-done.14
  54.1 0.3 collective-permute-start.18
  54.5 0.7 copy-done.16
  55.2 0.2 collective-permute-start.15
  55.4 5.7 %collective-permute-start.14 = (bf16[16,64,128]{2,1,0:T(8,128)(2,1)}, bf16[16,64,128]{2,1,0:T(8,128)(2,1)}, u32[]{:S(2)}, u32[]{:S(2)}) collective-permute-start(bf16[16,64,128]{2,1,0:T(8,128)(2,1)} %get-tuple-element.28), channel_id=1, source_target_pairs={{0,2},{2,0},{4,6},{6,4},{8,10},{10,8},{12,14},{14,12},{16,18},{18,... | collective-permute-start | bytes 786440 | tf_op jit(solution)/shard_map/ppermute | solution.py:142
  61.1 1.5 %collective-permute-start.7 = (bf16[16,64,128]{2,1,0:T(8,128)(2,1)}, bf16[16,64,128]{2,1,0:T(8,128)(2,1)}, u32[]{:S(2)}, u32[]{:S(2)}) collective-permute-start(bf16[16,64,128]{2,1,0:T(8,128)(2,1)} %get-tuple-element.33), channel_id=1, source_target_pairs={{0,4},{2,6},{4,0},{6,2},{8,12},{10,14},{12,8},{14,10},{16,20},{18,... | collective-permute-start | bytes 786440 | tf_op jit(solution)/shard_map/ppermute | solution.py:141
  62.5 4.1 %collective-permute-start.24 = (bf16[16,64,128]{2,1,0:T(8,128)(2,1)}, bf16[16,64,128]{2,1,0:T(8,128)(2,1)}, u32[]{:S(2)}, u32[]{:S(2)}) collective-permute-start(bf16[16,64,128]{2,1,0:T(8,128)(2,1)} %collective-permute-done.23.refs_2_), channel_id=1, source_target_pairs={{0,2},{2,0},{4,6},{6,4},{8,10},{10,8},{12,14},{14,12},{16,18},{18,... | collective-permute-start | bytes 786440 | tf_op jit(solution)/shard_map/ppermute | solution.py:143
  66.7 5.6 %collective-permute-start.20 = (bf16[16,64,128]{2,1,0:T(8,128)(2,1)}, bf16[16,64,128]{2,1,0:T(8,128)(2,1)}, u32[]{:S(2)}, u32[]{:S(2)}) collective-permute-start(bf16[16,64,128]{2,1,0:T(8,128)(2,1)} %collective-permute-done.19.refs_2_), channel_id=1, source_target_pairs={{0,2},{2,0},{4,6},{6,4},{8,10},{10,8},{12,14},{14,12},{16,18},{18,... | collective-permute-start | bytes 786440 | tf_op jit(solution)/shard_map/ppermute | solution.py:143
  72.3 0.1 convert_reduce_fusion
  72.4 0.1 slice.30
  72.5 0.6 slice.31
  73.1 0.1 collective-permute-start.10
  73.2 4.7 %collective-permute-start.6 = (bf16[16,64,128]{2,1,0:T(8,128)(2,1)}, bf16[16,64,128]{2,1,0:T(8,128)(2,1)}, u32[]{:S(2)}, u32[]{:S(2)}) collective-permute-start(bf16[16,64,128]{2,1,0:T(8,128)(2,1)} %get-tuple-element.32), channel_id=1, source_target_pairs={{0,2},{2,0},{4,6},{6,4},{8,10},{10,8},{12,14},{14,12},{16,18},{18,... | collective-permute-start | bytes 786440 | tf_op jit(solution)/shard_map/ppermute | solution.py:142
  77.9 2.9 %collective-permute-start.16 = (bf16[16,64,128]{2,1,0:T(8,128)(2,1)}, bf16[16,64,128]{2,1,0:T(8,128)(2,1)}, u32[]{:S(2)}, u32[]{:S(2)}) collective-permute-start(bf16[16,64,128]{2,1,0:T(8,128)(2,1)} %collective-permute-done.15.refs_2_), channel_id=1, source_target_pairs={{0,2},{2,0},{4,6},{6,4},{8,10},{10,8},{12,14},{14,12},{16,18},{18,... | collective-permute-start | bytes 786440 | tf_op jit(solution)/shard_map/ppermute | solution.py:143
  80.8 0.0 collective-permute-start.12
  80.8 0.5 collective-permute-start.8
  81.3 0.7 pad_add_fusion
  82.0 0.1 copy.10
  82.1 0.1 reshape.7
  82.1 0.1 pad_add_fusion.1.where_ref
  82.2 0.1 broadcast_in_dim.5.bands_ref
  82.3 1.0 copy-done.11
  83.3 0.9 copy-done.13
  84.2 0.9 copy-done.15
  85.2 0.9 copy-done.17
  86.1 4.0 %cross.6.refs_4_ = f32[2,4,4,128,128]{4,3,2,1,0:T(8,128)} custom-call(s32[9]{0:T(128)S(1)} %pad_add_fusion.1.where_ref, f32[4]{0:T(128)S(1)} %multiply_sqrt_fusion.norm_ref, bf16[4,256,1536]{2,1,0:T(8,128)(2,1)S(1)} %get-tuple-element.7.left_ref, s32[64,128]{1,0:T(8,128)S(1)} %broadcast_in_dim.5.bands_ref, f32[4,64,128]{2,1,0:T(8,128)S(1)} %pad_maximum_fusion.scales_ref, ...), custom_call_target="tpu_custom_call" | custom-call | tf_op jit(solution)/shard_map/cross/pallas_call | solution.py:191
  90.1 5.3 %cross.7.refs_4_ = f32[2,4,4,128,128]{4,3,2,1,0:T(8,128)} custom-call(s32[9]{0:T(128)S(1)} %pad_add_fusion.1.where_ref, f32[4]{0:T(128)S(1)} %multiply_sqrt_fusion.norm_ref, bf16[4,256,1536]{2,1,0:T(8,128)(2,1)S(1)} %get-tuple-element.7.left_ref, s32[64,128]{1,0:T(8,128)S(1)} %broadcast_in_dim.5.bands_ref, ...), custom_call_target="tpu_custom_call", output_to_operand_aliasing={{}: (9, {})} | custom-call | tf_op jit(solution)/shard_map/cross/pallas_call | solution.py:191
  95.5 5.3 %cross.8.refs_4_ = f32[2,4,4,128,128]{4,3,2,1,0:T(8,128)} custom-call(s32[9]{0:T(128)S(1)} %pad_add_fusion.1.where_ref, f32[4]{0:T(128)S(1)} %multiply_sqrt_fusion.norm_ref, bf16[4,256,1536]{2,1,0:T(8,128)(2,1)S(1)} %get-tuple-element.7.left_ref, s32[64,128]{1,0:T(8,128)S(1)} %broadcast_in_dim.5.bands_ref, ...), custom_call_target="tpu_custom_call", output_to_operand_aliasing={{}: (9, {})} | custom-call | tf_op jit(solution)/shard_map/cross/pallas_call | solution.py:191
  100.8 5.3 %cross.9.refs_4_ = f32[2,4,4,128,128]{4,3,2,1,0:T(8,128)} custom-call(s32[9]{0:T(128)S(1)} %pad_add_fusion.1.where_ref, f32[4]{0:T(128)S(1)} %multiply_sqrt_fusion.norm_ref, bf16[4,256,1536]{2,1,0:T(8,128)(2,1)S(1)} %get-tuple-element.7.left_ref, s32[64,128]{1,0:T(8,128)S(1)} %broadcast_in_dim.5.bands_ref, ...), custom_call_target="tpu_custom_call", output_to_operand_aliasing={{}: (9, {})} | custom-call | tf_op jit(solution)/shard_map/cross/pallas_call | solution.py:191
  106.2 5.3 %cross.10.refs_4_ = f32[2,4,4,128,128]{4,3,2,1,0:T(8,128)} custom-call(s32[9]{0:T(128)S(1)} %pad_add_fusion.1.where_ref, f32[4]{0:T(128)S(1)} %multiply_sqrt_fusion.norm_ref, bf16[4,256,1536]{2,1,0:T(8,128)(2,1)S(1)} %get-tuple-element.7.left_ref, s32[64,128]{1,0:T(8,128)S(1)} %broadcast_in_dim.5.bands_ref, ...), custom_call_target="tpu_custom_call", output_to_operand_aliasing={{}: (9, {})} | custom-call | tf_op jit(solution)/shard_map/cross/pallas_call | solution.py:191
  111.5 5.4 %cross.11 = f32[2,4,4,128,128]{4,3,2,1,0:T(8,128)} custom-call(s32[9]{0:T(128)S(1)} %pad_add_fusion.1.where_ref, f32[4]{0:T(128)S(1)} %multiply_sqrt_fusion.norm_ref, bf16[4,256,1536]{2,1,0:T(8,128)(2,1)S(1)} %get-tuple-element.7.left_ref, s32[64,128]{1,0:T(8,128)S(1)} %broadcast_in_dim.5.bands_ref, ...), custom_call_target="tpu_custom_call", output_to_operand_aliasing={{}: (9, {})} | custom-call | tf_op jit(solution)/shard_map/cross/pallas_call | solution.py:191
  (57 shorter events, 0.1 us)
Async XLA Ops:
  1.7 10.7 %collective-permute-start.25 = (bf16[16,64,128]{2,1,0:T(8,128)(2,1)}, bf16[16,64,128]{2,1,0:T(8,128)(2,1)S(1)}, u32[]{:S(2)}, u32[]{:S(2)}) collective-permute-start(bf16[16,64,128]{2,1,0:T(8,128)(2,1)} %slice.47), channel_id=1, source_target_pairs={{0,8},{2,10},{4,12},{6,14},{8,16},{10,18},{12,20},{14,22},{16,24},... | collective-permute-start | bytes 786440 | tf_op jit(solution)/shard_map/ppermute | solution.py:140
  3.8 1.4 %copy-start = (bf16[2,48,64,128]{3,2,1,0:T(8,128)(2,1)S(1)}, bf16[2,48,64,128]{3,2,1,0:T(8,128)(2,1)}, u32[]{:S(2)}) copy-start(bf16[2,48,64,128]{3,2,1,0:T(8,128)(2,1)} %param.2) | copy-start | bytes 4718596
  5.6 2.8 %collective-permute-start = (f32[4,128]{1,0:T(4,128)S(1)}, f32[4,128]{1,0:T(4,128)S(1)}, u32[]{:S(2)}, u32[]{:S(2)}) collective-permute-start(f32[4,128]{1,0:T(4,128)S(1)} %slice_select_fusion), channel_id=1, source_target_pairs={{0,1},{1,0},{2,3},{3,2},{4,5},{5,4},{6,7},{7,6},{8,9},{9,8},{10,11... | collective-permute-start | bytes 6152 | tf_op jit(solution)/shard_map/ppermute | solution.py:157
  8.4 1.4 %copy-start.1 = (bf16[2,48,64,128]{3,2,1,0:T(8,128)(2,1)S(1)}, bf16[2,48,64,128]{3,2,1,0:T(8,128)(2,1)}, u32[]{:S(2)}) copy-start(bf16[2,48,64,128]{3,2,1,0:T(8,128)(2,1)} %param.2) | copy-start | bytes 4718596
  11.0 4.6 %collective-permute-start.1 = (f32[64,128]{1,0:T(8,128)S(1)}, f32[64,128]{1,0:T(8,128)S(1)}, u32[]{:S(2)}, u32[]{:S(2)}) collective-permute-start(f32[64,128]{1,0:T(8,128)S(1)} %get-tuple-element.8), channel_id=1, source_target_pairs={{0,8},{2,10},{4,12},{6,14},{8,16},{10,18},{12,20},{14,22},{16,24},... | collective-permute-start | bytes 98312 | tf_op jit(solution)/shard_map/ppermute | solution.py:140
  12.4 6.7 %copy-start.10 = (bf16[16,64,128]{2,1,0:T(8,128)(2,1)}, bf16[16,64,128]{2,1,0:T(8,128)(2,1)S(1)}, u32[]{:S(2)}) copy-start(bf16[16,64,128]{2,1,0:T(8,128)(2,1)S(1)} %collective-permute-done.25.refs_3_) | copy-start | bytes 786436
  12.5 8.3 %collective-permute-start.27 = (bf16[16,64,128]{2,1,0:T(8,128)(2,1)S(1)}, bf16[16,64,128]{2,1,0:T(8,128)(2,1)S(1)}, u32[]{:S(2)}, u32[]{:S(2)}) collective-permute-start(bf16[16,64,128]{2,1,0:T(8,128)(2,1)S(1)} %get-tuple-element.9), channel_id=1, source_target_pairs={{0,4},{2,6},{4,0},{6,2},{8,12},{10,14},{12,8},{14,10},{16,20},{18,... | collective-permute-start | bytes 786440 | tf_op jit(solution)/shard_map/ppermute | solution.py:141
  15.6 3.5 %collective-permute-start.3 = (f32[64,128]{1,0:T(8,128)S(1)}, f32[64,128]{1,0:T(8,128)S(1)}, u32[]{:S(2)}, u32[]{:S(2)}) collective-permute-start(f32[64,128]{1,0:T(8,128)S(1)} %get-tuple-element.35), channel_id=1, source_target_pairs={{0,4},{2,6},{4,0},{6,2},{8,12},{10,14},{12,8},{14,10},{16,20},{18,... | collective-permute-start | bytes 98312 | tf_op jit(solution)/shard_map/ppermute | solution.py:141
  17.0 7.0 %collective-permute-start.13 = (bf16[16,64,128]{2,1,0:T(8,128)(2,1)S(1)}, bf16[16,64,128]{2,1,0:T(8,128)(2,1)S(1)}, u32[]{:S(2)}, u32[]{:S(2)}) collective-permute-start(bf16[16,64,128]{2,1,0:T(8,128)(2,1)S(1)} %get-tuple-element.23), channel_id=1, source_target_pairs={{0,8},{2,10},{4,12},{6,14},{8,16},{10,18},{12,20},{14,22},{16,24},... | collective-permute-start | bytes 786440 | tf_op jit(solution)/shard_map/ppermute | solution.py:140
  17.0 14.3 %collective-permute-start.17 = (bf16[16,64,128]{2,1,0:T(8,128)(2,1)S(1)}, bf16[16,64,128]{2,1,0:T(8,128)(2,1)S(1)}, u32[]{:S(2)}, u32[]{:S(2)}) collective-permute-start(bf16[16,64,128]{2,1,0:T(8,128)(2,1)S(1)} %get-tuple-element.22), channel_id=1, source_target_pairs={{0,8},{2,10},{4,12},{6,14},{8,16},{10,18},{12,20},{14,22},{16,24},... | collective-permute-start | bytes 786440 | tf_op jit(solution)/shard_map/ppermute | solution.py:140
  17.8 19.1 %collective-permute-start.21 = (bf16[16,64,128]{2,1,0:T(8,128)(2,1)S(1)}, bf16[16,64,128]{2,1,0:T(8,128)(2,1)S(1)}, u32[]{:S(2)}, u32[]{:S(2)}) collective-permute-start(bf16[16,64,128]{2,1,0:T(8,128)(2,1)S(1)} %get-tuple-element.21), channel_id=1, source_target_pairs={{0,8},{2,10},{4,12},{6,14},{8,16},{10,18},{12,20},{14,22},{16,24},... | collective-permute-start | bytes 786440 | tf_op jit(solution)/shard_map/ppermute | solution.py:140
  19.1 23.4 %collective-permute-start.5 = (bf16[16,64,128]{2,1,0:T(8,128)(2,1)S(1)}, bf16[16,64,128]{2,1,0:T(8,128)(2,1)S(1)}, u32[]{:S(2)}, u32[]{:S(2)}) collective-permute-start(bf16[16,64,128]{2,1,0:T(8,128)(2,1)S(1)} %get-tuple-element.25), channel_id=1, source_target_pairs={{0,8},{2,10},{4,12},{6,14},{8,16},{10,18},{12,20},{14,22},{16,24},... | collective-permute-start | bytes 786440 | tf_op jit(solution)/shard_map/ppermute | solution.py:140
  20.8 27.9 %copy-start.12 = (bf16[16,64,128]{2,1,0:T(8,128)(2,1)}, bf16[16,64,128]{2,1,0:T(8,128)(2,1)S(1)}, u32[]{:S(2)}) copy-start(bf16[16,64,128]{2,1,0:T(8,128)(2,1)S(1)} %collective-permute-done.27.refs_2_) | copy-start | bytes 786436
  20.8 26.3 %collective-permute-start.9 = (bf16[16,64,128]{2,1,0:T(8,128)(2,1)S(1)}, bf16[16,64,128]{2,1,0:T(8,128)(2,1)S(1)}, u32[]{:S(2)}, u32[]{:S(2)}) collective-permute-start(bf16[16,64,128]{2,1,0:T(8,128)(2,1)S(1)} %get-tuple-element.24), channel_id=1, source_target_pairs={{0,8},{2,10},{4,12},{6,14},{8,16},{10,18},{12,20},{14,22},{16,24},... | collective-permute-start | bytes 786440 | tf_op jit(solution)/shard_map/ppermute | solution.py:140
  24.0 24.8 %copy-start.2 = (bf16[16,64,128]{2,1,0:T(8,128)(2,1)}, bf16[16,64,128]{2,1,0:T(8,128)(2,1)S(1)}, u32[]{:S(2)}) copy-start(bf16[16,64,128]{2,1,0:T(8,128)(2,1)S(1)} %collective-permute-done.13.refs_3_) | copy-start | bytes 786436
  24.0 25.1 %collective-permute-start.2 = (f32[64,128]{1,0:T(8,128)S(1)}, f32[64,128]{1,0:T(8,128)S(1)}, u32[]{:S(2)}, u32[]{:S(2)}) collective-permute-start(f32[64,128]{1,0:T(8,128)S(1)} %get-tuple-element.34), channel_id=1, source_target_pairs={{0,2},{2,0},{4,6},{6,4},{8,10},{10,8},{12,14},{14,12},{16,18},{18,... | collective-permute-start | bytes 98312 | tf_op jit(solution)/shard_map/ppermute | solution.py:142
  31.2 17.5 %copy-start.6 = (bf16[16,64,128]{2,1,0:T(8,128)(2,1)}, bf16[16,64,128]{2,1,0:T(8,128)(2,1)S(1)}, u32[]{:S(2)}) copy-start(bf16[16,64,128]{2,1,0:T(8,128)(2,1)S(1)} %collective-permute-done.17.refs_3_) | copy-start | bytes 786436
  31.2 20.9 %collective-permute-start.4 = (f32[64,128]{1,0:T(8,128)S(1)}, f32[64,128]{1,0:T(8,128)S(1)}, u32[]{:S(2)}, u32[]{:S(2)}) collective-permute-start(f32[64,128]{1,0:T(8,128)S(1)} %collective-permute-done.3), channel_id=1, source_target_pairs={{0,2},{2,0},{4,6},{6,4},{8,10},{10,8},{12,14},{14,12},{16,18},{18,... | collective-permute-start | bytes 98312 | tf_op jit(solution)/shard_map/ppermute | solution.py:143
  36.9 11.9 %copy-start.8 = (bf16[16,64,128]{2,1,0:T(8,128)(2,1)}, bf16[16,64,128]{2,1,0:T(8,128)(2,1)S(1)}, u32[]{:S(2)}) copy-start(bf16[16,64,128]{2,1,0:T(8,128)(2,1)S(1)} %collective-permute-done.21.refs_3_) | copy-start | bytes 786436
  36.9 18.5 %copy-start.18 = (s32[64]{0:T(128)S(1)}, s32[64]{0:T(128)}, u32[]{:S(2)}) copy-start(s32[64]{0:T(128)} %param.3) | copy-start | bytes 772
  36.9 16.5 %collective-permute-start.26 = (bf16[16,64,128]{2,1,0:T(8,128)(2,1)S(1)}, bf16[16,64,128]{2,1,0:T(8,128)(2,1)S(1)}, u32[]{:S(2)}, u32[]{:S(2)}) collective-permute-start(bf16[16,64,128]{2,1,0:T(8,128)(2,1)S(1)} %get-tuple-element.10), channel_id=1, source_target_pairs={{0,2},{2,0},{4,6},{6,4},{8,10},{10,8},{12,14},{14,12},{16,18},{18,... | collective-permute-start | bytes 786440 | tf_op jit(solution)/shard_map/ppermute | solution.py:142
  42.5 12.0 %collective-permute-start.28 = (bf16[16,64,128]{2,1,0:T(8,128)(2,1)S(1)}, bf16[16,64,128]{2,1,0:T(8,128)(2,1)S(1)}, u32[]{:S(2)}, u32[]{:S(2)}) collective-permute-start(bf16[16,64,128]{2,1,0:T(8,128)(2,1)S(1)} %collective-permute-done.27.refs_2_), channel_id=1, source_target_pairs={{0,2},{2,0},{4,6},{6,4},{8,10},{10,8},{12,14},{14,12},{16,18},{18,... | collective-permute-start | bytes 786440 | tf_op jit(solution)/shard_map/ppermute | solution.py:143
  47.1 1.6 %copy-start.4 = (bf16[16,64,128]{2,1,0:T(8,128)(2,1)}, bf16[16,64,128]{2,1,0:T(8,128)(2,1)S(1)}, u32[]{:S(2)}) copy-start(bf16[16,64,128]{2,1,0:T(8,128)(2,1)S(1)} %collective-permute-done.9.refs_3_) | copy-start | bytes 786436
  48.8 6.7 %collective-permute-start.23 = (bf16[16,64,128]{2,1,0:T(8,128)(2,1)}, bf16[16,64,128]{2,1,0:T(8,128)(2,1)}, u32[]{:S(2)}, u32[]{:S(2)}) collective-permute-start(bf16[16,64,128]{2,1,0:T(8,128)(2,1)} %get-tuple-element.11), channel_id=1, source_target_pairs={{0,4},{2,6},{4,0},{6,2},{8,12},{10,14},{12,8},{14,10},{16,20},{18,... | collective-permute-start | bytes 786440 | tf_op jit(solution)/shard_map/ppermute | solution.py:141
  49.1 12.0 %collective-permute-start.22 = (bf16[16,64,128]{2,1,0:T(8,128)(2,1)}, bf16[16,64,128]{2,1,0:T(8,128)(2,1)}, u32[]{:S(2)}, u32[]{:S(2)}) collective-permute-start(bf16[16,64,128]{2,1,0:T(8,128)(2,1)} %get-tuple-element.12), channel_id=1, source_target_pairs={{0,2},{2,0},{4,6},{6,4},{8,10},{10,8},{12,14},{14,12},{16,18},{18,... | collective-permute-start | bytes 786440 | tf_op jit(solution)/shard_map/ppermute | solution.py:142
  52.1 8.9 %collective-permute-start.19 = (bf16[16,64,128]{2,1,0:T(8,128)(2,1)}, bf16[16,64,128]{2,1,0:T(8,128)(2,1)}, u32[]{:S(2)}, u32[]{:S(2)}) collective-permute-start(bf16[16,64,128]{2,1,0:T(8,128)(2,1)} %get-tuple-element.31), channel_id=1, source_target_pairs={{0,4},{2,6},{4,0},{6,2},{8,12},{10,14},{12,8},{14,10},{16,20},{18,... | collective-permute-start | bytes 786440 | tf_op jit(solution)/shard_map/ppermute | solution.py:141
  53.4 0.7 copy-start.14
  54.1 8.4 %collective-permute-start.18 = (bf16[16,64,128]{2,1,0:T(8,128)(2,1)}, bf16[16,64,128]{2,1,0:T(8,128)(2,1)}, u32[]{:S(2)}, u32[]{:S(2)}) collective-permute-start(bf16[16,64,128]{2,1,0:T(8,128)(2,1)} %get-tuple-element.30), channel_id=1, source_target_pairs={{0,2},{2,0},{4,6},{6,4},{8,10},{10,8},{12,14},{14,12},{16,18},{18,... | collective-permute-start | bytes 786440 | tf_op jit(solution)/shard_map/ppermute | solution.py:142
  54.5 0.7 copy-start.16
  55.2 11.5 %collective-permute-start.15 = (bf16[16,64,128]{2,1,0:T(8,128)(2,1)}, bf16[16,64,128]{2,1,0:T(8,128)(2,1)}, u32[]{:S(2)}, u32[]{:S(2)}) collective-permute-start(bf16[16,64,128]{2,1,0:T(8,128)(2,1)} %get-tuple-element.29), channel_id=1, source_target_pairs={{0,4},{2,6},{4,0},{6,2},{8,12},{10,14},{12,8},{14,10},{16,20},{18,... | collective-permute-start | bytes 786440 | tf_op jit(solution)/shard_map/ppermute | solution.py:141
  55.4 17.7 %collective-permute-start.14 = (bf16[16,64,128]{2,1,0:T(8,128)(2,1)}, bf16[16,64,128]{2,1,0:T(8,128)(2,1)}, u32[]{:S(2)}, u32[]{:S(2)}) collective-permute-start(bf16[16,64,128]{2,1,0:T(8,128)(2,1)} %get-tuple-element.28), channel_id=1, source_target_pairs={{0,2},{2,0},{4,6},{6,4},{8,10},{10,8},{12,14},{14,12},{16,18},{18,... | collective-permute-start | bytes 786440 | tf_op jit(solution)/shard_map/ppermute | solution.py:142
  61.1 12.1 %collective-permute-start.11 = (bf16[16,64,128]{2,1,0:T(8,128)(2,1)}, bf16[16,64,128]{2,1,0:T(8,128)(2,1)}, u32[]{:S(2)}, u32[]{:S(2)}) collective-permute-start(bf16[16,64,128]{2,1,0:T(8,128)(2,1)} %get-tuple-element.27), channel_id=1, source_target_pairs={{0,4},{2,6},{4,0},{6,2},{8,12},{10,14},{12,8},{14,10},{16,20},{18,... | collective-permute-start | bytes 786440 | tf_op jit(solution)/shard_map/ppermute | solution.py:141
  61.1 16.8 %collective-permute-start.7 = (bf16[16,64,128]{2,1,0:T(8,128)(2,1)}, bf16[16,64,128]{2,1,0:T(8,128)(2,1)}, u32[]{:S(2)}, u32[]{:S(2)}) collective-permute-start(bf16[16,64,128]{2,1,0:T(8,128)(2,1)} %get-tuple-element.33), channel_id=1, source_target_pairs={{0,4},{2,6},{4,0},{6,2},{8,12},{10,14},{12,8},{14,10},{16,20},{18,... | collective-permute-start | bytes 786440 | tf_op jit(solution)/shard_map/ppermute | solution.py:141
  62.5 18.2 %collective-permute-start.24 = (bf16[16,64,128]{2,1,0:T(8,128)(2,1)}, bf16[16,64,128]{2,1,0:T(8,128)(2,1)}, u32[]{:S(2)}, u32[]{:S(2)}) collective-permute-start(bf16[16,64,128]{2,1,0:T(8,128)(2,1)} %collective-permute-done.23.refs_2_), channel_id=1, source_target_pairs={{0,2},{2,0},{4,6},{6,4},{8,10},{10,8},{12,14},{14,12},{16,18},{18,... | collective-permute-start | bytes 786440 | tf_op jit(solution)/shard_map/ppermute | solution.py:143
  66.7 14.1 %collective-permute-start.20 = (bf16[16,64,128]{2,1,0:T(8,128)(2,1)}, bf16[16,64,128]{2,1,0:T(8,128)(2,1)}, u32[]{:S(2)}, u32[]{:S(2)}) collective-permute-start(bf16[16,64,128]{2,1,0:T(8,128)(2,1)} %collective-permute-done.19.refs_2_), channel_id=1, source_target_pairs={{0,2},{2,0},{4,6},{6,4},{8,10},{10,8},{12,14},{14,12},{16,18},{18,... | collective-permute-start | bytes 786440 | tf_op jit(solution)/shard_map/ppermute | solution.py:143
  73.1 33.0 %collective-permute-start.10 = (bf16[16,64,128]{2,1,0:T(8,128)(2,1)}, bf16[16,64,128]{2,1,0:T(8,128)(2,1)}, u32[]{:S(2)}, u32[]{:S(2)}) collective-permute-start(bf16[16,64,128]{2,1,0:T(8,128)(2,1)} %get-tuple-element.26), channel_id=1, source_target_pairs={{0,2},{2,0},{4,6},{6,4},{8,10},{10,8},{12,14},{14,12},{16,18},{18,... | collective-permute-start | bytes 786440 | tf_op jit(solution)/shard_map/ppermute | solution.py:142
  73.2 38.3 %collective-permute-start.6 = (bf16[16,64,128]{2,1,0:T(8,128)(2,1)}, bf16[16,64,128]{2,1,0:T(8,128)(2,1)}, u32[]{:S(2)}, u32[]{:S(2)}) collective-permute-start(bf16[16,64,128]{2,1,0:T(8,128)(2,1)} %get-tuple-element.32), channel_id=1, source_target_pairs={{0,2},{2,0},{4,6},{6,4},{8,10},{10,8},{12,14},{14,12},{16,18},{18,... | collective-permute-start | bytes 786440 | tf_op jit(solution)/shard_map/ppermute | solution.py:142
  77.9 22.9 %collective-permute-start.16 = (bf16[16,64,128]{2,1,0:T(8,128)(2,1)}, bf16[16,64,128]{2,1,0:T(8,128)(2,1)}, u32[]{:S(2)}, u32[]{:S(2)}) collective-permute-start(bf16[16,64,128]{2,1,0:T(8,128)(2,1)} %collective-permute-done.15.refs_2_), channel_id=1, source_target_pairs={{0,2},{2,0},{4,6},{6,4},{8,10},{10,8},{12,14},{14,12},{16,18},{18,... | collective-permute-start | bytes 786440 | tf_op jit(solution)/shard_map/ppermute | solution.py:143
  80.8 25.4 %collective-permute-start.12 = (bf16[16,64,128]{2,1,0:T(8,128)(2,1)}, bf16[16,64,128]{2,1,0:T(8,128)(2,1)}, u32[]{:S(2)}, u32[]{:S(2)}) collective-permute-start(bf16[16,64,128]{2,1,0:T(8,128)(2,1)} %collective-permute-done.11.refs_2_), channel_id=1, source_target_pairs={{0,2},{2,0},{4,6},{6,4},{8,10},{10,8},{12,14},{14,12},{16,18},{18,... | collective-permute-start | bytes 786440 | tf_op jit(solution)/shard_map/ppermute | solution.py:143
  80.8 30.7 %collective-permute-start.8 = (bf16[16,64,128]{2,1,0:T(8,128)(2,1)}, bf16[16,64,128]{2,1,0:T(8,128)(2,1)}, u32[]{:S(2)}, u32[]{:S(2)}) collective-permute-start(bf16[16,64,128]{2,1,0:T(8,128)(2,1)} %collective-permute-done.7.refs_2_), channel_id=1, source_target_pairs={{0,2},{2,0},{4,6},{6,4},{8,10},{10,8},{12,14},{14,12},{16,18},{18,... | collective-permute-start | bytes 786440 | tf_op jit(solution)/shard_map/ppermute | solution.py:143
  82.3 1.0 copy-start.11
  83.3 0.9 copy-start.13
  84.2 0.9 copy-start.15
  85.2 0.9 copy-start.17
  86.1 4.0 %copy-start.9 = (bf16[16,64,128]{2,1,0:T(8,128)(2,1)S(1)}, bf16[16,64,128]{2,1,0:T(8,128)(2,1)}, u32[]{:S(2)}) copy-start(bf16[16,64,128]{2,1,0:T(8,128)(2,1)} %copy-done.8) | copy-start | bytes 786436
  90.1 5.3 %copy-start.7 = (bf16[16,64,128]{2,1,0:T(8,128)(2,1)S(1)}, bf16[16,64,128]{2,1,0:T(8,128)(2,1)}, u32[]{:S(2)}) copy-start(bf16[16,64,128]{2,1,0:T(8,128)(2,1)} %copy-done.6) | copy-start | bytes 786436
  95.5 5.3 %copy-start.3 = (bf16[16,64,128]{2,1,0:T(8,128)(2,1)S(1)}, bf16[16,64,128]{2,1,0:T(8,128)(2,1)}, u32[]{:S(2)}) copy-start(bf16[16,64,128]{2,1,0:T(8,128)(2,1)} %copy-done.2) | copy-start | bytes 786436
  100.8 5.4 %copy-start.5 = (bf16[16,64,128]{2,1,0:T(8,128)(2,1)S(1)}, bf16[16,64,128]{2,1,0:T(8,128)(2,1)}, u32[]{:S(2)}) copy-start(bf16[16,64,128]{2,1,0:T(8,128)(2,1)} %copy-done.4) | copy-start | bytes 786436
where the time goes:
time: 117 us
  starting transfers between devices  63.3 us (54%)
  Pallas kernels  32.3 us (28%)
  local copies, waits for them, and re-layouts  10.7 us (9%)
  waiting for transfers between devices  7.77 us (7%)
  other arithmetic  2.67 us (2%)
    pallas_call x6, Pallas kernels, shards(): pl.pallas_call(functools.partial(cross_kernel, k * size, first, last), ou...  30.7 us
    ppermute x7, starting transfers between devices, spread(): mixed = lax.ppermute(jnp.where(core == 0, value, two), 'ch', mate)  26.7 us
    ppermute x7, starting transfers between devices, spread(): other = lax.ppermute(one, 'ch', mate)  23.4 us
    unnamed x38, local copies, waits for them, and re-layouts  8.09 us
    ppermute x7, starting transfers between devices, spread(): two = lax.ppermute(value, 'ch', ahead)  6.06 us
    ppermute x7, starting transfers between devices, spread(): one = lax.ppermute(jnp.where(odd_chip == 1, two, value), 'ch', beside)  5.83 us
    ppermute x7, waiting for transfers between devices, spread(): two = lax.ppermute(value, 'ch', ahead)  4.95 us
  transfers between devices with their start and end apart: 29, of which 4 were waited for; matrix products, arithmetic and copies ran while one was open for 3% of the time, Pallas kernels for 23%

commit v1 on v0

v1 whole, which is shorter than its diff:
```python
import functools

import jax
import jax.numpy as jnp
from jax import lax
from jax.experimental import pallas as pl
from jax.experimental.pallas import tpu as pltpu
from jax.sharding import PartitionSpec as P

BANDS = 8
ROUNDS = 4
SMOOTH = 4
EPS = 1e-06

GROUP = 16
PIECE = 8
RAW = 3
TERMS = 3
DEPTH = 2
AHEAD = 2
CHAIN = 1
SETS = (4, 4, 2, 1, 1)
SEND_AFTER = (5, 10, 12, 12, 12)
CROSS_BEFORE = (9, 11, 12, 12, 12)
VMEM_LIMIT = 16 * 1024 * 1024


def vmem():
    return pl.BlockSpec(memory_space=pltpu.VMEM)


def smem():
    return pl.BlockSpec(memory_space=pltpu.SMEM)


def call(kernel, name, out_shape, in_specs, flops, moved, **more):
    return pl.pallas_call(
        kernel,
        out_shape=out_shape,
        in_specs=in_specs,
        out_specs=jax.tree.map(lambda _: vmem(), out_shape),
        compiler_params=pltpu.CompilerParams(vmem_limit_bytes=VMEM_LIMIT),
        cost_estimate=pl.CostEstimate(flops=flops, bytes_accessed=moved, transcendentals=0),
        name=name,
        **more,
    )


def power_kernel(x_ref, power_ref, edge_ref, *pieces):
    rows, width, _ = x_ref.shape
    for index, piece in enumerate(pieces):
        piece[...] = x_ref[index * PIECE : (index + 1) * PIECE]

    def step(i, total):
        value = x_ref[i].astype(jnp.float32)
        return total + value * value

    total = lax.fori_loop(0, rows, step, jnp.zeros(power_ref.shape, jnp.float32), unroll=8)
    power = total / (rows // 2)
    power_ref[...] = power
    low = lax.axis_index("fq") == 0
    edge_ref[...] = jnp.where(low, power[width - SMOOTH :], power[:SMOOTH])


def left_kernel(x_ref, power_ref, halo_ref, left_ref, *refs):
    pieces, padded = refs[:-1], refs[-1]
    fq = lax.axis_index("fq")
    rows, width, channels = x_ref.shape
    bin_total = width * lax.axis_size("fq")
    padded[...] = jnp.zeros_like(padded)
    padded[8 : 8 + width, :] = power_ref[...]

    @pl.when(fq > 0)
    def _():
        padded[8 - SMOOTH : 8, :] = halo_ref[...]

    @pl.when(fq == 0)
    def _():
        padded[8 + width : 8 + width + SMOOTH, :] = halo_ref[...]

    total = padded[8 - SMOOTH : 8 - SMOOTH + width, :]
    for offset in range(1, 2 * SMOOTH + 1):
        total = total + padded[8 - SMOOTH + offset : 8 - SMOOTH + offset + width, :]
    bins = fq * width + lax.broadcasted_iota(jnp.int32, (width, channels), 0)
    counts = jnp.minimum(bins + SMOOTH, bin_total - 1) - jnp.maximum(bins - SMOOTH, 0) + 1
    scale = lax.rsqrt(total / counts.astype(jnp.float32) + EPS)
    rest = scale
    for term in range(TERMS):
        part = rest.astype(jnp.bfloat16)
        pieces[0][PIECE + term] = part
        rest = rest - part.astype(jnp.float32)

    step = 2 * PIECE
    span = step * GROUP
    steps = rows // step
    for group in range(width // GROUP):
        here = slice(group * GROUP, (group + 1) * GROUP)
        for index in range(steps):
            raw = x_ref[index * step : (index + 1) * step, here, :].astype(jnp.float32)
            white = (raw * scale[here][None]).astype(jnp.bfloat16)
            for half in range(2):
                piece = 2 * index + half - RAW
                if piece >= 0:
                    pieces[piece][:PIECE, here, :] = white[half * PIECE : (half + 1) * PIECE]
            turned = white.reshape(span, channels).T
            left_ref[group, :channels, index * span : (index + 1) * span] = turned
            if index < steps // 2:
                there = index + steps // 2
                turned = -turned
            else:
                there = index - steps // 2
            left_ref[group, channels:, there * span : (there + 1) * span] = turned


def cross_kernel(start, pieces, first, bounds_ref, norm_ref, left_ref, mate_ref, *refs):
    count = len(pieces)
    ones, twos = refs[:count], refs[count : 2 * count]
    out_ref = refs[-1]
    core = lax.axis_index("ch") % 2
    rounds = (2 - 2 * core, 2 * core, 1, 3)
    offsets = [sum(pieces[:k]) for k in range(count)]
    held = sum(pieces)
    rights = [
        [(mate_ref, offset) for offset in offsets],
        [(mate_ref, held + offset) for offset in offsets],
        [(ref, 0) for ref in ones],
        [(ref, 0) for ref in twos],
    ]
    width, channels = mate_ref.shape[1:]
    lanes = slice(start * GROUP, (start + count * PIECE) * GROUP)
    span = count * PIECE * GROUP

    if first:
        out_ref[...] = jnp.zeros_like(out_ref)
    else:
        out_ref[...] = refs[2 * count][...]

    def column(right, here):
        scale = None
        if first:
            ref, offset = right[RAW]
            for term in range(TERMS):
                part = ref[offset + PIECE + term, here, :].astype(jnp.float32)
                scale = part if scale is None else scale + part
        blocks = []
        for index, (ref, offset) in enumerate(right):
            block = ref[offset : offset + PIECE, here, :]
            if first and index < RAW:
                block = (block.astype(jnp.float32) * scale[None]).astype(jnp.bfloat16)
            blocks.append(block.reshape(PIECE * GROUP, channels))
        return jnp.concatenate(blocks, axis=0)

    def add(group, here, band, low, high):
        bins = group * GROUP + lax.broadcasted_iota(jnp.int32, (1, span), 1) % GROUP
        inside = ((bins >= low) & (bins < high)).astype(jnp.float32).astype(jnp.bfloat16)
        left = left_ref[group, :, lanes] * inside
        columns = jnp.concatenate([column(right, here) for right in rights], axis=1)
        product = jnp.dot(left, columns, preferred_element_type=jnp.float32)
        product = product / norm_ref[band]
        for index, turn in enumerate(rounds):
            part = slice(index * channels, (index + 1) * channels)
            out_ref[0, turn, band] += product[:channels, part]
            out_ref[1, turn, band] += product[channels:, part]

    bands = out_ref.shape[2]
    for group in range(width // GROUP):
        band = sum((bounds_ref[k] <= group * GROUP).astype(jnp.int32) for k in range(1, bands))
        here = slice(group * GROUP, (group + 1) * GROUP)
        add(group, here, band, bounds_ref[band], bounds_ref[band + 1])
    for band in range(1, bands):
        low, high = bounds_ref[band], bounds_ref[band + 1]

        @pl.when(low % GROUP != 0)
        def _():
            group = low // GROUP
            add(group, pl.ds(pl.multiple_of(group * GROUP, GROUP), GROUP), band, low, high)


def shards(spectra, band_ids):
    parts, windows, width, channels = spectra.shape
    rows = parts * windows
    count = lax.axis_size("ch")
    fq_count = lax.axis_size("fq")
    index = lax.axis_index("ch")
    fq = lax.axis_index("fq")
    even_core = index % 2 == 0
    odd_chip = (index // 2) % 2 == 1

    ahead = [(i, (i + 4) % count) for i in range(count)]
    beside = [(i, i ^ 2) for i in range(count)]
    mate = [(i, i ^ 1) for i in range(count)]

    own = spectra.reshape(rows, width, channels)
    total_pieces = rows // PIECE
    heights = [PIECE + (TERMS if k == RAW else 0) for k in range(total_pieces)]
    block = jax.ShapeDtypeStruct((width, channels), jnp.float32)
    edge = jax.ShapeDtypeStruct((SMOOTH, channels), jnp.float32)
    held = [jax.ShapeDtypeStruct((h, width, channels), jnp.bfloat16) for h in heights]
    groups = width // GROUP
    left_shape = jax.ShapeDtypeStruct((groups, 2 * channels, rows * GROUP), jnp.bfloat16)
    nbytes = rows * width * channels * 2

    power, edge, *early = call(
        power_kernel, "power", (block, edge, *held[:RAW]), [vmem()], 3 * nbytes, nbytes
    )(own)
    halo = lax.ppermute(edge, "fq", [(0, 1), (1, 0)])
    left, *late = call(
        left_kernel,
        "left",
        (left_shape, *held[RAW:]),
        [vmem()] * 3,
        3 * nbytes,
        4 * nbytes,
        scratch_shapes=[pltpu.VMEM((width + 16, channels), jnp.float32)],
    )(own, power, halo)
    mine = early + late

    band_width = BANDS // fq_count
    local_band = band_ids - fq * band_width
    below = local_band[:, None] < jnp.arange(band_width + 1, dtype=jnp.int32)[None, :]
    bounds = jnp.sum(below.astype(jnp.int32), axis=0)
    norms = jnp.sqrt(windows * (bounds[1:] - bounds[:-1]).astype(jnp.float32))

    shape = jax.ShapeDtypeStruct((2, ROUNDS, band_width, channels, channels), jnp.float32)

    def after(value, other):
        return lax.optimization_barrier((value, other))

    twos, ones, mixed, others, totals = {}, {}, {}, {}, {}
    sets = [range(sum(SETS[:s]), sum(SETS[: s + 1])) for s in range(len(SETS))]

    def send(s):
        these = sets[s]
        block = jnp.concatenate([mixed[i] for i in these] + [ones[i] for i in these], axis=0)
        if SEND_AFTER[s] < total_pieces:
            block, twos[SEND_AFTER[s]] = after(block, twos[SEND_AFTER[s]])
        others[s] = lax.ppermute(block, "ch", mate)

    def cross(s):
        these = sets[s]
        operands = [bounds, norms, left, others[s], *(ones[i] for i in these)]
        operands += [twos[i] for i in these]
        if s > 0:
            operands.append(totals[s - 1])
        totals[s] = call(
            functools.partial(cross_kernel, these[0] * PIECE, [heights[i] for i in these], s == 0),
            "cross",
            shape,
            [smem(), smem()] + [vmem()] * (len(operands) - 2),
            16 * len(these) * PIECE * width * channels * channels,
            12 * len(these) * PIECE * width * channels,
        )(*operands)

    for k in range(DEPTH):
        twos[k] = lax.ppermute(mine[k], "ch", ahead)
    for k in range(total_pieces):
        for s in range(len(SETS)):
            if CROSS_BEFORE[s] == k:
                cross(s)
                twos[k], totals[s] = after(twos[k], totals[s])
        if k >= AHEAD:
            twos[k], ones[k - AHEAD] = after(twos[k], ones[k - AHEAD])
        if CHAIN and k > 0:
            twos[k], mixed[k - 1] = after(twos[k], mixed[k - 1])
        if k + DEPTH < total_pieces:
            twos[k], later = after(twos[k], mine[k + DEPTH])
            twos[k + DEPTH] = lax.ppermute(later, "ch", ahead)
        ones[k] = lax.ppermute(jnp.where(odd_chip, twos[k], mine[k]), "ch", beside)
        mixed[k] = jnp.where(even_core, mine[k], twos[k])
        for s in range(len(SETS)):
            if SEND_AFTER[s] == k:
                send(s)
    for s in range(len(SETS)):
        if s not in others:
            send(s)
    for s in range(len(SETS)):
        if s not in totals:
            cross(s)
    total = totals[len(SETS) - 1]
    return total


def solution(mesh):
    placed = (P(None, None, "fq", "ch"), P("fq"))
    return jax.shard_map(
        shards,
        mesh=mesh,
        in_specs=placed,
        out_specs=P(None, None, "fq", "ch", None),
        check_vma=False,
    )
```

time: 117 us -> 78 us (0.67)
  starting transfers between devices: 63.3 us -> 27.5 us
  waiting for transfers between devices: 7.77 us -> 34.7 us
  Pallas kernels: 32.3 us -> 13.4 us
  local copies, waits for them, and re-layouts: 10.7 us -> 1.72 us
  other arithmetic: 2.67 us -> 0.61 us
    ppermute x28 -> x29, starting transfers between devices: 62 us -> 26.3 us  [the longest x5 12 us: send(): others[s] = lax.ppermute(block, 'ch', mate)]
    ppermute x28 -> x29, waiting for transfers between devices: 6.32 us -> 33.7 us  [the longest x10 18.6 us: shards(): twos[k + DEPTH] = lax.ppermute(later, 'ch', ahead)]
    pallas_call x8 -> x7, Pallas kernels: 32.3 us -> 13.4 us  [the longest x5 12.5 us: cross(): call(functools.partial(cross_kernel, these[0] * PIECE, [heights[i] for i...]
    unnamed x38 -> x20, local copies, waits for them, and re-layouts: 8.09 us -> 1.68 us
    slice x3 -> x0, local copies, waits for them, and re-layouts: 2.37 us -> none  [the longest x1 1.67 us: shards(): chunks = [spread(own[k * size:(k + 1) * size]) for k in range(CHUNKS)]]
    select_n x4 -> x12, other arithmetic: 1.72 us -> 0.29 us  [the longest x7 0.16 us: shards(): ones[k] = lax.ppermute(jnp.where(odd_chip, twos[k], mine[k]), 'ch', beside)]
  transfers between devices with their start and end apart: 29 -> 30, of which waited for: 4 -> 16; matrix products, arithmetic and copies ran while one was open for 3% -> 1% of each run, Pallas kernels for 23% -> 12%
where the time goes in v1:
time: 78 us; the launch traced here: 78.2 us
  waiting for transfers between devices  34.7 us (44%)
  starting transfers between devices  27.5 us (35%)
  Pallas kernels  13.4 us (17%)
  local copies, waits for them, and re-layouts  1.72 us (2%)
    ppermute x10, waiting for transfers between devices, shards(): twos[k + DEPTH] = lax.ppermute(later, 'ch', ahead)  18.6 us
    pallas_call x5, Pallas kernels, cross(): call(functools.partial(cross_kernel, these[0] * PIECE, [heights[i] for i...  12.5 us
    ppermute x5, starting transfers between devices, send(): others[s] = lax.ppermute(block, 'ch', mate)  12 us
    ppermute x12, waiting for transfers between devices, shards(): ones[k] = lax.ppermute(jnp.where(odd_chip, twos[k], mine[k]), 'ch', beside)  10.6 us
    ppermute x12, starting transfers between devices, shards(): ones[k] = lax.ppermute(jnp.where(odd_chip, twos[k], mine[k]), 'ch', beside)  7.82 us
    ppermute x2, waiting for transfers between devices, shards(): twos[k] = lax.ppermute(mine[k], 'ch', ahead)  3.74 us
    ppermute x2, starting transfers between devices, shards(): twos[k] = lax.ppermute(mine[k], 'ch', ahead)  3.47 us
    ppermute x10, starting transfers between devices, shards(): twos[k + DEPTH] = lax.ppermute(later, 'ch', ahead)  3.03 us
  transfers between devices with their start and end apart: 30, of which 16 were waited for; matrix products, arithmetic and copies ran while one was open for 1% of the time, Pallas kernels for 12%

profile of v1, /device:TPU:1, one launch (start us, length us, event | category | flops | bytes accessed | tf_op | source)
XLA Modules:
  0.0 78.2 jit_solution(2356210216666672707)
XLA Ops:
  0.0 1.4 %copy-done = bf16[2,48,64,128]{3,2,1,0:T(8,128)(2,1)S(1)} copy-done((bf16[2,48,64,128]{3,2,1,0:T(8,128)(2,1)S(1)}, bf16[2,48,64,128]{3,2,1,0:T(8,128)(2,1)}, u32[]{:S(2)}) %copy-start) | copy-done | bytes 1572888
  1.4 0.4 power.1
  1.8 2.2 %collective-permute-start.2 = (bf16[8,64,128]{2,1,0:T(8,128)(2,1)S(1)}, bf16[8,64,128]{2,1,0:T(8,128)(2,1)S(1)}, u32[]{:S(2)}, u32[]{:S(2)}) collective-permute-start(bf16[8,64,128]{2,1,0:T(8,128)(2,1)S(1)} %get-tuple-element.95), channel_id=1, source_target_pairs={{0,8},{2,10},{4,12},{6,14},{8,16},{10,18},{12,20},{14,22},{16,24},... | collective-permute-start | bytes 393224 | tf_op jit(solution)/shard_map/ppermute | solution.py:255
  4.0 1.3 %collective-permute-start.1 = (bf16[8,64,128]{2,1,0:T(8,128)(2,1)S(1)}, bf16[8,64,128]{2,1,0:T(8,128)(2,1)S(1)}, u32[]{:S(2)}, u32[]{:S(2)}) collective-permute-start(bf16[8,64,128]{2,1,0:T(8,128)(2,1)S(1)} %get-tuple-element.94), channel_id=1, source_target_pairs={{0,8},{2,10},{4,12},{6,14},{8,16},{10,18},{12,20},{14,22},{16,24},... | collective-permute-start | bytes 393224 | tf_op jit(solution)/shard_map/ppermute | solution.py:255
  5.3 1.2 %collective-permute-start = (f32[4,128]{1,0:T(4,128)S(1)}, f32[4,128]{1,0:T(4,128)S(1)}, u32[]{:S(2)}, u32[]{:S(2)}) collective-permute-start(f32[4,128]{1,0:T(4,128)S(1)} %get-tuple-element.91), channel_id=1, source_target_pairs={{0,1},{1,0},{2,3},{3,2},{4,5},{5,4},{6,7},{7,6},{8,9},{9,8},{10,11... | collective-permute-start | bytes 6152 | tf_op jit(solution)/shard_map/ppermute | solution.py:206
  6.5 0.1 convert_reduce_fusion.bounds_ref
  6.6 0.1 multiply_sqrt_fusion.norm_ref
  6.7 1.0 %collective-permute-done.halo_ref = f32[4,128]{1,0:T(4,128)S(1)} collective-permute-done((f32[4,128]{1,0:T(4,128)S(1)}, f32[4,128]{1,0:T(4,128)S(1)}, u32[]{:S(2)}, u32[]{:S(2)}) %collective-permute-start) | collective-permute-done | bytes 2080 | tf_op jit(solution)/shard_map/ppermute | solution.py:206
  7.7 0.5 left.1
  8.3 1.0 %collective-permute-done.2.refs_4_ = bf16[8,64,128]{2,1,0:T(8,128)(2,1)S(1)} collective-permute-done((bf16[8,64,128]{2,1,0:T(8,128)(2,1)S(1)}, bf16[8,64,128]{2,1,0:T(8,128)(2,1)S(1)}, u32[]{:S(2)}, u32[]{:S(2)}) %collective-permute-start.2) | collective-permute-done | bytes 131104 | tf_op jit(solution)/shard_map/ppermute | solution.py:255
  9.3 2.8 %collective-permute-done.1.refs_5_ = bf16[8,64,128]{2,1,0:T(8,128)(2,1)S(1)} collective-permute-done((bf16[8,64,128]{2,1,0:T(8,128)(2,1)S(1)}, bf16[8,64,128]{2,1,0:T(8,128)(2,1)S(1)}, u32[]{:S(2)}, u32[]{:S(2)}) %collective-permute-start.1) | collective-permute-done | bytes 131104 | tf_op jit(solution)/shard_map/ppermute | solution.py:255
  12.0 1.0 %collective-permute-start.6 = (bf16[8,64,128]{2,1,0:T(8,128)(2,1)S(1)}, bf16[8,64,128]{2,1,0:T(8,128)(2,1)S(1)}, u32[]{:S(2)}, u32[]{:S(2)}) collective-permute-start(bf16[8,64,128]{2,1,0:T(8,128)(2,1)S(1)} %get-tuple-element.197), channel_id=1, source_target_pairs={{0,4},{2,6},{4,0},{6,2},{8,12},{10,14},{12,8},{14,10},{16,20},{18,... | collective-permute-start | bytes 393224 | tf_op jit(solution)/shard_map/ppermute | solution.py:268
  13.0 0.0 collective-permute-start.5
  13.1 0.5 collective-permute-start.4
  13.6 0.4 collective-permute-start.3
  14.0 1.8 %collective-permute-done.6.refs_0_ = bf16[8,64,128]{2,1,0:T(8,128)(2,1)S(1)} collective-permute-done((bf16[8,64,128]{2,1,0:T(8,128)(2,1)S(1)}, bf16[8,64,128]{2,1,0:T(8,128)(2,1)S(1)}, u32[]{:S(2)}, u32[]{:S(2)}) %collective-permute-start.6) | collective-permute-done | bytes 131104 | tf_op jit(solution)/shard_map/ppermute | solution.py:268
  15.9 2.8 %collective-permute-done.5.refs_6_ = bf16[8,64,128]{2,1,0:T(8,128)(2,1)S(1)} collective-permute-done((bf16[8,64,128]{2,1,0:T(8,128)(2,1)S(1)}, bf16[8,64,128]{2,1,0:T(8,128)(2,1)S(1)}, u32[]{:S(2)}, u32[]{:S(2)}) %collective-permute-start.5) | collective-permute-done | bytes 131104 | tf_op jit(solution)/shard_map/ppermute | solution.py:267
  18.7 0.5 collective-permute-start.10
  19.2 0.0 collective-permute-start.9
  19.2 0.0 collective-permute-done.4.refs_1_
  19.3 2.7 %collective-permute-done.3.refs_7_ = bf16[11,64,128]{2,1,0:T(8,128)(2,1)S(1)} collective-permute-done((bf16[11,64,128]{2,1,0:T(8,128)(2,1)S(1)}, bf16[11,64,128]{2,1,0:T(8,128)(2,1)S(1)}, u32[]{:S(2)}, u32[]{:S(2)}) %collective-permute-start.3) | collective-permute-done | bytes 180256 | tf_op jit(solution)/shard_map/ppermute | solution.py:267
  22.0 0.8 collective-permute-start.8
  22.7 0.0 collective-permute-start.7
  22.8 0.1 collective-permute-done.10.refs_2_
  22.9 2.5 %collective-permute-done.9.refs_4_ = bf16[8,64,128]{2,1,0:T(8,128)(2,1)S(1)} collective-permute-done((bf16[8,64,128]{2,1,0:T(8,128)(2,1)S(1)}, bf16[8,64,128]{2,1,0:T(8,128)(2,1)S(1)}, u32[]{:S(2)}, u32[]{:S(2)}) %collective-permute-start.9) | collective-permute-done | bytes 131104 | tf_op jit(solution)/shard_map/ppermute | solution.py:267
  25.3 0.6 collective-permute-start.14
  25.9 0.0 collective-permute-start.13
  26.0 2.7 %collective-permute-done.7.refs_5_ = bf16[8,64,128]{2,1,0:T(8,128)(2,1)S(1)} collective-permute-done((bf16[8,64,128]{2,1,0:T(8,128)(2,1)S(1)}, bf16[8,64,128]{2,1,0:T(8,128)(2,1)S(1)}, u32[]{:S(2)}, u32[]{:S(2)}) %collective-permute-start.7) | collective-permute-done | bytes 131104 | tf_op jit(solution)/shard_map/ppermute | solution.py:267
  28.8 0.0 collective-permute-done.8.refs_3_
  28.8 0.4 collective-permute-start.12
  29.2 0.0 collective-permute-start.11
  29.2 5.8 %collective-permute-start.16 = (bf16[70,64,128]{2,1,0:T(8,128)(2,1)S(1)}, bf16[70,64,128]{2,1,0:T(8,128)(2,1)S(1)}, u32[]{:S(2)}, u32[]{:S(2)}) collective-permute-start(bf16[70,64,128]{2,1,0:T(8,128)(2,1)S(1)} %constant_dynamic-update-slice_fusion), channel_id=1, source_target_pairs={{0,2},{2,0},{4,6},{6,4},{8,10},{10,8},{12,14},{14,12},{16,18},{18,... | collective-permute-start | bytes 3440648 | tf_op jit(solution)/shard_map/ppermute | solution.py:237
  35.1 0.0 collective-permute-done.14.refs_0_
  35.1 0.6 collective-permute-start.19
  35.7 0.0 collective-permute-start.18
  35.7 0.0 collective-permute-done.12.refs_1_
  35.8 2.6 %collective-permute-start.15 = (bf16[8,64,128]{2,1,0:T(8,128)(2,1)S(1)}, bf16[8,64,128]{2,1,0:T(8,128)(2,1)S(1)}, u32[]{:S(2)}, u32[]{:S(2)}) collective-permute-start(bf16[8,64,128]{2,1,0:T(8,128)(2,1)S(1)} %get-tuple-element.130), channel_id=1, source_target_pairs={{0,8},{2,10},{4,12},{6,14},{8,16},{10,18},{12,20},{14,22},{16,24},... | collective-permute-start | bytes 393224 | tf_op jit(solution)/shard_map/ppermute | solution.py:267
  38.4 0.6 collective-permute-start.17
  39.0 0.4 collective-permute-done.19.refs_2_
  39.4 3.0 %collective-permute-done.18.refs_2_ = bf16[8,64,128]{2,1,0:T(8,128)(2,1)S(1)} collective-permute-done((bf16[8,64,128]{2,1,0:T(8,128)(2,1)S(1)}, bf16[8,64,128]{2,1,0:T(8,128)(2,1)S(1)}, u32[]{:S(2)}, u32[]{:S(2)}) %collective-permute-start.18) | collective-permute-done | bytes 131104 | tf_op jit(solution)/shard_map/ppermute | solution.py:267
  42.5 0.6 collective-permute-start.22
  43.2 4.2 %collective-permute-done.22.refs_0_ = bf16[8,64,128]{2,1,0:T(8,128)(2,1)S(1)} collective-permute-done((bf16[8,64,128]{2,1,0:T(8,128)(2,1)S(1)}, bf16[8,64,128]{2,1,0:T(8,128)(2,1)S(1)}, u32[]{:S(2)}, u32[]{:S(2)}) %collective-permute-start.22) | collective-permute-done | bytes 131104 | tf_op jit(solution)/shard_map/ppermute | solution.py:268
  47.4 2.8 %collective-permute-done.21.refs_1_ = bf16[8,64,128]{2,1,0:T(8,128)(2,1)S(1)} collective-permute-done((bf16[8,64,128]{2,1,0:T(8,128)(2,1)S(1)}, bf16[8,64,128]{2,1,0:T(8,128)(2,1)S(1)}, u32[]{:S(2)}, u32[]{:S(2)}) %collective-permute-start.21) | collective-permute-done | bytes 131104 | tf_op jit(solution)/shard_map/ppermute | solution.py:267
  50.2 0.0 collective-permute-done.16.mate_ref
  50.2 2.7 %cross.5.refs_8_ = f32[2,4,4,128,128]{4,3,2,1,0:T(8,128)S(1)} custom-call(s32[5]{0:T(128)S(1)} %convert_reduce_fusion.bounds_ref, f32[4]{0:T(128)S(1)} %multiply_sqrt_fusion.norm_ref, bf16[4,256,1536]{2,1,0:T(8,128)(2,1)S(1)} %get-tuple-element.92.left_ref, bf16[70,64,128]{2,1,0:T(8,128)(2,1)S(1)} %collective-permute-done.16.mate_ref, ...), custom_call_target="tpu_custom_call" | custom-call | flops 536870912 | bytes 3145728 | tf_op jit(solution)/shard_map/cross/pallas_call | solution.py:245
  53.0 0.0 collective-permute-done.17.refs_3_
  53.0 4.0 %collective-permute-start.23 = (bf16[64,64,128]{2,1,0:T(8,128)(2,1)S(1)}, bf16[64,64,128]{2,1,0:T(8,128)(2,1)S(1)}, u32[]{:S(2)}, u32[]{:S(2)}) collective-permute-start(bf16[64,64,128]{2,1,0:T(8,128)(2,1)S(1)} %constant_dynamic-update-slice_fusion.8), channel_id=1, source_target_pairs={{0,2},{2,0},{4,6},{6,4},{8,10},{10,8},{12,14},{14,12},{16,18},{18,... | collective-permute-start | bytes 3145736 | tf_op jit(solution)/shard_map/ppermute | solution.py:237
  57.0 0.0 collective-permute-start.20
  57.1 0.6 collective-permute-start.24
  57.7 0.9 %collective-permute-start.27 = (bf16[8,64,128]{2,1,0:T(8,128)(2,1)S(1)}, bf16[8,64,128]{2,1,0:T(8,128)(2,1)S(1)}, u32[]{:S(2)}, u32[]{:S(2)}) collective-permute-start(bf16[8,64,128]{2,1,0:T(8,128)(2,1)S(1)} %get-tuple-element.177), channel_id=1, source_target_pairs={{0,4},{2,6},{4,0},{6,2},{8,12},{10,14},{12,8},{14,10},{16,20},{18,... | collective-permute-start | bytes 393224 | tf_op jit(solution)/shard_map/ppermute | solution.py:268
  58.6 0.7 collective-permute-done.23.mate_ref
  59.3 2.5 %cross.6.refs_4_ = f32[2,4,4,128,128]{4,3,2,1,0:T(8,128)S(1)} custom-call(s32[5]{0:T(128)S(1)} %convert_reduce_fusion.bounds_ref, f32[4]{0:T(128)S(1)} %multiply_sqrt_fusion.norm_ref, bf16[4,256,1536]{2,1,0:T(8,128)(2,1)S(1)} %get-tuple-element.92.left_ref, bf16[64,64,128]{2,1,0:T(8,128)(2,1)S(1)} %collective-permute-done.23.mate_ref, ...), custom_call_target="tpu_custom_call" | custom-call | flops 536870912 | bytes 3145728 | tf_op jit(solution)/shard_map/cross/pallas_call | solution.py:245
  61.9 2.0 %collective-permute-done.20.refs_1_ = bf16[8,64,128]{2,1,0:T(8,128)(2,1)S(1)} collective-permute-done((bf16[8,64,128]{2,1,0:T(8,128)(2,1)S(1)}, bf16[8,64,128]{2,1,0:T(8,128)(2,1)S(1)}, u32[]{:S(2)}, u32[]{:S(2)}) %collective-permute-start.20) | collective-permute-done | bytes 131104 | tf_op jit(solution)/shard_map/ppermute | solution.py:267
  63.9 0.0 collective-permute-done.24.refs_1_
  63.9 0.1 pad_maximum_fusion
  64.0 0.9 %collective-permute-start.29 = (bf16[32,64,128]{2,1,0:T(8,128)(2,1)S(1)}, bf16[32,64,128]{2,1,0:T(8,128)(2,1)S(1)}, u32[]{:S(2)}, u32[]{:S(2)}) collective-permute-start(bf16[32,64,128]{2,1,0:T(8,128)(2,1)S(1)} %pad_maximum_fusion), channel_id=1, source_target_pairs={{0,2},{2,0},{4,6},{6,4},{8,10},{10,8},{12,14},{14,12},{16,18},{18,... | collective-permute-start | bytes 1572872 | tf_op jit(solution)/shard_map/ppermute | solution.py:237
  64.9 0.7 collective-permute-start.25
  65.6 0.0 collective-permute-done.27.refs_0_
  65.6 0.4 collective-permute-start.28
  66.0 4.1 %collective-permute-done.25.refs_0_ = bf16[8,64,128]{2,1,0:T(8,128)(2,1)S(1)} collective-permute-done((bf16[8,64,128]{2,1,0:T(8,128)(2,1)S(1)}, bf16[8,64,128]{2,1,0:T(8,128)(2,1)S(1)}, u32[]{:S(2)}, u32[]{:S(2)}) %collective-permute-start.25) | collective-permute-done | bytes 131104 | tf_op jit(solution)/shard_map/ppermute | solution.py:268
  70.1 0.9 %collective-permute-start.26 = (bf16[16,64,128]{2,1,0:T(8,128)(2,1)S(1)}, bf16[16,64,128]{2,1,0:T(8,128)(2,1)S(1)}, u32[]{:S(2)}, u32[]{:S(2)}) collective-permute-start(bf16[16,64,128]{2,1,0:T(8,128)(2,1)S(1)} %pad_maximum_fusion.1), channel_id=1, source_target_pairs={{0,2},{2,0},{4,6},{6,4},{8,10},{10,8},{12,14},{14,12},{16,18},{18,... | collective-permute-start | bytes 786440 | tf_op jit(solution)/shard_map/ppermute | solution.py:237
  71.0 2.0 %cross.7.refs_2_ = f32[2,4,4,128,128]{4,3,2,1,0:T(8,128)S(1)} custom-call(s32[5]{0:T(128)S(1)} %convert_reduce_fusion.bounds_ref, f32[4]{0:T(128)S(1)} %multiply_sqrt_fusion.norm_ref, bf16[4,256,1536]{2,1,0:T(8,128)(2,1)S(1)} %get-tuple-element.92.left_ref, bf16[32,64,128]{2,1,0:T(8,128)(2,1)S(1)} %collective-permute-done.29.mate_ref, ...), custom_call_target="tpu_custom_call" | custom-call | flops 268435456 | bytes 1572864 | tf_op jit(solution)/shard_map/cross/pallas_call | solution.py:245
  73.0 1.9 %cross.8.refs_2_ = f32[2,4,4,128,128]{4,3,2,1,0:T(8,128)S(1)} custom-call(s32[5]{0:T(128)S(1)} %convert_reduce_fusion.bounds_ref, f32[4]{0:T(128)S(1)} %multiply_sqrt_fusion.norm_ref, bf16[4,256,1536]{2,1,0:T(8,128)(2,1)S(1)} %get-tuple-element.92.left_ref, bf16[16,64,128]{2,1,0:T(8,128)(2,1)S(1)} %collective-permute-done.28.mate_ref, ...), custom_call_target="tpu_custom_call" | custom-call | flops 134217728 | bytes 786432 | tf_op jit(solution)/shard_map/cross/pallas_call | solution.py:245
  75.0 3.3 %cross.9 = f32[2,4,4,128,128]{4,3,2,1,0:T(8,128)} custom-call(s32[5]{0:T(128)S(1)} %convert_reduce_fusion.bounds_ref, f32[4]{0:T(128)S(1)} %multiply_sqrt_fusion.norm_ref, bf16[4,256,1536]{2,1,0:T(8,128)(2,1)S(1)} %get-tuple-element.92.left_ref, bf16[16,64,128]{2,1,0:T(8,128)(2,1)S(1)} %collective-permute-done.26.mate_ref, ...), custom_call_target="tpu_custom_call" | custom-call | flops 134217728 | bytes 786432 | tf_op jit(solution)/shard_map/cross/pallas_call | solution.py:245
  (43 shorter events, 0.7 us)
Async XLA Ops:
  0.0 6.5 %copy-start.2 = (s32[64]{0:T(128)S(1)}, s32[64]{0:T(128)}, u32[]{:S(2)}) copy-start(s32[64]{0:T(128)} %param.3) | copy-start | bytes 772
  0.0 1.4 %copy-start = (bf16[2,48,64,128]{3,2,1,0:T(8,128)(2,1)S(1)}, bf16[2,48,64,128]{3,2,1,0:T(8,128)(2,1)}, u32[]{:S(2)}) copy-start(bf16[2,48,64,128]{3,2,1,0:T(8,128)(2,1)} %param.2) | copy-start | bytes 4718596
  1.4 6.3 %copy-start.1 = (bf16[2,48,64,128]{3,2,1,0:T(8,128)(2,1)S(1)}, bf16[2,48,64,128]{3,2,1,0:T(8,128)(2,1)}, u32[]{:S(2)}) copy-start(bf16[2,48,64,128]{3,2,1,0:T(8,128)(2,1)} %param.2) | copy-start | bytes 4718596
  1.8 7.4 %collective-permute-start.2 = (bf16[8,64,128]{2,1,0:T(8,128)(2,1)S(1)}, bf16[8,64,128]{2,1,0:T(8,128)(2,1)S(1)}, u32[]{:S(2)}, u32[]{:S(2)}) collective-permute-start(bf16[8,64,128]{2,1,0:T(8,128)(2,1)S(1)} %get-tuple-element.95), channel_id=1, source_target_pairs={{0,8},{2,10},{4,12},{6,14},{8,16},{10,18},{12,20},{14,22},{16,24},... | collective-permute-start | bytes 393224 | tf_op jit(solution)/shard_map/ppermute | solution.py:255
  4.0 8.1 %collective-permute-start.1 = (bf16[8,64,128]{2,1,0:T(8,128)(2,1)S(1)}, bf16[8,64,128]{2,1,0:T(8,128)(2,1)S(1)}, u32[]{:S(2)}, u32[]{:S(2)}) collective-permute-start(bf16[8,64,128]{2,1,0:T(8,128)(2,1)S(1)} %get-tuple-element.94), channel_id=1, source_target_pairs={{0,8},{2,10},{4,12},{6,14},{8,16},{10,18},{12,20},{14,22},{16,24},... | collective-permute-start | bytes 393224 | tf_op jit(solution)/shard_map/ppermute | solution.py:255
  5.3 2.4 %collective-permute-start = (f32[4,128]{1,0:T(4,128)S(1)}, f32[4,128]{1,0:T(4,128)S(1)}, u32[]{:S(2)}, u32[]{:S(2)}) collective-permute-start(f32[4,128]{1,0:T(4,128)S(1)} %get-tuple-element.91), channel_id=1, source_target_pairs={{0,1},{1,0},{2,3},{3,2},{4,5},{5,4},{6,7},{7,6},{8,9},{9,8},{10,11... | collective-permute-start | bytes 6152 | tf_op jit(solution)/shard_map/ppermute | solution.py:206
  12.0 3.8 %collective-permute-start.6 = (bf16[8,64,128]{2,1,0:T(8,128)(2,1)S(1)}, bf16[8,64,128]{2,1,0:T(8,128)(2,1)S(1)}, u32[]{:S(2)}, u32[]{:S(2)}) collective-permute-start(bf16[8,64,128]{2,1,0:T(8,128)(2,1)S(1)} %get-tuple-element.197), channel_id=1, source_target_pairs={{0,4},{2,6},{4,0},{6,2},{8,12},{10,14},{12,8},{14,10},{16,20},{18,... | collective-permute-start | bytes 393224 | tf_op jit(solution)/shard_map/ppermute | solution.py:268
  13.0 5.6 %collective-permute-start.5 = (bf16[8,64,128]{2,1,0:T(8,128)(2,1)S(1)}, bf16[8,64,128]{2,1,0:T(8,128)(2,1)S(1)}, u32[]{:S(2)}, u32[]{:S(2)}) collective-permute-start(bf16[8,64,128]{2,1,0:T(8,128)(2,1)S(1)} %get-tuple-element.103), channel_id=1, source_target_pairs={{0,8},{2,10},{4,12},{6,14},{8,16},{10,18},{12,20},{14,22},{16,24},... | collective-permute-start | bytes 393224 | tf_op jit(solution)/shard_map/ppermute | solution.py:267
  13.1 6.2 %collective-permute-start.4 = (bf16[8,64,128]{2,1,0:T(8,128)(2,1)S(1)}, bf16[8,64,128]{2,1,0:T(8,128)(2,1)S(1)}, u32[]{:S(2)}, u32[]{:S(2)}) collective-permute-start(bf16[8,64,128]{2,1,0:T(8,128)(2,1)S(1)} %get-tuple-element.196), channel_id=1, source_target_pairs={{0,4},{2,6},{4,0},{6,2},{8,12},{10,14},{12,8},{14,10},{16,20},{18,... | collective-permute-start | bytes 393224 | tf_op jit(solution)/shard_map/ppermute | solution.py:268
  13.6 8.3 %collective-permute-start.3 = (bf16[11,64,128]{2,1,0:T(8,128)(2,1)S(1)}, bf16[11,64,128]{2,1,0:T(8,128)(2,1)S(1)}, u32[]{:S(2)}, u32[]{:S(2)}) collective-permute-start(bf16[11,64,128]{2,1,0:T(8,128)(2,1)S(1)} %get-tuple-element.100), channel_id=1, source_target_pairs={{0,8},{2,10},{4,12},{6,14},{8,16},{10,18},{12,20},{14,22},{16,24},... | collective-permute-start | bytes 540680 | tf_op jit(solution)/shard_map/ppermute | solution.py:267
  18.7 4.2 %collective-permute-start.10 = (bf16[8,64,128]{2,1,0:T(8,128)(2,1)S(1)}, bf16[8,64,128]{2,1,0:T(8,128)(2,1)S(1)}, u32[]{:S(2)}, u32[]{:S(2)}) collective-permute-start(bf16[8,64,128]{2,1,0:T(8,128)(2,1)S(1)} %get-tuple-element.193), channel_id=1, source_target_pairs={{0,4},{2,6},{4,0},{6,2},{8,12},{10,14},{12,8},{14,10},{16,20},{18,... | collective-permute-start | bytes 393224 | tf_op jit(solution)/shard_map/ppermute | solution.py:268
  19.2 6.1 %collective-permute-start.9 = (bf16[8,64,128]{2,1,0:T(8,128)(2,1)S(1)}, bf16[8,64,128]{2,1,0:T(8,128)(2,1)S(1)}, u32[]{:S(2)}, u32[]{:S(2)}) collective-permute-start(bf16[8,64,128]{2,1,0:T(8,128)(2,1)S(1)} %get-tuple-element.113), channel_id=1, source_target_pairs={{0,8},{2,10},{4,12},{6,14},{8,16},{10,18},{12,20},{14,22},{16,24},... | collective-permute-start | bytes 393224 | tf_op jit(solution)/shard_map/ppermute | solution.py:267
  22.0 6.8 %collective-permute-start.8 = (bf16[11,64,128]{2,1,0:T(8,128)(2,1)S(1)}, bf16[11,64,128]{2,1,0:T(8,128)(2,1)S(1)}, u32[]{:S(2)}, u32[]{:S(2)}) collective-permute-start(bf16[11,64,128]{2,1,0:T(8,128)(2,1)S(1)} %get-tuple-element.176), channel_id=1, source_target_pairs={{0,4},{2,6},{4,0},{6,2},{8,12},{10,14},{12,8},{14,10},{16,20},{18,... | collective-permute-start | bytes 540680 | tf_op jit(solution)/shard_map/ppermute | solution.py:268
  22.7 6.0 %collective-permute-start.7 = (bf16[8,64,128]{2,1,0:T(8,128)(2,1)S(1)}, bf16[8,64,128]{2,1,0:T(8,128)(2,1)S(1)}, u32[]{:S(2)}, u32[]{:S(2)}) collective-permute-start(bf16[8,64,128]{2,1,0:T(8,128)(2,1)S(1)} %get-tuple-element.110), channel_id=1, source_target_pairs={{0,8},{2,10},{4,12},{6,14},{8,16},{10,18},{12,20},{14,22},{16,24},... | collective-permute-start | bytes 393224 | tf_op jit(solution)/shard_map/ppermute | solution.py:267
  25.3 9.7 %collective-permute-start.14 = (bf16[8,64,128]{2,1,0:T(8,128)(2,1)S(1)}, bf16[8,64,128]{2,1,0:T(8,128)(2,1)S(1)}, u32[]{:S(2)}, u32[]{:S(2)}) collective-permute-start(bf16[8,64,128]{2,1,0:T(8,128)(2,1)S(1)} %get-tuple-element.191), channel_id=1, source_target_pairs={{0,4},{2,6},{4,0},{6,2},{8,12},{10,14},{12,8},{14,10},{16,20},{18,... | collective-permute-start | bytes 393224 | tf_op jit(solution)/shard_map/ppermute | solution.py:268
  25.9 9.2 %collective-permute-start.13 = (bf16[8,64,128]{2,1,0:T(8,128)(2,1)S(1)}, bf16[8,64,128]{2,1,0:T(8,128)(2,1)S(1)}, u32[]{:S(2)}, u32[]{:S(2)}) collective-permute-start(bf16[8,64,128]{2,1,0:T(8,128)(2,1)S(1)} %get-tuple-element.123), channel_id=1, source_target_pairs={{0,8},{2,10},{4,12},{6,14},{8,16},{10,18},{12,20},{14,22},{16,24},... | collective-permute-start | bytes 393224 | tf_op jit(solution)/shard_map/ppermute | solution.py:267
  28.8 6.9 %collective-permute-start.12 = (bf16[8,64,128]{2,1,0:T(8,128)(2,1)S(1)}, bf16[8,64,128]{2,1,0:T(8,128)(2,1)S(1)}, u32[]{:S(2)}, u32[]{:S(2)}) collective-permute-start(bf16[8,64,128]{2,1,0:T(8,128)(2,1)S(1)} %get-tuple-element.190), channel_id=1, source_target_pairs={{0,4},{2,6},{4,0},{6,2},{8,12},{10,14},{12,8},{14,10},{16,20},{18,... | collective-permute-start | bytes 393224 | tf_op jit(solution)/shard_map/ppermute | solution.py:268
  29.2 6.5 %collective-permute-start.11 = (bf16[8,64,128]{2,1,0:T(8,128)(2,1)S(1)}, bf16[8,64,128]{2,1,0:T(8,128)(2,1)S(1)}, u32[]{:S(2)}, u32[]{:S(2)}) collective-permute-start(bf16[8,64,128]{2,1,0:T(8,128)(2,1)S(1)} %get-tuple-element.120), channel_id=1, source_target_pairs={{0,8},{2,10},{4,12},{6,14},{8,16},{10,18},{12,20},{14,22},{16,24},... | collective-permute-start | bytes 393224 | tf_op jit(solution)/shard_map/ppermute | solution.py:267
  29.2 21.0 %collective-permute-start.16 = (bf16[70,64,128]{2,1,0:T(8,128)(2,1)S(1)}, bf16[70,64,128]{2,1,0:T(8,128)(2,1)S(1)}, u32[]{:S(2)}, u32[]{:S(2)}) collective-permute-start(bf16[70,64,128]{2,1,0:T(8,128)(2,1)S(1)} %constant_dynamic-update-slice_fusion), channel_id=1, source_target_pairs={{0,2},{2,0},{4,6},{6,4},{8,10},{10,8},{12,14},{14,12},{16,18},{18,... | collective-permute-start | bytes 3440648 | tf_op jit(solution)/shard_map/ppermute | solution.py:237
  35.1 4.3 %collective-permute-start.19 = (bf16[8,64,128]{2,1,0:T(8,128)(2,1)S(1)}, bf16[8,64,128]{2,1,0:T(8,128)(2,1)S(1)}, u32[]{:S(2)}, u32[]{:S(2)}) collective-permute-start(bf16[8,64,128]{2,1,0:T(8,128)(2,1)S(1)} %get-tuple-element.187), channel_id=1, source_target_pairs={{0,4},{2,6},{4,0},{6,2},{8,12},{10,14},{12,8},{14,10},{16,20},{18,... | collective-permute-start | bytes 393224 | tf_op jit(solution)/shard_map/ppermute | solution.py:268
  35.7 6.7 %collective-permute-start.18 = (bf16[8,64,128]{2,1,0:T(8,128)(2,1)S(1)}, bf16[8,64,128]{2,1,0:T(8,128)(2,1)S(1)}, u32[]{:S(2)}, u32[]{:S(2)}) collective-permute-start(bf16[8,64,128]{2,1,0:T(8,128)(2,1)S(1)} %get-tuple-element.143), channel_id=1, source_target_pairs={{0,8},{2,10},{4,12},{6,14},{8,16},{10,18},{12,20},{14,22},{16,24},... | collective-permute-start | bytes 393224 | tf_op jit(solution)/shard_map/ppermute | solution.py:267
  35.8 17.2 %collective-permute-start.15 = (bf16[8,64,128]{2,1,0:T(8,128)(2,1)S(1)}, bf16[8,64,128]{2,1,0:T(8,128)(2,1)S(1)}, u32[]{:S(2)}, u32[]{:S(2)}) collective-permute-start(bf16[8,64,128]{2,1,0:T(8,128)(2,1)S(1)} %get-tuple-element.130), channel_id=1, source_target_pairs={{0,8},{2,10},{4,12},{6,14},{8,16},{10,18},{12,20},{14,22},{16,24},... | collective-permute-start | bytes 393224 | tf_op jit(solution)/shard_map/ppermute | solution.py:267
  38.4 14.6 %collective-permute-start.17 = (bf16[8,64,128]{2,1,0:T(8,128)(2,1)S(1)}, bf16[8,64,128]{2,1,0:T(8,128)(2,1)S(1)}, u32[]{:S(2)}, u32[]{:S(2)}) collective-permute-start(bf16[8,64,128]{2,1,0:T(8,128)(2,1)S(1)} %get-tuple-element.186), channel_id=1, source_target_pairs={{0,4},{2,6},{4,0},{6,2},{8,12},{10,14},{12,8},{14,10},{16,20},{18,... | collective-permute-start | bytes 393224 | tf_op jit(solution)/shard_map/ppermute | solution.py:268
  42.5 4.9 %collective-permute-start.22 = (bf16[8,64,128]{2,1,0:T(8,128)(2,1)S(1)}, bf16[8,64,128]{2,1,0:T(8,128)(2,1)S(1)}, u32[]{:S(2)}, u32[]{:S(2)}) collective-permute-start(bf16[8,64,128]{2,1,0:T(8,128)(2,1)S(1)} %get-tuple-element.183), channel_id=1, source_target_pairs={{0,4},{2,6},{4,0},{6,2},{8,12},{10,14},{12,8},{14,10},{16,20},{18,... | collective-permute-start | bytes 393224 | tf_op jit(solution)/shard_map/ppermute | solution.py:268
  43.0 7.2 %collective-permute-start.21 = (bf16[8,64,128]{2,1,0:T(8,128)(2,1)S(1)}, bf16[8,64,128]{2,1,0:T(8,128)(2,1)S(1)}, u32[]{:S(2)}, u32[]{:S(2)}) collective-permute-start(bf16[8,64,128]{2,1,0:T(8,128)(2,1)S(1)} %get-tuple-element.158), channel_id=1, source_target_pairs={{0,8},{2,10},{4,12},{6,14},{8,16},{10,18},{12,20},{14,22},{16,24},... | collective-permute-start | bytes 393224 | tf_op jit(solution)/shard_map/ppermute | solution.py:267
  53.0 6.3 %collective-permute-start.23 = (bf16[64,64,128]{2,1,0:T(8,128)(2,1)S(1)}, bf16[64,64,128]{2,1,0:T(8,128)(2,1)S(1)}, u32[]{:S(2)}, u32[]{:S(2)}) collective-permute-start(bf16[64,64,128]{2,1,0:T(8,128)(2,1)S(1)} %constant_dynamic-update-slice_fusion.8), channel_id=1, source_target_pairs={{0,2},{2,0},{4,6},{6,4},{8,10},{10,8},{12,14},{14,12},{16,18},{18,... | collective-permute-start | bytes 3145736 | tf_op jit(solution)/shard_map/ppermute | solution.py:237
  57.0 6.9 %collective-permute-start.20 = (bf16[8,64,128]{2,1,0:T(8,128)(2,1)S(1)}, bf16[8,64,128]{2,1,0:T(8,128)(2,1)S(1)}, u32[]{:S(2)}, u32[]{:S(2)}) collective-permute-start(bf16[8,64,128]{2,1,0:T(8,128)(2,1)S(1)} %get-tuple-element.149), channel_id=1, source_target_pairs={{0,8},{2,10},{4,12},{6,14},{8,16},{10,18},{12,20},{14,22},{16,24},... | collective-permute-start | bytes 393224 | tf_op jit(solution)/shard_map/ppermute | solution.py:267
  57.1 6.9 %collective-permute-start.24 = (bf16[8,64,128]{2,1,0:T(8,128)(2,1)S(1)}, bf16[8,64,128]{2,1,0:T(8,128)(2,1)S(1)}, u32[]{:S(2)}, u32[]{:S(2)}) collective-permute-start(bf16[8,64,128]{2,1,0:T(8,128)(2,1)S(1)} %get-tuple-element.181), channel_id=1, source_target_pairs={{0,4},{2,6},{4,0},{6,2},{8,12},{10,14},{12,8},{14,10},{16,20},{18,... | collective-permute-start | bytes 393224 | tf_op jit(solution)/shard_map/ppermute | solution.py:268
  57.7 7.9 %collective-permute-start.27 = (bf16[8,64,128]{2,1,0:T(8,128)(2,1)S(1)}, bf16[8,64,128]{2,1,0:T(8,128)(2,1)S(1)}, u32[]{:S(2)}, u32[]{:S(2)}) collective-permute-start(bf16[8,64,128]{2,1,0:T(8,128)(2,1)S(1)} %get-tuple-element.177), channel_id=1, source_target_pairs={{0,4},{2,6},{4,0},{6,2},{8,12},{10,14},{12,8},{14,10},{16,20},{18,... | collective-permute-start | bytes 393224 | tf_op jit(solution)/shard_map/ppermute | solution.py:268
  64.0 7.0 %collective-permute-start.29 = (bf16[32,64,128]{2,1,0:T(8,128)(2,1)S(1)}, bf16[32,64,128]{2,1,0:T(8,128)(2,1)S(1)}, u32[]{:S(2)}, u32[]{:S(2)}) collective-permute-start(bf16[32,64,128]{2,1,0:T(8,128)(2,1)S(1)} %pad_maximum_fusion), channel_id=1, source_target_pairs={{0,2},{2,0},{4,6},{6,4},{8,10},{10,8},{12,14},{14,12},{16,18},{18,... | collective-permute-start | bytes 1572872 | tf_op jit(solution)/shard_map/ppermute | solution.py:237
  64.9 5.2 %collective-permute-start.25 = (bf16[8,64,128]{2,1,0:T(8,128)(2,1)S(1)}, bf16[8,64,128]{2,1,0:T(8,128)(2,1)S(1)}, u32[]{:S(2)}, u32[]{:S(2)}) collective-permute-start(bf16[8,64,128]{2,1,0:T(8,128)(2,1)S(1)} %get-tuple-element.180), channel_id=1, source_target_pairs={{0,4},{2,6},{4,0},{6,2},{8,12},{10,14},{12,8},{14,10},{16,20},{18,... | collective-permute-start | bytes 393224 | tf_op jit(solution)/shard_map/ppermute | solution.py:268
  65.6 7.4 %collective-permute-start.28 = (bf16[16,64,128]{2,1,0:T(8,128)(2,1)S(1)}, bf16[16,64,128]{2,1,0:T(8,128)(2,1)S(1)}, u32[]{:S(2)}, u32[]{:S(2)}) collective-permute-start(bf16[16,64,128]{2,1,0:T(8,128)(2,1)S(1)} %pad_maximum_fusion.2), channel_id=1, source_target_pairs={{0,2},{2,0},{4,6},{6,4},{8,10},{10,8},{12,14},{14,12},{16,18},{18,... | collective-permute-start | bytes 786440 | tf_op jit(solution)/shard_map/ppermute | solution.py:237
  70.1 4.8 %collective-permute-start.26 = (bf16[16,64,128]{2,1,0:T(8,128)(2,1)S(1)}, bf16[16,64,128]{2,1,0:T(8,128)(2,1)S(1)}, u32[]{:S(2)}, u32[]{:S(2)}) collective-permute-start(bf16[16,64,128]{2,1,0:T(8,128)(2,1)S(1)} %pad_maximum_fusion.1), channel_id=1, source_target_pairs={{0,2},{2,0},{4,6},{6,4},{8,10},{10,8},{12,14},{14,12},{16,18},{18,... | collective-permute-start | bytes 786440 | tf_op jit(solution)/shard_map/ppermute | solution.py:237

commit v2 on v1

v2 whole, which is shorter than its diff:
```python
import functools

import jax
import jax.numpy as jnp
from jax import lax
from jax.experimental import pallas as pl
from jax.experimental.pallas import tpu as pltpu
from jax.sharding import PartitionSpec as P

BANDS = 8
ROUNDS = 4
SMOOTH = 4
EPS = 1e-06

GROUP = 16
PIECE = 8
RAW = 3
TERMS = 3
DEPTH = 3
AHEAD = 2
MATES = (6, 4, 2)
MATE_AFTER = (8, 11, 12)
CROSSES = (1, 2)
CROSS_BEFORE = (12, 12)
VMEM_LIMIT = 16 * 1024 * 1024


def vmem():
    return pl.BlockSpec(memory_space=pltpu.VMEM)


def smem():
    return pl.BlockSpec(memory_space=pltpu.SMEM)


def hbm():
    return pl.BlockSpec(memory_space=pl.ANY)


def call(kernel, name, out_shape, in_specs, out_specs, flops, moved, **more):
    return pl.pallas_call(
        kernel,
        out_shape=out_shape,
        in_specs=in_specs,
        out_specs=out_specs,
        compiler_params=pltpu.CompilerParams(vmem_limit_bytes=VMEM_LIMIT),
        cost_estimate=pl.CostEstimate(flops=flops, bytes_accessed=moved, transcendentals=0),
        name=name,
        **more,
    )


def power_kernel(x_ref, power_ref, edge_ref, *refs):
    pieces, sems = refs[:-1], refs[-1]
    copies = [
        pltpu.make_async_copy(x_ref.at[pl.ds(k * PIECE, PIECE)], piece, sems.at[k])
        for k, piece in enumerate(pieces)
    ]
    for copy in copies:
        copy.start()
    total = jnp.zeros(power_ref.shape, jnp.float32)
    for copy, piece in zip(copies, pieces):
        copy.wait()

        def step(i, total):
            value = piece[i].astype(jnp.float32)
            return total + value * value

        total = lax.fori_loop(0, PIECE, step, total, unroll=8)
    width = power_ref.shape[0]
    power = total / (len(pieces) * PIECE // 2)
    power_ref[...] = power
    low = lax.axis_index("fq") == 0
    edge_ref[...] = jnp.where(low, power[width - SMOOTH :], power[:SMOOTH])


def left_kernel(count, power_ref, halo_ref, *refs):
    raws, left_ref, whites, padded = refs[:count], refs[count], refs[count + 1 : -1], refs[-1]
    fq = lax.axis_index("fq")
    width, channels = power_ref.shape
    bin_total = width * lax.axis_size("fq")
    padded[...] = jnp.zeros_like(padded)
    padded[8 : 8 + width, :] = power_ref[...]

    @pl.when(fq > 0)
    def _():
        padded[8 - SMOOTH : 8, :] = halo_ref[...]

    @pl.when(fq == 0)
    def _():
        padded[8 + width : 8 + width + SMOOTH, :] = halo_ref[...]

    total = padded[8 - SMOOTH : 8 - SMOOTH + width, :]
    for offset in range(1, 2 * SMOOTH + 1):
        total = total + padded[8 - SMOOTH + offset : 8 - SMOOTH + offset + width, :]
    bins = fq * width + lax.broadcasted_iota(jnp.int32, (width, channels), 0)
    counts = jnp.minimum(bins + SMOOTH, bin_total - 1) - jnp.maximum(bins - SMOOTH, 0) + 1
    scale = lax.rsqrt(total / counts.astype(jnp.float32) + EPS)
    rest = scale
    for term in range(TERMS):
        part = rest.astype(jnp.bfloat16)
        whites[0][PIECE + term] = part
        rest = rest - part.astype(jnp.float32)

    span = PIECE * GROUP
    for index in range(count):
        for group in range(width // GROUP):
            here = slice(group * GROUP, (group + 1) * GROUP)
            raw = raws[index][:, here, :].astype(jnp.float32)
            white = (raw * scale[here][None]).astype(jnp.bfloat16)
            if index >= RAW:
                whites[index - RAW][:PIECE, here, :] = white
            turned = white.reshape(span, channels).T
            left_ref[group, :channels, index * span : (index + 1) * span] = turned
            if index < count // 2:
                there = index + count // 2
                turned = -turned
            else:
                there = index - count // 2
            left_ref[group, channels:, there * span : (there + 1) * span] = turned


def cross_kernel(start, sets, first, last, bounds_ref, norm_ref, left_ref, *refs):
    mates, refs = refs[: len(sets)], refs[len(sets) :]
    heights = [height for these in sets for height in these]
    count = len(heights)
    ones, twos, refs = refs[:count], refs[count : 2 * count], refs[2 * count :]
    if not first:
        before_ref, refs = refs[0], refs[1:]
    out_ref = refs[0]
    sums = refs[1] if last else out_ref
    core = lax.axis_index("ch") % 2
    rounds = (2 - 2 * core, 2 * core, 1, 3)
    rights = [[], [], [(ref, 0) for ref in ones], [(ref, 0) for ref in twos]]
    for mate, these in zip(mates, sets):
        for half in range(2):
            for k in range(len(these)):
                rights[half].append((mate, half * sum(these) + sum(these[:k])))
    width, channels = mates[0].shape[1:]
    span = count * PIECE * GROUP
    lanes = slice(start * GROUP, start * GROUP + span)
    bands = sums.shape[2]
    groups = width // GROUP

    if first:
        sums[...] = jnp.zeros_like(sums)
    else:
        sums[...] = before_ref[...]

    def column(right, here):
        scale = None
        if first:
            ref, offset = right[RAW]
            for term in range(TERMS):
                part = ref[offset + PIECE + term, here, :].astype(jnp.float32)
                scale = part if scale is None else scale + part
        blocks = []
        for index, (ref, offset) in enumerate(right):
            block = ref[offset : offset + PIECE, here, :]
            if first and index < RAW:
                block = (block.astype(jnp.float32) * scale[None]).astype(jnp.bfloat16)
            blocks.append(block.reshape(PIECE * GROUP, channels))
        return jnp.concatenate(blocks, axis=0)

    def add(group, band):
        here = slice(group * GROUP, (group + 1) * GROUP)
        bins = group * GROUP + lax.broadcasted_iota(jnp.int32, (1, span), 1) % GROUP
        inside = (bins >= bounds_ref[band]) & (bins < bounds_ref[band + 1])
        left = left_ref[group, :, lanes] * inside.astype(jnp.float32).astype(jnp.bfloat16)
        columns = jnp.concatenate([column(right, here) for right in rights], axis=1)
        product = jnp.dot(left, columns, preferred_element_type=jnp.float32) * norm_ref[band]
        for index, turn in enumerate(rounds):
            part = slice(index * channels, (index + 1) * channels)
            sums[0, turn, band] += product[:channels, part]
            sums[1, turn, band] += product[channels:, part]

    def band_at(bin_index):
        return sum((bounds_ref[k] <= bin_index).astype(jnp.int32) for k in range(1, bands))

    def leave(band):
        return [
            pltpu.make_async_copy(sums.at[part, :, band], out_ref.at[part, :, band], refs[2].at[part, band])
            for part in range(2)
        ]

    for group in range(groups):
        low, high = band_at(group * GROUP), band_at((group + 1) * GROUP - 1)
        add(group, low)
        lax.fori_loop(low + 1, high + 1, lambda band, carry: add(group, band), None)
        if last:
            after = band_at((group + 1) * GROUP) if group + 1 < groups else bands

            def start_copies(band, carry):
                for copy in leave(band):
                    copy.start()

            lax.fori_loop(low, after, start_copies, None)
    if last:
        for band in range(bands):
            for copy in leave(band):
                copy.wait()


def shards(spectra, band_ids):
    parts, windows, width, channels = spectra.shape
    rows = parts * windows
    count = lax.axis_size("ch")
    fq_count = lax.axis_size("fq")
    index = lax.axis_index("ch")
    fq = lax.axis_index("fq")
    even_core = index % 2 == 0
    odd_chip = (index // 2) % 2 == 1

    ahead = [(i, (i + 4) % count) for i in range(count)]
    beside = [(i, i ^ 2) for i in range(count)]
    mate = [(i, i ^ 1) for i in range(count)]

    own = spectra.reshape(rows, width, channels)
    pieces = rows // PIECE
    heights = [PIECE + (TERMS if k == RAW else 0) for k in range(pieces)]
    block = jax.ShapeDtypeStruct((width, channels), jnp.float32)
    edge = jax.ShapeDtypeStruct((SMOOTH, channels), jnp.float32)
    plain = jax.ShapeDtypeStruct((PIECE, width, channels), jnp.bfloat16)
    held = [jax.ShapeDtypeStruct((h, width, channels), jnp.bfloat16) for h in heights]
    groups = width // GROUP
    left_shape = jax.ShapeDtypeStruct((groups, 2 * channels, rows * GROUP), jnp.bfloat16)
    nbytes = rows * width * channels * 2

    power, edge, *raws = call(
        power_kernel,
        "power",
        (block, edge, *[plain] * pieces),
        [hbm()],
        (vmem(),) * (2 + pieces),
        nbytes,
        nbytes,
        scratch_shapes=[pltpu.SemaphoreType.DMA((pieces,))],
    )(own)
    def after(value, other):
        return lax.optimization_barrier((value, other))

    band_width = BANDS // fq_count
    local_band = band_ids - fq * band_width
    below = local_band[:, None] < jnp.arange(band_width + 1, dtype=jnp.int32)[None, :]
    bounds = jnp.sum(below.astype(jnp.int32), axis=0)
    norms = 1.0 / jnp.sqrt(windows * (bounds[1:] - bounds[:-1]).astype(jnp.float32))
    power, norms = after(power, norms)

    halo = lax.ppermute(edge, "fq", [(0, 1), (1, 0)])
    left, *late = call(
        functools.partial(left_kernel, pieces),
        "left",
        (left_shape, *held[RAW:]),
        [vmem()] * (2 + pieces),
        (vmem(),) * (1 + pieces - RAW),
        nbytes,
        nbytes,
        scratch_shapes=[pltpu.VMEM((width + 16, channels), jnp.float32)],
    )(power, halo, *raws)
    mine = raws[:RAW] + late

    shape = jax.ShapeDtypeStruct((2, ROUNDS, band_width, channels, channels), jnp.float32)

    twos, ones, mixed, others, totals = {}, {}, {}, {}, {}
    mate_sets = [range(sum(MATES[:s]), sum(MATES[: s + 1])) for s in range(len(MATES))]
    cross_sets = [range(sum(CROSSES[:s]), sum(CROSSES[: s + 1])) for s in range(len(CROSSES))]

    def send(s):
        these = mate_sets[s]
        value = jnp.concatenate([mixed[i] for i in these] + [ones[i] for i in these], axis=0)
        if MATE_AFTER[s] < pieces:
            value, twos[MATE_AFTER[s]] = after(value, twos[MATE_AFTER[s]])
        others[s] = lax.ppermute(value, "ch", mate)

    def cross(s):
        sets = [mate_sets[t] for t in cross_sets[s]]
        these = [k for some in sets for k in some]
        first, last = s == 0, s == len(CROSSES) - 1
        operands = [bounds, norms, left, *(others[t] for t in cross_sets[s])]
        operands += [ones[k] for k in these] + [twos[k] for k in these]
        if not first:
            operands.append(totals[s - 1])
        scratch = []
        if last:
            scratch = [
                pltpu.VMEM(shape.shape, jnp.float32),
                pltpu.SemaphoreType.DMA((2, band_width)),
            ]
        totals[s] = call(
            functools.partial(
                cross_kernel,
                these[0] * PIECE,
                [[heights[k] for k in some] for some in sets],
                first,
                last,
            ),
            "cross",
            shape,
            [smem(), smem()] + [vmem()] * (len(operands) - 2),
            hbm() if last else vmem(),
            16 * len(these) * PIECE * width * channels * channels,
            12 * len(these) * PIECE * width * channels,
            scratch_shapes=scratch,
        )(*operands)

    for k in range(DEPTH):
        twos[k] = lax.ppermute(mine[k], "ch", ahead)
    for k in range(pieces):
        for s in range(len(CROSSES)):
            if CROSS_BEFORE[s] == k:
                cross(s)
                twos[k], totals[s] = after(twos[k], totals[s])
        if k >= AHEAD:
            twos[k], ones[k - AHEAD] = after(twos[k], ones[k - AHEAD])
        if k > 0:
            twos[k], mixed[k - 1] = after(twos[k], mixed[k - 1])
        if k + DEPTH < pieces:
            twos[k], later = after(twos[k], mine[k + DEPTH])
            twos[k + DEPTH] = lax.ppermute(later, "ch", ahead)
        ones[k] = lax.ppermute(jnp.where(odd_chip, twos[k], mine[k]), "ch", beside)
        mixed[k] = jnp.where(even_core, mine[k], twos[k])
        for s in range(len(MATES)):
            if MATE_AFTER[s] == k:
                send(s)
    for s in range(len(MATES)):
        if s not in others:
            send(s)
    for s in range(len(CROSSES)):
        if s not in totals:
            cross(s)
    return totals[len(CROSSES) - 1]


def solution(mesh):
    placed = (P(None, None, "fq", "ch"), P("fq"))
    return jax.shard_map(
        shards,
        mesh=mesh,
        in_specs=placed,
        out_specs=P(None, None, "fq", "ch", None),
        check_vma=False,
    )
```

time: 78 us -> 69.3 us (0.89)
  waiting for transfers between devices: 34.7 us -> 28 us
  Pallas kernels: 13.4 us -> 10.9 us
    ppermute x10 -> x9, waiting for transfers between devices: 18.6 us -> 10.2 us  [shards(): twos[k + DEPTH] = lax.ppermute(later, 'ch', ahead)]
    ppermute x12, starting transfers between devices: 7.82 us -> 11.4 us  [shards(): ones[k] = lax.ppermute(jnp.where(odd_chip, twos[k], mine[k]), 'ch', beside)]
    ppermute x12, waiting for transfers between devices: 10.6 us -> 13.9 us  [shards(): ones[k] = lax.ppermute(jnp.where(odd_chip, twos[k], mine[k]), 'ch', beside)]
    ppermute x5 -> x3, starting transfers between devices: 12 us -> 8.79 us  [send(): others[s] = lax.ppermute(value, 'ch', mate)]
    pallas_call x7 -> x4, Pallas kernels: 13.4 us -> 10.9 us  [the longest x2 8.11 us: cross(): call(functools.partial(cross_kernel, these[0] * PIECE, [[heights[k] for k...]
    ppermute x10 -> x9, starting transfers between devices: 3.03 us -> 0.75 us  [shards(): twos[k + DEPTH] = lax.ppermute(later, 'ch', ahead)]
    ppermute x1, waiting for transfers between devices: 1.02 us -> 0.01 us  [shards(): halo = lax.ppermute(edge, 'fq', [(0, 1), (1, 0)])]
    ppermute x1, starting transfers between devices: 1.21 us -> 2.11 us  [shards(): halo = lax.ppermute(edge, 'fq', [(0, 1), (1, 0)])]
  transfers between devices with their start and end apart: 30 -> 28, of which waited for: 16 -> 17; matrix products, arithmetic and copies ran while one was open for 1% -> 2% of each run, Pallas kernels for 12% -> 6%
where the time goes in v2:
time: 69.3 us; the launch traced here: 69.1 us
  waiting for transfers between devices  28 us (40%)
  starting transfers between devices  27 us (39%)
  Pallas kernels  10.9 us (16%)
  local copies, waits for them, and re-layouts  1.78 us (3%)
  other arithmetic  1.2 us (2%)
    ppermute x12, waiting for transfers between devices, shards(): ones[k] = lax.ppermute(jnp.where(odd_chip, twos[k], mine[k]), 'ch', beside)  13.9 us
    ppermute x12, starting transfers between devices, shards(): ones[k] = lax.ppermute(jnp.where(odd_chip, twos[k], mine[k]), 'ch', beside)  11.4 us
    ppermute x9, waiting for transfers between devices, shards(): twos[k + DEPTH] = lax.ppermute(later, 'ch', ahead)  10.2 us
    ppermute x3, starting transfers between devices, send(): others[s] = lax.ppermute(value, 'ch', mate)  8.79 us
    pallas_call x2, Pallas kernels, cross(): call(functools.partial(cross_kernel, these[0] * PIECE, [[heights[k] for k...  8.11 us
    ppermute x3, waiting for transfers between devices, shards(): twos[k] = lax.ppermute(mine[k], 'ch', ahead)  3.96 us
    ppermute x3, starting transfers between devices, shards(): twos[k] = lax.ppermute(mine[k], 'ch', ahead)  3.89 us
    pallas_call x1, Pallas kernels, shards(): call(power_kernel, 'power', (block, edge, *[plain] * pieces), [hbm()], (v...  2.2 us
  transfers between devices with their start and end apart: 28, of which 17 were waited for; matrix products, arithmetic and copies ran while one was open for 2% of the time, Pallas kernels for 6%

profile of v2, /device:TPU:1, one launch (start us, length us, event | category | flops | bytes accessed | tf_op | source)
XLA Modules:
  0.0 69.1 jit_solution(18078779804156384151)
XLA Ops:
  0.0 1.4 %copy-done = bf16[2,48,64,128]{3,2,1,0:T(8,128)(2,1)S(1)} copy-done((bf16[2,48,64,128]{3,2,1,0:T(8,128)(2,1)S(1)}, bf16[2,48,64,128]{3,2,1,0:T(8,128)(2,1)}, u32[]{:S(2)}) %copy-start) | copy-done | bytes 1572888
  1.4 2.2 %power.1 = (f32[64,128]{1,0:T(8,128)S(1)}, f32[4,128]{1,0:T(4,128)S(1)}, bf16[8,64,128]{2,1,0:T(8,128)(2,1)S(1)}, bf16[8,64,128]{2,1,0:T(8,128)(2,1)S(1)}, bf16[...) custom-call(bf16[96,64,128]{2,1,0:T(8,128)(2,1)S(1)} %bitcast.1), custom_call_target="tpu_custom_call" | custom-call | flops 1572864 | bytes 1572864 | tf_op jit(solution)/shard_map/power/pallas_call | solution.py:229
  3.6 2.1 %collective-permute-start = (f32[4,128]{1,0:T(4,128)S(1)}, f32[4,128]{1,0:T(4,128)S(1)}, u32[]{:S(2)}, u32[]{:S(2)}) collective-permute-start(f32[4,128]{1,0:T(4,128)S(1)} %get-tuple-element.98), channel_id=1, source_target_pairs={{0,1},{1,0},{2,3},{3,2},{4,5},{5,4},{6,7},{7,6},{8,9},{9,8},{10,11... | collective-permute-start | bytes 6152 | tf_op jit(solution)/shard_map/ppermute | solution.py:249
  5.7 1.3 %collective-permute-start.2 = (bf16[8,64,128]{2,1,0:T(8,128)(2,1)S(1)}, bf16[8,64,128]{2,1,0:T(8,128)(2,1)S(1)}, u32[]{:S(2)}, u32[]{:S(2)}) collective-permute-start(bf16[8,64,128]{2,1,0:T(8,128)(2,1)S(1)} %get-tuple-element.99.refs_0_), channel_id=1, source_target_pairs={{0,8},{2,10},{4,12},{6,14},{8,16},{10,18},{12,20},{14,22},{16,24},... | collective-permute-start | bytes 393224 | tf_op jit(solution)/shard_map/ppermute | solution.py:307
  7.0 1.3 %collective-permute-start.1 = (bf16[8,64,128]{2,1,0:T(8,128)(2,1)S(1)}, bf16[8,64,128]{2,1,0:T(8,128)(2,1)S(1)}, u32[]{:S(2)}, u32[]{:S(2)}) collective-permute-start(bf16[8,64,128]{2,1,0:T(8,128)(2,1)S(1)} %get-tuple-element.100.refs_1_), channel_id=1, source_target_pairs={{0,8},{2,10},{4,12},{6,14},{8,16},{10,18},{12,20},{14,22},{16,24},... | collective-permute-start | bytes 393224 | tf_op jit(solution)/shard_map/ppermute | solution.py:307
  8.3 1.3 %collective-permute-start.4 = (bf16[8,64,128]{2,1,0:T(8,128)(2,1)S(1)}, bf16[8,64,128]{2,1,0:T(8,128)(2,1)S(1)}, u32[]{:S(2)}, u32[]{:S(2)}) collective-permute-start(bf16[8,64,128]{2,1,0:T(8,128)(2,1)S(1)} %get-tuple-element.101.refs_2_), channel_id=1, source_target_pairs={{0,8},{2,10},{4,12},{6,14},{8,16},{10,18},{12,20},{14,22},{16,24},... | collective-permute-start | bytes 393224 | tf_op jit(solution)/shard_map/ppermute | solution.py:307
  9.6 0.7 broadcast_subtract_fusion
  10.3 0.1 convert_reduce_fusion.bounds_ref
  10.4 0.1 multiply_rsqrt_fusion.norm_ref
  10.5 0.0 collective-permute-done.halo_ref
  10.5 0.6 left.1
  11.1 0.3 collective-permute-done.2.refs_7_
  11.4 3.1 %collective-permute-done.1.refs_8_ = bf16[8,64,128]{2,1,0:T(8,128)(2,1)S(1)} collective-permute-done((bf16[8,64,128]{2,1,0:T(8,128)(2,1)S(1)}, bf16[8,64,128]{2,1,0:T(8,128)(2,1)S(1)}, u32[]{:S(2)}, u32[]{:S(2)}) %collective-permute-start.1) | collective-permute-done | bytes 131104 | tf_op jit(solution)/shard_map/ppermute | solution.py:307
  14.5 1.2 %collective-permute-start.5 = (bf16[8,64,128]{2,1,0:T(8,128)(2,1)S(1)}, bf16[8,64,128]{2,1,0:T(8,128)(2,1)S(1)}, u32[]{:S(2)}, u32[]{:S(2)}) collective-permute-start(bf16[8,64,128]{2,1,0:T(8,128)(2,1)S(1)} %get-tuple-element.207), channel_id=1, source_target_pairs={{0,4},{2,6},{4,0},{6,2},{8,12},{10,14},{12,8},{14,10},{16,20},{18,... | collective-permute-start | bytes 393224 | tf_op jit(solution)/shard_map/ppermute | solution.py:320
  15.8 0.3 collective-permute-start.8
  16.1 0.0 collective-permute-start.7
  16.1 0.7 collective-permute-start.3
  16.7 0.6 collective-permute-done.4.refs_9_
  17.3 1.3 %collective-permute-done.5.refs_1_ = bf16[8,64,128]{2,1,0:T(8,128)(2,1)S(1)} collective-permute-done((bf16[8,64,128]{2,1,0:T(8,128)(2,1)S(1)}, bf16[8,64,128]{2,1,0:T(8,128)(2,1)S(1)}, u32[]{:S(2)}, u32[]{:S(2)}) %collective-permute-start.5) | collective-permute-done | bytes 131104 | tf_op jit(solution)/shard_map/ppermute | solution.py:320
  18.6 1.3 %collective-permute-start.6 = (bf16[8,64,128]{2,1,0:T(8,128)(2,1)S(1)}, bf16[8,64,128]{2,1,0:T(8,128)(2,1)S(1)}, u32[]{:S(2)}, u32[]{:S(2)}) collective-permute-start(bf16[8,64,128]{2,1,0:T(8,128)(2,1)S(1)} %get-tuple-element.204), channel_id=1, source_target_pairs={{0,4},{2,6},{4,0},{6,2},{8,12},{10,14},{12,8},{14,10},{16,20},{18,... | collective-permute-start | bytes 393224 | tf_op jit(solution)/shard_map/ppermute | solution.py:320
  19.9 0.0 collective-permute-start.10
  20.0 0.0 collective-permute-done.8.refs_2_
  20.0 2.2 %collective-permute-done.7.refs_10_ = bf16[11,64,128]{2,1,0:T(8,128)(2,1)S(1)} collective-permute-done((bf16[11,64,128]{2,1,0:T(8,128)(2,1)S(1)}, bf16[11,64,128]{2,1,0:T(8,128)(2,1)S(1)}, u32[]{:S(2)}, u32[]{:S(2)}) %collective-permute-start.7) | collective-permute-done | bytes 180256 | tf_op jit(solution)/shard_map/ppermute | solution.py:319
  22.2 1.3 %collective-permute-start.11 = (bf16[11,64,128]{2,1,0:T(8,128)(2,1)S(1)}, bf16[11,64,128]{2,1,0:T(8,128)(2,1)S(1)}, u32[]{:S(2)}, u32[]{:S(2)}) collective-permute-start(bf16[11,64,128]{2,1,0:T(8,128)(2,1)S(1)} %get-tuple-element.185), channel_id=1, source_target_pairs={{0,4},{2,6},{4,0},{6,2},{8,12},{10,14},{12,8},{14,10},{16,20},{18,... | collective-permute-start | bytes 540680 | tf_op jit(solution)/shard_map/ppermute | solution.py:320
  23.5 0.0 collective-permute-start.13
  23.6 0.0 collective-permute-done.3.refs_11_
  23.6 0.5 collective-permute-done.6.refs_3_
  24.2 1.3 %collective-permute-start.14 = (bf16[8,64,128]{2,1,0:T(8,128)(2,1)S(1)}, bf16[8,64,128]{2,1,0:T(8,128)(2,1)S(1)}, u32[]{:S(2)}, u32[]{:S(2)}) collective-permute-start(bf16[8,64,128]{2,1,0:T(8,128)(2,1)S(1)} %get-tuple-element.201), channel_id=1, source_target_pairs={{0,4},{2,6},{4,0},{6,2},{8,12},{10,14},{12,8},{14,10},{16,20},{18,... | collective-permute-start | bytes 393224 | tf_op jit(solution)/shard_map/ppermute | solution.py:320
  25.5 0.0 collective-permute-start.9
  25.5 1.4 %collective-permute-done.10.refs_12_ = bf16[8,64,128]{2,1,0:T(8,128)(2,1)S(1)} collective-permute-done((bf16[8,64,128]{2,1,0:T(8,128)(2,1)S(1)}, bf16[8,64,128]{2,1,0:T(8,128)(2,1)S(1)}, u32[]{:S(2)}, u32[]{:S(2)}) %collective-permute-start.10) | collective-permute-done | bytes 131104 | tf_op jit(solution)/shard_map/ppermute | solution.py:319
  26.9 0.2 collective-permute-done.11.refs_4_
  27.1 1.3 %collective-permute-start.12 = (bf16[8,64,128]{2,1,0:T(8,128)(2,1)S(1)}, bf16[8,64,128]{2,1,0:T(8,128)(2,1)S(1)}, u32[]{:S(2)}, u32[]{:S(2)}) collective-permute-start(bf16[8,64,128]{2,1,0:T(8,128)(2,1)S(1)} %get-tuple-element.200), channel_id=1, source_target_pairs={{0,4},{2,6},{4,0},{6,2},{8,12},{10,14},{12,8},{14,10},{16,20},{18,... | collective-permute-start | bytes 393224 | tf_op jit(solution)/shard_map/ppermute | solution.py:320
  28.4 0.0 collective-permute-start.15
  28.5 2.5 %collective-permute-done.13.refs_8_ = bf16[8,64,128]{2,1,0:T(8,128)(2,1)S(1)} collective-permute-done((bf16[8,64,128]{2,1,0:T(8,128)(2,1)S(1)}, bf16[8,64,128]{2,1,0:T(8,128)(2,1)S(1)}, u32[]{:S(2)}, u32[]{:S(2)}) %collective-permute-start.13) | collective-permute-done | bytes 131104 | tf_op jit(solution)/shard_map/ppermute | solution.py:319
  30.9 0.0 collective-permute-done.14.refs_5_
  30.9 0.3 collective-permute-start.16
  31.2 0.0 collective-permute-start.17
  31.4 1.7 %collective-permute-done.9.refs_9_ = bf16[8,64,128]{2,1,0:T(8,128)(2,1)S(1)} collective-permute-done((bf16[8,64,128]{2,1,0:T(8,128)(2,1)S(1)}, bf16[8,64,128]{2,1,0:T(8,128)(2,1)S(1)}, u32[]{:S(2)}, u32[]{:S(2)}) %collective-permute-start.9) | collective-permute-done | bytes 131104 | tf_op jit(solution)/shard_map/ppermute | solution.py:319
  33.1 0.0 collective-permute-done.12.refs_6_
  33.1 0.9 %collective-permute-start.18 = (bf16[8,64,128]{2,1,0:T(8,128)(2,1)S(1)}, bf16[8,64,128]{2,1,0:T(8,128)(2,1)S(1)}, u32[]{:S(2)}, u32[]{:S(2)}) collective-permute-start(bf16[8,64,128]{2,1,0:T(8,128)(2,1)S(1)} %get-tuple-element.195), channel_id=1, source_target_pairs={{0,4},{2,6},{4,0},{6,2},{8,12},{10,14},{12,8},{14,10},{16,20},{18,... | collective-permute-start | bytes 393224 | tf_op jit(solution)/shard_map/ppermute | solution.py:320
  34.0 0.0 collective-permute-start.19
  34.1 1.1 %collective-permute-done.15.refs_10_ = bf16[8,64,128]{2,1,0:T(8,128)(2,1)S(1)} collective-permute-done((bf16[8,64,128]{2,1,0:T(8,128)(2,1)S(1)}, bf16[8,64,128]{2,1,0:T(8,128)(2,1)S(1)}, u32[]{:S(2)}, u32[]{:S(2)}) %collective-permute-start.15) | collective-permute-done | bytes 131104 | tf_op jit(solution)/shard_map/ppermute | solution.py:319
  35.2 1.1 %collective-permute-done.16.refs_2_ = bf16[8,64,128]{2,1,0:T(8,128)(2,1)S(1)} collective-permute-done((bf16[8,64,128]{2,1,0:T(8,128)(2,1)S(1)}, bf16[8,64,128]{2,1,0:T(8,128)(2,1)S(1)}, u32[]{:S(2)}, u32[]{:S(2)}) %collective-permute-start.16) | collective-permute-done | bytes 131104 | tf_op jit(solution)/shard_map/ppermute | solution.py:320
  36.4 6.2 %collective-permute-start.27 = (bf16[102,64,128]{2,1,0:T(8,128)(2,1)S(1)}, bf16[102,64,128]{2,1,0:T(8,128)(2,1)S(1)}, u32[]{:S(2)}, u32[]{:S(2)}) collective-permute-start(bf16[102,64,128]{2,1,0:T(8,128)(2,1)S(1)} %constant_dynamic-update-slice_fusion.8), channel_id=1, source_target_pairs={{0,2},{2,0},{4,6},{6,4},{8,10},{10,8},{12,14},{14,12},{16,18},{18,... | collective-permute-start | bytes 5013512 | tf_op jit(solution)/shard_map/ppermute | solution.py:273
  42.6 0.7 %collective-permute-start.20 = (bf16[8,64,128]{2,1,0:T(8,128)(2,1)S(1)}, bf16[8,64,128]{2,1,0:T(8,128)(2,1)S(1)}, u32[]{:S(2)}, u32[]{:S(2)}) collective-permute-start(bf16[8,64,128]{2,1,0:T(8,128)(2,1)S(1)} %get-tuple-element.193), channel_id=1, source_target_pairs={{0,4},{2,6},{4,0},{6,2},{8,12},{10,14},{12,8},{14,10},{16,20},{18,... | collective-permute-start | bytes 393224 | tf_op jit(solution)/shard_map/ppermute | solution.py:320
  43.3 0.0 collective-permute-done.17.refs_11_
  43.3 0.1 collective-permute-start.21
  43.4 0.0 collective-permute-done.18.refs_3_
  43.4 1.2 %collective-permute-start.22 = (bf16[8,64,128]{2,1,0:T(8,128)(2,1)S(1)}, bf16[8,64,128]{2,1,0:T(8,128)(2,1)S(1)}, u32[]{:S(2)}, u32[]{:S(2)}) collective-permute-start(bf16[8,64,128]{2,1,0:T(8,128)(2,1)S(1)} %get-tuple-element.191), channel_id=1, source_target_pairs={{0,4},{2,6},{4,0},{6,2},{8,12},{10,14},{12,8},{14,10},{16,20},{18,... | collective-permute-start | bytes 393224 | tf_op jit(solution)/shard_map/ppermute | solution.py:320
  44.7 0.0 collective-permute-done.19.refs_12_
  44.7 3.0 %collective-permute-done.20.refs_4_ = bf16[8,64,128]{2,1,0:T(8,128)(2,1)S(1)} collective-permute-done((bf16[8,64,128]{2,1,0:T(8,128)(2,1)S(1)}, bf16[8,64,128]{2,1,0:T(8,128)(2,1)S(1)}, u32[]{:S(2)}, u32[]{:S(2)}) %collective-permute-start.20) | collective-permute-done | bytes 131104 | tf_op jit(solution)/shard_map/ppermute | solution.py:320
  47.8 1.2 %collective-permute-done.21.refs_13_ = bf16[8,64,128]{2,1,0:T(8,128)(2,1)S(1)} collective-permute-done((bf16[8,64,128]{2,1,0:T(8,128)(2,1)S(1)}, bf16[8,64,128]{2,1,0:T(8,128)(2,1)S(1)}, u32[]{:S(2)}, u32[]{:S(2)}) %collective-permute-start.21) | collective-permute-done | bytes 131104 | tf_op jit(solution)/shard_map/ppermute | solution.py:319
  49.0 1.4 %collective-permute-done.22.refs_5_ = bf16[8,64,128]{2,1,0:T(8,128)(2,1)S(1)} collective-permute-done((bf16[8,64,128]{2,1,0:T(8,128)(2,1)S(1)}, bf16[8,64,128]{2,1,0:T(8,128)(2,1)S(1)}, u32[]{:S(2)}, u32[]{:S(2)}) %collective-permute-start.22) | collective-permute-done | bytes 131104 | tf_op jit(solution)/shard_map/ppermute | solution.py:320
  50.5 1.7 %collective-permute-start.23 = (bf16[64,64,128]{2,1,0:T(8,128)(2,1)S(1)}, bf16[64,64,128]{2,1,0:T(8,128)(2,1)S(1)}, u32[]{:S(2)}, u32[]{:S(2)}) collective-permute-start(bf16[64,64,128]{2,1,0:T(8,128)(2,1)S(1)} %constant_dynamic-update-slice_fusion), channel_id=1, source_target_pairs={{0,2},{2,0},{4,6},{6,4},{8,10},{10,8},{12,14},{14,12},{16,18},{18,... | collective-permute-start | bytes 3145736 | tf_op jit(solution)/shard_map/ppermute | solution.py:273
  52.1 0.5 collective-permute-start.24
  52.6 1.1 %collective-permute-start.25 = (bf16[8,64,128]{2,1,0:T(8,128)(2,1)S(1)}, bf16[8,64,128]{2,1,0:T(8,128)(2,1)S(1)}, u32[]{:S(2)}, u32[]{:S(2)}) collective-permute-start(bf16[8,64,128]{2,1,0:T(8,128)(2,1)S(1)} %get-tuple-element.188), channel_id=1, source_target_pairs={{0,4},{2,6},{4,0},{6,2},{8,12},{10,14},{12,8},{14,10},{16,20},{18,... | collective-permute-start | bytes 393224 | tf_op jit(solution)/shard_map/ppermute | solution.py:320
  53.7 3.5 %collective-permute-done.24.refs_6_ = bf16[8,64,128]{2,1,0:T(8,128)(2,1)S(1)} collective-permute-done((bf16[8,64,128]{2,1,0:T(8,128)(2,1)S(1)}, bf16[8,64,128]{2,1,0:T(8,128)(2,1)S(1)}, u32[]{:S(2)}, u32[]{:S(2)}) %collective-permute-start.24) | collective-permute-done | bytes 131104 | tf_op jit(solution)/shard_map/ppermute | solution.py:320
  57.2 2.8 %collective-permute-done.25.refs_7_ = bf16[8,64,128]{2,1,0:T(8,128)(2,1)S(1)} collective-permute-done((bf16[8,64,128]{2,1,0:T(8,128)(2,1)S(1)}, bf16[8,64,128]{2,1,0:T(8,128)(2,1)S(1)}, u32[]{:S(2)}, u32[]{:S(2)}) %collective-permute-start.25) | collective-permute-done | bytes 131104 | tf_op jit(solution)/shard_map/ppermute | solution.py:320
  60.0 0.1 pad_maximum_fusion
  60.1 0.9 %collective-permute-start.26 = (bf16[32,64,128]{2,1,0:T(8,128)(2,1)S(1)}, bf16[32,64,128]{2,1,0:T(8,128)(2,1)S(1)}, u32[]{:S(2)}, u32[]{:S(2)}) collective-permute-start(bf16[32,64,128]{2,1,0:T(8,128)(2,1)S(1)} %pad_maximum_fusion), channel_id=1, source_target_pairs={{0,2},{2,0},{4,6},{6,4},{8,10},{10,8},{12,14},{14,12},{16,18},{18,... | collective-permute-start | bytes 1572872 | tf_op jit(solution)/shard_map/ppermute | solution.py:273
  61.0 3.6 %cross.2.refs_14_ = f32[2,4,4,128,128]{4,3,2,1,0:T(8,128)S(1)} custom-call(s32[5]{0:T(128)S(1)} %convert_reduce_fusion.bounds_ref, f32[4]{0:T(128)S(1)} %multiply_rsqrt_fusion.norm_ref, bf16[4,256,1536]{2,1,0:T(8,128)(2,1)S(1)} %get-tuple-element.111.left_ref, bf16[102,64,128]{2,1,0:T(8,128)(2,1)S(1)} %collective-permute-done.27.refs_0_, ...), custom_call_target="tpu_custom_call" | custom-call | flops 805306368 | bytes 4718592 | tf_op jit(solution)/shard_map/cross/pallas_call | solution.py:289
  64.6 0.0 collective-permute-done.26.refs_1_
  64.6 0.0 collective-permute-done.23.refs_0_
  64.6 4.5 %cross.3 = f32[2,4,4,128,128]{4,3,2,1,0:T(8,128)} custom-call(s32[5]{0:T(128)S(1)} %convert_reduce_fusion.bounds_ref, f32[4]{0:T(128)S(1)} %multiply_rsqrt_fusion.norm_ref, bf16[4,256,1536]{2,1,0:T(8,128)(2,1)S(1)} %get-tuple-element.111.left_ref, bf16[64,64,128]{2,1,0:T(8,128)(2,1)S(1)} %collective-permute-done.23.refs_0_, ...), custom_call_target="tpu_custom_call" | custom-call | flops 805306368 | bytes 4718592 | tf_op jit(solution)/shard_map/cross/pallas_call | solution.py:289
  (34 shorter events, 0.7 us)
Async XLA Ops:
  0.0 1.4 %copy-start = (bf16[2,48,64,128]{3,2,1,0:T(8,128)(2,1)S(1)}, bf16[2,48,64,128]{3,2,1,0:T(8,128)(2,1)}, u32[]{:S(2)}) copy-start(bf16[2,48,64,128]{3,2,1,0:T(8,128)(2,1)} %param.2) | copy-start | bytes 4718596
  3.6 6.9 %collective-permute-start = (f32[4,128]{1,0:T(4,128)S(1)}, f32[4,128]{1,0:T(4,128)S(1)}, u32[]{:S(2)}, u32[]{:S(2)}) collective-permute-start(f32[4,128]{1,0:T(4,128)S(1)} %get-tuple-element.98), channel_id=1, source_target_pairs={{0,1},{1,0},{2,3},{3,2},{4,5},{5,4},{6,7},{7,6},{8,9},{9,8},{10,11... | collective-permute-start | bytes 6152 | tf_op jit(solution)/shard_map/ppermute | solution.py:249
  5.7 5.7 %collective-permute-start.2 = (bf16[8,64,128]{2,1,0:T(8,128)(2,1)S(1)}, bf16[8,64,128]{2,1,0:T(8,128)(2,1)S(1)}, u32[]{:S(2)}, u32[]{:S(2)}) collective-permute-start(bf16[8,64,128]{2,1,0:T(8,128)(2,1)S(1)} %get-tuple-element.99.refs_0_), channel_id=1, source_target_pairs={{0,8},{2,10},{4,12},{6,14},{8,16},{10,18},{12,20},{14,22},{16,24},... | collective-permute-start | bytes 393224 | tf_op jit(solution)/shard_map/ppermute | solution.py:307
  7.0 7.5 %collective-permute-start.1 = (bf16[8,64,128]{2,1,0:T(8,128)(2,1)S(1)}, bf16[8,64,128]{2,1,0:T(8,128)(2,1)S(1)}, u32[]{:S(2)}, u32[]{:S(2)}) collective-permute-start(bf16[8,64,128]{2,1,0:T(8,128)(2,1)S(1)} %get-tuple-element.100.refs_1_), channel_id=1, source_target_pairs={{0,8},{2,10},{4,12},{6,14},{8,16},{10,18},{12,20},{14,22},{16,24},... | collective-permute-start | bytes 393224 | tf_op jit(solution)/shard_map/ppermute | solution.py:307
  8.3 9.0 %collective-permute-start.4 = (bf16[8,64,128]{2,1,0:T(8,128)(2,1)S(1)}, bf16[8,64,128]{2,1,0:T(8,128)(2,1)S(1)}, u32[]{:S(2)}, u32[]{:S(2)}) collective-permute-start(bf16[8,64,128]{2,1,0:T(8,128)(2,1)S(1)} %get-tuple-element.101.refs_2_), channel_id=1, source_target_pairs={{0,8},{2,10},{4,12},{6,14},{8,16},{10,18},{12,20},{14,22},{16,24},... | collective-permute-start | bytes 393224 | tf_op jit(solution)/shard_map/ppermute | solution.py:307
  14.5 4.1 %collective-permute-start.5 = (bf16[8,64,128]{2,1,0:T(8,128)(2,1)S(1)}, bf16[8,64,128]{2,1,0:T(8,128)(2,1)S(1)}, u32[]{:S(2)}, u32[]{:S(2)}) collective-permute-start(bf16[8,64,128]{2,1,0:T(8,128)(2,1)S(1)} %get-tuple-element.207), channel_id=1, source_target_pairs={{0,4},{2,6},{4,0},{6,2},{8,12},{10,14},{12,8},{14,10},{16,20},{18,... | collective-permute-start | bytes 393224 | tf_op jit(solution)/shard_map/ppermute | solution.py:320
  15.8 4.2 %collective-permute-start.8 = (bf16[8,64,128]{2,1,0:T(8,128)(2,1)S(1)}, bf16[8,64,128]{2,1,0:T(8,128)(2,1)S(1)}, u32[]{:S(2)}, u32[]{:S(2)}) collective-permute-start(bf16[8,64,128]{2,1,0:T(8,128)(2,1)S(1)} %get-tuple-element.205), channel_id=1, source_target_pairs={{0,4},{2,6},{4,0},{6,2},{8,12},{10,14},{12,8},{14,10},{16,20},{18,... | collective-permute-start | bytes 393224 | tf_op jit(solution)/shard_map/ppermute | solution.py:320
  16.1 6.1 %collective-permute-start.7 = (bf16[11,64,128]{2,1,0:T(8,128)(2,1)S(1)}, bf16[11,64,128]{2,1,0:T(8,128)(2,1)S(1)}, u32[]{:S(2)}, u32[]{:S(2)}) collective-permute-start(bf16[11,64,128]{2,1,0:T(8,128)(2,1)S(1)} %get-tuple-element.123), channel_id=1, source_target_pairs={{0,8},{2,10},{4,12},{6,14},{8,16},{10,18},{12,20},{14,22},{16,24},... | collective-permute-start | bytes 540680 | tf_op jit(solution)/shard_map/ppermute | solution.py:319
  16.1 7.5 %collective-permute-start.3 = (bf16[8,64,128]{2,1,0:T(8,128)(2,1)S(1)}, bf16[8,64,128]{2,1,0:T(8,128)(2,1)S(1)}, u32[]{:S(2)}, u32[]{:S(2)}) collective-permute-start(bf16[8,64,128]{2,1,0:T(8,128)(2,1)S(1)} %get-tuple-element.116), channel_id=1, source_target_pairs={{0,8},{2,10},{4,12},{6,14},{8,16},{10,18},{12,20},{14,22},{16,24},... | collective-permute-start | bytes 393224 | tf_op jit(solution)/shard_map/ppermute | solution.py:319
  18.6 5.5 %collective-permute-start.6 = (bf16[8,64,128]{2,1,0:T(8,128)(2,1)S(1)}, bf16[8,64,128]{2,1,0:T(8,128)(2,1)S(1)}, u32[]{:S(2)}, u32[]{:S(2)}) collective-permute-start(bf16[8,64,128]{2,1,0:T(8,128)(2,1)S(1)} %get-tuple-element.204), channel_id=1, source_target_pairs={{0,4},{2,6},{4,0},{6,2},{8,12},{10,14},{12,8},{14,10},{16,20},{18,... | collective-permute-start | bytes 393224 | tf_op jit(solution)/shard_map/ppermute | solution.py:320
  19.9 7.0 %collective-permute-start.10 = (bf16[8,64,128]{2,1,0:T(8,128)(2,1)S(1)}, bf16[8,64,128]{2,1,0:T(8,128)(2,1)S(1)}, u32[]{:S(2)}, u32[]{:S(2)}) collective-permute-start(bf16[8,64,128]{2,1,0:T(8,128)(2,1)S(1)} %get-tuple-element.131), channel_id=1, source_target_pairs={{0,8},{2,10},{4,12},{6,14},{8,16},{10,18},{12,20},{14,22},{16,24},... | collective-permute-start | bytes 393224 | tf_op jit(solution)/shard_map/ppermute | solution.py:319
  22.2 4.9 %collective-permute-start.11 = (bf16[11,64,128]{2,1,0:T(8,128)(2,1)S(1)}, bf16[11,64,128]{2,1,0:T(8,128)(2,1)S(1)}, u32[]{:S(2)}, u32[]{:S(2)}) collective-permute-start(bf16[11,64,128]{2,1,0:T(8,128)(2,1)S(1)} %get-tuple-element.185), channel_id=1, source_target_pairs={{0,4},{2,6},{4,0},{6,2},{8,12},{10,14},{12,8},{14,10},{16,20},{18,... | collective-permute-start | bytes 540680 | tf_op jit(solution)/shard_map/ppermute | solution.py:320
  23.5 7.4 %collective-permute-start.13 = (bf16[8,64,128]{2,1,0:T(8,128)(2,1)S(1)}, bf16[8,64,128]{2,1,0:T(8,128)(2,1)S(1)}, u32[]{:S(2)}, u32[]{:S(2)}) collective-permute-start(bf16[8,64,128]{2,1,0:T(8,128)(2,1)S(1)} %get-tuple-element.138), channel_id=1, source_target_pairs={{0,8},{2,10},{4,12},{6,14},{8,16},{10,18},{12,20},{14,22},{16,24},... | collective-permute-start | bytes 393224 | tf_op jit(solution)/shard_map/ppermute | solution.py:319
  24.2 6.7 %collective-permute-start.14 = (bf16[8,64,128]{2,1,0:T(8,128)(2,1)S(1)}, bf16[8,64,128]{2,1,0:T(8,128)(2,1)S(1)}, u32[]{:S(2)}, u32[]{:S(2)}) collective-permute-start(bf16[8,64,128]{2,1,0:T(8,128)(2,1)S(1)} %get-tuple-element.201), channel_id=1, source_target_pairs={{0,4},{2,6},{4,0},{6,2},{8,12},{10,14},{12,8},{14,10},{16,20},{18,... | collective-permute-start | bytes 393224 | tf_op jit(solution)/shard_map/ppermute | solution.py:320
  25.5 7.6 %collective-permute-start.9 = (bf16[8,64,128]{2,1,0:T(8,128)(2,1)S(1)}, bf16[8,64,128]{2,1,0:T(8,128)(2,1)S(1)}, u32[]{:S(2)}, u32[]{:S(2)}) collective-permute-start(bf16[8,64,128]{2,1,0:T(8,128)(2,1)S(1)} %get-tuple-element.130), channel_id=1, source_target_pairs={{0,8},{2,10},{4,12},{6,14},{8,16},{10,18},{12,20},{14,22},{16,24},... | collective-permute-start | bytes 393224 | tf_op jit(solution)/shard_map/ppermute | solution.py:319
  27.1 6.0 %collective-permute-start.12 = (bf16[8,64,128]{2,1,0:T(8,128)(2,1)S(1)}, bf16[8,64,128]{2,1,0:T(8,128)(2,1)S(1)}, u32[]{:S(2)}, u32[]{:S(2)}) collective-permute-start(bf16[8,64,128]{2,1,0:T(8,128)(2,1)S(1)} %get-tuple-element.200), channel_id=1, source_target_pairs={{0,4},{2,6},{4,0},{6,2},{8,12},{10,14},{12,8},{14,10},{16,20},{18,... | collective-permute-start | bytes 393224 | tf_op jit(solution)/shard_map/ppermute | solution.py:320
  28.4 6.8 %collective-permute-start.15 = (bf16[8,64,128]{2,1,0:T(8,128)(2,1)S(1)}, bf16[8,64,128]{2,1,0:T(8,128)(2,1)S(1)}, u32[]{:S(2)}, u32[]{:S(2)}) collective-permute-start(bf16[8,64,128]{2,1,0:T(8,128)(2,1)S(1)} %get-tuple-element.144), channel_id=1, source_target_pairs={{0,8},{2,10},{4,12},{6,14},{8,16},{10,18},{12,20},{14,22},{16,24},... | collective-permute-start | bytes 393224 | tf_op jit(solution)/shard_map/ppermute | solution.py:319
  30.9 5.4 %collective-permute-start.16 = (bf16[8,64,128]{2,1,0:T(8,128)(2,1)S(1)}, bf16[8,64,128]{2,1,0:T(8,128)(2,1)S(1)}, u32[]{:S(2)}, u32[]{:S(2)}) collective-permute-start(bf16[8,64,128]{2,1,0:T(8,128)(2,1)S(1)} %get-tuple-element.197), channel_id=1, source_target_pairs={{0,4},{2,6},{4,0},{6,2},{8,12},{10,14},{12,8},{14,10},{16,20},{18,... | collective-permute-start | bytes 393224 | tf_op jit(solution)/shard_map/ppermute | solution.py:320
  31.2 12.1 %collective-permute-start.17 = (bf16[8,64,128]{2,1,0:T(8,128)(2,1)S(1)}, bf16[8,64,128]{2,1,0:T(8,128)(2,1)S(1)}, u32[]{:S(2)}, u32[]{:S(2)}) collective-permute-start(bf16[8,64,128]{2,1,0:T(8,128)(2,1)S(1)} %get-tuple-element.150), channel_id=1, source_target_pairs={{0,8},{2,10},{4,12},{6,14},{8,16},{10,18},{12,20},{14,22},{16,24},... | collective-permute-start | bytes 393224 | tf_op jit(solution)/shard_map/ppermute | solution.py:319
  33.1 10.3 %collective-permute-start.18 = (bf16[8,64,128]{2,1,0:T(8,128)(2,1)S(1)}, bf16[8,64,128]{2,1,0:T(8,128)(2,1)S(1)}, u32[]{:S(2)}, u32[]{:S(2)}) collective-permute-start(bf16[8,64,128]{2,1,0:T(8,128)(2,1)S(1)} %get-tuple-element.195), channel_id=1, source_target_pairs={{0,4},{2,6},{4,0},{6,2},{8,12},{10,14},{12,8},{14,10},{16,20},{18,... | collective-permute-start | bytes 393224 | tf_op jit(solution)/shard_map/ppermute | solution.py:320
  34.0 10.6 %collective-permute-start.19 = (bf16[8,64,128]{2,1,0:T(8,128)(2,1)S(1)}, bf16[8,64,128]{2,1,0:T(8,128)(2,1)S(1)}, u32[]{:S(2)}, u32[]{:S(2)}) collective-permute-start(bf16[8,64,128]{2,1,0:T(8,128)(2,1)S(1)} %get-tuple-element.156), channel_id=1, source_target_pairs={{0,8},{2,10},{4,12},{6,14},{8,16},{10,18},{12,20},{14,22},{16,24},... | collective-permute-start | bytes 393224 | tf_op jit(solution)/shard_map/ppermute | solution.py:319
  36.4 24.7 %collective-permute-start.27 = (bf16[102,64,128]{2,1,0:T(8,128)(2,1)S(1)}, bf16[102,64,128]{2,1,0:T(8,128)(2,1)S(1)}, u32[]{:S(2)}, u32[]{:S(2)}) collective-permute-start(bf16[102,64,128]{2,1,0:T(8,128)(2,1)S(1)} %constant_dynamic-update-slice_fusion.8), channel_id=1, source_target_pairs={{0,2},{2,0},{4,6},{6,4},{8,10},{10,8},{12,14},{14,12},{16,18},{18,... | collective-permute-start | bytes 5013512 | tf_op jit(solution)/shard_map/ppermute | solution.py:273
  42.6 5.1 %collective-permute-start.20 = (bf16[8,64,128]{2,1,0:T(8,128)(2,1)S(1)}, bf16[8,64,128]{2,1,0:T(8,128)(2,1)S(1)}, u32[]{:S(2)}, u32[]{:S(2)}) collective-permute-start(bf16[8,64,128]{2,1,0:T(8,128)(2,1)S(1)} %get-tuple-element.193), channel_id=1, source_target_pairs={{0,4},{2,6},{4,0},{6,2},{8,12},{10,14},{12,8},{14,10},{16,20},{18,... | collective-permute-start | bytes 393224 | tf_op jit(solution)/shard_map/ppermute | solution.py:320
  43.3 5.7 %collective-permute-start.21 = (bf16[8,64,128]{2,1,0:T(8,128)(2,1)S(1)}, bf16[8,64,128]{2,1,0:T(8,128)(2,1)S(1)}, u32[]{:S(2)}, u32[]{:S(2)}) collective-permute-start(bf16[8,64,128]{2,1,0:T(8,128)(2,1)S(1)} %get-tuple-element.163), channel_id=1, source_target_pairs={{0,8},{2,10},{4,12},{6,14},{8,16},{10,18},{12,20},{14,22},{16,24},... | collective-permute-start | bytes 393224 | tf_op jit(solution)/shard_map/ppermute | solution.py:319
  43.4 7.0 %collective-permute-start.22 = (bf16[8,64,128]{2,1,0:T(8,128)(2,1)S(1)}, bf16[8,64,128]{2,1,0:T(8,128)(2,1)S(1)}, u32[]{:S(2)}, u32[]{:S(2)}) collective-permute-start(bf16[8,64,128]{2,1,0:T(8,128)(2,1)S(1)} %get-tuple-element.191), channel_id=1, source_target_pairs={{0,4},{2,6},{4,0},{6,2},{8,12},{10,14},{12,8},{14,10},{16,20},{18,... | collective-permute-start | bytes 393224 | tf_op jit(solution)/shard_map/ppermute | solution.py:320
  50.5 14.1 %collective-permute-start.23 = (bf16[64,64,128]{2,1,0:T(8,128)(2,1)S(1)}, bf16[64,64,128]{2,1,0:T(8,128)(2,1)S(1)}, u32[]{:S(2)}, u32[]{:S(2)}) collective-permute-start(bf16[64,64,128]{2,1,0:T(8,128)(2,1)S(1)} %constant_dynamic-update-slice_fusion), channel_id=1, source_target_pairs={{0,2},{2,0},{4,6},{6,4},{8,10},{10,8},{12,14},{14,12},{16,18},{18,... | collective-permute-start | bytes 3145736 | tf_op jit(solution)/shard_map/ppermute | solution.py:273
  52.1 5.1 %collective-permute-start.24 = (bf16[8,64,128]{2,1,0:T(8,128)(2,1)S(1)}, bf16[8,64,128]{2,1,0:T(8,128)(2,1)S(1)}, u32[]{:S(2)}, u32[]{:S(2)}) collective-permute-start(bf16[8,64,128]{2,1,0:T(8,128)(2,1)S(1)} %get-tuple-element.189), channel_id=1, source_target_pairs={{0,4},{2,6},{4,0},{6,2},{8,12},{10,14},{12,8},{14,10},{16,20},{18,... | collective-permute-start | bytes 393224 | tf_op jit(solution)/shard_map/ppermute | solution.py:320
  52.6 7.4 %collective-permute-start.25 = (bf16[8,64,128]{2,1,0:T(8,128)(2,1)S(1)}, bf16[8,64,128]{2,1,0:T(8,128)(2,1)S(1)}, u32[]{:S(2)}, u32[]{:S(2)}) collective-permute-start(bf16[8,64,128]{2,1,0:T(8,128)(2,1)S(1)} %get-tuple-element.188), channel_id=1, source_target_pairs={{0,4},{2,6},{4,0},{6,2},{8,12},{10,14},{12,8},{14,10},{16,20},{18,... | collective-permute-start | bytes 393224 | tf_op jit(solution)/shard_map/ppermute | solution.py:320
  60.1 4.5 %collective-permute-start.26 = (bf16[32,64,128]{2,1,0:T(8,128)(2,1)S(1)}, bf16[32,64,128]{2,1,0:T(8,128)(2,1)S(1)}, u32[]{:S(2)}, u32[]{:S(2)}) collective-permute-start(bf16[32,64,128]{2,1,0:T(8,128)(2,1)S(1)} %pad_maximum_fusion), channel_id=1, source_target_pairs={{0,2},{2,0},{4,6},{6,4},{8,10},{10,8},{12,14},{14,12},{16,18},{18,... | collective-permute-start | bytes 1572872 | tf_op jit(solution)/shard_map/ppermute | solution.py:273

commit v3 on v1

v3 whole, which is shorter than its diff:
```python
import functools

import jax
import jax.numpy as jnp
from jax import lax
from jax.experimental import pallas as pl
from jax.experimental.pallas import tpu as pltpu
from jax.sharding import PartitionSpec as P

BANDS = 8
ROUNDS = 4
SMOOTH = 4
EPS = 1e-06

GROUP = 16
PIECE = 12
RAW = 3
TERMS = 3
DEPTH = 3
AHEAD = 2
SETS = (4, 2, 2)
OTHER_AFTER = 1
NEAR_BEFORE = 7
CROSS_BEFORE = (6, 8)
VMEM_LIMIT = 16 * 1024 * 1024


def vmem():
    return pl.BlockSpec(memory_space=pltpu.VMEM)


def smem():
    return pl.BlockSpec(memory_space=pltpu.SMEM)


def hbm():
    return pl.BlockSpec(memory_space=pltpu.HBM)


def call(kernel, name, out_shape, in_specs, out_specs, flops, moved, **more):
    return pl.pallas_call(
        kernel,
        out_shape=out_shape,
        in_specs=in_specs,
        out_specs=out_specs,
        compiler_params=pltpu.CompilerParams(vmem_limit_bytes=VMEM_LIMIT),
        cost_estimate=pl.CostEstimate(flops=flops, bytes_accessed=moved, transcendentals=0),
        name=name,
        **more,
    )


def power_kernel(x_ref, power_ref, edge_ref, *pieces):
    rows, width, _ = x_ref.shape
    for index, piece in enumerate(pieces):
        piece[...] = x_ref[index * PIECE : (index + 1) * PIECE]

    def step(i, total):
        value = x_ref[i].astype(jnp.float32)
        return total + value * value

    total = lax.fori_loop(0, rows, step, jnp.zeros(power_ref.shape, jnp.float32), unroll=8)
    power = total / (rows // 2)
    power_ref[...] = power
    low = lax.axis_index("fq") == 0
    edge_ref[...] = jnp.where(low, power[width - SMOOTH :], power[:SMOOTH])


def left_kernel(x_ref, power_ref, halo_ref, left_ref, *refs):
    whites, padded = refs[:-1], refs[-1]
    count = x_ref.shape[0] // PIECE
    fq = lax.axis_index("fq")
    width, channels = power_ref.shape
    bin_total = width * lax.axis_size("fq")
    padded[...] = jnp.zeros_like(padded)
    padded[8 : 8 + width, :] = power_ref[...]

    @pl.when(fq > 0)
    def _():
        padded[8 - SMOOTH : 8, :] = halo_ref[...]

    @pl.when(fq == 0)
    def _():
        padded[8 + width : 8 + width + SMOOTH, :] = halo_ref[...]

    total = padded[8 - SMOOTH : 8 - SMOOTH + width, :]
    for offset in range(1, 2 * SMOOTH + 1):
        total = total + padded[8 - SMOOTH + offset : 8 - SMOOTH + offset + width, :]
    bins = fq * width + lax.broadcasted_iota(jnp.int32, (width, channels), 0)
    counts = jnp.minimum(bins + SMOOTH, bin_total - 1) - jnp.maximum(bins - SMOOTH, 0) + 1
    scale = lax.rsqrt(total / counts.astype(jnp.float32) + EPS)
    rest = scale
    for term in range(TERMS):
        part = rest.astype(jnp.bfloat16)
        whites[0][PIECE + term] = part
        rest = rest - part.astype(jnp.float32)

    span = 2 * PIECE * GROUP
    for pair in range(count // 2):
        for group in range(width // GROUP):
            here = slice(group * GROUP, (group + 1) * GROUP)
            blocks = []
            for index in (2 * pair, 2 * pair + 1):
                raw = x_ref[index * PIECE : (index + 1) * PIECE, here, :].astype(jnp.float32)
                white = (raw * scale[here][None]).astype(jnp.bfloat16)
                if index >= RAW:
                    whites[index - RAW][:PIECE, here, :] = white
                blocks.append(white.reshape(PIECE * GROUP, channels))
            turned = jnp.concatenate(blocks, axis=0).T
            left_ref[group, :, pair * span : (pair + 1) * span] = turned


def band_at(bounds_ref, bands, bin_index):
    return sum((bounds_ref[k] <= bin_index).astype(jnp.int32) for k in range(1, bands))


def each_band(bounds_ref, groups, bands, add):
    for group in range(groups):
        low = band_at(bounds_ref, bands, group * GROUP)
        high = band_at(bounds_ref, bands, (group + 1) * GROUP - 1)
        add(group, low)
        lax.fori_loop(low + 1, high + 1, lambda band, carry: add(group, band), None)


def lefts(turned_ref, bounds_ref, group, band, start, stop):
    half = turned_ref.shape[2] // 2
    bins = group * GROUP + lax.broadcasted_iota(jnp.int32, (1, stop - start), 1) % GROUP
    inside = (bins >= bounds_ref[band]) & (bins < bounds_ref[band + 1])
    inside = inside.astype(jnp.float32).astype(jnp.bfloat16)
    real = turned_ref[group, :, start:stop] * inside
    parts = []
    if start < half:
        end = min(stop, half)
        parts.append(turned_ref[group, :, start + half : end + half] * inside[:, : end - start])
    if stop > half:
        begin = max(start, half)
        parts.append(turned_ref[group, :, begin - half : stop - half] * -inside[:, begin - start :])
    return [real, parts[0] if len(parts) == 1 else jnp.concatenate(parts, axis=1)]


def near_kernel(bounds_ref, norm_ref, own_ref, mate_ref, out_ref):
    groups, channels, span = own_ref.shape
    bands = out_ref.shape[1]
    out_ref[...] = jnp.zeros_like(out_ref)

    def add(group, band):
        left = jnp.concatenate(lefts(own_ref, bounds_ref, group, band, 0, span), axis=0)
        product = lax.dot_general(
            left, mate_ref[group], (((1,), (1,)), ((), ())), preferred_element_type=jnp.float32
        )
        product = product * norm_ref[band]
        out_ref[0, band] += product[:channels]
        out_ref[1, band] += product[channels:]

    @pl.when(lax.axis_index("ch") % 2 == 1)
    def _():
        each_band(bounds_ref, groups, bands, add)


def cross_kernel(start, count, kinds, first, last, bounds_ref, norm_ref, own_ref, mate_ref, *refs):
    rights = [refs[k * count : (k + 1) * count] for k in range(kinds)]
    refs = refs[kinds * count :]
    if not first:
        befores, refs = refs[:kinds], refs[kinds:]
    if last:
        beyond_ref, refs = refs[0], refs[1:]
    sums = refs[:kinds]
    width, channels = rights[0][0].shape[1:]
    bands = sums[0].shape[2]
    lanes = start * GROUP, (start + count * PIECE) * GROUP
    for k in range(kinds):
        sums[k][...] = jnp.zeros_like(sums[k]) if first else befores[k][...]

    def column(right, here):
        scale = None
        if first:
            for term in range(TERMS):
                part = right[RAW][PIECE + term, here, :].astype(jnp.float32)
                scale = part if scale is None else scale + part
        blocks = []
        for index, ref in enumerate(right):
            block = ref[:PIECE, here, :]
            if first and index < RAW:
                block = (block.astype(jnp.float32) * scale[None]).astype(jnp.bfloat16)
            blocks.append(block.reshape(PIECE * GROUP, channels))
        return jnp.concatenate(blocks, axis=0)

    def add(group, band):
        here = slice(group * GROUP, (group + 1) * GROUP)
        left = jnp.concatenate(
            lefts(own_ref, bounds_ref, group, band, *lanes)
            + lefts(mate_ref, bounds_ref, group, band, *lanes),
            axis=0,
        )
        right = jnp.concatenate([column(right, here) for right in rights], axis=1)
        product = jnp.dot(left, right, preferred_element_type=jnp.float32) * norm_ref[band]
        for k in range(kinds):
            for owner in range(2):
                for part in range(2):
                    row = (2 * owner + part) * channels
                    sums[k][part, owner, band] += product[
                        row : row + channels, k * channels : (k + 1) * channels
                    ]

    each_band(bounds_ref, width // GROUP, bands, add)
    if last:
        refs[kinds][0] = sums[0][:, 1].astype(jnp.bfloat16)
        refs[kinds][1] = beyond_ref[:, 1].astype(jnp.bfloat16)


def put_own_kernel(one_ref, two_ref, out_ref, sems):
    copies = [
        pltpu.make_async_copy(value.at[:, 0], out_ref.at[:, turn], sems.at[k])
        for k, (turn, value) in enumerate(((1, one_ref), (3, two_ref)))
    ]
    for copy in copies:
        copy.start()
    for copy in copies:
        copy.wait()


def put_got_kernel(got_ref, near_ref, before_ref, out_ref, wide, sems):
    core = lax.axis_index("ch") % 2
    wide[0] = got_ref[0].astype(jnp.float32)
    far = pltpu.make_async_copy(wide.at[0], out_ref.at[:, 2 * core], sems.at[0])
    far.start()
    wide[1] = jnp.where(core == 0, got_ref[1].astype(jnp.float32), near_ref[...])
    near = pltpu.make_async_copy(wide.at[1], out_ref.at[:, 2 - 2 * core], sems.at[1])
    near.start()
    far.wait()
    near.wait()


def after(value, other):
    return lax.optimization_barrier((value, other))


def shards(spectra, band_ids):
    parts, windows, width, channels = spectra.shape
    rows = parts * windows
    count = lax.axis_size("ch")
    fq_count = lax.axis_size("fq")
    index = lax.axis_index("ch")
    fq = lax.axis_index("fq")
    even_core = index % 2 == 0
    odd_chip = (index // 2) % 2 == 1

    ahead = [(i, (i + 4) % count) for i in range(count)]
    beside = [(i, i ^ 2) for i in range(count)]
    mate = [(i, i ^ 1) for i in range(count)]

    own = spectra.reshape(rows, width, channels)
    pieces = rows // PIECE
    heights = [PIECE + (TERMS if k == RAW else 0) for k in range(pieces)]
    block = jax.ShapeDtypeStruct((width, channels), jnp.float32)
    edge = jax.ShapeDtypeStruct((SMOOTH, channels), jnp.float32)
    held = [jax.ShapeDtypeStruct((h, width, channels), jnp.bfloat16) for h in heights]
    groups = width // GROUP
    left_shape = jax.ShapeDtypeStruct((groups, channels, rows * GROUP), jnp.bfloat16)
    nbytes = rows * width * channels * 2

    power, edge, *early = call(
        power_kernel,
        "power",
        (block, edge, *held[:RAW]),
        [vmem()],
        (vmem(),) * (2 + RAW),
        nbytes,
        nbytes,
    )(own)
    band_width = BANDS // fq_count
    local_band = band_ids - fq * band_width
    below = local_band[:, None] < jnp.arange(band_width + 1, dtype=jnp.int32)[None, :]
    bounds = jnp.sum(below.astype(jnp.int32), axis=0)
    norms = 1.0 / jnp.sqrt(windows * (bounds[1:] - bounds[:-1]).astype(jnp.float32))
    power, norms = after(power, norms)

    halo = lax.ppermute(edge, "fq", [(0, 1), (1, 0)])
    left, *late = call(
        left_kernel,
        "left",
        (left_shape, *held[RAW:]),
        [vmem()] * 3,
        (vmem(),) * (1 + pieces - RAW),
        nbytes,
        nbytes,
        scratch_shapes=[pltpu.VMEM((width + 16, channels), jnp.float32)],
    )(own, power, halo)
    mine = early + late

    out_shape = jax.ShapeDtypeStruct((2, ROUNDS, band_width, channels, channels), jnp.float32)
    sum_shape = jax.ShapeDtypeStruct((2, 2, band_width, channels, channels), jnp.float32)
    near_shape = jax.ShapeDtypeStruct((2, band_width, channels, channels), jnp.float32)
    send_shape = jax.ShapeDtypeStruct((2, 2, band_width, channels, channels), jnp.bfloat16)

    sets = [range(sum(SETS[:s]), sum(SETS[: s + 1])) for s in range(len(SETS))]
    twos, ones, onward = {}, {}, {}
    sums = {}

    def cross(these, flights, befores, last=()):
        first = befores is None
        operands = [bounds, norms, left, other]
        for flight in flights:
            operands += [flight[k] for k in these]
        operands += [*([] if first else befores), *last]
        kinds = len(flights)
        return call(
            functools.partial(
                cross_kernel, these[0] * PIECE, len(these), kinds, first, bool(last)
            ),
            "cross",
            (sum_shape,) * kinds + (send_shape,) * len(last),
            [smem(), smem()] + [vmem()] * (len(operands) - 2),
            (vmem(),) * (kinds + len(last)),
            8 * kinds * len(these) * PIECE * width * channels * channels,
            0 * nbytes,
        )(*operands)

    for k in range(DEPTH):
        twos[k] = lax.ppermute(mine[k], "ch", ahead)
    left, twos[OTHER_AFTER] = after(left, twos[OTHER_AFTER])
    other = lax.ppermute(left, "ch", mate)
    near = call(
        near_kernel,
        "near",
        near_shape,
        [smem(), smem(), vmem(), vmem()],
        vmem(),
        1000,
        1000,
    )(bounds, norms, left, other)

    for k in range(pieces):
        if k == NEAR_BEFORE:
            twos[k], near = after(twos[k], near)
        for s in range(len(SETS) - 1):
            if CROSS_BEFORE[s] == k:
                sums[s] = list(cross(sets[s], (ones, twos), sums.get(s - 1)))
                twos[k], sums[s][0] = after(twos[k], sums[s][0])
        if k >= AHEAD:
            twos[k], ones[k - AHEAD] = after(twos[k], ones[k - AHEAD])
        if k > 0:
            twos[k], onward[k - 1] = after(twos[k], onward[k - 1])
        if k + DEPTH < pieces:
            twos[k], later = after(twos[k], mine[k + DEPTH])
            twos[k + DEPTH] = lax.ppermute(later, "ch", ahead)
        onward[k] = jnp.where(odd_chip, twos[k], mine[k])
        if k < pieces - 1:
            ones[k] = lax.ppermute(onward[k], "ch", beside)
    final = pieces - 1
    for s in range(len(SETS) - 1):
        if s not in sums:
            onward[final], twos[sets[s][0]] = after(onward[final], twos[sets[s][0]])
            ones[final - 1], twos[sets[s][0]] = after(ones[final - 1], twos[sets[s][0]])
            sums[s] = list(cross(sets[s], (ones, twos), sums.get(s - 1)))
    one_sum, two_sum = sums[len(SETS) - 2]

    ones[final] = lax.ppermute(onward[final], "ch", beside)
    (two_sum,) = cross(sets[-1], (twos,), [two_sum])
    one_sum, sent = cross(sets[-1], (ones,), [one_sum], (two_sum,))
    got = lax.ppermute(sent, "ch", mate)
    out = call(
        put_own_kernel,
        "put",
        out_shape,
        [vmem()] * 2,
        hbm(),
        1000,
        1000,
        scratch_shapes=[pltpu.SemaphoreType.DMA((2,))],
    )(one_sum, two_sum)
    return call(
        put_got_kernel,
        "put",
        out_shape,
        [vmem(), vmem(), hbm()],
        hbm(),
        1000,
        1000,
        input_output_aliases={2: 0},
        scratch_shapes=[
            pltpu.VMEM((2,) + near_shape.shape, jnp.float32),
            pltpu.SemaphoreType.DMA((2,)),
        ],
    )(got, near, out)


def solution(mesh):
    placed = (P(None, None, "fq", "ch"), P("fq"))
    return jax.shard_map(
        shards,
        mesh=mesh,
        in_specs=placed,
        out_specs=P(None, None, "fq", "ch", None),
        check_vma=False,
    )
```

time: 78 us -> 65.2 us (0.84); the launches traced: 78.2 us -> 64.6 us
  waiting for transfers between devices: 34.7 us -> 17.4 us
  starting transfers between devices: 27.5 us -> 19.3 us
  Pallas kernels: 13.4 us -> 18.3 us
  local copies, waits for them, and re-layouts: 1.72 us -> 6.23 us
  other arithmetic: 0.61 us -> 3.19 us
    ppermute x10 -> x5, waiting for transfers between devices: 18.6 us -> 8.28 us  [shards(): twos[k + DEPTH] = lax.ppermute(later, 'ch', ahead)]
    ppermute x17 -> x10, waiting for transfers between devices: 11.4 us -> 3.02 us  [the longest x7 2.46 us: shards(): ones[k] = lax.ppermute(onward[k], 'ch', beside)]
    ppermute x17 -> x10, starting transfers between devices: 19.8 us -> 14.6 us  [the longest x7 6.17 us: shards(): ones[k] = lax.ppermute(onward[k], 'ch', beside)]
    pallas_call x7 -> x9, Pallas kernels: 13.4 us -> 18.3 us  [the longest x4 11.5 us: cross(): call(functools.partial(cross_kernel, these[0] * PIECE, len(these), kinds,...]
    unnamed x20 -> x30, local copies, waits for them, and re-layouts: 1.68 us -> 6.23 us
    ppermute x10 -> x5, starting transfers between devices: 3.03 us -> 0.01 us  [shards(): twos[k + DEPTH] = lax.ppermute(later, 'ch', ahead)]
    select_n x12 -> x8, other arithmetic: 0.29 us -> 2.99 us  [shards(): onward[k] = jnp.where(odd_chip, twos[k], mine[k])]
    ppermute x2 -> x3, waiting for transfers between devices: 3.74 us -> 6.11 us  [shards(): twos[k] = lax.ppermute(mine[k], 'ch', ahead)]
  transfers between devices with their start and end apart: 30 -> 19, of which waited for: 16 -> 10; matrix products, arithmetic and copies ran while one was open for 1% -> 5% of each run, Pallas kernels for 12% -> 21%
where the time goes in v3:
time: 65.2 us; the launch traced here: 64.6 us
  starting transfers between devices  19.3 us (30%)
  Pallas kernels  18.3 us (28%)
  waiting for transfers between devices  17.4 us (27%)
  local copies, waits for them, and re-layouts  6.23 us (10%)
  other arithmetic  3.19 us (5%)
    pallas_call x4, Pallas kernels, cross(): call(functools.partial(cross_kernel, these[0] * PIECE, len(these), kinds,...  11.5 us
    ppermute x5, waiting for transfers between devices, shards(): twos[k + DEPTH] = lax.ppermute(later, 'ch', ahead)  8.28 us
    unnamed x30, local copies, waits for them, and re-layouts  6.23 us
    ppermute x7, starting transfers between devices, shards(): ones[k] = lax.ppermute(onward[k], 'ch', beside)  6.17 us
    ppermute x3, waiting for transfers between devices, shards(): twos[k] = lax.ppermute(mine[k], 'ch', ahead)  6.11 us
    ppermute x1, starting transfers between devices, shards(): got = lax.ppermute(sent, 'ch', mate)  4.97 us
    ppermute x1, starting transfers between devices, shards(): other = lax.ppermute(left, 'ch', mate)  3.2 us
    pallas_call x1, Pallas kernels, shards(): call(near_kernel, 'near', near_shape, [smem(), smem(), vmem(), vmem()], v...  3.17 us
  transfers between devices with their start and end apart: 19, of which 10 were waited for; matrix products, arithmetic and copies ran while one was open for 5% of the time, Pallas kernels for 21%

profile of v3, /device:TPU:1, one launch (start us, length us, event | category | flops | bytes accessed | tf_op | source)
XLA Modules:
  0.0 64.6 jit_solution(17552200058870050856)
XLA Ops:
  0.0 1.4 %copy-done = bf16[2,48,64,128]{3,2,1,0:T(8,128)(2,1)S(1)} copy-done((bf16[2,48,64,128]{3,2,1,0:T(8,128)(2,1)S(1)}, bf16[2,48,64,128]{3,2,1,0:T(8,128)(2,1)}, u32[]{:S(2)}) %copy-start) | copy-done | bytes 1572888
  1.4 1.2 %power.1 = (f32[64,128]{1,0:T(8,128)S(1)}, f32[4,128]{1,0:T(4,128)S(1)}, bf16[12,64,128]{2,1,0:T(8,128)(2,1)}, bf16[12,64,128]{2,1,0:T(8,128)(2,1)}, bf16[12,64,128]{2,1,0:T(8,128)(2,1)}) custom-call(bf16[96,64,128]{2,1,0:T(8,128)(2,1)S(1)} %bitcast.1), custom_call_target="tpu_custom_call" | custom-call | flops 1572864 | bytes 1572864 | tf_op jit(solution)/shard_map/power/pallas_call | solution.py:262
  2.6 0.6 copy-done.12
  3.2 2.0 %collective-permute-start = (f32[4,128]{1,0:T(4,128)S(1)}, f32[4,128]{1,0:T(4,128)S(1)}, u32[]{:S(2)}, u32[]{:S(2)}) collective-permute-start(f32[4,128]{1,0:T(4,128)S(1)} %get-tuple-element.66), channel_id=1, source_target_pairs={{0,1},{1,0},{2,3},{3,2},{4,5},{5,4},{6,7},{7,6},{8,9},{9,8},{10,11... | collective-permute-start | bytes 6152 | tf_op jit(solution)/shard_map/ppermute | solution.py:278
  5.3 1.3 %collective-permute-start.1 = (bf16[12,64,128]{2,1,0:T(8,128)(2,1)}, bf16[12,64,128]{2,1,0:T(8,128)(2,1)S(1)}, u32[]{:S(2)}, u32[]{:S(2)}) collective-permute-start(bf16[12,64,128]{2,1,0:T(8,128)(2,1)} %get-tuple-element.68), channel_id=1, source_target_pairs={{0,8},{2,10},{4,12},{6,14},{8,16},{10,18},{12,20},{14,22},{16,24},... | collective-permute-start | bytes 589832 | tf_op jit(solution)/shard_map/ppermute | solution.py:320
  6.6 1.3 %collective-permute-start.3 = (bf16[12,64,128]{2,1,0:T(8,128)(2,1)}, bf16[12,64,128]{2,1,0:T(8,128)(2,1)S(1)}, u32[]{:S(2)}, u32[]{:S(2)}) collective-permute-start(bf16[12,64,128]{2,1,0:T(8,128)(2,1)} %get-tuple-element.70), channel_id=1, source_target_pairs={{0,8},{2,10},{4,12},{6,14},{8,16},{10,18},{12,20},{14,22},{16,24},... | collective-permute-start | bytes 589832 | tf_op jit(solution)/shard_map/ppermute | solution.py:320
  7.8 0.0 copy-done.14
  7.9 0.1 convert_reduce_fusion.bounds_ref
  8.0 0.1 multiply_rsqrt_fusion.norm_ref
  8.1 0.0 collective-permute-done.halo_ref
  8.1 0.0 copy-done.1
  8.1 0.8 %copy-done.13 = f32[64,128]{1,0:T(8,128)S(1)} copy-done((f32[64,128]{1,0:T(8,128)S(1)}, f32[64,128]{1,0:T(8,128)}, u32[]{:S(2)}) %copy-start.13) | copy-done | bytes 32792
  8.8 0.5 left.1
  9.3 0.0 copy-start.2
  9.4 0.7 %copy-done.2 = bf16[15,64,128]{2,1,0:T(8,128)(2,1)} copy-done((bf16[15,64,128]{2,1,0:T(8,128)(2,1)}, bf16[15,64,128]{2,1,0:T(8,128)(2,1)S(1)}, u32[]{:S(2)}) %copy-start.2) | copy-done | bytes 245784
  10.0 0.7 %copy-done.4 = bf16[12,64,128]{2,1,0:T(8,128)(2,1)} copy-done((bf16[12,64,128]{2,1,0:T(8,128)(2,1)}, bf16[12,64,128]{2,1,0:T(8,128)(2,1)S(1)}, u32[]{:S(2)}) %copy-start.4) | copy-done | bytes 196632
  10.7 0.7 %copy-done.6 = bf16[12,64,128]{2,1,0:T(8,128)(2,1)} copy-done((bf16[12,64,128]{2,1,0:T(8,128)(2,1)}, bf16[12,64,128]{2,1,0:T(8,128)(2,1)S(1)}, u32[]{:S(2)}) %copy-start.6) | copy-done | bytes 196632
  11.4 0.7 %copy-done.8 = bf16[12,64,128]{2,1,0:T(8,128)(2,1)} copy-done((bf16[12,64,128]{2,1,0:T(8,128)(2,1)}, bf16[12,64,128]{2,1,0:T(8,128)(2,1)S(1)}, u32[]{:S(2)}) %copy-start.8) | copy-done | bytes 196632
  12.1 0.7 %copy-done.10 = bf16[12,64,128]{2,1,0:T(8,128)(2,1)} copy-done((bf16[12,64,128]{2,1,0:T(8,128)(2,1)}, bf16[12,64,128]{2,1,0:T(8,128)(2,1)S(1)}, u32[]{:S(2)}) %copy-start.10) | copy-done | bytes 196632
  12.8 0.1 collective-permute-done.1.refs_5_
  12.8 3.2 %collective-permute-start.2 = (bf16[4,128,1536]{2,1,0:T(8,128)(2,1)S(1)}, bf16[4,128,1536]{2,1,0:T(8,128)(2,1)S(1)}, u32[]{:S(2)}, u32[]{:S(2)}) collective-permute-start(bf16[4,128,1536]{2,1,0:T(8,128)(2,1)S(1)} %get-tuple-element.69.own_ref), channel_id=1, source_target_pairs={{0,2},{2,0},{4,6},{6,4},{8,10},{10,8},{12,14},{14,12},{16,18},{18,... | collective-permute-start | bytes 4718600 | tf_op jit(solution)/shard_map/ppermute | solution.py:322
  16.0 0.0 collective-permute-start.6
  16.1 0.0 copy-start.11
  16.1 1.0 %collective-permute-done.3.refs_4_ = bf16[12,64,128]{2,1,0:T(8,128)(2,1)S(1)} collective-permute-done((bf16[12,64,128]{2,1,0:T(8,128)(2,1)}, bf16[12,64,128]{2,1,0:T(8,128)(2,1)S(1)}, u32[]{:S(2)}, u32[]{:S(2)}) %collective-permute-start.3) | collective-permute-done | bytes 196640 | tf_op jit(solution)/shard_map/ppermute | solution.py:320
  17.1 0.9 %broadcast_select_fusion.7 = bf16[12,64,128]{2,1,0:T(8,128)(2,1)S(1)} fusion(bf16[12,64,128]{2,1,0:T(8,128)(2,1)S(1)} %collective-permute-done.3.refs_4_, bf16[12,64,128]{2,1,0:T(8,128)(2,1)} %get-tuple-element.70, pred[]{:T(512)S(6)} %eq.5), kind=kLoop, calls=%fused_computation.7 | loop fusion | flops 98304 | bytes 589825 | tf_op jit(solution)/shard_map/jit(_where)/select_n | solution.py:347
  18.0 0.4 collective-permute-start.7
  18.4 0.0 collective-permute-start.4
  18.4 0.9 %broadcast_select_fusion.6 = bf16[12,64,128]{2,1,0:T(8,128)(2,1)S(1)} fusion(bf16[12,64,128]{2,1,0:T(8,128)(2,1)S(1)} %collective-permute-done.1.refs_5_, bf16[12,64,128]{2,1,0:T(8,128)(2,1)} %get-tuple-element.68, pred[]{:T(512)S(6)} %eq.5), kind=kLoop, calls=%fused_computation.6 | loop fusion | flops 98304 | bytes 589825 | tf_op jit(solution)/shard_map/jit(_where)/select_n | solution.py:347
  19.3 0.3 collective-permute-start.5
  19.6 5.0 %collective-permute-done.6.refs_6_ = bf16[12,64,128]{2,1,0:T(8,128)(2,1)} collective-permute-done((bf16[12,64,128]{2,1,0:T(8,128)(2,1)}, bf16[12,64,128]{2,1,0:T(8,128)(2,1)}, u32[]{:S(2)}, u32[]{:S(2)}) %collective-permute-start.6) | collective-permute-done | bytes 196640 | tf_op jit(solution)/shard_map/ppermute | solution.py:320
  24.7 0.0 collective-permute-start.9
  24.7 0.0 collective-permute-done.7.refs_0_
  24.7 1.0 %broadcast_select_fusion.5 = bf16[12,64,128]{2,1,0:T(8,128)(2,1)S(1)} fusion(bf16[12,64,128]{2,1,0:T(8,128)(2,1)} %collective-permute-done.6.refs_6_, bf16[12,64,128]{2,1,0:T(8,128)(2,1)} %get-tuple-element.79, pred[]{:T(512)S(6)} %eq.5), kind=kLoop, calls=%fused_computation.5 | loop fusion | flops 98304 | bytes 589825 | tf_op jit(solution)/shard_map/jit(_where)/select_n | solution.py:347
  25.7 1.3 %collective-permute-start.10 = (bf16[12,64,128]{2,1,0:T(8,128)(2,1)S(1)}, bf16[12,64,128]{2,1,0:T(8,128)(2,1)S(1)}, u32[]{:S(2)}, u32[]{:S(2)}) collective-permute-start(bf16[12,64,128]{2,1,0:T(8,128)(2,1)S(1)} %broadcast_select_fusion.5), channel_id=1, source_target_pairs={{0,4},{2,6},{4,0},{6,2},{8,12},{10,14},{12,8},{14,10},{16,20},{18,... | collective-permute-start | bytes 589832 | tf_op jit(solution)/shard_map/ppermute | solution.py:349
  27.0 0.0 collective-permute-done.5.refs_1_
  27.0 2.5 %collective-permute-done.4.refs_7_ = bf16[15,64,128]{2,1,0:T(8,128)(2,1)S(1)} collective-permute-done((bf16[15,64,128]{2,1,0:T(8,128)(2,1)}, bf16[15,64,128]{2,1,0:T(8,128)(2,1)S(1)}, u32[]{:S(2)}, u32[]{:S(2)}) %collective-permute-start.4) | collective-permute-done | bytes 245792 | tf_op jit(solution)/shard_map/ppermute | solution.py:346
  29.5 1.4 %collective-permute-start.12 = (bf16[15,64,128]{2,1,0:T(8,128)(2,1)S(1)}, bf16[15,64,128]{2,1,0:T(8,128)(2,1)S(1)}, u32[]{:S(2)}, u32[]{:S(2)}) collective-permute-start(bf16[15,64,128]{2,1,0:T(8,128)(2,1)S(1)} %broadcast_select_fusion), channel_id=1, source_target_pairs={{0,4},{2,6},{4,0},{6,2},{8,12},{10,14},{12,8},{14,10},{16,20},{18,... | collective-permute-start | bytes 737288 | tf_op jit(solution)/shard_map/ppermute | solution.py:349
  30.9 0.0 collective-permute-start.11
  30.9 2.7 %collective-permute-done.9.refs_2_ = bf16[12,64,128]{2,1,0:T(8,128)(2,1)S(1)} collective-permute-done((bf16[12,64,128]{2,1,0:T(8,128)(2,1)}, bf16[12,64,128]{2,1,0:T(8,128)(2,1)S(1)}, u32[]{:S(2)}, u32[]{:S(2)}) %collective-permute-start.9) | collective-permute-done | bytes 196640 | tf_op jit(solution)/shard_map/ppermute | solution.py:346
  33.6 0.0 collective-permute-start.8
  33.6 0.0 collective-permute-done.10.refs_2_
  33.6 1.3 %collective-permute-start.13 = (bf16[12,64,128]{2,1,0:T(8,128)(2,1)S(1)}, bf16[12,64,128]{2,1,0:T(8,128)(2,1)S(1)}, u32[]{:S(2)}, u32[]{:S(2)}) collective-permute-start(bf16[12,64,128]{2,1,0:T(8,128)(2,1)S(1)} %broadcast_select_fusion.4), channel_id=1, source_target_pairs={{0,4},{2,6},{4,0},{6,2},{8,12},{10,14},{12,8},{14,10},{16,20},{18,... | collective-permute-start | bytes 589832 | tf_op jit(solution)/shard_map/ppermute | solution.py:349
  34.9 2.3 %collective-permute-done.11.refs_3_ = bf16[12,64,128]{2,1,0:T(8,128)(2,1)S(1)} collective-permute-done((bf16[12,64,128]{2,1,0:T(8,128)(2,1)S(1)}, bf16[12,64,128]{2,1,0:T(8,128)(2,1)S(1)}, u32[]{:S(2)}, u32[]{:S(2)}) %collective-permute-start.11) | collective-permute-done | bytes 196640 | tf_op jit(solution)/shard_map/ppermute | solution.py:346
  37.3 0.0 collective-permute-start.15
  37.3 0.3 collective-permute-done.12.refs_3_
  37.5 0.2 collective-permute-start.16
  37.7 0.0 collective-permute-done.2.mate_ref
  37.7 3.8 %cross.4 = (f32[2,2,4,128,128]{4,3,2,1,0:T(8,128)S(1)}, f32[2,2,4,128,128]{4,3,2,1,0:T(8,128)S(1)}) custom-call(s32[5]{0:T(128)S(1)} %convert_reduce_fusion.bounds_ref, f32[4]{0:T(128)S(1)} %multiply_rsqrt_fusion.norm_ref, bf16[4,128,1536]{2,1,0:T(8,128)(2,1)S(1)} %get-tuple-element.69.own_ref, bf16[4,128,1536]{2,1,0:T(8,128)(2,1)S(1)} %collective-permute-done.2.mate_ref, ...), custom_call_target="tpu_custom_call" | custom-call | flops 805306368 | tf_op jit(solution)/shard_map/cross/pallas_call | solution.py:307
  41.5 0.8 %collective-permute-done.8.refs_0_ = bf16[12,64,128]{2,1,0:T(8,128)(2,1)S(1)} collective-permute-done((bf16[12,64,128]{2,1,0:T(8,128)(2,1)S(1)}, bf16[12,64,128]{2,1,0:T(8,128)(2,1)S(1)}, u32[]{:S(2)}, u32[]{:S(2)}) %collective-permute-start.8) | collective-permute-done | bytes 196640 | tf_op jit(solution)/shard_map/ppermute | solution.py:346
  42.3 0.0 collective-permute-done.13.refs_0_
  42.3 1.3 %collective-permute-start.14 = (bf16[12,64,128]{2,1,0:T(8,128)(2,1)S(1)}, bf16[12,64,128]{2,1,0:T(8,128)(2,1)S(1)}, u32[]{:S(2)}, u32[]{:S(2)}) collective-permute-start(bf16[12,64,128]{2,1,0:T(8,128)(2,1)S(1)} %broadcast_select_fusion.2), channel_id=1, source_target_pairs={{0,4},{2,6},{4,0},{6,2},{8,12},{10,14},{12,8},{14,10},{16,20},{18,... | collective-permute-start | bytes 589832 | tf_op jit(solution)/shard_map/ppermute | solution.py:349
  43.7 3.2 %near.1.near_ref = f32[2,4,128,128]{3,2,1,0:T(8,128)S(1)} custom-call(s32[5]{0:T(128)S(1)} %convert_reduce_fusion.bounds_ref, f32[4]{0:T(128)S(1)} %multiply_rsqrt_fusion.norm_ref, bf16[4,128,1536]{2,1,0:T(8,128)(2,1)S(1)} %get-tuple-element.69.own_ref, bf16[4,128,1536]{2,1,0:T(8,128)(2,1)S(1)} %collective-permute-done.2.mate_ref), custom_call_target="tpu_custom_call" | custom-call | flops 1000 | bytes 1000 | tf_op jit(solution)/shard_map/near/pallas_call | solution.py:323
  46.8 0.0 collective-permute-done.15.refs_1_
  46.9 0.0 collective-permute-done.16.refs_1_
  46.9 0.3 collective-permute-start.17
  47.2 2.2 %collective-permute-done.14.refs_0_ = bf16[12,64,128]{2,1,0:T(8,128)(2,1)S(1)} collective-permute-done((bf16[12,64,128]{2,1,0:T(8,128)(2,1)S(1)}, bf16[12,64,128]{2,1,0:T(8,128)(2,1)S(1)}, u32[]{:S(2)}, u32[]{:S(2)}) %collective-permute-start.14) | collective-permute-done | bytes 196640 | tf_op jit(solution)/shard_map/ppermute | solution.py:349
  49.4 2.7 %cross.5 = (f32[2,2,4,128,128]{4,3,2,1,0:T(8,128)S(1)}, f32[2,2,4,128,128]{4,3,2,1,0:T(8,128)S(1)}) custom-call(s32[5]{0:T(128)S(1)} %convert_reduce_fusion.bounds_ref, f32[4]{0:T(128)S(1)} %multiply_rsqrt_fusion.norm_ref, bf16[4,128,1536]{2,1,0:T(8,128)(2,1)S(1)} %get-tuple-element.69.own_ref, bf16[4,128,1536]{2,1,0:T(8,128)(2,1)S(1)} %collective-permute-done.2.mate_ref, ...), custom_call_target="tpu_custom_call" | custom-call | flops 402653184 | tf_op jit(solution)/shard_map/cross/pallas_call | solution.py:307
  52.1 2.5 %cross.6.refs_3_.two_ref = f32[2,2,4,128,128]{4,3,2,1,0:T(8,128)S(1)} custom-call(s32[5]{0:T(128)S(1)} %convert_reduce_fusion.bounds_ref, f32[4]{0:T(128)S(1)} %multiply_rsqrt_fusion.norm_ref, bf16[4,128,1536]{2,1,0:T(8,128)(2,1)S(1)} %get-tuple-element.69.own_ref, bf16[4,128,1536]{2,1,0:T(8,128)(2,1)S(1)} %collective-permute-done.2.mate_ref, ...), custom_call_target="tpu_custom_call" | custom-call | flops 201326592 | tf_op jit(solution)/shard_map/cross/pallas_call | solution.py:307
  54.5 0.0 collective-permute-done.17.refs_1_
  54.5 2.5 %cross.7 = (f32[2,2,4,128,128]{4,3,2,1,0:T(8,128)S(1)}, bf16[2,2,4,128,128]{4,3,2,1,0:T(8,128)(2,1)S(1)}) custom-call(s32[5]{0:T(128)S(1)} %convert_reduce_fusion.bounds_ref, f32[4]{0:T(128)S(1)} %multiply_rsqrt_fusion.norm_ref, bf16[4,128,1536]{2,1,0:T(8,128)(2,1)S(1)} %get-tuple-element.69.own_ref, ...), custom_call_target="tpu_custom_call" | custom-call | flops 201326592 | tf_op jit(solution)/shard_map/cross/pallas_call | solution.py:307
  57.1 5.0 %collective-permute-start.18 = (bf16[2,2,4,128,128]{4,3,2,1,0:T(8,128)(2,1)S(1)}, bf16[2,2,4,128,128]{4,3,2,1,0:T(8,128)(2,1)S(1)}, u32[]{:S(2)}, u32[]{:S(2)}) collective-permute-start(bf16[2,2,4,128,128]{4,3,2,1,0:T(8,128)(2,1)S(1)} %get-tuple-element.118), channel_id=1, source_target_pairs={{0,2},{2,0},{4,6},{6,4},{8,10},{10,8},{12,14},{14,12},{16,18},{18,... | collective-permute-start | bytes 1572872 | tf_op jit(solution)/shard_map/ppermute | solution.py:361
  62.0 1.0 %put.2.before_ref = f32[2,4,4,128,128]{4,3,2,1,0:T(8,128)} custom-call(f32[2,2,4,128,128]{4,3,2,1,0:T(8,128)S(1)} %get-tuple-element.120.one_ref, f32[2,2,4,128,128]{4,3,2,1,0:T(8,128)S(1)} %cross.6.refs_3_.two_ref), custom_call_target="tpu_custom_call" | custom-call | flops 1000 | bytes 1000 | tf_op jit(solution)/shard_map/put/pallas_call | solution.py:362
  63.0 0.5 collective-permute-done.18.got_ref
  63.6 1.0 %put.3 = f32[2,4,4,128,128]{4,3,2,1,0:T(8,128)} custom-call(bf16[2,2,4,128,128]{4,3,2,1,0:T(8,128)(2,1)S(1)} %collective-permute-done.18.got_ref, f32[2,4,128,128]{3,2,1,0:T(8,128)S(1)} %near.1.near_ref, f32[2,4,4,128,128]{4,3,2,1,0:T(8,128)} %put.2.before_ref), custom_call_target="tpu_custom_call", output_to_operand_aliasing={{}: (2, {})} | custom-call | flops 1000 | bytes 1000 | tf_op jit(solution)/shard_map/put/pallas_call | solution.py:372
  (24 shorter events, 0.2 us)
Async XLA Ops:
  0.0 7.8 %copy-start.14 = (s32[64]{0:T(128)S(1)}, s32[64]{0:T(128)}, u32[]{:S(2)}) copy-start(s32[64]{0:T(128)} %param.3) | copy-start | bytes 772
  0.0 1.4 %copy-start = (bf16[2,48,64,128]{3,2,1,0:T(8,128)(2,1)S(1)}, bf16[2,48,64,128]{3,2,1,0:T(8,128)(2,1)}, u32[]{:S(2)}) copy-start(bf16[2,48,64,128]{3,2,1,0:T(8,128)(2,1)} %param.2) | copy-start | bytes 4718596
  1.4 6.6 %copy-start.1 = (bf16[2,48,64,128]{3,2,1,0:T(8,128)(2,1)S(1)}, bf16[2,48,64,128]{3,2,1,0:T(8,128)(2,1)}, u32[]{:S(2)}) copy-start(bf16[2,48,64,128]{3,2,1,0:T(8,128)(2,1)} %param.2) | copy-start | bytes 4718596
  2.6 0.6 copy-start.12
  3.2 4.8 %collective-permute-start = (f32[4,128]{1,0:T(4,128)S(1)}, f32[4,128]{1,0:T(4,128)S(1)}, u32[]{:S(2)}, u32[]{:S(2)}) collective-permute-start(f32[4,128]{1,0:T(4,128)S(1)} %get-tuple-element.66), channel_id=1, source_target_pairs={{0,1},{1,0},{2,3},{3,2},{4,5},{5,4},{6,7},{7,6},{8,9},{9,8},{10,11... | collective-permute-start | bytes 6152 | tf_op jit(solution)/shard_map/ppermute | solution.py:278
  5.3 7.6 %collective-permute-start.1 = (bf16[12,64,128]{2,1,0:T(8,128)(2,1)}, bf16[12,64,128]{2,1,0:T(8,128)(2,1)S(1)}, u32[]{:S(2)}, u32[]{:S(2)}) collective-permute-start(bf16[12,64,128]{2,1,0:T(8,128)(2,1)} %get-tuple-element.68), channel_id=1, source_target_pairs={{0,8},{2,10},{4,12},{6,14},{8,16},{10,18},{12,20},{14,22},{16,24},... | collective-permute-start | bytes 589832 | tf_op jit(solution)/shard_map/ppermute | solution.py:320
  6.6 10.5 %collective-permute-start.3 = (bf16[12,64,128]{2,1,0:T(8,128)(2,1)}, bf16[12,64,128]{2,1,0:T(8,128)(2,1)S(1)}, u32[]{:S(2)}, u32[]{:S(2)}) collective-permute-start(bf16[12,64,128]{2,1,0:T(8,128)(2,1)} %get-tuple-element.70), channel_id=1, source_target_pairs={{0,8},{2,10},{4,12},{6,14},{8,16},{10,18},{12,20},{14,22},{16,24},... | collective-permute-start | bytes 589832 | tf_op jit(solution)/shard_map/ppermute | solution.py:320
  8.1 0.8 %copy-start.13 = (f32[64,128]{1,0:T(8,128)S(1)}, f32[64,128]{1,0:T(8,128)}, u32[]{:S(2)}) copy-start(f32[64,128]{1,0:T(8,128)} %copy-done.12) | copy-start | bytes 98308
  9.3 0.7 %copy-start.2 = (bf16[15,64,128]{2,1,0:T(8,128)(2,1)}, bf16[15,64,128]{2,1,0:T(8,128)(2,1)S(1)}, u32[]{:S(2)}) copy-start(bf16[15,64,128]{2,1,0:T(8,128)(2,1)S(1)} %get-tuple-element.72) | copy-start | bytes 737284
  10.0 0.7 %copy-start.4 = (bf16[12,64,128]{2,1,0:T(8,128)(2,1)}, bf16[12,64,128]{2,1,0:T(8,128)(2,1)S(1)}, u32[]{:S(2)}) copy-start(bf16[12,64,128]{2,1,0:T(8,128)(2,1)S(1)} %get-tuple-element.104) | copy-start | bytes 589828
  10.7 0.7 %copy-start.6 = (bf16[12,64,128]{2,1,0:T(8,128)(2,1)}, bf16[12,64,128]{2,1,0:T(8,128)(2,1)S(1)}, u32[]{:S(2)}) copy-start(bf16[12,64,128]{2,1,0:T(8,128)(2,1)S(1)} %get-tuple-element.86) | copy-start | bytes 589828
  11.4 0.7 %copy-start.8 = (bf16[12,64,128]{2,1,0:T(8,128)(2,1)}, bf16[12,64,128]{2,1,0:T(8,128)(2,1)S(1)}, u32[]{:S(2)}) copy-start(bf16[12,64,128]{2,1,0:T(8,128)(2,1)S(1)} %get-tuple-element.91) | copy-start | bytes 589828
  12.1 0.7 %copy-start.10 = (bf16[12,64,128]{2,1,0:T(8,128)(2,1)}, bf16[12,64,128]{2,1,0:T(8,128)(2,1)S(1)}, u32[]{:S(2)}) copy-start(bf16[12,64,128]{2,1,0:T(8,128)(2,1)S(1)} %get-tuple-element.89) | copy-start | bytes 589828
  12.8 24.9 %collective-permute-start.2 = (bf16[4,128,1536]{2,1,0:T(8,128)(2,1)S(1)}, bf16[4,128,1536]{2,1,0:T(8,128)(2,1)S(1)}, u32[]{:S(2)}, u32[]{:S(2)}) collective-permute-start(bf16[4,128,1536]{2,1,0:T(8,128)(2,1)S(1)} %get-tuple-element.69.own_ref), channel_id=1, source_target_pairs={{0,2},{2,0},{4,6},{6,4},{8,10},{10,8},{12,14},{14,12},{16,18},{18,... | collective-permute-start | bytes 4718600 | tf_op jit(solution)/shard_map/ppermute | solution.py:322
  16.0 8.6 %collective-permute-start.6 = (bf16[12,64,128]{2,1,0:T(8,128)(2,1)}, bf16[12,64,128]{2,1,0:T(8,128)(2,1)}, u32[]{:S(2)}, u32[]{:S(2)}) collective-permute-start(bf16[12,64,128]{2,1,0:T(8,128)(2,1)} %get-tuple-element.79), channel_id=1, source_target_pairs={{0,8},{2,10},{4,12},{6,14},{8,16},{10,18},{12,20},{14,22},{16,24},... | collective-permute-start | bytes 589832 | tf_op jit(solution)/shard_map/ppermute | solution.py:320
  16.0 13.5 %copy-start.3 = (bf16[15,64,128]{2,1,0:T(8,128)(2,1)S(1)}, bf16[15,64,128]{2,1,0:T(8,128)(2,1)}, u32[]{:S(2)}) copy-start(bf16[15,64,128]{2,1,0:T(8,128)(2,1)} %copy-done.2) | copy-start | bytes 737284
  16.0 14.9 %copy-start.9 = (bf16[12,64,128]{2,1,0:T(8,128)(2,1)S(1)}, bf16[12,64,128]{2,1,0:T(8,128)(2,1)}, u32[]{:S(2)}) copy-start(bf16[12,64,128]{2,1,0:T(8,128)(2,1)} %copy-done.8) | copy-start | bytes 589828
  16.0 17.5 %copy-start.7 = (bf16[12,64,128]{2,1,0:T(8,128)(2,1)S(1)}, bf16[12,64,128]{2,1,0:T(8,128)(2,1)}, u32[]{:S(2)}) copy-start(bf16[12,64,128]{2,1,0:T(8,128)(2,1)} %copy-done.6) | copy-start | bytes 589828
  16.1 17.6 %copy-start.11 = (bf16[12,64,128]{2,1,0:T(8,128)(2,1)S(1)}, bf16[12,64,128]{2,1,0:T(8,128)(2,1)}, u32[]{:S(2)}) copy-start(bf16[12,64,128]{2,1,0:T(8,128)(2,1)} %copy-done.10) | copy-start | bytes 589828
  16.1 21.2 %copy-start.5 = (bf16[12,64,128]{2,1,0:T(8,128)(2,1)S(1)}, bf16[12,64,128]{2,1,0:T(8,128)(2,1)}, u32[]{:S(2)}) copy-start(bf16[12,64,128]{2,1,0:T(8,128)(2,1)} %copy-done.4) | copy-start | bytes 589828
  18.0 6.7 %collective-permute-start.7 = (bf16[12,64,128]{2,1,0:T(8,128)(2,1)S(1)}, bf16[12,64,128]{2,1,0:T(8,128)(2,1)S(1)}, u32[]{:S(2)}, u32[]{:S(2)}) collective-permute-start(bf16[12,64,128]{2,1,0:T(8,128)(2,1)S(1)} %broadcast_select_fusion.7), channel_id=1, source_target_pairs={{0,4},{2,6},{4,0},{6,2},{8,12},{10,14},{12,8},{14,10},{16,20},{18,... | collective-permute-start | bytes 589832 | tf_op jit(solution)/shard_map/ppermute | solution.py:349
  18.4 11.1 %collective-permute-start.4 = (bf16[15,64,128]{2,1,0:T(8,128)(2,1)}, bf16[15,64,128]{2,1,0:T(8,128)(2,1)S(1)}, u32[]{:S(2)}, u32[]{:S(2)}) collective-permute-start(bf16[15,64,128]{2,1,0:T(8,128)(2,1)} %copy-done.2), channel_id=1, source_target_pairs={{0,8},{2,10},{4,12},{6,14},{8,16},{10,18},{12,20},{14,22},{16,24},... | collective-permute-start | bytes 737288 | tf_op jit(solution)/shard_map/ppermute | solution.py:346
  19.3 7.6 %collective-permute-start.5 = (bf16[12,64,128]{2,1,0:T(8,128)(2,1)S(1)}, bf16[12,64,128]{2,1,0:T(8,128)(2,1)S(1)}, u32[]{:S(2)}, u32[]{:S(2)}) collective-permute-start(bf16[12,64,128]{2,1,0:T(8,128)(2,1)S(1)} %broadcast_select_fusion.6), channel_id=1, source_target_pairs={{0,4},{2,6},{4,0},{6,2},{8,12},{10,14},{12,8},{14,10},{16,20},{18,... | collective-permute-start | bytes 589832 | tf_op jit(solution)/shard_map/ppermute | solution.py:349
  24.7 8.9 %collective-permute-start.9 = (bf16[12,64,128]{2,1,0:T(8,128)(2,1)}, bf16[12,64,128]{2,1,0:T(8,128)(2,1)S(1)}, u32[]{:S(2)}, u32[]{:S(2)}) collective-permute-start(bf16[12,64,128]{2,1,0:T(8,128)(2,1)} %copy-done.10), channel_id=1, source_target_pairs={{0,8},{2,10},{4,12},{6,14},{8,16},{10,18},{12,20},{14,22},{16,24},... | collective-permute-start | bytes 589832 | tf_op jit(solution)/shard_map/ppermute | solution.py:346
  25.7 7.9 %collective-permute-start.10 = (bf16[12,64,128]{2,1,0:T(8,128)(2,1)S(1)}, bf16[12,64,128]{2,1,0:T(8,128)(2,1)S(1)}, u32[]{:S(2)}, u32[]{:S(2)}) collective-permute-start(bf16[12,64,128]{2,1,0:T(8,128)(2,1)S(1)} %broadcast_select_fusion.5), channel_id=1, source_target_pairs={{0,4},{2,6},{4,0},{6,2},{8,12},{10,14},{12,8},{14,10},{16,20},{18,... | collective-permute-start | bytes 589832 | tf_op jit(solution)/shard_map/ppermute | solution.py:349
  29.5 8.0 %collective-permute-start.12 = (bf16[15,64,128]{2,1,0:T(8,128)(2,1)S(1)}, bf16[15,64,128]{2,1,0:T(8,128)(2,1)S(1)}, u32[]{:S(2)}, u32[]{:S(2)}) collective-permute-start(bf16[15,64,128]{2,1,0:T(8,128)(2,1)S(1)} %broadcast_select_fusion), channel_id=1, source_target_pairs={{0,4},{2,6},{4,0},{6,2},{8,12},{10,14},{12,8},{14,10},{16,20},{18,... | collective-permute-start | bytes 737288 | tf_op jit(solution)/shard_map/ppermute | solution.py:349
  30.9 6.3 %collective-permute-start.11 = (bf16[12,64,128]{2,1,0:T(8,128)(2,1)S(1)}, bf16[12,64,128]{2,1,0:T(8,128)(2,1)S(1)}, u32[]{:S(2)}, u32[]{:S(2)}) collective-permute-start(bf16[12,64,128]{2,1,0:T(8,128)(2,1)S(1)} %copy-done.9), channel_id=1, source_target_pairs={{0,8},{2,10},{4,12},{6,14},{8,16},{10,18},{12,20},{14,22},{16,24},... | collective-permute-start | bytes 589832 | tf_op jit(solution)/shard_map/ppermute | solution.py:346
  33.6 8.7 %collective-permute-start.8 = (bf16[12,64,128]{2,1,0:T(8,128)(2,1)S(1)}, bf16[12,64,128]{2,1,0:T(8,128)(2,1)S(1)}, u32[]{:S(2)}, u32[]{:S(2)}) collective-permute-start(bf16[12,64,128]{2,1,0:T(8,128)(2,1)S(1)} %copy-done.7), channel_id=1, source_target_pairs={{0,8},{2,10},{4,12},{6,14},{8,16},{10,18},{12,20},{14,22},{16,24},... | collective-permute-start | bytes 589832 | tf_op jit(solution)/shard_map/ppermute | solution.py:346
  33.6 8.7 %collective-permute-start.13 = (bf16[12,64,128]{2,1,0:T(8,128)(2,1)S(1)}, bf16[12,64,128]{2,1,0:T(8,128)(2,1)S(1)}, u32[]{:S(2)}, u32[]{:S(2)}) collective-permute-start(bf16[12,64,128]{2,1,0:T(8,128)(2,1)S(1)} %broadcast_select_fusion.4), channel_id=1, source_target_pairs={{0,4},{2,6},{4,0},{6,2},{8,12},{10,14},{12,8},{14,10},{16,20},{18,... | collective-permute-start | bytes 589832 | tf_op jit(solution)/shard_map/ppermute | solution.py:349
  37.3 9.6 %collective-permute-start.15 = (bf16[12,64,128]{2,1,0:T(8,128)(2,1)S(1)}, bf16[12,64,128]{2,1,0:T(8,128)(2,1)S(1)}, u32[]{:S(2)}, u32[]{:S(2)}) collective-permute-start(bf16[12,64,128]{2,1,0:T(8,128)(2,1)S(1)} %copy-done.5), channel_id=1, source_target_pairs={{0,8},{2,10},{4,12},{6,14},{8,16},{10,18},{12,20},{14,22},{16,24},... | collective-permute-start | bytes 589832 | tf_op jit(solution)/shard_map/ppermute | solution.py:346
  37.5 9.3 %collective-permute-start.16 = (bf16[12,64,128]{2,1,0:T(8,128)(2,1)S(1)}, bf16[12,64,128]{2,1,0:T(8,128)(2,1)S(1)}, u32[]{:S(2)}, u32[]{:S(2)}) collective-permute-start(bf16[12,64,128]{2,1,0:T(8,128)(2,1)S(1)} %broadcast_select_fusion.3), channel_id=1, source_target_pairs={{0,4},{2,6},{4,0},{6,2},{8,12},{10,14},{12,8},{14,10},{16,20},{18,... | collective-permute-start | bytes 589832 | tf_op jit(solution)/shard_map/ppermute | solution.py:349
  42.3 7.0 %collective-permute-start.14 = (bf16[12,64,128]{2,1,0:T(8,128)(2,1)S(1)}, bf16[12,64,128]{2,1,0:T(8,128)(2,1)S(1)}, u32[]{:S(2)}, u32[]{:S(2)}) collective-permute-start(bf16[12,64,128]{2,1,0:T(8,128)(2,1)S(1)} %broadcast_select_fusion.2), channel_id=1, source_target_pairs={{0,4},{2,6},{4,0},{6,2},{8,12},{10,14},{12,8},{14,10},{16,20},{18,... | collective-permute-start | bytes 589832 | tf_op jit(solution)/shard_map/ppermute | solution.py:349
  46.9 7.6 %collective-permute-start.17 = (bf16[12,64,128]{2,1,0:T(8,128)(2,1)S(1)}, bf16[12,64,128]{2,1,0:T(8,128)(2,1)S(1)}, u32[]{:S(2)}, u32[]{:S(2)}) collective-permute-start(bf16[12,64,128]{2,1,0:T(8,128)(2,1)S(1)} %broadcast_select_fusion.1), channel_id=1, source_target_pairs={{0,4},{2,6},{4,0},{6,2},{8,12},{10,14},{12,8},{14,10},{16,20},{18,... | collective-permute-start | bytes 589832 | tf_op jit(solution)/shard_map/ppermute | solution.py:358
  57.1 6.5 %collective-permute-start.18 = (bf16[2,2,4,128,128]{4,3,2,1,0:T(8,128)(2,1)S(1)}, bf16[2,2,4,128,128]{4,3,2,1,0:T(8,128)(2,1)S(1)}, u32[]{:S(2)}, u32[]{:S(2)}) collective-permute-start(bf16[2,2,4,128,128]{4,3,2,1,0:T(8,128)(2,1)S(1)} %get-tuple-element.118), channel_id=1, source_target_pairs={{0,2},{2,0},{4,6},{6,4},{8,10},{10,8},{12,14},{14,12},{16,18},{18,... | collective-permute-start | bytes 1572872 | tf_op jit(solution)/shard_map/ppermute | solution.py:361

commit v4 on v3

--- a/solution.py
+++ b/solution.py
@@ -18,11 +18,13 @@
 TERMS = 3
 DEPTH = 3
 AHEAD = 2
+CHAIN = 1
 SETS = (4, 2, 2)
+LEFT_AFTER = 0
 OTHER_AFTER = 1
-NEAR_BEFORE = 7
-CROSS_BEFORE = (6, 8)
-VMEM_LIMIT = 16 * 1024 * 1024
+NEAR_BEFORE = 8
+CROSS_BEFORE = (7, 8)
+VMEM_LIMIT = 10 * 1024 * 1024
 
 
 def vmem():
@@ -122,35 +124,36 @@
         lax.fori_loop(low + 1, high + 1, lambda band, carry: add(group, band), None)
 
 
-def lefts(turned_ref, bounds_ref, group, band, start, stop):
-    half = turned_ref.shape[2] // 2
-    bins = group * GROUP + lax.broadcasted_iota(jnp.int32, (1, stop - start), 1) % GROUP
-    inside = (bins >= bounds_ref[band]) & (bins < bounds_ref[band + 1])
-    inside = inside.astype(jnp.float32).astype(jnp.bfloat16)
-    real = turned_ref[group, :, start:stop] * inside
-    parts = []
-    if start < half:
-        end = min(stop, half)
-        parts.append(turned_ref[group, :, start + half : end + half] * inside[:, : end - start])
-    if stop > half:
-        begin = max(start, half)
-        parts.append(turned_ref[group, :, begin - half : stop - half] * -inside[:, begin - start :])
-    return [real, parts[0] if len(parts) == 1 else jnp.concatenate(parts, axis=1)]
+def inside(bounds_ref, group, band, shape, dimension):
+    bins = group * GROUP + lax.broadcasted_iota(jnp.int32, shape, dimension) % GROUP
+    held = (bins >= bounds_ref[band]) & (bins < bounds_ref[band + 1])
+    return held.astype(jnp.float32).astype(jnp.bfloat16)
 
 
 def near_kernel(bounds_ref, norm_ref, own_ref, mate_ref, out_ref):
     groups, channels, span = own_ref.shape
+    half = span // 2
     bands = out_ref.shape[1]
     out_ref[...] = jnp.zeros_like(out_ref)
 
     def add(group, band):
-        left = jnp.concatenate(lefts(own_ref, bounds_ref, group, band, 0, span), axis=0)
-        product = lax.dot_general(
-            left, mate_ref[group], (((1,), (1,)), ((), ())), preferred_element_type=jnp.float32
-        )
-        product = product * norm_ref[band]
-        out_ref[0, band] += product[:channels]
-        out_ref[1, band] += product[channels:]
+        right = mate_ref[group] * inside(bounds_ref, group, band, (1, span), 1)
+        halves = []
+        for start in (0, half):
+            left = jnp.concatenate(
+                [own_ref[group, :, begin : begin + half] for begin in (start, half - start)], axis=0
+            )
+            halves.append(
+                lax.dot_general(
+                    left,
+                    right[:, start : start + half],
+                    (((1,), (1,)), ((), ())),
+                    preferred_element_type=jnp.float32,
+                )
+            )
+        low, high = halves
+        out_ref[0, band] += (low[:channels] + high[:channels]) * norm_ref[band]
+        out_ref[1, band] += (low[channels:] - high[channels:]) * norm_ref[band]
 
     @pl.when(lax.axis_index("ch") % 2 == 1)
     def _():
@@ -167,11 +170,15 @@
     sums = refs[:kinds]
     width, channels = rights[0][0].shape[1:]
     bands = sums[0].shape[2]
-    lanes = start * GROUP, (start + count * PIECE) * GROUP
+    half = own_ref.shape[2] // 2
+    lanes = slice(start * GROUP, (start + count * PIECE) * GROUP)
+    turned = lanes.start >= half
+    shift = -half if turned else half
+    across = slice(lanes.start + shift, lanes.stop + shift)
     for k in range(kinds):
         sums[k][...] = jnp.zeros_like(sums[k]) if first else befores[k][...]
 
-    def column(right, here):
+    def column(right, here, held):
         scale = None
         if first:
             for term in range(TERMS):
@@ -182,25 +189,23 @@
             block = ref[:PIECE, here, :]
             if first and index < RAW:
                 block = (block.astype(jnp.float32) * scale[None]).astype(jnp.bfloat16)
-            blocks.append(block.reshape(PIECE * GROUP, channels))
+            blocks.append((block * held[None]).reshape(PIECE * GROUP, channels))
         return jnp.concatenate(blocks, axis=0)
 
     def add(group, band):
         here = slice(group * GROUP, (group + 1) * GROUP)
+        held = inside(bounds_ref, group, band, (GROUP, channels), 0)
         left = jnp.concatenate(
-            lefts(own_ref, bounds_ref, group, band, *lanes)
-            + lefts(mate_ref, bounds_ref, group, band, *lanes),
-            axis=0,
+            [ref[group, :, part] for ref in (own_ref, mate_ref) for part in (lanes, across)], axis=0
         )
-        right = jnp.concatenate([column(right, here) for right in rights], axis=1)
+        right = jnp.concatenate([column(right, here, held) for right in rights], axis=1)
         product = jnp.dot(left, right, preferred_element_type=jnp.float32) * norm_ref[band]
         for k in range(kinds):
             for owner in range(2):
                 for part in range(2):
                     row = (2 * owner + part) * channels
-                    sums[k][part, owner, band] += product[
-                        row : row + channels, k * channels : (k + 1) * channels
-                    ]
+                    term = product[row : row + channels, k * channels : (k + 1) * channels]
+                    sums[k][part, owner, band] += -term if part and turned else term
 
     each_band(bounds_ref, width // GROUP, bands, add)
     if last:
@@ -209,10 +214,15 @@
 
 
 def put_own_kernel(one_ref, two_ref, out_ref, sems):
-    copies = [
-        pltpu.make_async_copy(value.at[:, 0], out_ref.at[:, turn], sems.at[k])
-        for k, (turn, value) in enumerate(((1, one_ref), (3, two_ref)))
-    ]
+    copies = []
+    for turn, value in ((1, one_ref), (3, two_ref)):
+        for part in range(2):
+            for band in range(out_ref.shape[2]):
+                copies.append(
+                    pltpu.make_async_copy(
+                        value.at[part, 0, band], out_ref.at[part, turn, band], sems.at[turn // 2, part, band]
+                    )
+                )
     for copy in copies:
         copy.start()
     for copy in copies:
@@ -221,14 +231,22 @@
 
 def put_got_kernel(got_ref, near_ref, before_ref, out_ref, wide, sems):
     core = lax.axis_index("ch") % 2
-    wide[0] = got_ref[0].astype(jnp.float32)
-    far = pltpu.make_async_copy(wide.at[0], out_ref.at[:, 2 * core], sems.at[0])
-    far.start()
-    wide[1] = jnp.where(core == 0, got_ref[1].astype(jnp.float32), near_ref[...])
-    near = pltpu.make_async_copy(wide.at[1], out_ref.at[:, 2 - 2 * core], sems.at[1])
-    near.start()
-    far.wait()
-    near.wait()
+    copies = []
+    for k, turn in enumerate((2 * core, 2 - 2 * core)):
+        for part in range(2):
+            for band in range(out_ref.shape[2]):
+                value = got_ref[k, part, band].astype(jnp.float32)
+                if k == 1:
+                    value = jnp.where(core == 0, value, near_ref[part, band])
+                wide[k, part, band] = value
+                copies.append(
+                    pltpu.make_async_copy(
+                        wide.at[k, part, band], out_ref.at[part, turn, band], sems.at[k, part, band]
+                    )
+                )
+                copies[-1].start()
+    for copy in copies:
+        copy.wait()
 
 
 def after(value, other):
@@ -276,6 +294,9 @@
     power, norms = after(power, norms)
 
     halo = lax.ppermute(edge, "fq", [(0, 1), (1, 0)])
+    twos = {k: lax.ppermute(early[k], "ch", ahead) for k in range(RAW)}
+    if LEFT_AFTER >= 0:
+        twos[LEFT_AFTER], halo = after(twos[LEFT_AFTER], halo)
     left, *late = call(
         left_kernel,
         "left",
@@ -294,7 +315,7 @@
     send_shape = jax.ShapeDtypeStruct((2, 2, band_width, channels, channels), jnp.bfloat16)
 
     sets = [range(sum(SETS[:s]), sum(SETS[: s + 1])) for s in range(len(SETS))]
-    twos, ones, onward = {}, {}, {}
+    ones, onward = {}, {}
     sums = {}
 
     def cross(these, flights, befores, last=()):
@@ -316,7 +337,7 @@
             0 * nbytes,
         )(*operands)
 
-    for k in range(DEPTH):
+    for k in range(RAW, DEPTH):
         twos[k] = lax.ppermute(mine[k], "ch", ahead)
     left, twos[OTHER_AFTER] = after(left, twos[OTHER_AFTER])
     other = lax.ppermute(left, "ch", mate)
@@ -339,7 +360,7 @@
                 twos[k], sums[s][0] = after(twos[k], sums[s][0])
         if k >= AHEAD:
             twos[k], ones[k - AHEAD] = after(twos[k], ones[k - AHEAD])
-        if k > 0:
+        if CHAIN and k > 0:
             twos[k], onward[k - 1] = after(twos[k], onward[k - 1])
         if k + DEPTH < pieces:
             twos[k], later = after(twos[k], mine[k + DEPTH])
@@ -367,7 +388,7 @@
         hbm(),
         1000,
         1000,
-        scratch_shapes=[pltpu.SemaphoreType.DMA((2,))],
+        scratch_shapes=[pltpu.SemaphoreType.DMA((2, 2, band_width))],
     )(one_sum, two_sum)
     return call(
         put_got_kernel,
@@ -380,7 +401,7 @@
         input_output_aliases={2: 0},
         scratch_shapes=[
             pltpu.VMEM((2,) + near_shape.shape, jnp.float32),
-            pltpu.SemaphoreType.DMA((2,)),
+            pltpu.SemaphoreType.DMA((2, 2, band_width)),
         ],
     )(got, near, out)
 

time: 65.2 us -> 65.1 us (level)
  waiting for transfers between devices: 17.4 us -> 23.3 us
  local copies, waits for them, and re-layouts: 6.23 us -> 1.43 us
  starting transfers between devices: 19.3 us -> 22.2 us
  other arithmetic: 3.19 us -> 0.39 us
  Pallas kernels: 18.3 us -> 17.5 us
    ppermute x7, waiting for transfers between devices: 2.46 us -> 11.8 us  [shards(): ones[k] = lax.ppermute(onward[k], 'ch', beside)]
    unnamed x30 -> x6, local copies, waits for them, and re-layouts: 6.23 us -> 1.43 us
    ppermute x5, waiting for transfers between devices: 8.28 us -> 4.64 us  [shards(): twos[k + DEPTH] = lax.ppermute(later, 'ch', ahead)]
    ppermute x7, starting transfers between devices: 6.17 us -> 9.29 us  [shards(): ones[k] = lax.ppermute(onward[k], 'ch', beside)]
    select_n x8, other arithmetic: 2.99 us -> 0.19 us  [shards(): onward[k] = jnp.where(odd_chip, twos[k], mine[k])]
    ppermute x1, starting transfers between devices: 4.97 us -> 2.53 us  [shards(): got = lax.ppermute(sent, 'ch', mate)]
    ppermute x3, starting transfers between devices: 2.6 us -> 4.77 us  [shards(): twos = {k: lax.ppermute(early[k], 'ch', ahead) for k in range(RAW)}]
    ppermute x5, starting transfers between devices: 0.01 us -> 1.64 us  [shards(): twos[k + DEPTH] = lax.ppermute(later, 'ch', ahead)]
  transfers between devices with their start and end apart: 19 -> 19, of which waited for: 10 -> 12; matrix products, arithmetic and copies ran while one was open for 5% -> 1% of each run, Pallas kernels for 21% -> 21%
where the time goes in v4:
time: 65.1 us; the launch traced here: 65 us
  waiting for transfers between devices  23.3 us (36%)
  starting transfers between devices  22.2 us (34%)
  Pallas kernels  17.5 us (27%)
  local copies, waits for them, and re-layouts  1.43 us (2%)
    ppermute x7, waiting for transfers between devices, shards(): ones[k] = lax.ppermute(onward[k], 'ch', beside)  11.8 us
    pallas_call x4, Pallas kernels, cross(): call(functools.partial(cross_kernel, these[0] * PIECE, len(these), kinds,...  11.2 us
    ppermute x7, starting transfers between devices, shards(): ones[k] = lax.ppermute(onward[k], 'ch', beside)  9.29 us
    ppermute x3, waiting for transfers between devices, shards(): twos = {k: lax.ppermute(early[k], 'ch', ahead) for k in range(RAW)}  6.8 us
    ppermute x3, starting transfers between devices, shards(): twos = {k: lax.ppermute(early[k], 'ch', ahead) for k in range(RAW)}  4.77 us
    ppermute x5, waiting for transfers between devices, shards(): twos[k + DEPTH] = lax.ppermute(later, 'ch', ahead)  4.64 us
    pallas_call x1, Pallas kernels, shards(): call(near_kernel, 'near', near_shape, [smem(), smem(), vmem(), vmem()], v...  3.22 us
    ppermute x1, starting transfers between devices, shards(): got = lax.ppermute(sent, 'ch', mate)  2.53 us
  transfers between devices with their start and end apart: 19, of which 12 were waited for; matrix products, arithmetic and copies ran while one was open for 1% of the time, Pallas kernels for 21%

profile of v4, /device:TPU:1, one launch (start us, length us, event | category | flops | bytes accessed | tf_op | source)
XLA Modules:
  0.0 65.0 jit_solution(13992299038045038588)
XLA Ops:
  0.0 0.0 copy-start.2
  0.0 0.0 copy-start
  0.0 1.4 %copy-done = bf16[2,48,64,128]{3,2,1,0:T(8,128)(2,1)S(1)} copy-done((bf16[2,48,64,128]{3,2,1,0:T(8,128)(2,1)S(1)}, bf16[2,48,64,128]{3,2,1,0:T(8,128)(2,1)}, u32[]{:S(2)}) %copy-start) | copy-done | bytes 1572888
  1.4 0.0 copy-start.1
  1.4 0.4 power.1
  1.8 2.2 %collective-permute-start = (bf16[12,64,128]{2,1,0:T(8,128)(2,1)S(1)}, bf16[12,64,128]{2,1,0:T(8,128)(2,1)S(1)}, u32[]{:S(2)}, u32[]{:S(2)}) collective-permute-start(bf16[12,64,128]{2,1,0:T(8,128)(2,1)S(1)} %get-tuple-element.66), channel_id=1, source_target_pairs={{0,8},{2,10},{4,12},{6,14},{8,16},{10,18},{12,20},{14,22},{16,24},... | collective-permute-start | bytes 589832 | tf_op jit(solution)/shard_map/ppermute | solution.py:297
  4.0 1.2 %collective-permute-start.1 = (f32[4,128]{1,0:T(4,128)S(1)}, f32[4,128]{1,0:T(4,128)S(1)}, u32[]{:S(2)}, u32[]{:S(2)}) collective-permute-start(f32[4,128]{1,0:T(4,128)S(1)} %get-tuple-element.67), channel_id=1, source_target_pairs={{0,1},{1,0},{2,3},{3,2},{4,5},{5,4},{6,7},{7,6},{8,9},{9,8},{10,11... | collective-permute-start | bytes 6152 | tf_op jit(solution)/shard_map/ppermute | solution.py:296
  5.2 1.3 %collective-permute-start.2 = (bf16[12,64,128]{2,1,0:T(8,128)(2,1)S(1)}, bf16[12,64,128]{2,1,0:T(8,128)(2,1)S(1)}, u32[]{:S(2)}, u32[]{:S(2)}) collective-permute-start(bf16[12,64,128]{2,1,0:T(8,128)(2,1)S(1)} %get-tuple-element.70), channel_id=1, source_target_pairs={{0,8},{2,10},{4,12},{6,14},{8,16},{10,18},{12,20},{14,22},{16,24},... | collective-permute-start | bytes 589832 | tf_op jit(solution)/shard_map/ppermute | solution.py:297
  6.5 1.3 %collective-permute-start.6 = (bf16[12,64,128]{2,1,0:T(8,128)(2,1)S(1)}, bf16[12,64,128]{2,1,0:T(8,128)(2,1)S(1)}, u32[]{:S(2)}, u32[]{:S(2)}) collective-permute-start(bf16[12,64,128]{2,1,0:T(8,128)(2,1)S(1)} %get-tuple-element.81), channel_id=1, source_target_pairs={{0,8},{2,10},{4,12},{6,14},{8,16},{10,18},{12,20},{14,22},{16,24},... | collective-permute-start | bytes 589832 | tf_op jit(solution)/shard_map/ppermute | solution.py:297
  7.8 0.0 copy-done.2
  7.8 0.1 convert_reduce_fusion.bounds_ref
  7.9 0.1 multiply_rsqrt_fusion.norm_ref
  8.0 0.0 collective-permute-done.1.halo_ref
  8.0 2.6 %collective-permute-done.refs_4_ = bf16[12,64,128]{2,1,0:T(8,128)(2,1)S(1)} collective-permute-done((bf16[12,64,128]{2,1,0:T(8,128)(2,1)S(1)}, bf16[12,64,128]{2,1,0:T(8,128)(2,1)S(1)}, u32[]{:S(2)}, u32[]{:S(2)}) %collective-permute-start) | collective-permute-done | bytes 196640 | tf_op jit(solution)/shard_map/ppermute | solution.py:297
  10.6 0.0 copy-done.1
  10.7 0.5 left.1
  11.2 3.7 %collective-permute-done.2.refs_5_ = bf16[12,64,128]{2,1,0:T(8,128)(2,1)S(1)} collective-permute-done((bf16[12,64,128]{2,1,0:T(8,128)(2,1)S(1)}, bf16[12,64,128]{2,1,0:T(8,128)(2,1)S(1)}, u32[]{:S(2)}, u32[]{:S(2)}) %collective-permute-start.2) | collective-permute-done | bytes 196640 | tf_op jit(solution)/shard_map/ppermute | solution.py:297
  14.9 2.1 %collective-permute-start.3 = (bf16[4,128,1536]{2,1,0:T(8,128)(2,1)S(1)}, bf16[4,128,1536]{2,1,0:T(8,128)(2,1)S(1)}, u32[]{:S(2)}, u32[]{:S(2)}) collective-permute-start(bf16[4,128,1536]{2,1,0:T(8,128)(2,1)S(1)} %get-tuple-element.71.own_ref), channel_id=1, source_target_pairs={{0,2},{2,0},{4,6},{6,4},{8,10},{10,8},{12,14},{14,12},{16,18},{18,... | collective-permute-start | bytes 4718600 | tf_op jit(solution)/shard_map/ppermute | solution.py:343
  16.9 0.0 collective-permute-start.4
  16.9 1.6 %collective-permute-start.7 = (bf16[12,64,128]{2,1,0:T(8,128)(2,1)S(1)}, bf16[12,64,128]{2,1,0:T(8,128)(2,1)S(1)}, u32[]{:S(2)}, u32[]{:S(2)}) collective-permute-start(bf16[12,64,128]{2,1,0:T(8,128)(2,1)S(1)} %broadcast_select_fusion.7), channel_id=1, source_target_pairs={{0,4},{2,6},{4,0},{6,2},{8,12},{10,14},{12,8},{14,10},{16,20},{18,... | collective-permute-start | bytes 589832 | tf_op jit(solution)/shard_map/ppermute | solution.py:370
  18.5 0.1 collective-permute-start.5
  18.6 0.5 collective-permute-done.6.refs_6_
  19.1 0.5 collective-permute-start.9
  19.6 3.9 %collective-permute-done.7.refs_0_ = bf16[12,64,128]{2,1,0:T(8,128)(2,1)S(1)} collective-permute-done((bf16[12,64,128]{2,1,0:T(8,128)(2,1)S(1)}, bf16[12,64,128]{2,1,0:T(8,128)(2,1)S(1)}, u32[]{:S(2)}, u32[]{:S(2)}) %collective-permute-start.7) | collective-permute-done | bytes 196640 | tf_op jit(solution)/shard_map/ppermute | solution.py:370
  23.6 1.5 %collective-permute-start.10 = (bf16[12,64,128]{2,1,0:T(8,128)(2,1)S(1)}, bf16[12,64,128]{2,1,0:T(8,128)(2,1)S(1)}, u32[]{:S(2)}, u32[]{:S(2)}) collective-permute-start(bf16[12,64,128]{2,1,0:T(8,128)(2,1)S(1)} %broadcast_select_fusion.5), channel_id=1, source_target_pairs={{0,4},{2,6},{4,0},{6,2},{8,12},{10,14},{12,8},{14,10},{16,20},{18,... | collective-permute-start | bytes 589832 | tf_op jit(solution)/shard_map/ppermute | solution.py:370
  25.1 2.7 %collective-permute-done.5.refs_1_ = bf16[12,64,128]{2,1,0:T(8,128)(2,1)S(1)} collective-permute-done((bf16[12,64,128]{2,1,0:T(8,128)(2,1)S(1)}, bf16[12,64,128]{2,1,0:T(8,128)(2,1)S(1)}, u32[]{:S(2)}, u32[]{:S(2)}) %collective-permute-start.5) | collective-permute-done | bytes 196640 | tf_op jit(solution)/shard_map/ppermute | solution.py:370
  27.8 0.0 collective-permute-done.4.refs_7_
  27.8 1.5 %collective-permute-start.13 = (bf16[15,64,128]{2,1,0:T(8,128)(2,1)S(1)}, bf16[15,64,128]{2,1,0:T(8,128)(2,1)S(1)}, u32[]{:S(2)}, u32[]{:S(2)}) collective-permute-start(bf16[15,64,128]{2,1,0:T(8,128)(2,1)S(1)} %broadcast_select_fusion), channel_id=1, source_target_pairs={{0,4},{2,6},{4,0},{6,2},{8,12},{10,14},{12,8},{14,10},{16,20},{18,... | collective-permute-start | bytes 737288 | tf_op jit(solution)/shard_map/ppermute | solution.py:370
  29.3 0.5 collective-permute-start.12
  29.8 0.7 %collective-permute-done.9.refs_2_ = bf16[12,64,128]{2,1,0:T(8,128)(2,1)S(1)} collective-permute-done((bf16[12,64,128]{2,1,0:T(8,128)(2,1)S(1)}, bf16[12,64,128]{2,1,0:T(8,128)(2,1)S(1)}, u32[]{:S(2)}, u32[]{:S(2)}) %collective-permute-start.9) | collective-permute-done | bytes 196640 | tf_op jit(solution)/shard_map/ppermute | solution.py:367
  30.5 0.6 collective-permute-start.8
  31.1 0.9 %collective-permute-done.10.refs_2_ = bf16[12,64,128]{2,1,0:T(8,128)(2,1)S(1)} collective-permute-done((bf16[12,64,128]{2,1,0:T(8,128)(2,1)S(1)}, bf16[12,64,128]{2,1,0:T(8,128)(2,1)S(1)}, u32[]{:S(2)}, u32[]{:S(2)}) %collective-permute-start.10) | collective-permute-done | bytes 196640 | tf_op jit(solution)/shard_map/ppermute | solution.py:370
  32.0 1.5 %collective-permute-start.11 = (bf16[12,64,128]{2,1,0:T(8,128)(2,1)S(1)}, bf16[12,64,128]{2,1,0:T(8,128)(2,1)S(1)}, u32[]{:S(2)}, u32[]{:S(2)}) collective-permute-start(bf16[12,64,128]{2,1,0:T(8,128)(2,1)S(1)} %broadcast_select_fusion.4), channel_id=1, source_target_pairs={{0,4},{2,6},{4,0},{6,2},{8,12},{10,14},{12,8},{14,10},{16,20},{18,... | collective-permute-start | bytes 589832 | tf_op jit(solution)/shard_map/ppermute | solution.py:370
  33.5 2.5 %collective-permute-done.12.refs_3_ = bf16[12,64,128]{2,1,0:T(8,128)(2,1)S(1)} collective-permute-done((bf16[12,64,128]{2,1,0:T(8,128)(2,1)S(1)}, bf16[12,64,128]{2,1,0:T(8,128)(2,1)S(1)}, u32[]{:S(2)}, u32[]{:S(2)}) %collective-permute-start.12) | collective-permute-done | bytes 196640 | tf_op jit(solution)/shard_map/ppermute | solution.py:367
  36.1 0.0 collective-permute-start.15
  36.1 1.2 %collective-permute-done.13.refs_3_ = bf16[15,64,128]{2,1,0:T(8,128)(2,1)S(1)} collective-permute-done((bf16[15,64,128]{2,1,0:T(8,128)(2,1)S(1)}, bf16[15,64,128]{2,1,0:T(8,128)(2,1)S(1)}, u32[]{:S(2)}, u32[]{:S(2)}) %collective-permute-start.13) | collective-permute-done | bytes 245792 | tf_op jit(solution)/shard_map/ppermute | solution.py:370
  37.3 1.5 %collective-permute-start.16 = (bf16[12,64,128]{2,1,0:T(8,128)(2,1)S(1)}, bf16[12,64,128]{2,1,0:T(8,128)(2,1)S(1)}, u32[]{:S(2)}, u32[]{:S(2)}) collective-permute-start(bf16[12,64,128]{2,1,0:T(8,128)(2,1)S(1)} %broadcast_select_fusion.3), channel_id=1, source_target_pairs={{0,4},{2,6},{4,0},{6,2},{8,12},{10,14},{12,8},{14,10},{16,20},{18,... | collective-permute-start | bytes 589832 | tf_op jit(solution)/shard_map/ppermute | solution.py:370
  38.8 1.4 %collective-permute-done.8.refs_0_ = bf16[12,64,128]{2,1,0:T(8,128)(2,1)S(1)} collective-permute-done((bf16[12,64,128]{2,1,0:T(8,128)(2,1)S(1)}, bf16[12,64,128]{2,1,0:T(8,128)(2,1)S(1)}, u32[]{:S(2)}, u32[]{:S(2)}) %collective-permute-start.8) | collective-permute-done | bytes 196640 | tf_op jit(solution)/shard_map/ppermute | solution.py:367
  40.3 1.2 %collective-permute-done.11.refs_0_ = bf16[12,64,128]{2,1,0:T(8,128)(2,1)S(1)} collective-permute-done((bf16[12,64,128]{2,1,0:T(8,128)(2,1)S(1)}, bf16[12,64,128]{2,1,0:T(8,128)(2,1)S(1)}, u32[]{:S(2)}, u32[]{:S(2)}) %collective-permute-start.11) | collective-permute-done | bytes 196640 | tf_op jit(solution)/shard_map/ppermute | solution.py:370
  41.5 1.5 %collective-permute-start.14 = (bf16[12,64,128]{2,1,0:T(8,128)(2,1)S(1)}, bf16[12,64,128]{2,1,0:T(8,128)(2,1)S(1)}, u32[]{:S(2)}, u32[]{:S(2)}) collective-permute-start(bf16[12,64,128]{2,1,0:T(8,128)(2,1)S(1)} %broadcast_select_fusion.2), channel_id=1, source_target_pairs={{0,4},{2,6},{4,0},{6,2},{8,12},{10,14},{12,8},{14,10},{16,20},{18,... | collective-permute-start | bytes 589832 | tf_op jit(solution)/shard_map/ppermute | solution.py:370
  43.0 0.0 collective-permute-done.3.mate_ref
  43.0 3.4 %cross.4 = (f32[2,2,4,128,128]{4,3,2,1,0:T(8,128)S(1)}, f32[2,2,4,128,128]{4,3,2,1,0:T(8,128)S(1)}) custom-call(s32[5]{0:T(128)S(1)} %convert_reduce_fusion.bounds_ref, f32[4]{0:T(128)S(1)} %multiply_rsqrt_fusion.norm_ref, bf16[4,128,1536]{2,1,0:T(8,128)(2,1)S(1)} %get-tuple-element.71.own_ref, bf16[4,128,1536]{2,1,0:T(8,128)(2,1)S(1)} %collective-permute-done.3.mate_ref, ...), custom_call_target="tpu_custom_call" | custom-call | flops 805306368 | tf_op jit(solution)/shard_map/cross/pallas_call | solution.py:328
  46.5 0.0 collective-permute-done.15.refs_1_
  46.5 0.0 collective-permute-done.16.refs_1_
  46.5 0.7 %collective-permute-start.17 = (bf16[12,64,128]{2,1,0:T(8,128)(2,1)S(1)}, bf16[12,64,128]{2,1,0:T(8,128)(2,1)S(1)}, u32[]{:S(2)}, u32[]{:S(2)}) collective-permute-start(bf16[12,64,128]{2,1,0:T(8,128)(2,1)S(1)} %broadcast_select_fusion.1), channel_id=1, source_target_pairs={{0,4},{2,6},{4,0},{6,2},{8,12},{10,14},{12,8},{14,10},{16,20},{18,... | collective-permute-start | bytes 589832 | tf_op jit(solution)/shard_map/ppermute | solution.py:379
  47.2 1.9 %collective-permute-done.14.refs_0_ = bf16[12,64,128]{2,1,0:T(8,128)(2,1)S(1)} collective-permute-done((bf16[12,64,128]{2,1,0:T(8,128)(2,1)S(1)}, bf16[12,64,128]{2,1,0:T(8,128)(2,1)S(1)}, u32[]{:S(2)}, u32[]{:S(2)}) %collective-permute-start.14) | collective-permute-done | bytes 196640 | tf_op jit(solution)/shard_map/ppermute | solution.py:370
  49.2 2.7 %cross.5 = (f32[2,2,4,128,128]{4,3,2,1,0:T(8,128)S(1)}, f32[2,2,4,128,128]{4,3,2,1,0:T(8,128)S(1)}) custom-call(s32[5]{0:T(128)S(1)} %convert_reduce_fusion.bounds_ref, f32[4]{0:T(128)S(1)} %multiply_rsqrt_fusion.norm_ref, bf16[4,128,1536]{2,1,0:T(8,128)(2,1)S(1)} %get-tuple-element.71.own_ref, bf16[4,128,1536]{2,1,0:T(8,128)(2,1)S(1)} %collective-permute-done.3.mate_ref, ...), custom_call_target="tpu_custom_call" | custom-call | flops 402653184 | tf_op jit(solution)/shard_map/cross/pallas_call | solution.py:328
  51.9 2.5 %cross.6.refs_3_.two_ref = f32[2,2,4,128,128]{4,3,2,1,0:T(8,128)S(1)} custom-call(s32[5]{0:T(128)S(1)} %convert_reduce_fusion.bounds_ref, f32[4]{0:T(128)S(1)} %multiply_rsqrt_fusion.norm_ref, bf16[4,128,1536]{2,1,0:T(8,128)(2,1)S(1)} %get-tuple-element.71.own_ref, bf16[4,128,1536]{2,1,0:T(8,128)(2,1)S(1)} %collective-permute-done.3.mate_ref, ...), custom_call_target="tpu_custom_call" | custom-call | flops 201326592 | tf_op jit(solution)/shard_map/cross/pallas_call | solution.py:328
  54.4 0.0 collective-permute-done.17.refs_1_
  54.4 2.6 %cross.7 = (f32[2,2,4,128,128]{4,3,2,1,0:T(8,128)S(1)}, bf16[2,2,4,128,128]{4,3,2,1,0:T(8,128)(2,1)S(1)}) custom-call(s32[5]{0:T(128)S(1)} %convert_reduce_fusion.bounds_ref, f32[4]{0:T(128)S(1)} %multiply_rsqrt_fusion.norm_ref, bf16[4,128,1536]{2,1,0:T(8,128)(2,1)S(1)} %get-tuple-element.71.own_ref, ...), custom_call_target="tpu_custom_call" | custom-call | flops 201326592 | tf_op jit(solution)/shard_map/cross/pallas_call | solution.py:328
  57.0 2.5 %collective-permute-start.18 = (bf16[2,2,4,128,128]{4,3,2,1,0:T(8,128)(2,1)S(1)}, bf16[2,2,4,128,128]{4,3,2,1,0:T(8,128)(2,1)S(1)}, u32[]{:S(2)}, u32[]{:S(2)}) collective-permute-start(bf16[2,2,4,128,128]{4,3,2,1,0:T(8,128)(2,1)S(1)} %get-tuple-element.119), channel_id=1, source_target_pairs={{0,2},{2,0},{4,6},{6,4},{8,10},{10,8},{12,14},{14,12},{16,18},{18,... | collective-permute-start | bytes 1572872 | tf_op jit(solution)/shard_map/ppermute | solution.py:382
  59.5 3.2 %near.1.near_ref = f32[2,4,128,128]{3,2,1,0:T(8,128)S(1)} custom-call(s32[5]{0:T(128)S(1)} %convert_reduce_fusion.bounds_ref, f32[4]{0:T(128)S(1)} %multiply_rsqrt_fusion.norm_ref, bf16[4,128,1536]{2,1,0:T(8,128)(2,1)S(1)} %get-tuple-element.71.own_ref, bf16[4,128,1536]{2,1,0:T(8,128)(2,1)S(1)} %collective-permute-done.3.mate_ref), custom_call_target="tpu_custom_call" | custom-call | flops 1000 | bytes 1000 | tf_op jit(solution)/shard_map/near/pallas_call | solution.py:344
  62.8 1.1 %put.2.before_ref = f32[2,4,4,128,128]{4,3,2,1,0:T(8,128)} custom-call(f32[2,2,4,128,128]{4,3,2,1,0:T(8,128)S(1)} %get-tuple-element.120.one_ref, f32[2,2,4,128,128]{4,3,2,1,0:T(8,128)S(1)} %cross.6.refs_3_.two_ref), custom_call_target="tpu_custom_call" | custom-call | flops 1000 | bytes 1000 | tf_op jit(solution)/shard_map/put/pallas_call | solution.py:383
  63.9 0.0 collective-permute-done.18.got_ref
  63.9 1.1 %put.3 = f32[2,4,4,128,128]{4,3,2,1,0:T(8,128)} custom-call(bf16[2,2,4,128,128]{4,3,2,1,0:T(8,128)(2,1)S(1)} %collective-permute-done.18.got_ref, f32[2,4,128,128]{3,2,1,0:T(8,128)S(1)} %near.1.near_ref, f32[2,4,4,128,128]{4,3,2,1,0:T(8,128)} %put.2.before_ref), custom_call_target="tpu_custom_call", output_to_operand_aliasing={{}: (2, {})} | custom-call | flops 1000 | bytes 1000 | tf_op jit(solution)/shard_map/put/pallas_call | solution.py:393
  (9 shorter events, 0.2 us)
Async XLA Ops:
  0.0 7.8 %copy-start.2 = (s32[64]{0:T(128)S(1)}, s32[64]{0:T(128)}, u32[]{:S(2)}) copy-start(s32[64]{0:T(128)} %param.3) | copy-start | bytes 772
  0.0 1.4 %copy-start = (bf16[2,48,64,128]{3,2,1,0:T(8,128)(2,1)S(1)}, bf16[2,48,64,128]{3,2,1,0:T(8,128)(2,1)}, u32[]{:S(2)}) copy-start(bf16[2,48,64,128]{3,2,1,0:T(8,128)(2,1)} %param.2) | copy-start | bytes 4718596
  1.4 9.2 %copy-start.1 = (bf16[2,48,64,128]{3,2,1,0:T(8,128)(2,1)S(1)}, bf16[2,48,64,128]{3,2,1,0:T(8,128)(2,1)}, u32[]{:S(2)}) copy-start(bf16[2,48,64,128]{3,2,1,0:T(8,128)(2,1)} %param.2) | copy-start | bytes 4718596
  1.8 8.8 %collective-permute-start = (bf16[12,64,128]{2,1,0:T(8,128)(2,1)S(1)}, bf16[12,64,128]{2,1,0:T(8,128)(2,1)S(1)}, u32[]{:S(2)}, u32[]{:S(2)}) collective-permute-start(bf16[12,64,128]{2,1,0:T(8,128)(2,1)S(1)} %get-tuple-element.66), channel_id=1, source_target_pairs={{0,8},{2,10},{4,12},{6,14},{8,16},{10,18},{12,20},{14,22},{16,24},... | collective-permute-start | bytes 589832 | tf_op jit(solution)/shard_map/ppermute | solution.py:297
  4.0 4.0 %collective-permute-start.1 = (f32[4,128]{1,0:T(4,128)S(1)}, f32[4,128]{1,0:T(4,128)S(1)}, u32[]{:S(2)}, u32[]{:S(2)}) collective-permute-start(f32[4,128]{1,0:T(4,128)S(1)} %get-tuple-element.67), channel_id=1, source_target_pairs={{0,1},{1,0},{2,3},{3,2},{4,5},{5,4},{6,7},{7,6},{8,9},{9,8},{10,11... | collective-permute-start | bytes 6152 | tf_op jit(solution)/shard_map/ppermute | solution.py:296
  5.2 9.7 %collective-permute-start.2 = (bf16[12,64,128]{2,1,0:T(8,128)(2,1)S(1)}, bf16[12,64,128]{2,1,0:T(8,128)(2,1)S(1)}, u32[]{:S(2)}, u32[]{:S(2)}) collective-permute-start(bf16[12,64,128]{2,1,0:T(8,128)(2,1)S(1)} %get-tuple-element.70), channel_id=1, source_target_pairs={{0,8},{2,10},{4,12},{6,14},{8,16},{10,18},{12,20},{14,22},{16,24},... | collective-permute-start | bytes 589832 | tf_op jit(solution)/shard_map/ppermute | solution.py:297
  6.5 12.6 %collective-permute-start.6 = (bf16[12,64,128]{2,1,0:T(8,128)(2,1)S(1)}, bf16[12,64,128]{2,1,0:T(8,128)(2,1)S(1)}, u32[]{:S(2)}, u32[]{:S(2)}) collective-permute-start(bf16[12,64,128]{2,1,0:T(8,128)(2,1)S(1)} %get-tuple-element.81), channel_id=1, source_target_pairs={{0,8},{2,10},{4,12},{6,14},{8,16},{10,18},{12,20},{14,22},{16,24},... | collective-permute-start | bytes 589832 | tf_op jit(solution)/shard_map/ppermute | solution.py:297
  14.9 28.2 %collective-permute-start.3 = (bf16[4,128,1536]{2,1,0:T(8,128)(2,1)S(1)}, bf16[4,128,1536]{2,1,0:T(8,128)(2,1)S(1)}, u32[]{:S(2)}, u32[]{:S(2)}) collective-permute-start(bf16[4,128,1536]{2,1,0:T(8,128)(2,1)S(1)} %get-tuple-element.71.own_ref), channel_id=1, source_target_pairs={{0,2},{2,0},{4,6},{6,4},{8,10},{10,8},{12,14},{14,12},{16,18},{18,... | collective-permute-start | bytes 4718600 | tf_op jit(solution)/shard_map/ppermute | solution.py:343
  16.9 10.9 %collective-permute-start.4 = (bf16[15,64,128]{2,1,0:T(8,128)(2,1)S(1)}, bf16[15,64,128]{2,1,0:T(8,128)(2,1)S(1)}, u32[]{:S(2)}, u32[]{:S(2)}) collective-permute-start(bf16[15,64,128]{2,1,0:T(8,128)(2,1)S(1)} %get-tuple-element.74), channel_id=1, source_target_pairs={{0,8},{2,10},{4,12},{6,14},{8,16},{10,18},{12,20},{14,22},{16,24},... | collective-permute-start | bytes 737288 | tf_op jit(solution)/shard_map/ppermute | solution.py:367
  16.9 6.6 %collective-permute-start.7 = (bf16[12,64,128]{2,1,0:T(8,128)(2,1)S(1)}, bf16[12,64,128]{2,1,0:T(8,128)(2,1)S(1)}, u32[]{:S(2)}, u32[]{:S(2)}) collective-permute-start(bf16[12,64,128]{2,1,0:T(8,128)(2,1)S(1)} %broadcast_select_fusion.7), channel_id=1, source_target_pairs={{0,4},{2,6},{4,0},{6,2},{8,12},{10,14},{12,8},{14,10},{16,20},{18,... | collective-permute-start | bytes 589832 | tf_op jit(solution)/shard_map/ppermute | solution.py:370
  18.5 9.3 %collective-permute-start.5 = (bf16[12,64,128]{2,1,0:T(8,128)(2,1)S(1)}, bf16[12,64,128]{2,1,0:T(8,128)(2,1)S(1)}, u32[]{:S(2)}, u32[]{:S(2)}) collective-permute-start(bf16[12,64,128]{2,1,0:T(8,128)(2,1)S(1)} %broadcast_select_fusion.6), channel_id=1, source_target_pairs={{0,4},{2,6},{4,0},{6,2},{8,12},{10,14},{12,8},{14,10},{16,20},{18,... | collective-permute-start | bytes 589832 | tf_op jit(solution)/shard_map/ppermute | solution.py:370
  19.1 11.4 %collective-permute-start.9 = (bf16[12,64,128]{2,1,0:T(8,128)(2,1)S(1)}, bf16[12,64,128]{2,1,0:T(8,128)(2,1)S(1)}, u32[]{:S(2)}, u32[]{:S(2)}) collective-permute-start(bf16[12,64,128]{2,1,0:T(8,128)(2,1)S(1)} %get-tuple-element.89), channel_id=1, source_target_pairs={{0,8},{2,10},{4,12},{6,14},{8,16},{10,18},{12,20},{14,22},{16,24},... | collective-permute-start | bytes 589832 | tf_op jit(solution)/shard_map/ppermute | solution.py:367
  23.6 8.4 %collective-permute-start.10 = (bf16[12,64,128]{2,1,0:T(8,128)(2,1)S(1)}, bf16[12,64,128]{2,1,0:T(8,128)(2,1)S(1)}, u32[]{:S(2)}, u32[]{:S(2)}) collective-permute-start(bf16[12,64,128]{2,1,0:T(8,128)(2,1)S(1)} %broadcast_select_fusion.5), channel_id=1, source_target_pairs={{0,4},{2,6},{4,0},{6,2},{8,12},{10,14},{12,8},{14,10},{16,20},{18,... | collective-permute-start | bytes 589832 | tf_op jit(solution)/shard_map/ppermute | solution.py:370
  27.8 9.4 %collective-permute-start.13 = (bf16[15,64,128]{2,1,0:T(8,128)(2,1)S(1)}, bf16[15,64,128]{2,1,0:T(8,128)(2,1)S(1)}, u32[]{:S(2)}, u32[]{:S(2)}) collective-permute-start(bf16[15,64,128]{2,1,0:T(8,128)(2,1)S(1)} %broadcast_select_fusion), channel_id=1, source_target_pairs={{0,4},{2,6},{4,0},{6,2},{8,12},{10,14},{12,8},{14,10},{16,20},{18,... | collective-permute-start | bytes 737288 | tf_op jit(solution)/shard_map/ppermute | solution.py:370
  29.3 6.7 %collective-permute-start.12 = (bf16[12,64,128]{2,1,0:T(8,128)(2,1)S(1)}, bf16[12,64,128]{2,1,0:T(8,128)(2,1)S(1)}, u32[]{:S(2)}, u32[]{:S(2)}) collective-permute-start(bf16[12,64,128]{2,1,0:T(8,128)(2,1)S(1)} %get-tuple-element.96), channel_id=1, source_target_pairs={{0,8},{2,10},{4,12},{6,14},{8,16},{10,18},{12,20},{14,22},{16,24},... | collective-permute-start | bytes 589832 | tf_op jit(solution)/shard_map/ppermute | solution.py:367
  30.5 9.8 %collective-permute-start.8 = (bf16[12,64,128]{2,1,0:T(8,128)(2,1)S(1)}, bf16[12,64,128]{2,1,0:T(8,128)(2,1)S(1)}, u32[]{:S(2)}, u32[]{:S(2)}) collective-permute-start(bf16[12,64,128]{2,1,0:T(8,128)(2,1)S(1)} %get-tuple-element.88), channel_id=1, source_target_pairs={{0,8},{2,10},{4,12},{6,14},{8,16},{10,18},{12,20},{14,22},{16,24},... | collective-permute-start | bytes 589832 | tf_op jit(solution)/shard_map/ppermute | solution.py:367
  32.0 9.5 %collective-permute-start.11 = (bf16[12,64,128]{2,1,0:T(8,128)(2,1)S(1)}, bf16[12,64,128]{2,1,0:T(8,128)(2,1)S(1)}, u32[]{:S(2)}, u32[]{:S(2)}) collective-permute-start(bf16[12,64,128]{2,1,0:T(8,128)(2,1)S(1)} %broadcast_select_fusion.4), channel_id=1, source_target_pairs={{0,4},{2,6},{4,0},{6,2},{8,12},{10,14},{12,8},{14,10},{16,20},{18,... | collective-permute-start | bytes 589832 | tf_op jit(solution)/shard_map/ppermute | solution.py:370
  36.1 10.4 %collective-permute-start.15 = (bf16[12,64,128]{2,1,0:T(8,128)(2,1)S(1)}, bf16[12,64,128]{2,1,0:T(8,128)(2,1)S(1)}, u32[]{:S(2)}, u32[]{:S(2)}) collective-permute-start(bf16[12,64,128]{2,1,0:T(8,128)(2,1)S(1)} %get-tuple-element.100), channel_id=1, source_target_pairs={{0,8},{2,10},{4,12},{6,14},{8,16},{10,18},{12,20},{14,22},{16,24},... | collective-permute-start | bytes 589832 | tf_op jit(solution)/shard_map/ppermute | solution.py:367
  37.3 9.2 %collective-permute-start.16 = (bf16[12,64,128]{2,1,0:T(8,128)(2,1)S(1)}, bf16[12,64,128]{2,1,0:T(8,128)(2,1)S(1)}, u32[]{:S(2)}, u32[]{:S(2)}) collective-permute-start(bf16[12,64,128]{2,1,0:T(8,128)(2,1)S(1)} %broadcast_select_fusion.3), channel_id=1, source_target_pairs={{0,4},{2,6},{4,0},{6,2},{8,12},{10,14},{12,8},{14,10},{16,20},{18,... | collective-permute-start | bytes 589832 | tf_op jit(solution)/shard_map/ppermute | solution.py:370
  41.5 7.7 %collective-permute-start.14 = (bf16[12,64,128]{2,1,0:T(8,128)(2,1)S(1)}, bf16[12,64,128]{2,1,0:T(8,128)(2,1)S(1)}, u32[]{:S(2)}, u32[]{:S(2)}) collective-permute-start(bf16[12,64,128]{2,1,0:T(8,128)(2,1)S(1)} %broadcast_select_fusion.2), channel_id=1, source_target_pairs={{0,4},{2,6},{4,0},{6,2},{8,12},{10,14},{12,8},{14,10},{16,20},{18,... | collective-permute-start | bytes 589832 | tf_op jit(solution)/shard_map/ppermute | solution.py:370
  46.5 7.9 %collective-permute-start.17 = (bf16[12,64,128]{2,1,0:T(8,128)(2,1)S(1)}, bf16[12,64,128]{2,1,0:T(8,128)(2,1)S(1)}, u32[]{:S(2)}, u32[]{:S(2)}) collective-permute-start(bf16[12,64,128]{2,1,0:T(8,128)(2,1)S(1)} %broadcast_select_fusion.1), channel_id=1, source_target_pairs={{0,4},{2,6},{4,0},{6,2},{8,12},{10,14},{12,8},{14,10},{16,20},{18,... | collective-permute-start | bytes 589832 | tf_op jit(solution)/shard_map/ppermute | solution.py:379
  57.0 6.9 %collective-permute-start.18 = (bf16[2,2,4,128,128]{4,3,2,1,0:T(8,128)(2,1)S(1)}, bf16[2,2,4,128,128]{4,3,2,1,0:T(8,128)(2,1)S(1)}, u32[]{:S(2)}, u32[]{:S(2)}) collective-permute-start(bf16[2,2,4,128,128]{4,3,2,1,0:T(8,128)(2,1)S(1)} %get-tuple-element.119), channel_id=1, source_target_pairs={{0,2},{2,0},{4,6},{6,4},{8,10},{10,8},{12,14},{14,12},{16,18},{18,... | collective-permute-start | bytes 1572872 | tf_op jit(solution)/shard_map/ppermute | solution.py:382

commit v5 on v4

--- a/solution.py
+++ b/solution.py
@@ -16,14 +16,14 @@
 PIECE = 12
 RAW = 3
 TERMS = 3
-DEPTH = 3
-AHEAD = 2
+Z_AFTER = (-1, -1, -1, 0, 1, 2, 3, 4)
+Y_AFTER = (-1, -1, 0, 1, 2, 3, 4, 5)
 CHAIN = 1
 SETS = (4, 2, 2)
 LEFT_AFTER = 0
-OTHER_AFTER = 1
-NEAR_BEFORE = 8
-CROSS_BEFORE = (7, 8)
+OTHER_AFTER = 0
+NEAR_BEFORE = 7
+CROSS_BEFORE = (8, 8)
 VMEM_LIMIT = 10 * 1024 * 1024
 
 
@@ -118,16 +118,17 @@
 
 def each_band(bounds_ref, groups, bands, add):
     for group in range(groups):
-        low = band_at(bounds_ref, bands, group * GROUP)
-        high = band_at(bounds_ref, bands, (group + 1) * GROUP - 1)
-        add(group, low)
-        lax.fori_loop(low + 1, high + 1, lambda band, carry: add(group, band), None)
-
-
-def inside(bounds_ref, group, band, shape, dimension):
+        band = band_at(bounds_ref, bands, group * GROUP)
+        add(group, band, bounds_ref[band], bounds_ref[band + 1])
+    for band in range(1, bands):
+        low = bounds_ref[band]
+        high = jnp.where(low % GROUP == 0, low, bounds_ref[band + 1])
+        add(jnp.minimum(low // GROUP, groups - 1), band, low, high)
+
+
+def inside(group, low, high, shape, dimension):
     bins = group * GROUP + lax.broadcasted_iota(jnp.int32, shape, dimension) % GROUP
-    held = (bins >= bounds_ref[band]) & (bins < bounds_ref[band + 1])
-    return held.astype(jnp.float32).astype(jnp.bfloat16)
+    return ((bins >= low) & (bins < high)).astype(jnp.float32).astype(jnp.bfloat16)
 
 
 def near_kernel(bounds_ref, norm_ref, own_ref, mate_ref, out_ref):
@@ -136,8 +137,8 @@
     bands = out_ref.shape[1]
     out_ref[...] = jnp.zeros_like(out_ref)
 
-    def add(group, band):
-        right = mate_ref[group] * inside(bounds_ref, group, band, (1, span), 1)
+    def add(group, band, low, high):
+        right = mate_ref[group] * inside(group, low, high, (1, span), 1)
         halves = []
         for start in (0, half):
             left = jnp.concatenate(
@@ -151,9 +152,8 @@
                     preferred_element_type=jnp.float32,
                 )
             )
-        low, high = halves
-        out_ref[0, band] += (low[:channels] + high[:channels]) * norm_ref[band]
-        out_ref[1, band] += (low[channels:] - high[channels:]) * norm_ref[band]
+        out_ref[0, band] += (halves[0][:channels] + halves[1][:channels]) * norm_ref[band]
+        out_ref[1, band] += (halves[0][channels:] - halves[1][channels:]) * norm_ref[band]
 
     @pl.when(lax.axis_index("ch") % 2 == 1)
     def _():
@@ -192,9 +192,10 @@
             blocks.append((block * held[None]).reshape(PIECE * GROUP, channels))
         return jnp.concatenate(blocks, axis=0)
 
-    def add(group, band):
-        here = slice(group * GROUP, (group + 1) * GROUP)
-        held = inside(bounds_ref, group, band, (GROUP, channels), 0)
+    def add(group, band, low, high):
+        begin = group * GROUP
+        here = pl.ds(begin if isinstance(group, int) else pl.multiple_of(begin, GROUP), GROUP)
+        held = inside(group, low, high, (GROUP, channels), 0)
         left = jnp.concatenate(
             [ref[group, :, part] for ref in (own_ref, mate_ref) for part in (lanes, across)], axis=0
         )
@@ -337,8 +338,9 @@
             0 * nbytes,
         )(*operands)
 
-    for k in range(RAW, DEPTH):
-        twos[k] = lax.ppermute(mine[k], "ch", ahead)
+    for k in range(RAW, pieces):
+        if Z_AFTER[k] < 0:
+            twos[k] = lax.ppermute(mine[k], "ch", ahead)
     left, twos[OTHER_AFTER] = after(left, twos[OTHER_AFTER])
     other = lax.ppermute(left, "ch", mate)
     near = call(
@@ -358,13 +360,14 @@
             if CROSS_BEFORE[s] == k:
                 sums[s] = list(cross(sets[s], (ones, twos), sums.get(s - 1)))
                 twos[k], sums[s][0] = after(twos[k], sums[s][0])
-        if k >= AHEAD:
-            twos[k], ones[k - AHEAD] = after(twos[k], ones[k - AHEAD])
+        if Y_AFTER[k] >= 0:
+            twos[k], ones[Y_AFTER[k]] = after(twos[k], ones[Y_AFTER[k]])
         if CHAIN and k > 0:
             twos[k], onward[k - 1] = after(twos[k], onward[k - 1])
-        if k + DEPTH < pieces:
-            twos[k], later = after(twos[k], mine[k + DEPTH])
-            twos[k + DEPTH] = lax.ppermute(later, "ch", ahead)
+        for later in range(pieces):
+            if Z_AFTER[later] == k:
+                twos[k], mine[later] = after(twos[k], mine[later])
+                twos[later] = lax.ppermute(mine[later], "ch", ahead)
         onward[k] = jnp.where(odd_chip, twos[k], mine[k])
         if k < pieces - 1:
             ones[k] = lax.ppermute(onward[k], "ch", beside)

time: 65.1 us -> 61.4 us (0.943)
  Pallas kernels: 17.5 us -> 13 us
  starting transfers between devices: 22.2 us -> 23.2 us
    pallas_call x4, Pallas kernels: 11.2 us -> 7.62 us  [cross(): call(functools.partial(cross_kernel, these[0] * PIECE, len(these), kinds,...]
    ppermute x1, starting transfers between devices: 2.53 us -> 4.06 us  [shards(): got = lax.ppermute(sent, 'ch', mate)]
    ppermute x5, starting transfers between devices: 1.64 us -> 0.31 us  [shards(): twos[later] = lax.ppermute(mine[later], 'ch', ahead)]
    ppermute x1, starting transfers between devices: 2.06 us -> 3.26 us  [shards(): other = lax.ppermute(left, 'ch', mate)]
    ppermute x7, starting transfers between devices: 9.29 us -> 8.23 us  [shards(): ones[k] = lax.ppermute(onward[k], 'ch', beside)]
    pallas_call x1, Pallas kernels: 3.22 us -> 2.3 us  [shards(): call(near_kernel, 'near', near_shape, [smem(), smem(), vmem(), vmem()], v...]
    ppermute x1, starting transfers between devices: 1.21 us -> 2.11 us  [shards(): halo = lax.ppermute(edge, 'fq', [(0, 1), (1, 0)])]
    ppermute x3, starting transfers between devices: 4.77 us -> 3.89 us  [shards(): twos = {k: lax.ppermute(early[k], 'ch', ahead) for k in range(RAW)}]
  transfers between devices with their start and end apart: 19 -> 19, of which waited for: 12 -> 14; matrix products, arithmetic and copies ran while one was open for 1% -> 1% of each run, Pallas kernels for 21% -> 16%
where the time goes in v5:
time: 61.4 us; the launch traced here: 61 us
  starting transfers between devices  23.2 us (38%)
  waiting for transfers between devices  22.8 us (37%)
  Pallas kernels  13 us (21%)
  local copies, waits for them, and re-layouts  1.43 us (2%)
    ppermute x7, waiting for transfers between devices, shards(): ones[k] = lax.ppermute(onward[k], 'ch', beside)  11.7 us
    ppermute x7, starting transfers between devices, shards(): ones[k] = lax.ppermute(onward[k], 'ch', beside)  8.23 us
    pallas_call x4, Pallas kernels, cross(): call(functools.partial(cross_kernel, these[0] * PIECE, len(these), kinds,...  7.62 us
    ppermute x3, waiting for transfers between devices, shards(): twos = {k: lax.ppermute(early[k], 'ch', ahead) for k in range(RAW)}  6.16 us
    ppermute x5, waiting for transfers between devices, shards(): twos[later] = lax.ppermute(mine[later], 'ch', ahead)  4.49 us
    ppermute x1, starting transfers between devices, shards(): got = lax.ppermute(sent, 'ch', mate)  4.06 us
    ppermute x3, starting transfers between devices, shards(): twos = {k: lax.ppermute(early[k], 'ch', ahead) for k in range(RAW)}  3.89 us
    ppermute x1, starting transfers between devices, shards(): other = lax.ppermute(left, 'ch', mate)  3.26 us
  transfers between devices with their start and end apart: 19, of which 14 were waited for; matrix products, arithmetic and copies ran while one was open for 1% of the time, Pallas kernels for 16%

profile of v5, /device:TPU:1, one launch (start us, length us, event | category | flops | bytes accessed | tf_op | source)
XLA Modules:
  0.0 61.0 jit_solution(15217400263920872857)
XLA Ops:
  0.0 0.0 copy-start.2
  0.0 0.0 copy-start
  0.0 1.4 %copy-done = bf16[2,48,64,128]{3,2,1,0:T(8,128)(2,1)S(1)} copy-done((bf16[2,48,64,128]{3,2,1,0:T(8,128)(2,1)S(1)}, bf16[2,48,64,128]{3,2,1,0:T(8,128)(2,1)}, u32[]{:S(2)}) %copy-start) | copy-done | bytes 1572888
  1.4 0.0 copy-start.1
  1.4 0.4 power.1
  1.8 2.1 %collective-permute-start.1 = (f32[4,128]{1,0:T(4,128)S(1)}, f32[4,128]{1,0:T(4,128)S(1)}, u32[]{:S(2)}, u32[]{:S(2)}) collective-permute-start(f32[4,128]{1,0:T(4,128)S(1)} %get-tuple-element.71), channel_id=1, source_target_pairs={{0,1},{1,0},{2,3},{3,2},{4,5},{5,4},{6,7},{7,6},{8,9},{9,8},{10,11... | collective-permute-start | bytes 6152 | tf_op jit(solution)/shard_map/ppermute | solution.py:297
  3.9 1.3 %collective-permute-start = (bf16[12,64,128]{2,1,0:T(8,128)(2,1)S(1)}, bf16[12,64,128]{2,1,0:T(8,128)(2,1)S(1)}, u32[]{:S(2)}, u32[]{:S(2)}) collective-permute-start(bf16[12,64,128]{2,1,0:T(8,128)(2,1)S(1)} %get-tuple-element.70), channel_id=1, source_target_pairs={{0,8},{2,10},{4,12},{6,14},{8,16},{10,18},{12,20},{14,22},{16,24},... | collective-permute-start | bytes 589832 | tf_op jit(solution)/shard_map/ppermute | solution.py:298
  5.2 1.3 %collective-permute-start.4 = (bf16[12,64,128]{2,1,0:T(8,128)(2,1)S(1)}, bf16[12,64,128]{2,1,0:T(8,128)(2,1)S(1)}, u32[]{:S(2)}, u32[]{:S(2)}) collective-permute-start(bf16[12,64,128]{2,1,0:T(8,128)(2,1)S(1)} %get-tuple-element.79), channel_id=1, source_target_pairs={{0,8},{2,10},{4,12},{6,14},{8,16},{10,18},{12,20},{14,22},{16,24},... | collective-permute-start | bytes 589832 | tf_op jit(solution)/shard_map/ppermute | solution.py:298
  6.5 1.3 %collective-permute-start.6 = (bf16[12,64,128]{2,1,0:T(8,128)(2,1)S(1)}, bf16[12,64,128]{2,1,0:T(8,128)(2,1)S(1)}, u32[]{:S(2)}, u32[]{:S(2)}) collective-permute-start(bf16[12,64,128]{2,1,0:T(8,128)(2,1)S(1)} %get-tuple-element.85), channel_id=1, source_target_pairs={{0,8},{2,10},{4,12},{6,14},{8,16},{10,18},{12,20},{14,22},{16,24},... | collective-permute-start | bytes 589832 | tf_op jit(solution)/shard_map/ppermute | solution.py:298
  7.8 0.0 copy-done.2
  7.8 0.1 convert_reduce_fusion.bounds_ref
  7.9 0.1 multiply_rsqrt_fusion.norm_ref
  8.0 0.0 collective-permute-done.1.halo_ref
  8.0 3.3 %collective-permute-done.refs_4_ = bf16[12,64,128]{2,1,0:T(8,128)(2,1)S(1)} collective-permute-done((bf16[12,64,128]{2,1,0:T(8,128)(2,1)S(1)}, bf16[12,64,128]{2,1,0:T(8,128)(2,1)S(1)}, u32[]{:S(2)}, u32[]{:S(2)}) %collective-permute-start) | collective-permute-done | bytes 196640 | tf_op jit(solution)/shard_map/ppermute | solution.py:298
  11.3 0.0 copy-done.1
  11.3 0.5 left.1
  11.8 3.3 %collective-permute-start.2 = (bf16[4,128,1536]{2,1,0:T(8,128)(2,1)S(1)}, bf16[4,128,1536]{2,1,0:T(8,128)(2,1)S(1)}, u32[]{:S(2)}, u32[]{:S(2)}) collective-permute-start(bf16[4,128,1536]{2,1,0:T(8,128)(2,1)S(1)} %get-tuple-element.75.own_ref), channel_id=1, source_target_pairs={{0,2},{2,0},{4,6},{6,4},{8,10},{10,8},{12,14},{14,12},{16,18},{18,... | collective-permute-start | bytes 4718600 | tf_op jit(solution)/shard_map/ppermute | solution.py:345
  15.1 1.3 %collective-permute-start.7 = (bf16[12,64,128]{2,1,0:T(8,128)(2,1)S(1)}, bf16[12,64,128]{2,1,0:T(8,128)(2,1)S(1)}, u32[]{:S(2)}, u32[]{:S(2)}) collective-permute-start(bf16[12,64,128]{2,1,0:T(8,128)(2,1)S(1)} %broadcast_select_fusion.7), channel_id=1, source_target_pairs={{0,4},{2,6},{4,0},{6,2},{8,12},{10,14},{12,8},{14,10},{16,20},{18,... | collective-permute-start | bytes 589832 | tf_op jit(solution)/shard_map/ppermute | solution.py:373
  16.4 0.0 collective-permute-done.4.refs_5_
  16.4 0.0 collective-permute-start.3
  16.4 0.4 collective-permute-start.5
  16.8 2.9 %collective-permute-done.6.refs_6_ = bf16[12,64,128]{2,1,0:T(8,128)(2,1)S(1)} collective-permute-done((bf16[12,64,128]{2,1,0:T(8,128)(2,1)S(1)}, bf16[12,64,128]{2,1,0:T(8,128)(2,1)S(1)}, u32[]{:S(2)}, u32[]{:S(2)}) %collective-permute-start.6) | collective-permute-done | bytes 196640 | tf_op jit(solution)/shard_map/ppermute | solution.py:298
  19.7 0.0 collective-permute-start.9
  19.7 2.0 %collective-permute-done.7.refs_0_ = bf16[12,64,128]{2,1,0:T(8,128)(2,1)S(1)} collective-permute-done((bf16[12,64,128]{2,1,0:T(8,128)(2,1)S(1)}, bf16[12,64,128]{2,1,0:T(8,128)(2,1)S(1)}, u32[]{:S(2)}, u32[]{:S(2)}) %collective-permute-start.7) | collective-permute-done | bytes 196640 | tf_op jit(solution)/shard_map/ppermute | solution.py:373
  21.7 1.3 %collective-permute-start.10 = (bf16[12,64,128]{2,1,0:T(8,128)(2,1)S(1)}, bf16[12,64,128]{2,1,0:T(8,128)(2,1)S(1)}, u32[]{:S(2)}, u32[]{:S(2)}) collective-permute-start(bf16[12,64,128]{2,1,0:T(8,128)(2,1)S(1)} %broadcast_select_fusion.5), channel_id=1, source_target_pairs={{0,4},{2,6},{4,0},{6,2},{8,12},{10,14},{12,8},{14,10},{16,20},{18,... | collective-permute-start | bytes 589832 | tf_op jit(solution)/shard_map/ppermute | solution.py:373
  23.0 2.9 %collective-permute-done.5.refs_1_ = bf16[12,64,128]{2,1,0:T(8,128)(2,1)S(1)} collective-permute-done((bf16[12,64,128]{2,1,0:T(8,128)(2,1)S(1)}, bf16[12,64,128]{2,1,0:T(8,128)(2,1)S(1)}, u32[]{:S(2)}, u32[]{:S(2)}) %collective-permute-start.5) | collective-permute-done | bytes 196640 | tf_op jit(solution)/shard_map/ppermute | solution.py:373
  25.9 0.0 collective-permute-done.3.refs_7_
  25.9 1.3 %collective-permute-start.13 = (bf16[15,64,128]{2,1,0:T(8,128)(2,1)S(1)}, bf16[15,64,128]{2,1,0:T(8,128)(2,1)S(1)}, u32[]{:S(2)}, u32[]{:S(2)}) collective-permute-start(bf16[15,64,128]{2,1,0:T(8,128)(2,1)S(1)} %broadcast_select_fusion), channel_id=1, source_target_pairs={{0,4},{2,6},{4,0},{6,2},{8,12},{10,14},{12,8},{14,10},{16,20},{18,... | collective-permute-start | bytes 737288 | tf_op jit(solution)/shard_map/ppermute | solution.py:373
  27.2 0.0 collective-permute-start.12
  27.2 1.1 %collective-permute-done.9.refs_2_ = bf16[12,64,128]{2,1,0:T(8,128)(2,1)S(1)} collective-permute-done((bf16[12,64,128]{2,1,0:T(8,128)(2,1)S(1)}, bf16[12,64,128]{2,1,0:T(8,128)(2,1)S(1)}, u32[]{:S(2)}, u32[]{:S(2)}) %collective-permute-start.9) | collective-permute-done | bytes 196640 | tf_op jit(solution)/shard_map/ppermute | solution.py:370
  28.4 0.3 collective-permute-start.8
  28.7 1.4 %collective-permute-done.10.refs_2_ = bf16[12,64,128]{2,1,0:T(8,128)(2,1)S(1)} collective-permute-done((bf16[12,64,128]{2,1,0:T(8,128)(2,1)S(1)}, bf16[12,64,128]{2,1,0:T(8,128)(2,1)S(1)}, u32[]{:S(2)}, u32[]{:S(2)}) %collective-permute-start.10) | collective-permute-done | bytes 196640 | tf_op jit(solution)/shard_map/ppermute | solution.py:373
  30.1 1.3 %collective-permute-start.11 = (bf16[12,64,128]{2,1,0:T(8,128)(2,1)S(1)}, bf16[12,64,128]{2,1,0:T(8,128)(2,1)S(1)}, u32[]{:S(2)}, u32[]{:S(2)}) collective-permute-start(bf16[12,64,128]{2,1,0:T(8,128)(2,1)S(1)} %broadcast_select_fusion.4), channel_id=1, source_target_pairs={{0,4},{2,6},{4,0},{6,2},{8,12},{10,14},{12,8},{14,10},{16,20},{18,... | collective-permute-start | bytes 589832 | tf_op jit(solution)/shard_map/ppermute | solution.py:373
  31.4 2.1 %collective-permute-done.12.refs_3_ = bf16[12,64,128]{2,1,0:T(8,128)(2,1)S(1)} collective-permute-done((bf16[12,64,128]{2,1,0:T(8,128)(2,1)S(1)}, bf16[12,64,128]{2,1,0:T(8,128)(2,1)S(1)}, u32[]{:S(2)}, u32[]{:S(2)}) %collective-permute-start.12) | collective-permute-done | bytes 196640 | tf_op jit(solution)/shard_map/ppermute | solution.py:370
  33.6 0.0 collective-permute-start.15
  33.6 0.5 collective-permute-done.13.refs_3_
  34.1 1.3 %collective-permute-start.16 = (bf16[12,64,128]{2,1,0:T(8,128)(2,1)S(1)}, bf16[12,64,128]{2,1,0:T(8,128)(2,1)S(1)}, u32[]{:S(2)}, u32[]{:S(2)}) collective-permute-start(bf16[12,64,128]{2,1,0:T(8,128)(2,1)S(1)} %broadcast_select_fusion.3), channel_id=1, source_target_pairs={{0,4},{2,6},{4,0},{6,2},{8,12},{10,14},{12,8},{14,10},{16,20},{18,... | collective-permute-start | bytes 589832 | tf_op jit(solution)/shard_map/ppermute | solution.py:373
  35.4 1.0 %collective-permute-done.8.refs_0_ = bf16[12,64,128]{2,1,0:T(8,128)(2,1)S(1)} collective-permute-done((bf16[12,64,128]{2,1,0:T(8,128)(2,1)S(1)}, bf16[12,64,128]{2,1,0:T(8,128)(2,1)S(1)}, u32[]{:S(2)}, u32[]{:S(2)}) %collective-permute-start.8) | collective-permute-done | bytes 196640 | tf_op jit(solution)/shard_map/ppermute | solution.py:370
  36.4 1.9 %collective-permute-done.11.refs_0_ = bf16[12,64,128]{2,1,0:T(8,128)(2,1)S(1)} collective-permute-done((bf16[12,64,128]{2,1,0:T(8,128)(2,1)S(1)}, bf16[12,64,128]{2,1,0:T(8,128)(2,1)S(1)}, u32[]{:S(2)}, u32[]{:S(2)}) %collective-permute-start.11) | collective-permute-done | bytes 196640 | tf_op jit(solution)/shard_map/ppermute | solution.py:373
  38.3 1.3 %collective-permute-start.14 = (bf16[12,64,128]{2,1,0:T(8,128)(2,1)S(1)}, bf16[12,64,128]{2,1,0:T(8,128)(2,1)S(1)}, u32[]{:S(2)}, u32[]{:S(2)}) collective-permute-start(bf16[12,64,128]{2,1,0:T(8,128)(2,1)S(1)} %broadcast_select_fusion.2), channel_id=1, source_target_pairs={{0,4},{2,6},{4,0},{6,2},{8,12},{10,14},{12,8},{14,10},{16,20},{18,... | collective-permute-start | bytes 589832 | tf_op jit(solution)/shard_map/ppermute | solution.py:373
  39.6 0.0 collective-permute-done.2.mate_ref
  39.6 2.3 %near.1.near_ref = f32[2,4,128,128]{3,2,1,0:T(8,128)S(1)} custom-call(s32[5]{0:T(128)S(1)} %convert_reduce_fusion.bounds_ref, f32[4]{0:T(128)S(1)} %multiply_rsqrt_fusion.norm_ref, bf16[4,128,1536]{2,1,0:T(8,128)(2,1)S(1)} %get-tuple-element.75.own_ref, bf16[4,128,1536]{2,1,0:T(8,128)(2,1)S(1)} %collective-permute-done.2.mate_ref), custom_call_target="tpu_custom_call" | custom-call | flops 1000 | bytes 1000 | tf_op jit(solution)/shard_map/near/pallas_call | solution.py:346
  41.9 0.3 collective-permute-done.15.refs_1_
  42.2 0.2 collective-permute-done.16.refs_1_
  42.5 1.4 %collective-permute-start.17 = (bf16[12,64,128]{2,1,0:T(8,128)(2,1)S(1)}, bf16[12,64,128]{2,1,0:T(8,128)(2,1)S(1)}, u32[]{:S(2)}, u32[]{:S(2)}) collective-permute-start(bf16[12,64,128]{2,1,0:T(8,128)(2,1)S(1)} %broadcast_select_fusion.1), channel_id=1, source_target_pairs={{0,4},{2,6},{4,0},{6,2},{8,12},{10,14},{12,8},{14,10},{16,20},{18,... | collective-permute-start | bytes 589832 | tf_op jit(solution)/shard_map/ppermute | solution.py:382
  43.8 2.8 %collective-permute-done.14.refs_0_ = bf16[12,64,128]{2,1,0:T(8,128)(2,1)S(1)} collective-permute-done((bf16[12,64,128]{2,1,0:T(8,128)(2,1)S(1)}, bf16[12,64,128]{2,1,0:T(8,128)(2,1)S(1)}, u32[]{:S(2)}, u32[]{:S(2)}) %collective-permute-start.14) | collective-permute-done | bytes 196640 | tf_op jit(solution)/shard_map/ppermute | solution.py:373
  46.6 2.6 %cross.4 = (f32[2,2,4,128,128]{4,3,2,1,0:T(8,128)S(1)}, f32[2,2,4,128,128]{4,3,2,1,0:T(8,128)S(1)}) custom-call(s32[5]{0:T(128)S(1)} %convert_reduce_fusion.bounds_ref, f32[4]{0:T(128)S(1)} %multiply_rsqrt_fusion.norm_ref, bf16[4,128,1536]{2,1,0:T(8,128)(2,1)S(1)} %get-tuple-element.75.own_ref, bf16[4,128,1536]{2,1,0:T(8,128)(2,1)S(1)} %collective-permute-done.2.mate_ref, ...), custom_call_target="tpu_custom_call" | custom-call | flops 805306368 | tf_op jit(solution)/shard_map/cross/pallas_call | solution.py:329
  49.2 2.1 %cross.5 = (f32[2,2,4,128,128]{4,3,2,1,0:T(8,128)S(1)}, f32[2,2,4,128,128]{4,3,2,1,0:T(8,128)S(1)}) custom-call(s32[5]{0:T(128)S(1)} %convert_reduce_fusion.bounds_ref, f32[4]{0:T(128)S(1)} %multiply_rsqrt_fusion.norm_ref, bf16[4,128,1536]{2,1,0:T(8,128)(2,1)S(1)} %get-tuple-element.75.own_ref, bf16[4,128,1536]{2,1,0:T(8,128)(2,1)S(1)} %collective-permute-done.2.mate_ref, ...), custom_call_target="tpu_custom_call" | custom-call | flops 402653184 | tf_op jit(solution)/shard_map/cross/pallas_call | solution.py:329
  51.3 1.5 %cross.6.refs_3_.two_ref = f32[2,2,4,128,128]{4,3,2,1,0:T(8,128)S(1)} custom-call(s32[5]{0:T(128)S(1)} %convert_reduce_fusion.bounds_ref, f32[4]{0:T(128)S(1)} %multiply_rsqrt_fusion.norm_ref, bf16[4,128,1536]{2,1,0:T(8,128)(2,1)S(1)} %get-tuple-element.75.own_ref, bf16[4,128,1536]{2,1,0:T(8,128)(2,1)S(1)} %collective-permute-done.2.mate_ref, ...), custom_call_target="tpu_custom_call" | custom-call | flops 201326592 | tf_op jit(solution)/shard_map/cross/pallas_call | solution.py:329
  52.8 0.0 collective-permute-done.17.refs_1_
  52.8 1.5 %cross.7 = (f32[2,2,4,128,128]{4,3,2,1,0:T(8,128)S(1)}, bf16[2,2,4,128,128]{4,3,2,1,0:T(8,128)(2,1)S(1)}) custom-call(s32[5]{0:T(128)S(1)} %convert_reduce_fusion.bounds_ref, f32[4]{0:T(128)S(1)} %multiply_rsqrt_fusion.norm_ref, bf16[4,128,1536]{2,1,0:T(8,128)(2,1)S(1)} %get-tuple-element.75.own_ref, ...), custom_call_target="tpu_custom_call" | custom-call | flops 201326592 | tf_op jit(solution)/shard_map/cross/pallas_call | solution.py:329
  54.3 4.1 %collective-permute-start.18 = (bf16[2,2,4,128,128]{4,3,2,1,0:T(8,128)(2,1)S(1)}, bf16[2,2,4,128,128]{4,3,2,1,0:T(8,128)(2,1)S(1)}, u32[]{:S(2)}, u32[]{:S(2)}) collective-permute-start(bf16[2,2,4,128,128]{4,3,2,1,0:T(8,128)(2,1)S(1)} %get-tuple-element.126), channel_id=1, source_target_pairs={{0,2},{2,0},{4,6},{6,4},{8,10},{10,8},{12,14},{14,12},{16,18},{18,... | collective-permute-start | bytes 1572872 | tf_op jit(solution)/shard_map/ppermute | solution.py:385
  58.3 1.1 %put.2.before_ref = f32[2,4,4,128,128]{4,3,2,1,0:T(8,128)} custom-call(f32[2,2,4,128,128]{4,3,2,1,0:T(8,128)S(1)} %get-tuple-element.128.one_ref, f32[2,2,4,128,128]{4,3,2,1,0:T(8,128)S(1)} %cross.6.refs_3_.two_ref), custom_call_target="tpu_custom_call" | custom-call | flops 1000 | bytes 1000 | tf_op jit(solution)/shard_map/put/pallas_call | solution.py:386
  59.4 0.4 collective-permute-done.18.got_ref
  59.9 1.1 %put.3 = f32[2,4,4,128,128]{4,3,2,1,0:T(8,128)} custom-call(bf16[2,2,4,128,128]{4,3,2,1,0:T(8,128)(2,1)S(1)} %collective-permute-done.18.got_ref, f32[2,4,128,128]{3,2,1,0:T(8,128)S(1)} %near.1.near_ref, f32[2,4,4,128,128]{4,3,2,1,0:T(8,128)} %put.2.before_ref), custom_call_target="tpu_custom_call", output_to_operand_aliasing={{}: (2, {})} | custom-call | flops 1000 | bytes 1000 | tf_op jit(solution)/shard_map/put/pallas_call | solution.py:396
  (9 shorter events, 0.2 us)
Async XLA Ops:
  0.0 7.8 %copy-start.2 = (s32[64]{0:T(128)S(1)}, s32[64]{0:T(128)}, u32[]{:S(2)}) copy-start(s32[64]{0:T(128)} %param.3) | copy-start | bytes 772
  0.0 1.4 %copy-start = (bf16[2,48,64,128]{3,2,1,0:T(8,128)(2,1)S(1)}, bf16[2,48,64,128]{3,2,1,0:T(8,128)(2,1)}, u32[]{:S(2)}) copy-start(bf16[2,48,64,128]{3,2,1,0:T(8,128)(2,1)} %param.2) | copy-start | bytes 4718596
  1.4 9.9 %copy-start.1 = (bf16[2,48,64,128]{3,2,1,0:T(8,128)(2,1)S(1)}, bf16[2,48,64,128]{3,2,1,0:T(8,128)(2,1)}, u32[]{:S(2)}) copy-start(bf16[2,48,64,128]{3,2,1,0:T(8,128)(2,1)} %param.2) | copy-start | bytes 4718596
  1.8 6.2 %collective-permute-start.1 = (f32[4,128]{1,0:T(4,128)S(1)}, f32[4,128]{1,0:T(4,128)S(1)}, u32[]{:S(2)}, u32[]{:S(2)}) collective-permute-start(f32[4,128]{1,0:T(4,128)S(1)} %get-tuple-element.71), channel_id=1, source_target_pairs={{0,1},{1,0},{2,3},{3,2},{4,5},{5,4},{6,7},{7,6},{8,9},{9,8},{10,11... | collective-permute-start | bytes 6152 | tf_op jit(solution)/shard_map/ppermute | solution.py:297
  3.9 7.4 %collective-permute-start = (bf16[12,64,128]{2,1,0:T(8,128)(2,1)S(1)}, bf16[12,64,128]{2,1,0:T(8,128)(2,1)S(1)}, u32[]{:S(2)}, u32[]{:S(2)}) collective-permute-start(bf16[12,64,128]{2,1,0:T(8,128)(2,1)S(1)} %get-tuple-element.70), channel_id=1, source_target_pairs={{0,8},{2,10},{4,12},{6,14},{8,16},{10,18},{12,20},{14,22},{16,24},... | collective-permute-start | bytes 589832 | tf_op jit(solution)/shard_map/ppermute | solution.py:298
  5.2 11.2 %collective-permute-start.4 = (bf16[12,64,128]{2,1,0:T(8,128)(2,1)S(1)}, bf16[12,64,128]{2,1,0:T(8,128)(2,1)S(1)}, u32[]{:S(2)}, u32[]{:S(2)}) collective-permute-start(bf16[12,64,128]{2,1,0:T(8,128)(2,1)S(1)} %get-tuple-element.79), channel_id=1, source_target_pairs={{0,8},{2,10},{4,12},{6,14},{8,16},{10,18},{12,20},{14,22},{16,24},... | collective-permute-start | bytes 589832 | tf_op jit(solution)/shard_map/ppermute | solution.py:298
  6.5 13.2 %collective-permute-start.6 = (bf16[12,64,128]{2,1,0:T(8,128)(2,1)S(1)}, bf16[12,64,128]{2,1,0:T(8,128)(2,1)S(1)}, u32[]{:S(2)}, u32[]{:S(2)}) collective-permute-start(bf16[12,64,128]{2,1,0:T(8,128)(2,1)S(1)} %get-tuple-element.85), channel_id=1, source_target_pairs={{0,8},{2,10},{4,12},{6,14},{8,16},{10,18},{12,20},{14,22},{16,24},... | collective-permute-start | bytes 589832 | tf_op jit(solution)/shard_map/ppermute | solution.py:298
  11.8 27.8 %collective-permute-start.2 = (bf16[4,128,1536]{2,1,0:T(8,128)(2,1)S(1)}, bf16[4,128,1536]{2,1,0:T(8,128)(2,1)S(1)}, u32[]{:S(2)}, u32[]{:S(2)}) collective-permute-start(bf16[4,128,1536]{2,1,0:T(8,128)(2,1)S(1)} %get-tuple-element.75.own_ref), channel_id=1, source_target_pairs={{0,2},{2,0},{4,6},{6,4},{8,10},{10,8},{12,14},{14,12},{16,18},{18,... | collective-permute-start | bytes 4718600 | tf_op jit(solution)/shard_map/ppermute | solution.py:345
  15.1 6.6 %collective-permute-start.7 = (bf16[12,64,128]{2,1,0:T(8,128)(2,1)S(1)}, bf16[12,64,128]{2,1,0:T(8,128)(2,1)S(1)}, u32[]{:S(2)}, u32[]{:S(2)}) collective-permute-start(bf16[12,64,128]{2,1,0:T(8,128)(2,1)S(1)} %broadcast_select_fusion.7), channel_id=1, source_target_pairs={{0,4},{2,6},{4,0},{6,2},{8,12},{10,14},{12,8},{14,10},{16,20},{18,... | collective-permute-start | bytes 589832 | tf_op jit(solution)/shard_map/ppermute | solution.py:373
  16.4 9.5 %collective-permute-start.3 = (bf16[15,64,128]{2,1,0:T(8,128)(2,1)S(1)}, bf16[15,64,128]{2,1,0:T(8,128)(2,1)S(1)}, u32[]{:S(2)}, u32[]{:S(2)}) collective-permute-start(bf16[15,64,128]{2,1,0:T(8,128)(2,1)S(1)} %get-tuple-element.78), channel_id=1, source_target_pairs={{0,8},{2,10},{4,12},{6,14},{8,16},{10,18},{12,20},{14,22},{16,24},... | collective-permute-start | bytes 737288 | tf_op jit(solution)/shard_map/ppermute | solution.py:370
  16.4 9.5 %collective-permute-start.5 = (bf16[12,64,128]{2,1,0:T(8,128)(2,1)S(1)}, bf16[12,64,128]{2,1,0:T(8,128)(2,1)S(1)}, u32[]{:S(2)}, u32[]{:S(2)}) collective-permute-start(bf16[12,64,128]{2,1,0:T(8,128)(2,1)S(1)} %broadcast_select_fusion.6), channel_id=1, source_target_pairs={{0,4},{2,6},{4,0},{6,2},{8,12},{10,14},{12,8},{14,10},{16,20},{18,... | collective-permute-start | bytes 589832 | tf_op jit(solution)/shard_map/ppermute | solution.py:373
  19.7 8.7 %collective-permute-start.9 = (bf16[12,64,128]{2,1,0:T(8,128)(2,1)S(1)}, bf16[12,64,128]{2,1,0:T(8,128)(2,1)S(1)}, u32[]{:S(2)}, u32[]{:S(2)}) collective-permute-start(bf16[12,64,128]{2,1,0:T(8,128)(2,1)S(1)} %get-tuple-element.93), channel_id=1, source_target_pairs={{0,8},{2,10},{4,12},{6,14},{8,16},{10,18},{12,20},{14,22},{16,24},... | collective-permute-start | bytes 589832 | tf_op jit(solution)/shard_map/ppermute | solution.py:370
  21.7 8.4 %collective-permute-start.10 = (bf16[12,64,128]{2,1,0:T(8,128)(2,1)S(1)}, bf16[12,64,128]{2,1,0:T(8,128)(2,1)S(1)}, u32[]{:S(2)}, u32[]{:S(2)}) collective-permute-start(bf16[12,64,128]{2,1,0:T(8,128)(2,1)S(1)} %broadcast_select_fusion.5), channel_id=1, source_target_pairs={{0,4},{2,6},{4,0},{6,2},{8,12},{10,14},{12,8},{14,10},{16,20},{18,... | collective-permute-start | bytes 589832 | tf_op jit(solution)/shard_map/ppermute | solution.py:373
  25.9 8.1 %collective-permute-start.13 = (bf16[15,64,128]{2,1,0:T(8,128)(2,1)S(1)}, bf16[15,64,128]{2,1,0:T(8,128)(2,1)S(1)}, u32[]{:S(2)}, u32[]{:S(2)}) collective-permute-start(bf16[15,64,128]{2,1,0:T(8,128)(2,1)S(1)} %broadcast_select_fusion), channel_id=1, source_target_pairs={{0,4},{2,6},{4,0},{6,2},{8,12},{10,14},{12,8},{14,10},{16,20},{18,... | collective-permute-start | bytes 737288 | tf_op jit(solution)/shard_map/ppermute | solution.py:373
  27.2 6.3 %collective-permute-start.12 = (bf16[12,64,128]{2,1,0:T(8,128)(2,1)S(1)}, bf16[12,64,128]{2,1,0:T(8,128)(2,1)S(1)}, u32[]{:S(2)}, u32[]{:S(2)}) collective-permute-start(bf16[12,64,128]{2,1,0:T(8,128)(2,1)S(1)} %get-tuple-element.100), channel_id=1, source_target_pairs={{0,8},{2,10},{4,12},{6,14},{8,16},{10,18},{12,20},{14,22},{16,24},... | collective-permute-start | bytes 589832 | tf_op jit(solution)/shard_map/ppermute | solution.py:370
  28.4 8.0 %collective-permute-start.8 = (bf16[12,64,128]{2,1,0:T(8,128)(2,1)S(1)}, bf16[12,64,128]{2,1,0:T(8,128)(2,1)S(1)}, u32[]{:S(2)}, u32[]{:S(2)}) collective-permute-start(bf16[12,64,128]{2,1,0:T(8,128)(2,1)S(1)} %get-tuple-element.92), channel_id=1, source_target_pairs={{0,8},{2,10},{4,12},{6,14},{8,16},{10,18},{12,20},{14,22},{16,24},... | collective-permute-start | bytes 589832 | tf_op jit(solution)/shard_map/ppermute | solution.py:370
  30.1 8.2 %collective-permute-start.11 = (bf16[12,64,128]{2,1,0:T(8,128)(2,1)S(1)}, bf16[12,64,128]{2,1,0:T(8,128)(2,1)S(1)}, u32[]{:S(2)}, u32[]{:S(2)}) collective-permute-start(bf16[12,64,128]{2,1,0:T(8,128)(2,1)S(1)} %broadcast_select_fusion.4), channel_id=1, source_target_pairs={{0,4},{2,6},{4,0},{6,2},{8,12},{10,14},{12,8},{14,10},{16,20},{18,... | collective-permute-start | bytes 589832 | tf_op jit(solution)/shard_map/ppermute | solution.py:373
  33.6 8.7 %collective-permute-start.15 = (bf16[12,64,128]{2,1,0:T(8,128)(2,1)S(1)}, bf16[12,64,128]{2,1,0:T(8,128)(2,1)S(1)}, u32[]{:S(2)}, u32[]{:S(2)}) collective-permute-start(bf16[12,64,128]{2,1,0:T(8,128)(2,1)S(1)} %get-tuple-element.104), channel_id=1, source_target_pairs={{0,8},{2,10},{4,12},{6,14},{8,16},{10,18},{12,20},{14,22},{16,24},... | collective-permute-start | bytes 589832 | tf_op jit(solution)/shard_map/ppermute | solution.py:370
  34.1 8.3 %collective-permute-start.16 = (bf16[12,64,128]{2,1,0:T(8,128)(2,1)S(1)}, bf16[12,64,128]{2,1,0:T(8,128)(2,1)S(1)}, u32[]{:S(2)}, u32[]{:S(2)}) collective-permute-start(bf16[12,64,128]{2,1,0:T(8,128)(2,1)S(1)} %broadcast_select_fusion.3), channel_id=1, source_target_pairs={{0,4},{2,6},{4,0},{6,2},{8,12},{10,14},{12,8},{14,10},{16,20},{18,... | collective-permute-start | bytes 589832 | tf_op jit(solution)/shard_map/ppermute | solution.py:373
  38.3 8.3 %collective-permute-start.14 = (bf16[12,64,128]{2,1,0:T(8,128)(2,1)S(1)}, bf16[12,64,128]{2,1,0:T(8,128)(2,1)S(1)}, u32[]{:S(2)}, u32[]{:S(2)}) collective-permute-start(bf16[12,64,128]{2,1,0:T(8,128)(2,1)S(1)} %broadcast_select_fusion.2), channel_id=1, source_target_pairs={{0,4},{2,6},{4,0},{6,2},{8,12},{10,14},{12,8},{14,10},{16,20},{18,... | collective-permute-start | bytes 589832 | tf_op jit(solution)/shard_map/ppermute | solution.py:373
  42.5 10.3 %collective-permute-start.17 = (bf16[12,64,128]{2,1,0:T(8,128)(2,1)S(1)}, bf16[12,64,128]{2,1,0:T(8,128)(2,1)S(1)}, u32[]{:S(2)}, u32[]{:S(2)}) collective-permute-start(bf16[12,64,128]{2,1,0:T(8,128)(2,1)S(1)} %broadcast_select_fusion.1), channel_id=1, source_target_pairs={{0,4},{2,6},{4,0},{6,2},{8,12},{10,14},{12,8},{14,10},{16,20},{18,... | collective-permute-start | bytes 589832 | tf_op jit(solution)/shard_map/ppermute | solution.py:382
  54.3 5.6 %collective-permute-start.18 = (bf16[2,2,4,128,128]{4,3,2,1,0:T(8,128)(2,1)S(1)}, bf16[2,2,4,128,128]{4,3,2,1,0:T(8,128)(2,1)S(1)}, u32[]{:S(2)}, u32[]{:S(2)}) collective-permute-start(bf16[2,2,4,128,128]{4,3,2,1,0:T(8,128)(2,1)S(1)} %get-tuple-element.126), channel_id=1, source_target_pairs={{0,2},{2,0},{4,6},{6,4},{8,10},{10,8},{12,14},{14,12},{16,18},{18,... | collective-permute-start | bytes 1572872 | tf_op jit(solution)/shard_map/ppermute | solution.py:385

commit v6 on v5

--- a/solution.py
+++ b/solution.py
@@ -16,14 +16,15 @@
 PIECE = 12
 RAW = 3
 TERMS = 3
-Z_AFTER = (-1, -1, -1, 0, 1, 2, 3, 4)
+Z_AFTER = (-1, -1, -1, 0, 2, 2, 3, 4)
 Y_AFTER = (-1, -1, 0, 1, 2, 3, 4, 5)
-CHAIN = 1
+LAST_TIE = 0
+CHAIN = 0
 SETS = (4, 2, 2)
-LEFT_AFTER = 0
+LEFT_AFTER = -1
 OTHER_AFTER = 0
-NEAR_BEFORE = 7
-CROSS_BEFORE = (8, 8)
+NEAR_BEFORE = 8
+CROSS_BEFORE = (7, 8)
 VMEM_LIMIT = 10 * 1024 * 1024
 
 
@@ -294,8 +295,8 @@
     norms = 1.0 / jnp.sqrt(windows * (bounds[1:] - bounds[:-1]).astype(jnp.float32))
     power, norms = after(power, norms)
 
+    twos = {k: lax.ppermute(early[k], "ch", ahead) for k in range(RAW)}
     halo = lax.ppermute(edge, "fq", [(0, 1), (1, 0)])
-    twos = {k: lax.ppermute(early[k], "ch", ahead) for k in range(RAW)}
     if LEFT_AFTER >= 0:
         twos[LEFT_AFTER], halo = after(twos[LEFT_AFTER], halo)
     left, *late = call(
@@ -375,7 +376,10 @@
     for s in range(len(SETS) - 1):
         if s not in sums:
             onward[final], twos[sets[s][0]] = after(onward[final], twos[sets[s][0]])
-            ones[final - 1], twos[sets[s][0]] = after(ones[final - 1], twos[sets[s][0]])
+            if NEAR_BEFORE == pieces:
+                twos[sets[s][0]], near = after(twos[sets[s][0]], near)
+            if LAST_TIE:
+                ones[final - 1], twos[sets[s][0]] = after(ones[final - 1], twos[sets[s][0]])
             sums[s] = list(cross(sets[s], (ones, twos), sums.get(s - 1)))
     one_sum, two_sum = sums[len(SETS) - 2]
 

time: 61.4 us -> 57.1 us (0.930)
  waiting for transfers between devices: 22.8 us -> 20.3 us
  starting transfers between devices: 23.2 us -> 21.5 us
    ppermute x7, waiting for transfers between devices: 11.7 us -> 8.92 us  [shards(): ones[k] = lax.ppermute(onward[k], 'ch', beside)]
    ppermute x1, starting transfers between devices: 4.06 us -> 2.32 us  [shards(): got = lax.ppermute(sent, 'ch', mate)]
    ppermute x5, waiting for transfers between devices: 4.49 us -> 5.27 us  [shards(): twos[later] = lax.ppermute(mine[later], 'ch', ahead)]
  transfers between devices with their start and end apart: 19 -> 19, of which waited for: 14 -> 11; matrix products, arithmetic and copies ran while one was open for 1% -> 1% of each run, Pallas kernels for 16% -> 18%
where the time goes in v6:
time: 57.1 us; the launch traced here: 56.6 us
  starting transfers between devices  21.5 us (38%)
  waiting for transfers between devices  20.3 us (36%)
  Pallas kernels  13 us (23%)
  local copies, waits for them, and re-layouts  1.43 us (3%)
    ppermute x7, waiting for transfers between devices, shards(): ones[k] = lax.ppermute(onward[k], 'ch', beside)  8.92 us
    ppermute x7, starting transfers between devices, shards(): ones[k] = lax.ppermute(onward[k], 'ch', beside)  8.45 us
    pallas_call x4, Pallas kernels, cross(): call(functools.partial(cross_kernel, these[0] * PIECE, len(these), kinds,...  7.58 us
    ppermute x3, waiting for transfers between devices, shards(): twos = {k: lax.ppermute(early[k], 'ch', ahead) for k in range(RAW)}  5.63 us
    ppermute x5, waiting for transfers between devices, shards(): twos[later] = lax.ppermute(mine[later], 'ch', ahead)  5.27 us
    ppermute x3, starting transfers between devices, shards(): twos = {k: lax.ppermute(early[k], 'ch', ahead) for k in range(RAW)}  3.89 us
    ppermute x1, starting transfers between devices, shards(): other = lax.ppermute(left, 'ch', mate)  3.2 us
    ppermute x1, starting transfers between devices, shards(): got = lax.ppermute(sent, 'ch', mate)  2.32 us
  transfers between devices with their start and end apart: 19, of which 11 were waited for; matrix products, arithmetic and copies ran while one was open for 1% of the time, Pallas kernels for 18%

profile of v6, /device:TPU:1, one launch (start us, length us, event | category | flops | bytes accessed | tf_op | source)
XLA Modules:
  0.0 56.6 jit_solution(14290094935427239124)
XLA Ops:
  0.0 0.0 copy-start.2
  0.0 0.0 copy-start
  0.0 1.4 %copy-done = bf16[2,48,64,128]{3,2,1,0:T(8,128)(2,1)S(1)} copy-done((bf16[2,48,64,128]{3,2,1,0:T(8,128)(2,1)S(1)}, bf16[2,48,64,128]{3,2,1,0:T(8,128)(2,1)}, u32[]{:S(2)}) %copy-start) | copy-done | bytes 1572888
  1.4 0.0 copy-start.1
  1.4 0.4 power.1
  1.8 2.1 %collective-permute-start = (f32[4,128]{1,0:T(4,128)S(1)}, f32[4,128]{1,0:T(4,128)S(1)}, u32[]{:S(2)}, u32[]{:S(2)}) collective-permute-start(f32[4,128]{1,0:T(4,128)S(1)} %get-tuple-element.57), channel_id=1, source_target_pairs={{0,1},{1,0},{2,3},{3,2},{4,5},{5,4},{6,7},{7,6},{8,9},{9,8},{10,11... | collective-permute-start | bytes 6152 | tf_op jit(solution)/shard_map/ppermute | solution.py:299
  3.9 1.3 %collective-permute-start.1 = (bf16[12,64,128]{2,1,0:T(8,128)(2,1)S(1)}, bf16[12,64,128]{2,1,0:T(8,128)(2,1)S(1)}, u32[]{:S(2)}, u32[]{:S(2)}) collective-permute-start(bf16[12,64,128]{2,1,0:T(8,128)(2,1)S(1)} %get-tuple-element.59), channel_id=1, source_target_pairs={{0,8},{2,10},{4,12},{6,14},{8,16},{10,18},{12,20},{14,22},{16,24},... | collective-permute-start | bytes 589832 | tf_op jit(solution)/shard_map/ppermute | solution.py:298
  5.2 1.3 %collective-permute-start.4 = (bf16[12,64,128]{2,1,0:T(8,128)(2,1)S(1)}, bf16[12,64,128]{2,1,0:T(8,128)(2,1)S(1)}, u32[]{:S(2)}, u32[]{:S(2)}) collective-permute-start(bf16[12,64,128]{2,1,0:T(8,128)(2,1)S(1)} %get-tuple-element.64), channel_id=1, source_target_pairs={{0,8},{2,10},{4,12},{6,14},{8,16},{10,18},{12,20},{14,22},{16,24},... | collective-permute-start | bytes 589832 | tf_op jit(solution)/shard_map/ppermute | solution.py:298
  6.5 1.3 %collective-permute-start.7 = (bf16[12,64,128]{2,1,0:T(8,128)(2,1)S(1)}, bf16[12,64,128]{2,1,0:T(8,128)(2,1)S(1)}, u32[]{:S(2)}, u32[]{:S(2)}) collective-permute-start(bf16[12,64,128]{2,1,0:T(8,128)(2,1)S(1)} %get-tuple-element.68), channel_id=1, source_target_pairs={{0,8},{2,10},{4,12},{6,14},{8,16},{10,18},{12,20},{14,22},{16,24},... | collective-permute-start | bytes 589832 | tf_op jit(solution)/shard_map/ppermute | solution.py:298
  7.8 0.0 copy-done.2
  7.8 0.1 convert_reduce_fusion.bounds_ref
  7.9 0.1 multiply_rsqrt_fusion.norm_ref
  8.0 0.0 collective-permute-done.halo_ref
  8.0 0.0 copy-done.1
  8.0 0.5 left.1
  8.6 2.7 %collective-permute-done.1.refs_4_ = bf16[12,64,128]{2,1,0:T(8,128)(2,1)S(1)} collective-permute-done((bf16[12,64,128]{2,1,0:T(8,128)(2,1)S(1)}, bf16[12,64,128]{2,1,0:T(8,128)(2,1)S(1)}, u32[]{:S(2)}, u32[]{:S(2)}) %collective-permute-start.1) | collective-permute-done | bytes 196640 | tf_op jit(solution)/shard_map/ppermute | solution.py:298
  11.3 3.2 %collective-permute-start.2 = (bf16[4,128,1536]{2,1,0:T(8,128)(2,1)S(1)}, bf16[4,128,1536]{2,1,0:T(8,128)(2,1)S(1)}, u32[]{:S(2)}, u32[]{:S(2)}) collective-permute-start(bf16[4,128,1536]{2,1,0:T(8,128)(2,1)S(1)} %get-tuple-element.60.own_ref), channel_id=1, source_target_pairs={{0,2},{2,0},{4,6},{6,4},{8,10},{10,8},{12,14},{14,12},{16,18},{18,... | collective-permute-start | bytes 4718600 | tf_op jit(solution)/shard_map/ppermute | solution.py:346
  14.5 1.3 %collective-permute-start.8 = (bf16[12,64,128]{2,1,0:T(8,128)(2,1)S(1)}, bf16[12,64,128]{2,1,0:T(8,128)(2,1)S(1)}, u32[]{:S(2)}, u32[]{:S(2)}) collective-permute-start(bf16[12,64,128]{2,1,0:T(8,128)(2,1)S(1)} %broadcast_select_fusion.6), channel_id=1, source_target_pairs={{0,4},{2,6},{4,0},{6,2},{8,12},{10,14},{12,8},{14,10},{16,20},{18,... | collective-permute-start | bytes 589832 | tf_op jit(solution)/shard_map/ppermute | solution.py:374
  15.8 0.0 collective-permute-start.3
  15.8 0.0 collective-permute-done.4.refs_5_
  15.9 1.0 %collective-permute-start.5 = (bf16[12,64,128]{2,1,0:T(8,128)(2,1)S(1)}, bf16[12,64,128]{2,1,0:T(8,128)(2,1)S(1)}, u32[]{:S(2)}, u32[]{:S(2)}) collective-permute-start(bf16[12,64,128]{2,1,0:T(8,128)(2,1)S(1)} %broadcast_select_fusion.7), channel_id=1, source_target_pairs={{0,4},{2,6},{4,0},{6,2},{8,12},{10,14},{12,8},{14,10},{16,20},{18,... | collective-permute-start | bytes 589832 | tf_op jit(solution)/shard_map/ppermute | solution.py:374
  16.8 2.9 %collective-permute-done.7.refs_6_ = bf16[12,64,128]{2,1,0:T(8,128)(2,1)S(1)} collective-permute-done((bf16[12,64,128]{2,1,0:T(8,128)(2,1)S(1)}, bf16[12,64,128]{2,1,0:T(8,128)(2,1)S(1)}, u32[]{:S(2)}, u32[]{:S(2)}) %collective-permute-start.7) | collective-permute-done | bytes 196640 | tf_op jit(solution)/shard_map/ppermute | solution.py:298
  19.7 1.4 %collective-permute-done.8.refs_0_ = bf16[12,64,128]{2,1,0:T(8,128)(2,1)S(1)} collective-permute-done((bf16[12,64,128]{2,1,0:T(8,128)(2,1)S(1)}, bf16[12,64,128]{2,1,0:T(8,128)(2,1)S(1)}, u32[]{:S(2)}, u32[]{:S(2)}) %collective-permute-start.8) | collective-permute-done | bytes 196640 | tf_op jit(solution)/shard_map/ppermute | solution.py:374
  21.1 1.3 %collective-permute-start.10 = (bf16[12,64,128]{2,1,0:T(8,128)(2,1)S(1)}, bf16[12,64,128]{2,1,0:T(8,128)(2,1)S(1)}, u32[]{:S(2)}, u32[]{:S(2)}) collective-permute-start(bf16[12,64,128]{2,1,0:T(8,128)(2,1)S(1)} %broadcast_select_fusion.5), channel_id=1, source_target_pairs={{0,4},{2,6},{4,0},{6,2},{8,12},{10,14},{12,8},{14,10},{16,20},{18,... | collective-permute-start | bytes 589832 | tf_op jit(solution)/shard_map/ppermute | solution.py:374
  22.5 0.0 collective-permute-start.9
  22.5 2.7 %collective-permute-done.5.refs_1_ = bf16[12,64,128]{2,1,0:T(8,128)(2,1)S(1)} collective-permute-done((bf16[12,64,128]{2,1,0:T(8,128)(2,1)S(1)}, bf16[12,64,128]{2,1,0:T(8,128)(2,1)S(1)}, u32[]{:S(2)}, u32[]{:S(2)}) %collective-permute-start.5) | collective-permute-done | bytes 196640 | tf_op jit(solution)/shard_map/ppermute | solution.py:374
  25.2 0.5 collective-permute-done.3.refs_7_
  25.7 0.8 %collective-permute-start.15 = (bf16[15,64,128]{2,1,0:T(8,128)(2,1)S(1)}, bf16[15,64,128]{2,1,0:T(8,128)(2,1)S(1)}, u32[]{:S(2)}, u32[]{:S(2)}) collective-permute-start(bf16[15,64,128]{2,1,0:T(8,128)(2,1)S(1)} %broadcast_select_fusion), channel_id=1, source_target_pairs={{0,4},{2,6},{4,0},{6,2},{8,12},{10,14},{12,8},{14,10},{16,20},{18,... | collective-permute-start | bytes 737288 | tf_op jit(solution)/shard_map/ppermute | solution.py:374
  26.5 0.0 collective-permute-start.14
  26.5 2.9 %collective-permute-done.10.refs_2_ = bf16[12,64,128]{2,1,0:T(8,128)(2,1)S(1)} collective-permute-done((bf16[12,64,128]{2,1,0:T(8,128)(2,1)S(1)}, bf16[12,64,128]{2,1,0:T(8,128)(2,1)S(1)}, u32[]{:S(2)}, u32[]{:S(2)}) %collective-permute-start.10) | collective-permute-done | bytes 196640 | tf_op jit(solution)/shard_map/ppermute | solution.py:374
  29.4 0.0 collective-permute-start.6
  29.4 0.0 collective-permute-done.9.refs_2_
  29.4 1.3 %collective-permute-start.11 = (bf16[12,64,128]{2,1,0:T(8,128)(2,1)S(1)}, bf16[12,64,128]{2,1,0:T(8,128)(2,1)S(1)}, u32[]{:S(2)}, u32[]{:S(2)}) collective-permute-start(bf16[12,64,128]{2,1,0:T(8,128)(2,1)S(1)} %broadcast_select_fusion.4), channel_id=1, source_target_pairs={{0,4},{2,6},{4,0},{6,2},{8,12},{10,14},{12,8},{14,10},{16,20},{18,... | collective-permute-start | bytes 589832 | tf_op jit(solution)/shard_map/ppermute | solution.py:374
  30.7 2.7 %collective-permute-done.14.refs_3_ = bf16[12,64,128]{2,1,0:T(8,128)(2,1)S(1)} collective-permute-done((bf16[12,64,128]{2,1,0:T(8,128)(2,1)S(1)}, bf16[12,64,128]{2,1,0:T(8,128)(2,1)S(1)}, u32[]{:S(2)}, u32[]{:S(2)}) %collective-permute-start.14) | collective-permute-done | bytes 196640 | tf_op jit(solution)/shard_map/ppermute | solution.py:371
  33.4 0.0 collective-permute-start.13
  33.4 1.2 %collective-permute-done.15.refs_3_ = bf16[15,64,128]{2,1,0:T(8,128)(2,1)S(1)} collective-permute-done((bf16[15,64,128]{2,1,0:T(8,128)(2,1)S(1)}, bf16[15,64,128]{2,1,0:T(8,128)(2,1)S(1)}, u32[]{:S(2)}, u32[]{:S(2)}) %collective-permute-start.15) | collective-permute-done | bytes 245792 | tf_op jit(solution)/shard_map/ppermute | solution.py:374
  34.7 1.3 %collective-permute-start.16 = (bf16[12,64,128]{2,1,0:T(8,128)(2,1)S(1)}, bf16[12,64,128]{2,1,0:T(8,128)(2,1)S(1)}, u32[]{:S(2)}, u32[]{:S(2)}) collective-permute-start(bf16[12,64,128]{2,1,0:T(8,128)(2,1)S(1)} %broadcast_select_fusion.2), channel_id=1, source_target_pairs={{0,4},{2,6},{4,0},{6,2},{8,12},{10,14},{12,8},{14,10},{16,20},{18,... | collective-permute-start | bytes 589832 | tf_op jit(solution)/shard_map/ppermute | solution.py:374
  36.0 2.1 %collective-permute-done.6.refs_0_ = bf16[12,64,128]{2,1,0:T(8,128)(2,1)S(1)} collective-permute-done((bf16[12,64,128]{2,1,0:T(8,128)(2,1)S(1)}, bf16[12,64,128]{2,1,0:T(8,128)(2,1)S(1)}, u32[]{:S(2)}, u32[]{:S(2)}) %collective-permute-start.6) | collective-permute-done | bytes 196640 | tf_op jit(solution)/shard_map/ppermute | solution.py:371
  38.1 0.7 %collective-permute-done.11.refs_0_ = bf16[12,64,128]{2,1,0:T(8,128)(2,1)S(1)} collective-permute-done((bf16[12,64,128]{2,1,0:T(8,128)(2,1)S(1)}, bf16[12,64,128]{2,1,0:T(8,128)(2,1)S(1)}, u32[]{:S(2)}, u32[]{:S(2)}) %collective-permute-start.11) | collective-permute-done | bytes 196640 | tf_op jit(solution)/shard_map/ppermute | solution.py:374
  38.8 1.4 %collective-permute-start.12 = (bf16[12,64,128]{2,1,0:T(8,128)(2,1)S(1)}, bf16[12,64,128]{2,1,0:T(8,128)(2,1)S(1)}, u32[]{:S(2)}, u32[]{:S(2)}) collective-permute-start(bf16[12,64,128]{2,1,0:T(8,128)(2,1)S(1)} %broadcast_select_fusion.3), channel_id=1, source_target_pairs={{0,4},{2,6},{4,0},{6,2},{8,12},{10,14},{12,8},{14,10},{16,20},{18,... | collective-permute-start | bytes 589832 | tf_op jit(solution)/shard_map/ppermute | solution.py:374
  40.2 0.0 collective-permute-done.2.mate_ref
  40.2 2.6 %cross.4 = (f32[2,2,4,128,128]{4,3,2,1,0:T(8,128)S(1)}, f32[2,2,4,128,128]{4,3,2,1,0:T(8,128)S(1)}) custom-call(s32[5]{0:T(128)S(1)} %convert_reduce_fusion.bounds_ref, f32[4]{0:T(128)S(1)} %multiply_rsqrt_fusion.norm_ref, bf16[4,128,1536]{2,1,0:T(8,128)(2,1)S(1)} %get-tuple-element.60.own_ref, bf16[4,128,1536]{2,1,0:T(8,128)(2,1)S(1)} %collective-permute-done.2.mate_ref, ...), custom_call_target="tpu_custom_call" | custom-call | flops 805306368 | tf_op jit(solution)/shard_map/cross/pallas_call | solution.py:330
  42.8 0.0 collective-permute-done.13.refs_1_
  42.8 0.0 collective-permute-done.16.refs_1_
  42.9 1.5 %collective-permute-start.17 = (bf16[12,64,128]{2,1,0:T(8,128)(2,1)S(1)}, bf16[12,64,128]{2,1,0:T(8,128)(2,1)S(1)}, u32[]{:S(2)}, u32[]{:S(2)}) collective-permute-start(bf16[12,64,128]{2,1,0:T(8,128)(2,1)S(1)} %broadcast_select_fusion.1), channel_id=1, source_target_pairs={{0,4},{2,6},{4,0},{6,2},{8,12},{10,14},{12,8},{14,10},{16,20},{18,... | collective-permute-start | bytes 589832 | tf_op jit(solution)/shard_map/ppermute | solution.py:386
  44.4 2.3 %near.1.near_ref = f32[2,4,128,128]{3,2,1,0:T(8,128)S(1)} custom-call(s32[5]{0:T(128)S(1)} %convert_reduce_fusion.bounds_ref, f32[4]{0:T(128)S(1)} %multiply_rsqrt_fusion.norm_ref, bf16[4,128,1536]{2,1,0:T(8,128)(2,1)S(1)} %get-tuple-element.60.own_ref, bf16[4,128,1536]{2,1,0:T(8,128)(2,1)S(1)} %collective-permute-done.2.mate_ref), custom_call_target="tpu_custom_call" | custom-call | flops 1000 | bytes 1000 | tf_op jit(solution)/shard_map/near/pallas_call | solution.py:347
  46.7 2.0 %cross.5 = (f32[2,2,4,128,128]{4,3,2,1,0:T(8,128)S(1)}, f32[2,2,4,128,128]{4,3,2,1,0:T(8,128)S(1)}) custom-call(s32[5]{0:T(128)S(1)} %convert_reduce_fusion.bounds_ref, f32[4]{0:T(128)S(1)} %multiply_rsqrt_fusion.norm_ref, bf16[4,128,1536]{2,1,0:T(8,128)(2,1)S(1)} %get-tuple-element.60.own_ref, bf16[4,128,1536]{2,1,0:T(8,128)(2,1)S(1)} %collective-permute-done.2.mate_ref, ...), custom_call_target="tpu_custom_call" | custom-call | flops 402653184 | tf_op jit(solution)/shard_map/cross/pallas_call | solution.py:330
  48.7 1.5 %cross.6.refs_3_.two_ref = f32[2,2,4,128,128]{4,3,2,1,0:T(8,128)S(1)} custom-call(s32[5]{0:T(128)S(1)} %convert_reduce_fusion.bounds_ref, f32[4]{0:T(128)S(1)} %multiply_rsqrt_fusion.norm_ref, bf16[4,128,1536]{2,1,0:T(8,128)(2,1)S(1)} %get-tuple-element.60.own_ref, bf16[4,128,1536]{2,1,0:T(8,128)(2,1)S(1)} %collective-permute-done.2.mate_ref, ...), custom_call_target="tpu_custom_call" | custom-call | flops 201326592 | tf_op jit(solution)/shard_map/cross/pallas_call | solution.py:330
  50.2 0.0 collective-permute-done.12.refs_0_
  50.2 0.0 collective-permute-done.17.refs_1_
  50.2 1.5 %cross.7 = (f32[2,2,4,128,128]{4,3,2,1,0:T(8,128)S(1)}, bf16[2,2,4,128,128]{4,3,2,1,0:T(8,128)(2,1)S(1)}) custom-call(s32[5]{0:T(128)S(1)} %convert_reduce_fusion.bounds_ref, f32[4]{0:T(128)S(1)} %multiply_rsqrt_fusion.norm_ref, bf16[4,128,1536]{2,1,0:T(8,128)(2,1)S(1)} %get-tuple-element.60.own_ref, ...), custom_call_target="tpu_custom_call" | custom-call | flops 201326592 | tf_op jit(solution)/shard_map/cross/pallas_call | solution.py:330
  51.7 2.3 %collective-permute-start.18 = (bf16[2,2,4,128,128]{4,3,2,1,0:T(8,128)(2,1)S(1)}, bf16[2,2,4,128,128]{4,3,2,1,0:T(8,128)(2,1)S(1)}, u32[]{:S(2)}, u32[]{:S(2)}) collective-permute-start(bf16[2,2,4,128,128]{4,3,2,1,0:T(8,128)(2,1)S(1)} %get-tuple-element.100), channel_id=1, source_target_pairs={{0,2},{2,0},{4,6},{6,4},{8,10},{10,8},{12,14},{14,12},{16,18},{18,... | collective-permute-start | bytes 1572872 | tf_op jit(solution)/shard_map/ppermute | solution.py:389
  54.0 1.1 %put.2.before_ref = f32[2,4,4,128,128]{4,3,2,1,0:T(8,128)} custom-call(f32[2,2,4,128,128]{4,3,2,1,0:T(8,128)S(1)} %get-tuple-element.102.one_ref, f32[2,2,4,128,128]{4,3,2,1,0:T(8,128)S(1)} %cross.6.refs_3_.two_ref), custom_call_target="tpu_custom_call" | custom-call | flops 1000 | bytes 1000 | tf_op jit(solution)/shard_map/put/pallas_call | solution.py:390
  55.1 0.4 collective-permute-done.18.got_ref
  55.5 1.1 %put.3 = f32[2,4,4,128,128]{4,3,2,1,0:T(8,128)} custom-call(bf16[2,2,4,128,128]{4,3,2,1,0:T(8,128)(2,1)S(1)} %collective-permute-done.18.got_ref, f32[2,4,128,128]{3,2,1,0:T(8,128)S(1)} %near.1.near_ref, f32[2,4,4,128,128]{4,3,2,1,0:T(8,128)} %put.2.before_ref), custom_call_target="tpu_custom_call", output_to_operand_aliasing={{}: (2, {})} | custom-call | flops 1000 | bytes 1000 | tf_op jit(solution)/shard_map/put/pallas_call | solution.py:400
  (9 shorter events, 0.2 us)
Async XLA Ops:
  0.0 7.8 %copy-start.2 = (s32[64]{0:T(128)S(1)}, s32[64]{0:T(128)}, u32[]{:S(2)}) copy-start(s32[64]{0:T(128)} %param.3) | copy-start | bytes 772
  0.0 1.4 %copy-start = (bf16[2,48,64,128]{3,2,1,0:T(8,128)(2,1)S(1)}, bf16[2,48,64,128]{3,2,1,0:T(8,128)(2,1)}, u32[]{:S(2)}) copy-start(bf16[2,48,64,128]{3,2,1,0:T(8,128)(2,1)} %param.2) | copy-start | bytes 4718596
  1.4 6.6 %copy-start.1 = (bf16[2,48,64,128]{3,2,1,0:T(8,128)(2,1)S(1)}, bf16[2,48,64,128]{3,2,1,0:T(8,128)(2,1)}, u32[]{:S(2)}) copy-start(bf16[2,48,64,128]{3,2,1,0:T(8,128)(2,1)} %param.2) | copy-start | bytes 4718596
  1.8 6.2 %collective-permute-start = (f32[4,128]{1,0:T(4,128)S(1)}, f32[4,128]{1,0:T(4,128)S(1)}, u32[]{:S(2)}, u32[]{:S(2)}) collective-permute-start(f32[4,128]{1,0:T(4,128)S(1)} %get-tuple-element.57), channel_id=1, source_target_pairs={{0,1},{1,0},{2,3},{3,2},{4,5},{5,4},{6,7},{7,6},{8,9},{9,8},{10,11... | collective-permute-start | bytes 6152 | tf_op jit(solution)/shard_map/ppermute | solution.py:299
  3.9 7.4 %collective-permute-start.1 = (bf16[12,64,128]{2,1,0:T(8,128)(2,1)S(1)}, bf16[12,64,128]{2,1,0:T(8,128)(2,1)S(1)}, u32[]{:S(2)}, u32[]{:S(2)}) collective-permute-start(bf16[12,64,128]{2,1,0:T(8,128)(2,1)S(1)} %get-tuple-element.59), channel_id=1, source_target_pairs={{0,8},{2,10},{4,12},{6,14},{8,16},{10,18},{12,20},{14,22},{16,24},... | collective-permute-start | bytes 589832 | tf_op jit(solution)/shard_map/ppermute | solution.py:298
  5.2 10.6 %collective-permute-start.4 = (bf16[12,64,128]{2,1,0:T(8,128)(2,1)S(1)}, bf16[12,64,128]{2,1,0:T(8,128)(2,1)S(1)}, u32[]{:S(2)}, u32[]{:S(2)}) collective-permute-start(bf16[12,64,128]{2,1,0:T(8,128)(2,1)S(1)} %get-tuple-element.64), channel_id=1, source_target_pairs={{0,8},{2,10},{4,12},{6,14},{8,16},{10,18},{12,20},{14,22},{16,24},... | collective-permute-start | bytes 589832 | tf_op jit(solution)/shard_map/ppermute | solution.py:298
  6.5 13.2 %collective-permute-start.7 = (bf16[12,64,128]{2,1,0:T(8,128)(2,1)S(1)}, bf16[12,64,128]{2,1,0:T(8,128)(2,1)S(1)}, u32[]{:S(2)}, u32[]{:S(2)}) collective-permute-start(bf16[12,64,128]{2,1,0:T(8,128)(2,1)S(1)} %get-tuple-element.68), channel_id=1, source_target_pairs={{0,8},{2,10},{4,12},{6,14},{8,16},{10,18},{12,20},{14,22},{16,24},... | collective-permute-start | bytes 589832 | tf_op jit(solution)/shard_map/ppermute | solution.py:298
  11.3 28.9 %collective-permute-start.2 = (bf16[4,128,1536]{2,1,0:T(8,128)(2,1)S(1)}, bf16[4,128,1536]{2,1,0:T(8,128)(2,1)S(1)}, u32[]{:S(2)}, u32[]{:S(2)}) collective-permute-start(bf16[4,128,1536]{2,1,0:T(8,128)(2,1)S(1)} %get-tuple-element.60.own_ref), channel_id=1, source_target_pairs={{0,2},{2,0},{4,6},{6,4},{8,10},{10,8},{12,14},{14,12},{16,18},{18,... | collective-permute-start | bytes 4718600 | tf_op jit(solution)/shard_map/ppermute | solution.py:346
  14.5 6.6 %collective-permute-start.8 = (bf16[12,64,128]{2,1,0:T(8,128)(2,1)S(1)}, bf16[12,64,128]{2,1,0:T(8,128)(2,1)S(1)}, u32[]{:S(2)}, u32[]{:S(2)}) collective-permute-start(bf16[12,64,128]{2,1,0:T(8,128)(2,1)S(1)} %broadcast_select_fusion.6), channel_id=1, source_target_pairs={{0,4},{2,6},{4,0},{6,2},{8,12},{10,14},{12,8},{14,10},{16,20},{18,... | collective-permute-start | bytes 589832 | tf_op jit(solution)/shard_map/ppermute | solution.py:374
  15.8 9.8 %collective-permute-start.3 = (bf16[15,64,128]{2,1,0:T(8,128)(2,1)S(1)}, bf16[15,64,128]{2,1,0:T(8,128)(2,1)S(1)}, u32[]{:S(2)}, u32[]{:S(2)}) collective-permute-start(bf16[15,64,128]{2,1,0:T(8,128)(2,1)S(1)} %get-tuple-element.63), channel_id=1, source_target_pairs={{0,8},{2,10},{4,12},{6,14},{8,16},{10,18},{12,20},{14,22},{16,24},... | collective-permute-start | bytes 737288 | tf_op jit(solution)/shard_map/ppermute | solution.py:371
  15.9 9.3 %collective-permute-start.5 = (bf16[12,64,128]{2,1,0:T(8,128)(2,1)S(1)}, bf16[12,64,128]{2,1,0:T(8,128)(2,1)S(1)}, u32[]{:S(2)}, u32[]{:S(2)}) collective-permute-start(bf16[12,64,128]{2,1,0:T(8,128)(2,1)S(1)} %broadcast_select_fusion.7), channel_id=1, source_target_pairs={{0,4},{2,6},{4,0},{6,2},{8,12},{10,14},{12,8},{14,10},{16,20},{18,... | collective-permute-start | bytes 589832 | tf_op jit(solution)/shard_map/ppermute | solution.py:374
  21.1 8.3 %collective-permute-start.10 = (bf16[12,64,128]{2,1,0:T(8,128)(2,1)S(1)}, bf16[12,64,128]{2,1,0:T(8,128)(2,1)S(1)}, u32[]{:S(2)}, u32[]{:S(2)}) collective-permute-start(bf16[12,64,128]{2,1,0:T(8,128)(2,1)S(1)} %broadcast_select_fusion.5), channel_id=1, source_target_pairs={{0,4},{2,6},{4,0},{6,2},{8,12},{10,14},{12,8},{14,10},{16,20},{18,... | collective-permute-start | bytes 589832 | tf_op jit(solution)/shard_map/ppermute | solution.py:374
  22.5 7.0 %collective-permute-start.9 = (bf16[12,64,128]{2,1,0:T(8,128)(2,1)S(1)}, bf16[12,64,128]{2,1,0:T(8,128)(2,1)S(1)}, u32[]{:S(2)}, u32[]{:S(2)}) collective-permute-start(bf16[12,64,128]{2,1,0:T(8,128)(2,1)S(1)} %get-tuple-element.72), channel_id=1, source_target_pairs={{0,8},{2,10},{4,12},{6,14},{8,16},{10,18},{12,20},{14,22},{16,24},... | collective-permute-start | bytes 589832 | tf_op jit(solution)/shard_map/ppermute | solution.py:371
  25.7 9.0 %collective-permute-start.15 = (bf16[15,64,128]{2,1,0:T(8,128)(2,1)S(1)}, bf16[15,64,128]{2,1,0:T(8,128)(2,1)S(1)}, u32[]{:S(2)}, u32[]{:S(2)}) collective-permute-start(bf16[15,64,128]{2,1,0:T(8,128)(2,1)S(1)} %broadcast_select_fusion), channel_id=1, source_target_pairs={{0,4},{2,6},{4,0},{6,2},{8,12},{10,14},{12,8},{14,10},{16,20},{18,... | collective-permute-start | bytes 737288 | tf_op jit(solution)/shard_map/ppermute | solution.py:374
  26.5 6.9 %collective-permute-start.14 = (bf16[12,64,128]{2,1,0:T(8,128)(2,1)S(1)}, bf16[12,64,128]{2,1,0:T(8,128)(2,1)S(1)}, u32[]{:S(2)}, u32[]{:S(2)}) collective-permute-start(bf16[12,64,128]{2,1,0:T(8,128)(2,1)S(1)} %get-tuple-element.84), channel_id=1, source_target_pairs={{0,8},{2,10},{4,12},{6,14},{8,16},{10,18},{12,20},{14,22},{16,24},... | collective-permute-start | bytes 589832 | tf_op jit(solution)/shard_map/ppermute | solution.py:371
  29.4 8.7 %collective-permute-start.6 = (bf16[12,64,128]{2,1,0:T(8,128)(2,1)S(1)}, bf16[12,64,128]{2,1,0:T(8,128)(2,1)S(1)}, u32[]{:S(2)}, u32[]{:S(2)}) collective-permute-start(bf16[12,64,128]{2,1,0:T(8,128)(2,1)S(1)} %get-tuple-element.67), channel_id=1, source_target_pairs={{0,8},{2,10},{4,12},{6,14},{8,16},{10,18},{12,20},{14,22},{16,24},... | collective-permute-start | bytes 589832 | tf_op jit(solution)/shard_map/ppermute | solution.py:371
  29.4 9.3 %collective-permute-start.11 = (bf16[12,64,128]{2,1,0:T(8,128)(2,1)S(1)}, bf16[12,64,128]{2,1,0:T(8,128)(2,1)S(1)}, u32[]{:S(2)}, u32[]{:S(2)}) collective-permute-start(bf16[12,64,128]{2,1,0:T(8,128)(2,1)S(1)} %broadcast_select_fusion.4), channel_id=1, source_target_pairs={{0,4},{2,6},{4,0},{6,2},{8,12},{10,14},{12,8},{14,10},{16,20},{18,... | collective-permute-start | bytes 589832 | tf_op jit(solution)/shard_map/ppermute | solution.py:374
  33.4 9.4 %collective-permute-start.13 = (bf16[12,64,128]{2,1,0:T(8,128)(2,1)S(1)}, bf16[12,64,128]{2,1,0:T(8,128)(2,1)S(1)}, u32[]{:S(2)}, u32[]{:S(2)}) collective-permute-start(bf16[12,64,128]{2,1,0:T(8,128)(2,1)S(1)} %get-tuple-element.80), channel_id=1, source_target_pairs={{0,8},{2,10},{4,12},{6,14},{8,16},{10,18},{12,20},{14,22},{16,24},... | collective-permute-start | bytes 589832 | tf_op jit(solution)/shard_map/ppermute | solution.py:371
  34.7 8.1 %collective-permute-start.16 = (bf16[12,64,128]{2,1,0:T(8,128)(2,1)S(1)}, bf16[12,64,128]{2,1,0:T(8,128)(2,1)S(1)}, u32[]{:S(2)}, u32[]{:S(2)}) collective-permute-start(bf16[12,64,128]{2,1,0:T(8,128)(2,1)S(1)} %broadcast_select_fusion.2), channel_id=1, source_target_pairs={{0,4},{2,6},{4,0},{6,2},{8,12},{10,14},{12,8},{14,10},{16,20},{18,... | collective-permute-start | bytes 589832 | tf_op jit(solution)/shard_map/ppermute | solution.py:374
  38.8 11.4 %collective-permute-start.12 = (bf16[12,64,128]{2,1,0:T(8,128)(2,1)S(1)}, bf16[12,64,128]{2,1,0:T(8,128)(2,1)S(1)}, u32[]{:S(2)}, u32[]{:S(2)}) collective-permute-start(bf16[12,64,128]{2,1,0:T(8,128)(2,1)S(1)} %broadcast_select_fusion.3), channel_id=1, source_target_pairs={{0,4},{2,6},{4,0},{6,2},{8,12},{10,14},{12,8},{14,10},{16,20},{18,... | collective-permute-start | bytes 589832 | tf_op jit(solution)/shard_map/ppermute | solution.py:374
  42.9 7.3 %collective-permute-start.17 = (bf16[12,64,128]{2,1,0:T(8,128)(2,1)S(1)}, bf16[12,64,128]{2,1,0:T(8,128)(2,1)S(1)}, u32[]{:S(2)}, u32[]{:S(2)}) collective-permute-start(bf16[12,64,128]{2,1,0:T(8,128)(2,1)S(1)} %broadcast_select_fusion.1), channel_id=1, source_target_pairs={{0,4},{2,6},{4,0},{6,2},{8,12},{10,14},{12,8},{14,10},{16,20},{18,... | collective-permute-start | bytes 589832 | tf_op jit(solution)/shard_map/ppermute | solution.py:386
  51.7 3.9 %collective-permute-start.18 = (bf16[2,2,4,128,128]{4,3,2,1,0:T(8,128)(2,1)S(1)}, bf16[2,2,4,128,128]{4,3,2,1,0:T(8,128)(2,1)S(1)}, u32[]{:S(2)}, u32[]{:S(2)}) collective-permute-start(bf16[2,2,4,128,128]{4,3,2,1,0:T(8,128)(2,1)S(1)} %get-tuple-element.100), channel_id=1, source_target_pairs={{0,2},{2,0},{4,6},{6,4},{8,10},{10,8},{12,14},{14,12},{16,18},{18,... | collective-permute-start | bytes 1572872 | tf_op jit(solution)/shard_map/ppermute | solution.py:389

commit v7 on v6

--- a/solution.py
+++ b/solution.py
@@ -13,18 +13,20 @@
 EPS = 1e-06
 
 GROUP = 16
-PIECE = 12
+SIZES = (8,8,8,12,12,12,12,12,12)
+BLOCK = 24
 RAW = 3
 TERMS = 3
-Z_AFTER = (-1, -1, -1, 0, 2, 2, 3, 4)
-Y_AFTER = (-1, -1, 0, 1, 2, 3, 4, 5)
+Z_AFTER = (-1, -1, -1, 0, 2, 2, 3, 4, 5)
+Y_AFTER = (-1, -1, 0, 1, 2, 3, 4, 5, 6)
 LAST_TIE = 0
+PUT_TIE = 1
 CHAIN = 0
-SETS = (4, 2, 2)
+SETS = (5, 2, 2)
 LEFT_AFTER = -1
 OTHER_AFTER = 0
-NEAR_BEFORE = 8
-CROSS_BEFORE = (7, 8)
+NEAR_BEFORE = 9
+CROSS_BEFORE = (8, 9)
 VMEM_LIMIT = 10 * 1024 * 1024
 
 
@@ -56,7 +58,7 @@
 def power_kernel(x_ref, power_ref, edge_ref, *pieces):
     rows, width, _ = x_ref.shape
     for index, piece in enumerate(pieces):
-        piece[...] = x_ref[index * PIECE : (index + 1) * PIECE]
+        piece[...] = x_ref[sum(SIZES[:index]) : sum(SIZES[: index + 1])]
 
     def step(i, total):
         value = x_ref[i].astype(jnp.float32)
@@ -71,7 +73,7 @@
 
 def left_kernel(x_ref, power_ref, halo_ref, left_ref, *refs):
     whites, padded = refs[:-1], refs[-1]
-    count = x_ref.shape[0] // PIECE
+    rows = x_ref.shape[0]
     fq = lax.axis_index("fq")
     width, channels = power_ref.shape
     bin_total = width * lax.axis_size("fq")
@@ -95,22 +97,23 @@
     rest = scale
     for term in range(TERMS):
         part = rest.astype(jnp.bfloat16)
-        whites[0][PIECE + term] = part
+        whites[0][SIZES[RAW] + term] = part
         rest = rest - part.astype(jnp.float32)
 
-    span = 2 * PIECE * GROUP
-    for pair in range(count // 2):
+    span = BLOCK * GROUP
+    for block in range(rows // BLOCK):
+        first = block * BLOCK
         for group in range(width // GROUP):
             here = slice(group * GROUP, (group + 1) * GROUP)
-            blocks = []
-            for index in (2 * pair, 2 * pair + 1):
-                raw = x_ref[index * PIECE : (index + 1) * PIECE, here, :].astype(jnp.float32)
-                white = (raw * scale[here][None]).astype(jnp.bfloat16)
-                if index >= RAW:
-                    whites[index - RAW][:PIECE, here, :] = white
-                blocks.append(white.reshape(PIECE * GROUP, channels))
-            turned = jnp.concatenate(blocks, axis=0).T
-            left_ref[group, :, pair * span : (pair + 1) * span] = turned
+            raw = x_ref[first : first + BLOCK, here, :].astype(jnp.float32)
+            white = (raw * scale[here][None]).astype(jnp.bfloat16)
+            for index, piece in enumerate(whites):
+                start = sum(SIZES[: RAW + index])
+                low, high = max(start, first), min(start + SIZES[RAW + index], first + BLOCK)
+                if low < high:
+                    piece[low - start : high - start, here, :] = white[low - first : high - first]
+            turned = white.reshape(span, channels).T
+            left_ref[group, :, block * span : (block + 1) * span] = turned
 
 
 def band_at(bounds_ref, bands, bin_index):
@@ -161,18 +164,17 @@
         each_band(bounds_ref, groups, bands, add)
 
 
-def cross_kernel(start, count, kinds, first, last, bounds_ref, norm_ref, own_ref, mate_ref, *refs):
+def cross_kernel(these, kinds, first, last, bounds_ref, norm_ref, own_ref, mate_ref, *refs):
+    count, start = len(these), sum(SIZES[: these[0]])
     rights = [refs[k * count : (k + 1) * count] for k in range(kinds)]
     refs = refs[kinds * count :]
     if not first:
         befores, refs = refs[:kinds], refs[kinds:]
-    if last:
-        beyond_ref, refs = refs[0], refs[1:]
     sums = refs[:kinds]
     width, channels = rights[0][0].shape[1:]
     bands = sums[0].shape[2]
     half = own_ref.shape[2] // 2
-    lanes = slice(start * GROUP, (start + count * PIECE) * GROUP)
+    lanes = slice(start * GROUP, sum(SIZES[: these[-1] + 1]) * GROUP)
     turned = lanes.start >= half
     shift = -half if turned else half
     across = slice(lanes.start + shift, lanes.stop + shift)
@@ -183,14 +185,15 @@
         scale = None
         if first:
             for term in range(TERMS):
-                part = right[RAW][PIECE + term, here, :].astype(jnp.float32)
+                part = right[RAW][SIZES[RAW] + term, here, :].astype(jnp.float32)
                 scale = part if scale is None else scale + part
         blocks = []
         for index, ref in enumerate(right):
-            block = ref[:PIECE, here, :]
+            size = SIZES[these[index]]
+            block = ref[:size, here, :]
             if first and index < RAW:
                 block = (block.astype(jnp.float32) * scale[None]).astype(jnp.bfloat16)
-            blocks.append((block * held[None]).reshape(PIECE * GROUP, channels))
+            blocks.append((block * held[None]).reshape(size * GROUP, channels))
         return jnp.concatenate(blocks, axis=0)
 
     def add(group, band, low, high):
@@ -211,42 +214,31 @@
 
     each_band(bounds_ref, width // GROUP, bands, add)
     if last:
-        refs[kinds][0] = sums[0][:, 1].astype(jnp.bfloat16)
-        refs[kinds][1] = beyond_ref[:, 1].astype(jnp.bfloat16)
-
-
-def put_own_kernel(one_ref, two_ref, out_ref, sems):
+        refs[kinds][...] = sums[0][:, 1].astype(jnp.bfloat16)
+
+
+def put_kernel(kind, *refs):
+    value_ref, refs = refs[0], refs[1:]
+    core = lax.axis_index("ch") % 2
+    if kind == "near":
+        near_ref, refs = refs[0], refs[1:]
+    out_ref, wide, sems = refs[-3:]
+    turn = {"one": 1, "two": 3, "far": 2 * core, "near": 2 - 2 * core}[kind]
     copies = []
-    for turn, value in ((1, one_ref), (3, two_ref)):
-        for part in range(2):
-            for band in range(out_ref.shape[2]):
-                copies.append(
-                    pltpu.make_async_copy(
-                        value.at[part, 0, band], out_ref.at[part, turn, band], sems.at[turn // 2, part, band]
-                    )
-                )
-    for copy in copies:
-        copy.start()
-    for copy in copies:
-        copy.wait()
-
-
-def put_got_kernel(got_ref, near_ref, before_ref, out_ref, wide, sems):
-    core = lax.axis_index("ch") % 2
-    copies = []
-    for k, turn in enumerate((2 * core, 2 - 2 * core)):
-        for part in range(2):
-            for band in range(out_ref.shape[2]):
-                value = got_ref[k, part, band].astype(jnp.float32)
-                if k == 1:
+    for part in range(2):
+        for band in range(out_ref.shape[2]):
+            if kind in ("one", "two"):
+                source = value_ref.at[part, 0, band]
+            else:
+                value = value_ref[part, band].astype(jnp.float32)
+                if kind == "near":
                     value = jnp.where(core == 0, value, near_ref[part, band])
-                wide[k, part, band] = value
-                copies.append(
-                    pltpu.make_async_copy(
-                        wide.at[k, part, band], out_ref.at[part, turn, band], sems.at[k, part, band]
-                    )
-                )
-                copies[-1].start()
+                wide[part, band] = value
+                source = wide.at[part, band]
+            copies.append(
+                pltpu.make_async_copy(source, out_ref.at[part, turn, band], sems.at[part, band])
+            )
+            copies[-1].start()
     for copy in copies:
         copy.wait()
 
@@ -270,8 +262,8 @@
     mate = [(i, i ^ 1) for i in range(count)]
 
     own = spectra.reshape(rows, width, channels)
-    pieces = rows // PIECE
-    heights = [PIECE + (TERMS if k == RAW else 0) for k in range(pieces)]
+    pieces = len(SIZES)
+    heights = [size + (TERMS if k == RAW else 0) for k, size in enumerate(SIZES)]
     block = jax.ShapeDtypeStruct((width, channels), jnp.float32)
     edge = jax.ShapeDtypeStruct((SMOOTH, channels), jnp.float32)
     held = [jax.ShapeDtypeStruct((h, width, channels), jnp.bfloat16) for h in heights]
@@ -314,28 +306,28 @@
     out_shape = jax.ShapeDtypeStruct((2, ROUNDS, band_width, channels, channels), jnp.float32)
     sum_shape = jax.ShapeDtypeStruct((2, 2, band_width, channels, channels), jnp.float32)
     near_shape = jax.ShapeDtypeStruct((2, band_width, channels, channels), jnp.float32)
-    send_shape = jax.ShapeDtypeStruct((2, 2, band_width, channels, channels), jnp.bfloat16)
+    send_shape = jax.ShapeDtypeStruct((2, band_width, channels, channels), jnp.bfloat16)
 
     sets = [range(sum(SETS[:s]), sum(SETS[: s + 1])) for s in range(len(SETS))]
     ones, onward = {}, {}
     sums = {}
 
-    def cross(these, flights, befores, last=()):
+    def cross(these, flights, befores, last=False):
         first = befores is None
         operands = [bounds, norms, left, other]
         for flight in flights:
             operands += [flight[k] for k in these]
-        operands += [*([] if first else befores), *last]
+        operands += [] if first else befores
         kinds = len(flights)
         return call(
             functools.partial(
-                cross_kernel, these[0] * PIECE, len(these), kinds, first, bool(last)
+                cross_kernel, tuple(these), kinds, first, last
             ),
             "cross",
-            (sum_shape,) * kinds + (send_shape,) * len(last),
+            (sum_shape,) * kinds + (send_shape,) * last,
             [smem(), smem()] + [vmem()] * (len(operands) - 2),
-            (vmem(),) * (kinds + len(last)),
-            8 * kinds * len(these) * PIECE * width * channels * channels,
+            (vmem(),) * (kinds + last),
+            8 * kinds * sum(SIZES[k] for k in these) * width * channels * channels,
             0 * nbytes,
         )(*operands)
 
@@ -383,34 +375,35 @@
             sums[s] = list(cross(sets[s], (ones, twos), sums.get(s - 1)))
     one_sum, two_sum = sums[len(SETS) - 2]
 
+    def put(kind, out, *values):
+        aliased = out is not None
+        operands = [*values, out] if aliased else list(values)
+        return call(
+            functools.partial(put_kernel, kind),
+            "put",
+            out_shape,
+            [vmem()] * len(values) + [hbm()] * aliased,
+            hbm(),
+            1000,
+            4 * nbytes,
+            input_output_aliases={len(values): 0} if aliased else {},
+            scratch_shapes=[
+                pltpu.VMEM(near_shape.shape, jnp.float32),
+                pltpu.SemaphoreType.DMA((2, band_width)),
+            ],
+        )(*operands)
+
     ones[final] = lax.ppermute(onward[final], "ch", beside)
-    (two_sum,) = cross(sets[-1], (twos,), [two_sum])
-    one_sum, sent = cross(sets[-1], (ones,), [one_sum], (two_sum,))
-    got = lax.ppermute(sent, "ch", mate)
-    out = call(
-        put_own_kernel,
-        "put",
-        out_shape,
-        [vmem()] * 2,
-        hbm(),
-        1000,
-        1000,
-        scratch_shapes=[pltpu.SemaphoreType.DMA((2, 2, band_width))],
-    )(one_sum, two_sum)
-    return call(
-        put_got_kernel,
-        "put",
-        out_shape,
-        [vmem(), vmem(), hbm()],
-        hbm(),
-        1000,
-        1000,
-        input_output_aliases={2: 0},
-        scratch_shapes=[
-            pltpu.VMEM((2,) + near_shape.shape, jnp.float32),
-            pltpu.SemaphoreType.DMA((2, 2, band_width)),
-        ],
-    )(got, near, out)
+    two_sum, two_sent = cross(sets[-1], (twos,), [two_sum], True)
+    two_got = lax.ppermute(two_sent, "ch", mate)
+    out = put("two", None, two_sum)
+    if PUT_TIE:
+        one_sum, out = after(one_sum, out)
+    one_sum, one_sent = cross(sets[-1], (ones,), [one_sum], True)
+    one_got = lax.ppermute(one_sent, "ch", mate)
+    out = put("one", out, one_sum)
+    out = put("near", out, two_got, near)
+    return put("far", out, one_got)
 
 
 def solution(mesh):

time: 57.1 us -> 57.8 us (1.012)
  waiting for transfers between devices: 20.3 us -> 18 us
  Pallas kernels: 13 us -> 14.2 us
  starting transfers between devices: 21.5 us -> 22.3 us
  other arithmetic: 0.38 us -> 1.04 us
    ppermute x5 -> x6, waiting for transfers between devices: 5.27 us -> 14.5 us  [shards(): twos[later] = lax.ppermute(mine[later], 'ch', ahead)]
    ppermute x7 -> x8, waiting for transfers between devices: 8.92 us -> 2.3 us  [shards(): ones[k] = lax.ppermute(onward[k], 'ch', beside)]
    ppermute x3, waiting for transfers between devices: 5.63 us -> 1.2 us  [shards(): twos = {k: lax.ppermute(early[k], 'ch', ahead) for k in range(RAW)}]
    ppermute x7 -> x8, starting transfers between devices: 8.45 us -> 6.37 us  [shards(): ones[k] = lax.ppermute(onward[k], 'ch', beside)]
    ppermute x1 -> x2, starting transfers between devices: 2.32 us -> 3.67 us  [the longest x1 3.59 us: shards(): two_got = lax.ppermute(two_sent, 'ch', mate)]
    ppermute x5 -> x6, starting transfers between devices: 0.01 us -> 1.35 us  [shards(): twos[later] = lax.ppermute(mine[later], 'ch', ahead)]
    pallas_call x6 -> x8, Pallas kernels: 9.76 us -> 11 us  [the longest x4 7.59 us: cross(): call(functools.partial(cross_kernel, tuple(these), kinds, first, last), '...]
    sub x1, other arithmetic: 0.01 us -> 0.66 us  [shards(): local_band = band_ids - fq * band_width]
  transfers between devices with their start and end apart: 19 -> 22, of which waited for: 11 -> 8; matrix products, arithmetic and copies ran while one was open for 1% -> 2% of each run, Pallas kernels for 18% -> 23%
where the time goes in v7:
time: 57.8 us; the launch traced here: 57.2 us
  starting transfers between devices  22.3 us (39%)
  waiting for transfers between devices  18 us (31%)
  Pallas kernels  14.2 us (25%)
  local copies, waits for them, and re-layouts  1.41 us (2%)
  other arithmetic  1.04 us (2%)
    ppermute x6, waiting for transfers between devices, shards(): twos[later] = lax.ppermute(mine[later], 'ch', ahead)  14.5 us
    pallas_call x4, Pallas kernels, cross(): call(functools.partial(cross_kernel, tuple(these), kinds, first, last), '...  7.59 us
    ppermute x8, starting transfers between devices, shards(): ones[k] = lax.ppermute(onward[k], 'ch', beside)  6.37 us
    ppermute x3, starting transfers between devices, shards(): twos = {k: lax.ppermute(early[k], 'ch', ahead) for k in range(RAW)}  3.89 us
    ppermute x1, starting transfers between devices, shards(): other = lax.ppermute(left, 'ch', mate)  3.77 us
    ppermute x1, starting transfers between devices, shards(): two_got = lax.ppermute(two_sent, 'ch', mate)  3.59 us
    pallas_call x4, Pallas kernels, put(): call(functools.partial(put_kernel, kind), 'put', out_shape, [vmem()] * le...  3.43 us
    ppermute x8, waiting for transfers between devices, shards(): ones[k] = lax.ppermute(onward[k], 'ch', beside)  2.3 us
  transfers between devices with their start and end apart: 22, of which 8 were waited for; matrix products, arithmetic and copies ran while one was open for 2% of the time, Pallas kernels for 23%

profile of v7, /device:TPU:1, one launch (start us, length us, event | category | flops | bytes accessed | tf_op | source)
XLA Modules:
  0.0 57.2 jit_solution(11530716593234507313)
XLA Ops:
  0.0 0.0 copy-start
  0.0 1.4 %copy-done = bf16[2,48,64,128]{3,2,1,0:T(8,128)(2,1)S(1)} copy-done((bf16[2,48,64,128]{3,2,1,0:T(8,128)(2,1)S(1)}, bf16[2,48,64,128]{3,2,1,0:T(8,128)(2,1)}, u32[]{:S(2)}) %copy-start) | copy-done | bytes 1572888
  1.4 0.0 copy-start.1
  1.4 0.4 power.1
  1.8 2.1 %collective-permute-start = (f32[4,128]{1,0:T(4,128)S(1)}, f32[4,128]{1,0:T(4,128)S(1)}, u32[]{:S(2)}, u32[]{:S(2)}) collective-permute-start(f32[4,128]{1,0:T(4,128)S(1)} %get-tuple-element.66), channel_id=1, source_target_pairs={{0,1},{1,0},{2,3},{3,2},{4,5},{5,4},{6,7},{7,6},{8,9},{9,8},{10,11... | collective-permute-start | bytes 6152 | tf_op jit(solution)/shard_map/ppermute | solution.py:291
  3.9 1.3 %collective-permute-start.1 = (bf16[8,64,128]{2,1,0:T(8,128)(2,1)S(1)}, bf16[8,64,128]{2,1,0:T(8,128)(2,1)S(1)}, u32[]{:S(2)}, u32[]{:S(2)}) collective-permute-start(bf16[8,64,128]{2,1,0:T(8,128)(2,1)S(1)} %get-tuple-element.68), channel_id=1, source_target_pairs={{0,8},{2,10},{4,12},{6,14},{8,16},{10,18},{12,20},{14,22},{16,24},... | collective-permute-start | bytes 393224 | tf_op jit(solution)/shard_map/ppermute | solution.py:290
  5.2 1.3 %collective-permute-start.3 = (bf16[8,64,128]{2,1,0:T(8,128)(2,1)S(1)}, bf16[8,64,128]{2,1,0:T(8,128)(2,1)S(1)}, u32[]{:S(2)}, u32[]{:S(2)}) collective-permute-start(bf16[8,64,128]{2,1,0:T(8,128)(2,1)S(1)} %get-tuple-element.70), channel_id=1, source_target_pairs={{0,8},{2,10},{4,12},{6,14},{8,16},{10,18},{12,20},{14,22},{16,24},... | collective-permute-start | bytes 393224 | tf_op jit(solution)/shard_map/ppermute | solution.py:290
  6.5 1.3 %collective-permute-start.10 = (bf16[8,64,128]{2,1,0:T(8,128)(2,1)S(1)}, bf16[8,64,128]{2,1,0:T(8,128)(2,1)S(1)}, u32[]{:S(2)}, u32[]{:S(2)}) collective-permute-start(bf16[8,64,128]{2,1,0:T(8,128)(2,1)S(1)} %get-tuple-element.85), channel_id=1, source_target_pairs={{0,8},{2,10},{4,12},{6,14},{8,16},{10,18},{12,20},{14,22},{16,24},... | collective-permute-start | bytes 393224 | tf_op jit(solution)/shard_map/ppermute | solution.py:290
  7.8 0.7 %broadcast_subtract_fusion = s32[64]{0:T(128)S(1)} fusion(s32[64]{0:T(128)} %param.3, s32[]{:T(128)S(6)} %mul.6), kind=kLoop, calls=%fused_computation.12 | loop fusion | flops 64 | bytes 516 | tf_op jit(solution)/shard_map/sub | solution.py:284
  8.4 0.1 convert_reduce_fusion.bounds_ref
  8.6 0.1 multiply_rsqrt_fusion.norm_ref
  8.6 0.0 collective-permute-done.halo_ref
  8.6 0.0 copy-done.1
  8.6 0.5 left.1
  9.2 0.4 collective-permute-done.1.refs_5_
  9.6 1.3 %collective-permute-start.4 = (bf16[8,64,128]{2,1,0:T(8,128)(2,1)S(1)}, bf16[8,64,128]{2,1,0:T(8,128)(2,1)S(1)}, u32[]{:S(2)}, u32[]{:S(2)}) collective-permute-start(bf16[8,64,128]{2,1,0:T(8,128)(2,1)S(1)} %broadcast_select_fusion.8), channel_id=1, source_target_pairs={{0,4},{2,6},{4,0},{6,2},{8,12},{10,14},{12,8},{14,10},{16,20},{18,... | collective-permute-start | bytes 393224 | tf_op jit(solution)/shard_map/ppermute | solution.py:366
  10.9 0.0 collective-permute-start.9
  10.9 3.8 %collective-permute-start.2 = (bf16[4,128,1536]{2,1,0:T(8,128)(2,1)S(1)}, bf16[4,128,1536]{2,1,0:T(8,128)(2,1)S(1)}, u32[]{:S(2)}, u32[]{:S(2)}) collective-permute-start(bf16[4,128,1536]{2,1,0:T(8,128)(2,1)S(1)} %get-tuple-element.69.own_ref), channel_id=1, source_target_pairs={{0,2},{2,0},{4,6},{6,4},{8,10},{10,8},{12,14},{14,12},{16,18},{18,... | collective-permute-start | bytes 4718600 | tf_op jit(solution)/shard_map/ppermute | solution.py:338
  14.7 0.8 %collective-permute-done.10.refs_6_ = bf16[8,64,128]{2,1,0:T(8,128)(2,1)S(1)} collective-permute-done((bf16[8,64,128]{2,1,0:T(8,128)(2,1)S(1)}, bf16[8,64,128]{2,1,0:T(8,128)(2,1)S(1)}, u32[]{:S(2)}, u32[]{:S(2)}) %collective-permute-start.10) | collective-permute-done | bytes 131104 | tf_op jit(solution)/shard_map/ppermute | solution.py:290
  15.5 1.3 %collective-permute-start.11 = (bf16[8,64,128]{2,1,0:T(8,128)(2,1)S(1)}, bf16[8,64,128]{2,1,0:T(8,128)(2,1)S(1)}, u32[]{:S(2)}, u32[]{:S(2)}) collective-permute-start(bf16[8,64,128]{2,1,0:T(8,128)(2,1)S(1)} %broadcast_select_fusion.6), channel_id=1, source_target_pairs={{0,4},{2,6},{4,0},{6,2},{8,12},{10,14},{12,8},{14,10},{16,20},{18,... | collective-permute-start | bytes 393224 | tf_op jit(solution)/shard_map/ppermute | solution.py:366
  16.8 0.0 collective-permute-done.3.refs_7_
  16.8 0.0 collective-permute-done.4.refs_0_
  16.8 0.3 collective-permute-start.6
  17.1 0.3 collective-permute-start.5
  17.4 2.3 %collective-permute-done.11.refs_1_ = bf16[8,64,128]{2,1,0:T(8,128)(2,1)S(1)} collective-permute-done((bf16[8,64,128]{2,1,0:T(8,128)(2,1)S(1)}, bf16[8,64,128]{2,1,0:T(8,128)(2,1)S(1)}, u32[]{:S(2)}, u32[]{:S(2)}) %collective-permute-start.11) | collective-permute-done | bytes 131104 | tf_op jit(solution)/shard_map/ppermute | solution.py:366
  19.7 0.0 collective-permute-done.9.refs_8_
  19.7 2.0 %collective-permute-start.12 = (bf16[15,64,128]{2,1,0:T(8,128)(2,1)S(1)}, bf16[15,64,128]{2,1,0:T(8,128)(2,1)S(1)}, u32[]{:S(2)}, u32[]{:S(2)}) collective-permute-start(bf16[15,64,128]{2,1,0:T(8,128)(2,1)S(1)} %broadcast_select_fusion), channel_id=1, source_target_pairs={{0,4},{2,6},{4,0},{6,2},{8,12},{10,14},{12,8},{14,10},{16,20},{18,... | collective-permute-start | bytes 737288 | tf_op jit(solution)/shard_map/ppermute | solution.py:366
  21.7 0.0 collective-permute-start.8
  21.7 0.0 collective-permute-done.6.refs_2_
  21.7 1.1 %collective-permute-start.16 = (bf16[12,64,128]{2,1,0:T(8,128)(2,1)S(1)}, bf16[12,64,128]{2,1,0:T(8,128)(2,1)S(1)}, u32[]{:S(2)}, u32[]{:S(2)}) collective-permute-start(bf16[12,64,128]{2,1,0:T(8,128)(2,1)S(1)} %get-tuple-element.98), channel_id=1, source_target_pairs={{0,8},{2,10},{4,12},{6,14},{8,16},{10,18},{12,20},{14,22},{16,24},... | collective-permute-start | bytes 589832 | tf_op jit(solution)/shard_map/ppermute | solution.py:363
  22.8 1.3 %collective-permute-done.5.refs_9_ = bf16[12,64,128]{2,1,0:T(8,128)(2,1)S(1)} collective-permute-done((bf16[12,64,128]{2,1,0:T(8,128)(2,1)S(1)}, bf16[12,64,128]{2,1,0:T(8,128)(2,1)S(1)}, u32[]{:S(2)}, u32[]{:S(2)}) %collective-permute-start.5) | collective-permute-done | bytes 196640 | tf_op jit(solution)/shard_map/ppermute | solution.py:363
  24.1 1.2 %collective-permute-start.17 = (bf16[12,64,128]{2,1,0:T(8,128)(2,1)S(1)}, bf16[12,64,128]{2,1,0:T(8,128)(2,1)S(1)}, u32[]{:S(2)}, u32[]{:S(2)}) collective-permute-start(bf16[12,64,128]{2,1,0:T(8,128)(2,1)S(1)} %broadcast_select_fusion.3), channel_id=1, source_target_pairs={{0,4},{2,6},{4,0},{6,2},{8,12},{10,14},{12,8},{14,10},{16,20},{18,... | collective-permute-start | bytes 589832 | tf_op jit(solution)/shard_map/ppermute | solution.py:366
  25.3 4.5 %collective-permute-done.8.refs_2_ = bf16[12,64,128]{2,1,0:T(8,128)(2,1)S(1)} collective-permute-done((bf16[12,64,128]{2,1,0:T(8,128)(2,1)S(1)}, bf16[12,64,128]{2,1,0:T(8,128)(2,1)S(1)}, u32[]{:S(2)}, u32[]{:S(2)}) %collective-permute-start.8) | collective-permute-done | bytes 196640 | tf_op jit(solution)/shard_map/ppermute | solution.py:363
  29.8 0.0 collective-permute-start.7
  29.8 0.0 collective-permute-done.12.refs_3_
  29.8 0.1 collective-permute-start.13
  29.9 3.9 %collective-permute-done.16.refs_3_ = bf16[12,64,128]{2,1,0:T(8,128)(2,1)S(1)} collective-permute-done((bf16[12,64,128]{2,1,0:T(8,128)(2,1)S(1)}, bf16[12,64,128]{2,1,0:T(8,128)(2,1)S(1)}, u32[]{:S(2)}, u32[]{:S(2)}) %collective-permute-start.16) | collective-permute-done | bytes 196640 | tf_op jit(solution)/shard_map/ppermute | solution.py:363
  33.8 0.0 collective-permute-start.15
  33.8 0.0 collective-permute-done.17.refs_4_
  33.8 0.1 collective-permute-start.18
  34.0 4.4 %collective-permute-done.7.refs_0_ = bf16[12,64,128]{2,1,0:T(8,128)(2,1)S(1)} collective-permute-done((bf16[12,64,128]{2,1,0:T(8,128)(2,1)S(1)}, bf16[12,64,128]{2,1,0:T(8,128)(2,1)S(1)}, u32[]{:S(2)}, u32[]{:S(2)}) %collective-permute-start.7) | collective-permute-done | bytes 196640 | tf_op jit(solution)/shard_map/ppermute | solution.py:363
  38.4 0.0 collective-permute-done.13.refs_0_
  38.5 0.1 collective-permute-start.14
  38.5 0.0 collective-permute-done.2.mate_ref
  38.5 2.6 %cross.4 = (f32[2,2,4,128,128]{4,3,2,1,0:T(8,128)S(1)}, f32[2,2,4,128,128]{4,3,2,1,0:T(8,128)S(1)}) custom-call(s32[5]{0:T(128)S(1)} %convert_reduce_fusion.bounds_ref, f32[4]{0:T(128)S(1)} %multiply_rsqrt_fusion.norm_ref, bf16[4,128,1536]{2,1,0:T(8,128)(2,1)S(1)} %get-tuple-element.69.own_ref, bf16[4,128,1536]{2,1,0:T(8,128)(2,1)S(1)} %collective-permute-done.2.mate_ref, ...), custom_call_target="tpu_custom_call" | custom-call | flops 805306368 | tf_op jit(solution)/shard_map/cross/pallas_call | solution.py:322
  41.1 0.3 collective-permute-done.15.refs_1_
  41.5 0.0 collective-permute-done.18.refs_1_
  41.5 1.2 %collective-permute-start.19 = (bf16[12,64,128]{2,1,0:T(8,128)(2,1)S(1)}, bf16[12,64,128]{2,1,0:T(8,128)(2,1)S(1)}, u32[]{:S(2)}, u32[]{:S(2)}) collective-permute-start(bf16[12,64,128]{2,1,0:T(8,128)(2,1)S(1)} %broadcast_select_fusion.1), channel_id=1, source_target_pairs={{0,4},{2,6},{4,0},{6,2},{8,12},{10,14},{12,8},{14,10},{16,20},{18,... | collective-permute-start | bytes 589832 | tf_op jit(solution)/shard_map/ppermute | solution.py:396
  42.7 2.3 %near.1.refs_1_ = f32[2,4,128,128]{3,2,1,0:T(8,128)S(1)} custom-call(s32[5]{0:T(128)S(1)} %convert_reduce_fusion.bounds_ref, f32[4]{0:T(128)S(1)} %multiply_rsqrt_fusion.norm_ref, bf16[4,128,1536]{2,1,0:T(8,128)(2,1)S(1)} %get-tuple-element.69.own_ref, bf16[4,128,1536]{2,1,0:T(8,128)(2,1)S(1)} %collective-permute-done.2.mate_ref), custom_call_target="tpu_custom_call" | custom-call | flops 1000 | bytes 1000 | tf_op jit(solution)/shard_map/near/pallas_call | solution.py:339
  45.0 2.0 %cross.5 = (f32[2,2,4,128,128]{4,3,2,1,0:T(8,128)S(1)}, f32[2,2,4,128,128]{4,3,2,1,0:T(8,128)S(1)}) custom-call(s32[5]{0:T(128)S(1)} %convert_reduce_fusion.bounds_ref, f32[4]{0:T(128)S(1)} %multiply_rsqrt_fusion.norm_ref, bf16[4,128,1536]{2,1,0:T(8,128)(2,1)S(1)} %get-tuple-element.69.own_ref, bf16[4,128,1536]{2,1,0:T(8,128)(2,1)S(1)} %collective-permute-done.2.mate_ref, ...), custom_call_target="tpu_custom_call" | custom-call | flops 402653184 | tf_op jit(solution)/shard_map/cross/pallas_call | solution.py:322
  47.0 1.5 %cross.6 = (f32[2,2,4,128,128]{4,3,2,1,0:T(8,128)S(1)}, bf16[2,4,128,128]{3,2,1,0:T(8,128)(2,1)S(1)}) custom-call(s32[5]{0:T(128)S(1)} %convert_reduce_fusion.bounds_ref, f32[4]{0:T(128)S(1)} %multiply_rsqrt_fusion.norm_ref, bf16[4,128,1536]{2,1,0:T(8,128)(2,1)S(1)} %get-tuple-element.69.own_ref, bf16[4,128,1536]{2,1,0:T(8,128)(2,1)S(1)} %collective-permute-done.2.mate_ref, ...), custom_call_target="tpu_custom_call" | custom-call | flops 201326592 | tf_op jit(solution)/shard_map/cross/pallas_call | solution.py:322
  48.5 3.6 %collective-permute-start.21 = (bf16[2,4,128,128]{3,2,1,0:T(8,128)(2,1)S(1)}, bf16[2,4,128,128]{3,2,1,0:T(8,128)(2,1)S(1)}, u32[]{:S(2)}, u32[]{:S(2)}) collective-permute-start(bf16[2,4,128,128]{3,2,1,0:T(8,128)(2,1)S(1)} %get-tuple-element.117), channel_id=1, source_target_pairs={{0,2},{2,0},{4,6},{6,4},{8,10},{10,8},{12,14},{14,12},{16,18},{18,... | collective-permute-start | bytes 786440 | tf_op jit(solution)/shard_map/ppermute | solution.py:398
  52.1 0.8 %put.4.refs_1_ = f32[2,4,4,128,128]{4,3,2,1,0:T(8,128)} custom-call(f32[2,2,4,128,128]{4,3,2,1,0:T(8,128)S(1)} %get-tuple-element.114.refs_0_), custom_call_target="tpu_custom_call" | custom-call | flops 1000 | bytes 6291456 | tf_op jit(solution)/shard_map/put/pallas_call | solution.py:381
  53.0 0.0 collective-permute-done.14.refs_0_
  53.0 0.0 collective-permute-done.19.refs_1_
  53.0 1.5 %cross.7 = (f32[2,2,4,128,128]{4,3,2,1,0:T(8,128)S(1)}, bf16[2,4,128,128]{3,2,1,0:T(8,128)(2,1)S(1)}) custom-call(s32[5]{0:T(128)S(1)} %convert_reduce_fusion.bounds_ref, f32[4]{0:T(128)S(1)} %multiply_rsqrt_fusion.norm_ref, bf16[4,128,1536]{2,1,0:T(8,128)(2,1)S(1)} %get-tuple-element.69.own_ref, bf16[4,128,1536]{2,1,0:T(8,128)(2,1)S(1)} %collective-permute-done.2.mate_ref, ...), custom_call_target="tpu_custom_call" | custom-call | flops 201326592 | tf_op jit(solution)/shard_map/cross/pallas_call | solution.py:322
  54.5 0.1 collective-permute-start.20
  54.6 0.8 %put.5.refs_2_ = f32[2,4,4,128,128]{4,3,2,1,0:T(8,128)} custom-call(f32[2,2,4,128,128]{4,3,2,1,0:T(8,128)S(1)} %get-tuple-element.119.refs_0_, f32[2,4,4,128,128]{4,3,2,1,0:T(8,128)} %put.4.refs_1_), custom_call_target="tpu_custom_call", output_to_operand_aliasing={{}: (1, {})} | custom-call | flops 1000 | bytes 6291456 | tf_op jit(solution)/shard_map/put/pallas_call | solution.py:381
  55.4 0.0 collective-permute-done.21.refs_0_
  55.4 0.9 %put.6.refs_1_ = f32[2,4,4,128,128]{4,3,2,1,0:T(8,128)} custom-call(bf16[2,4,128,128]{3,2,1,0:T(8,128)(2,1)S(1)} %collective-permute-done.21.refs_0_, f32[2,4,128,128]{3,2,1,0:T(8,128)S(1)} %near.1.refs_1_, f32[2,4,4,128,128]{4,3,2,1,0:T(8,128)} %put.5.refs_2_), custom_call_target="tpu_custom_call", output_to_operand_aliasing={{}: (2, {})} | custom-call | flops 1000 | bytes 6291456 | tf_op jit(solution)/shard_map/put/pallas_call | solution.py:381
  56.3 0.0 collective-permute-done.20.refs_0_
  56.3 0.9 %put.7 = f32[2,4,4,128,128]{4,3,2,1,0:T(8,128)} custom-call(bf16[2,4,128,128]{3,2,1,0:T(8,128)(2,1)S(1)} %collective-permute-done.20.refs_0_, f32[2,4,4,128,128]{4,3,2,1,0:T(8,128)} %put.6.refs_1_), custom_call_target="tpu_custom_call", output_to_operand_aliasing={{}: (1, {})} | custom-call | flops 1000 | bytes 6291456 | tf_op jit(solution)/shard_map/put/pallas_call | solution.py:381
  (9 shorter events, 0.2 us)
Async XLA Ops:
  0.0 1.4 %copy-start = (bf16[2,48,64,128]{3,2,1,0:T(8,128)(2,1)S(1)}, bf16[2,48,64,128]{3,2,1,0:T(8,128)(2,1)}, u32[]{:S(2)}) copy-start(bf16[2,48,64,128]{3,2,1,0:T(8,128)(2,1)} %param.2) | copy-start | bytes 4718596
  1.4 7.2 %copy-start.1 = (bf16[2,48,64,128]{3,2,1,0:T(8,128)(2,1)S(1)}, bf16[2,48,64,128]{3,2,1,0:T(8,128)(2,1)}, u32[]{:S(2)}) copy-start(bf16[2,48,64,128]{3,2,1,0:T(8,128)(2,1)} %param.2) | copy-start | bytes 4718596
  1.8 6.9 %collective-permute-start = (f32[4,128]{1,0:T(4,128)S(1)}, f32[4,128]{1,0:T(4,128)S(1)}, u32[]{:S(2)}, u32[]{:S(2)}) collective-permute-start(f32[4,128]{1,0:T(4,128)S(1)} %get-tuple-element.66), channel_id=1, source_target_pairs={{0,1},{1,0},{2,3},{3,2},{4,5},{5,4},{6,7},{7,6},{8,9},{9,8},{10,11... | collective-permute-start | bytes 6152 | tf_op jit(solution)/shard_map/ppermute | solution.py:291
  3.9 5.7 %collective-permute-start.1 = (bf16[8,64,128]{2,1,0:T(8,128)(2,1)S(1)}, bf16[8,64,128]{2,1,0:T(8,128)(2,1)S(1)}, u32[]{:S(2)}, u32[]{:S(2)}) collective-permute-start(bf16[8,64,128]{2,1,0:T(8,128)(2,1)S(1)} %get-tuple-element.68), channel_id=1, source_target_pairs={{0,8},{2,10},{4,12},{6,14},{8,16},{10,18},{12,20},{14,22},{16,24},... | collective-permute-start | bytes 393224 | tf_op jit(solution)/shard_map/ppermute | solution.py:290
  5.2 11.6 %collective-permute-start.3 = (bf16[8,64,128]{2,1,0:T(8,128)(2,1)S(1)}, bf16[8,64,128]{2,1,0:T(8,128)(2,1)S(1)}, u32[]{:S(2)}, u32[]{:S(2)}) collective-permute-start(bf16[8,64,128]{2,1,0:T(8,128)(2,1)S(1)} %get-tuple-element.70), channel_id=1, source_target_pairs={{0,8},{2,10},{4,12},{6,14},{8,16},{10,18},{12,20},{14,22},{16,24},... | collective-permute-start | bytes 393224 | tf_op jit(solution)/shard_map/ppermute | solution.py:290
  6.5 9.0 %collective-permute-start.10 = (bf16[8,64,128]{2,1,0:T(8,128)(2,1)S(1)}, bf16[8,64,128]{2,1,0:T(8,128)(2,1)S(1)}, u32[]{:S(2)}, u32[]{:S(2)}) collective-permute-start(bf16[8,64,128]{2,1,0:T(8,128)(2,1)S(1)} %get-tuple-element.85), channel_id=1, source_target_pairs={{0,8},{2,10},{4,12},{6,14},{8,16},{10,18},{12,20},{14,22},{16,24},... | collective-permute-start | bytes 393224 | tf_op jit(solution)/shard_map/ppermute | solution.py:290
  9.6 7.2 %collective-permute-start.4 = (bf16[8,64,128]{2,1,0:T(8,128)(2,1)S(1)}, bf16[8,64,128]{2,1,0:T(8,128)(2,1)S(1)}, u32[]{:S(2)}, u32[]{:S(2)}) collective-permute-start(bf16[8,64,128]{2,1,0:T(8,128)(2,1)S(1)} %broadcast_select_fusion.8), channel_id=1, source_target_pairs={{0,4},{2,6},{4,0},{6,2},{8,12},{10,14},{12,8},{14,10},{16,20},{18,... | collective-permute-start | bytes 393224 | tf_op jit(solution)/shard_map/ppermute | solution.py:366
  10.9 8.8 %collective-permute-start.9 = (bf16[15,64,128]{2,1,0:T(8,128)(2,1)S(1)}, bf16[15,64,128]{2,1,0:T(8,128)(2,1)S(1)}, u32[]{:S(2)}, u32[]{:S(2)}) collective-permute-start(bf16[15,64,128]{2,1,0:T(8,128)(2,1)S(1)} %get-tuple-element.84), channel_id=1, source_target_pairs={{0,8},{2,10},{4,12},{6,14},{8,16},{10,18},{12,20},{14,22},{16,24},... | collective-permute-start | bytes 737288 | tf_op jit(solution)/shard_map/ppermute | solution.py:363
  10.9 27.6 %collective-permute-start.2 = (bf16[4,128,1536]{2,1,0:T(8,128)(2,1)S(1)}, bf16[4,128,1536]{2,1,0:T(8,128)(2,1)S(1)}, u32[]{:S(2)}, u32[]{:S(2)}) collective-permute-start(bf16[4,128,1536]{2,1,0:T(8,128)(2,1)S(1)} %get-tuple-element.69.own_ref), channel_id=1, source_target_pairs={{0,2},{2,0},{4,6},{6,4},{8,10},{10,8},{12,14},{14,12},{16,18},{18,... | collective-permute-start | bytes 4718600 | tf_op jit(solution)/shard_map/ppermute | solution.py:338
  15.5 4.2 %collective-permute-start.11 = (bf16[8,64,128]{2,1,0:T(8,128)(2,1)S(1)}, bf16[8,64,128]{2,1,0:T(8,128)(2,1)S(1)}, u32[]{:S(2)}, u32[]{:S(2)}) collective-permute-start(bf16[8,64,128]{2,1,0:T(8,128)(2,1)S(1)} %broadcast_select_fusion.6), channel_id=1, source_target_pairs={{0,4},{2,6},{4,0},{6,2},{8,12},{10,14},{12,8},{14,10},{16,20},{18,... | collective-permute-start | bytes 393224 | tf_op jit(solution)/shard_map/ppermute | solution.py:366
  16.8 4.9 %collective-permute-start.6 = (bf16[8,64,128]{2,1,0:T(8,128)(2,1)S(1)}, bf16[8,64,128]{2,1,0:T(8,128)(2,1)S(1)}, u32[]{:S(2)}, u32[]{:S(2)}) collective-permute-start(bf16[8,64,128]{2,1,0:T(8,128)(2,1)S(1)} %broadcast_select_fusion.7), channel_id=1, source_target_pairs={{0,4},{2,6},{4,0},{6,2},{8,12},{10,14},{12,8},{14,10},{16,20},{18,... | collective-permute-start | bytes 393224 | tf_op jit(solution)/shard_map/ppermute | solution.py:366
  17.1 7.0 %collective-permute-start.5 = (bf16[12,64,128]{2,1,0:T(8,128)(2,1)S(1)}, bf16[12,64,128]{2,1,0:T(8,128)(2,1)S(1)}, u32[]{:S(2)}, u32[]{:S(2)}) collective-permute-start(bf16[12,64,128]{2,1,0:T(8,128)(2,1)S(1)} %get-tuple-element.76), channel_id=1, source_target_pairs={{0,8},{2,10},{4,12},{6,14},{8,16},{10,18},{12,20},{14,22},{16,24},... | collective-permute-start | bytes 589832 | tf_op jit(solution)/shard_map/ppermute | solution.py:363
  19.7 10.1 %collective-permute-start.12 = (bf16[15,64,128]{2,1,0:T(8,128)(2,1)S(1)}, bf16[15,64,128]{2,1,0:T(8,128)(2,1)S(1)}, u32[]{:S(2)}, u32[]{:S(2)}) collective-permute-start(bf16[15,64,128]{2,1,0:T(8,128)(2,1)S(1)} %broadcast_select_fusion), channel_id=1, source_target_pairs={{0,4},{2,6},{4,0},{6,2},{8,12},{10,14},{12,8},{14,10},{16,20},{18,... | collective-permute-start | bytes 737288 | tf_op jit(solution)/shard_map/ppermute | solution.py:366
  21.7 8.1 %collective-permute-start.8 = (bf16[12,64,128]{2,1,0:T(8,128)(2,1)S(1)}, bf16[12,64,128]{2,1,0:T(8,128)(2,1)S(1)}, u32[]{:S(2)}, u32[]{:S(2)}) collective-permute-start(bf16[12,64,128]{2,1,0:T(8,128)(2,1)S(1)} %get-tuple-element.83), channel_id=1, source_target_pairs={{0,8},{2,10},{4,12},{6,14},{8,16},{10,18},{12,20},{14,22},{16,24},... | collective-permute-start | bytes 589832 | tf_op jit(solution)/shard_map/ppermute | solution.py:363
  21.7 12.1 %collective-permute-start.16 = (bf16[12,64,128]{2,1,0:T(8,128)(2,1)S(1)}, bf16[12,64,128]{2,1,0:T(8,128)(2,1)S(1)}, u32[]{:S(2)}, u32[]{:S(2)}) collective-permute-start(bf16[12,64,128]{2,1,0:T(8,128)(2,1)S(1)} %get-tuple-element.98), channel_id=1, source_target_pairs={{0,8},{2,10},{4,12},{6,14},{8,16},{10,18},{12,20},{14,22},{16,24},... | collective-permute-start | bytes 589832 | tf_op jit(solution)/shard_map/ppermute | solution.py:363
  24.1 9.7 %collective-permute-start.17 = (bf16[12,64,128]{2,1,0:T(8,128)(2,1)S(1)}, bf16[12,64,128]{2,1,0:T(8,128)(2,1)S(1)}, u32[]{:S(2)}, u32[]{:S(2)}) collective-permute-start(bf16[12,64,128]{2,1,0:T(8,128)(2,1)S(1)} %broadcast_select_fusion.3), channel_id=1, source_target_pairs={{0,4},{2,6},{4,0},{6,2},{8,12},{10,14},{12,8},{14,10},{16,20},{18,... | collective-permute-start | bytes 589832 | tf_op jit(solution)/shard_map/ppermute | solution.py:366
  29.8 8.7 %collective-permute-start.7 = (bf16[12,64,128]{2,1,0:T(8,128)(2,1)S(1)}, bf16[12,64,128]{2,1,0:T(8,128)(2,1)S(1)}, u32[]{:S(2)}, u32[]{:S(2)}) collective-permute-start(bf16[12,64,128]{2,1,0:T(8,128)(2,1)S(1)} %get-tuple-element.82), channel_id=1, source_target_pairs={{0,8},{2,10},{4,12},{6,14},{8,16},{10,18},{12,20},{14,22},{16,24},... | collective-permute-start | bytes 589832 | tf_op jit(solution)/shard_map/ppermute | solution.py:363
  29.8 8.6 %collective-permute-start.13 = (bf16[12,64,128]{2,1,0:T(8,128)(2,1)S(1)}, bf16[12,64,128]{2,1,0:T(8,128)(2,1)S(1)}, u32[]{:S(2)}, u32[]{:S(2)}) collective-permute-start(bf16[12,64,128]{2,1,0:T(8,128)(2,1)S(1)} %broadcast_select_fusion.5), channel_id=1, source_target_pairs={{0,4},{2,6},{4,0},{6,2},{8,12},{10,14},{12,8},{14,10},{16,20},{18,... | collective-permute-start | bytes 589832 | tf_op jit(solution)/shard_map/ppermute | solution.py:366
  33.8 7.7 %collective-permute-start.15 = (bf16[12,64,128]{2,1,0:T(8,128)(2,1)S(1)}, bf16[12,64,128]{2,1,0:T(8,128)(2,1)S(1)}, u32[]{:S(2)}, u32[]{:S(2)}) collective-permute-start(bf16[12,64,128]{2,1,0:T(8,128)(2,1)S(1)} %get-tuple-element.93), channel_id=1, source_target_pairs={{0,8},{2,10},{4,12},{6,14},{8,16},{10,18},{12,20},{14,22},{16,24},... | collective-permute-start | bytes 589832 | tf_op jit(solution)/shard_map/ppermute | solution.py:363
  33.8 7.7 %collective-permute-start.18 = (bf16[12,64,128]{2,1,0:T(8,128)(2,1)S(1)}, bf16[12,64,128]{2,1,0:T(8,128)(2,1)S(1)}, u32[]{:S(2)}, u32[]{:S(2)}) collective-permute-start(bf16[12,64,128]{2,1,0:T(8,128)(2,1)S(1)} %broadcast_select_fusion.2), channel_id=1, source_target_pairs={{0,4},{2,6},{4,0},{6,2},{8,12},{10,14},{12,8},{14,10},{16,20},{18,... | collective-permute-start | bytes 589832 | tf_op jit(solution)/shard_map/ppermute | solution.py:366
  38.5 14.5 %collective-permute-start.14 = (bf16[12,64,128]{2,1,0:T(8,128)(2,1)S(1)}, bf16[12,64,128]{2,1,0:T(8,128)(2,1)S(1)}, u32[]{:S(2)}, u32[]{:S(2)}) collective-permute-start(bf16[12,64,128]{2,1,0:T(8,128)(2,1)S(1)} %broadcast_select_fusion.4), channel_id=1, source_target_pairs={{0,4},{2,6},{4,0},{6,2},{8,12},{10,14},{12,8},{14,10},{16,20},{18,... | collective-permute-start | bytes 589832 | tf_op jit(solution)/shard_map/ppermute | solution.py:366
  41.5 11.5 %collective-permute-start.19 = (bf16[12,64,128]{2,1,0:T(8,128)(2,1)S(1)}, bf16[12,64,128]{2,1,0:T(8,128)(2,1)S(1)}, u32[]{:S(2)}, u32[]{:S(2)}) collective-permute-start(bf16[12,64,128]{2,1,0:T(8,128)(2,1)S(1)} %broadcast_select_fusion.1), channel_id=1, source_target_pairs={{0,4},{2,6},{4,0},{6,2},{8,12},{10,14},{12,8},{14,10},{16,20},{18,... | collective-permute-start | bytes 589832 | tf_op jit(solution)/shard_map/ppermute | solution.py:396
  48.5 6.9 %collective-permute-start.21 = (bf16[2,4,128,128]{3,2,1,0:T(8,128)(2,1)S(1)}, bf16[2,4,128,128]{3,2,1,0:T(8,128)(2,1)S(1)}, u32[]{:S(2)}, u32[]{:S(2)}) collective-permute-start(bf16[2,4,128,128]{3,2,1,0:T(8,128)(2,1)S(1)} %get-tuple-element.117), channel_id=1, source_target_pairs={{0,2},{2,0},{4,6},{6,4},{8,10},{10,8},{12,14},{14,12},{16,18},{18,... | collective-permute-start | bytes 786440 | tf_op jit(solution)/shard_map/ppermute | solution.py:398
  54.5 1.8 %collective-permute-start.20 = (bf16[2,4,128,128]{3,2,1,0:T(8,128)(2,1)S(1)}, bf16[2,4,128,128]{3,2,1,0:T(8,128)(2,1)S(1)}, u32[]{:S(2)}, u32[]{:S(2)}) collective-permute-start(bf16[2,4,128,128]{3,2,1,0:T(8,128)(2,1)S(1)} %get-tuple-element.116), channel_id=1, source_target_pairs={{0,2},{2,0},{4,6},{6,4},{8,10},{10,8},{12,14},{14,12},{16,18},{18,... | collective-permute-start | bytes 786440 | tf_op jit(solution)/shard_map/ppermute | solution.py:403

commit v8 on v7

--- a/solution.py
+++ b/solution.py
@@ -13,7 +13,7 @@
 EPS = 1e-06
 
 GROUP = 16
-SIZES = (8,8,8,12,12,12,12,12,12)
+SIZES = (4,8,12,12,12,12,12,12,12)
 BLOCK = 24
 RAW = 3
 TERMS = 3
@@ -25,8 +25,8 @@
 SETS = (5, 2, 2)
 LEFT_AFTER = -1
 OTHER_AFTER = 0
-NEAR_BEFORE = 9
-CROSS_BEFORE = (8, 9)
+NEAR_BEFORE = 8
+CROSS_BEFORE = (7, 9)
 VMEM_LIMIT = 10 * 1024 * 1024
 
 

time: 57.8 us -> 56.5 us (0.978)
  waiting for transfers between devices: 18 us -> 13 us
  starting transfers between devices: 22.3 us -> 26.4 us
    ppermute x6, waiting for transfers between devices: 14.5 us -> 10.1 us  [shards(): twos[later] = lax.ppermute(mine[later], 'ch', ahead)]
    ppermute x8, starting transfers between devices: 6.37 us -> 10.8 us  [shards(): ones[k] = lax.ppermute(onward[k], 'ch', beside)]
    ppermute x1, starting transfers between devices: 3.59 us -> 5.34 us  [shards(): two_got = lax.ppermute(two_sent, 'ch', mate)]
    ppermute x1, starting transfers between devices: 3.77 us -> 2.42 us  [shards(): other = lax.ppermute(left, 'ch', mate)]
    ppermute x6, starting transfers between devices: 1.35 us -> 0.67 us  [shards(): twos[later] = lax.ppermute(mine[later], 'ch', ahead)]
where the time goes in v8:
time: 56.5 us; the launch traced here: 56.2 us
  starting transfers between devices  26.4 us (47%)
  Pallas kernels  14.2 us (25%)
  waiting for transfers between devices  13 us (23%)
  local copies, waits for them, and re-layouts  1.41 us (2%)
  other arithmetic  1.04 us (2%)
    ppermute x8, starting transfers between devices, shards(): ones[k] = lax.ppermute(onward[k], 'ch', beside)  10.8 us
    ppermute x6, waiting for transfers between devices, shards(): twos[later] = lax.ppermute(mine[later], 'ch', ahead)  10.1 us
    pallas_call x4, Pallas kernels, cross(): call(functools.partial(cross_kernel, tuple(these), kinds, first, last), '...  7.54 us
    ppermute x1, starting transfers between devices, shards(): two_got = lax.ppermute(two_sent, 'ch', mate)  5.34 us
    ppermute x3, starting transfers between devices, shards(): twos = {k: lax.ppermute(early[k], 'ch', ahead) for k in range(RAW)}  3.89 us
    pallas_call x4, Pallas kernels, put(): call(functools.partial(put_kernel, kind), 'put', out_shape, [vmem()] * le...  3.43 us
    ppermute x1, starting transfers between devices, shards(): other = lax.ppermute(left, 'ch', mate)  2.42 us
    pallas_call x1, Pallas kernels, shards(): call(near_kernel, 'near', near_shape, [smem(), smem(), vmem(), vmem()], v...  2.29 us
  transfers between devices with their start and end apart: 22, of which 8 were waited for; matrix products, arithmetic and copies ran while one was open for 2% of the time, Pallas kernels for 23%

profile of v8, /device:TPU:1, one launch (start us, length us, event | category | flops | bytes accessed | tf_op | source)
XLA Modules:
  0.0 56.2 jit_solution(5612091086193202935)
XLA Ops:
  0.0 0.0 copy-start
  0.0 1.4 %copy-done = bf16[2,48,64,128]{3,2,1,0:T(8,128)(2,1)S(1)} copy-done((bf16[2,48,64,128]{3,2,1,0:T(8,128)(2,1)S(1)}, bf16[2,48,64,128]{3,2,1,0:T(8,128)(2,1)}, u32[]{:S(2)}) %copy-start) | copy-done | bytes 1572888
  1.4 0.0 copy-start.1
  1.4 0.4 power.1
  1.8 2.1 %collective-permute-start = (f32[4,128]{1,0:T(4,128)S(1)}, f32[4,128]{1,0:T(4,128)S(1)}, u32[]{:S(2)}, u32[]{:S(2)}) collective-permute-start(f32[4,128]{1,0:T(4,128)S(1)} %get-tuple-element.66), channel_id=1, source_target_pairs={{0,1},{1,0},{2,3},{3,2},{4,5},{5,4},{6,7},{7,6},{8,9},{9,8},{10,11... | collective-permute-start | bytes 6152 | tf_op jit(solution)/shard_map/ppermute | solution.py:291
  3.9 1.3 %collective-permute-start.1 = (bf16[4,64,128]{2,1,0:T(8,128)(2,1)S(1)}, bf16[4,64,128]{2,1,0:T(8,128)(2,1)S(1)}, u32[]{:S(2)}, u32[]{:S(2)}) collective-permute-start(bf16[4,64,128]{2,1,0:T(8,128)(2,1)S(1)} %get-tuple-element.68), channel_id=1, source_target_pairs={{0,8},{2,10},{4,12},{6,14},{8,16},{10,18},{12,20},{14,22},{16,24},... | collective-permute-start | bytes 196616 | tf_op jit(solution)/shard_map/ppermute | solution.py:290
  5.2 1.3 %collective-permute-start.9 = (bf16[8,64,128]{2,1,0:T(8,128)(2,1)S(1)}, bf16[8,64,128]{2,1,0:T(8,128)(2,1)S(1)}, u32[]{:S(2)}, u32[]{:S(2)}) collective-permute-start(bf16[8,64,128]{2,1,0:T(8,128)(2,1)S(1)} %get-tuple-element.85), channel_id=1, source_target_pairs={{0,8},{2,10},{4,12},{6,14},{8,16},{10,18},{12,20},{14,22},{16,24},... | collective-permute-start | bytes 393224 | tf_op jit(solution)/shard_map/ppermute | solution.py:290
  6.5 1.3 %collective-permute-start.3 = (bf16[12,64,128]{2,1,0:T(8,128)(2,1)S(1)}, bf16[12,64,128]{2,1,0:T(8,128)(2,1)S(1)}, u32[]{:S(2)}, u32[]{:S(2)}) collective-permute-start(bf16[12,64,128]{2,1,0:T(8,128)(2,1)S(1)} %get-tuple-element.70), channel_id=1, source_target_pairs={{0,8},{2,10},{4,12},{6,14},{8,16},{10,18},{12,20},{14,22},{16,24},... | collective-permute-start | bytes 589832 | tf_op jit(solution)/shard_map/ppermute | solution.py:290
  7.8 0.7 %broadcast_subtract_fusion = s32[64]{0:T(128)S(1)} fusion(s32[64]{0:T(128)} %param.3, s32[]{:T(128)S(6)} %mul.6), kind=kLoop, calls=%fused_computation.12 | loop fusion | flops 64 | bytes 516 | tf_op jit(solution)/shard_map/sub | solution.py:284
  8.4 0.1 convert_reduce_fusion.bounds_ref
  8.6 0.1 multiply_rsqrt_fusion.norm_ref
  8.6 0.0 collective-permute-done.halo_ref
  8.6 0.0 copy-done.1
  8.6 0.5 left.1
  9.2 0.0 collective-permute-done.1.refs_5_
  9.2 2.4 %collective-permute-start.2 = (bf16[4,128,1536]{2,1,0:T(8,128)(2,1)S(1)}, bf16[4,128,1536]{2,1,0:T(8,128)(2,1)S(1)}, u32[]{:S(2)}, u32[]{:S(2)}) collective-permute-start(bf16[4,128,1536]{2,1,0:T(8,128)(2,1)S(1)} %get-tuple-element.69.own_ref), channel_id=1, source_target_pairs={{0,2},{2,0},{4,6},{6,4},{8,10},{10,8},{12,14},{14,12},{16,18},{18,... | collective-permute-start | bytes 4718600 | tf_op jit(solution)/shard_map/ppermute | solution.py:338
  11.6 1.3 %collective-permute-start.4 = (bf16[4,64,128]{2,1,0:T(8,128)(2,1)S(1)}, bf16[4,64,128]{2,1,0:T(8,128)(2,1)S(1)}, u32[]{:S(2)}, u32[]{:S(2)}) collective-permute-start(bf16[4,64,128]{2,1,0:T(8,128)(2,1)S(1)} %broadcast_select_fusion.8), channel_id=1, source_target_pairs={{0,4},{2,6},{4,0},{6,2},{8,12},{10,14},{12,8},{14,10},{16,20},{18,... | collective-permute-start | bytes 196616 | tf_op jit(solution)/shard_map/ppermute | solution.py:366
  12.9 0.0 collective-permute-start.8
  12.9 0.0 collective-permute-done.9.refs_6_
  13.0 0.5 collective-permute-start.10
  13.5 1.9 %collective-permute-done.4.refs_0_ = bf16[4,64,128]{2,1,0:T(8,128)(2,1)S(1)} collective-permute-done((bf16[4,64,128]{2,1,0:T(8,128)(2,1)S(1)}, bf16[4,64,128]{2,1,0:T(8,128)(2,1)S(1)}, u32[]{:S(2)}, u32[]{:S(2)}) %collective-permute-start.4) | collective-permute-done | bytes 65568 | tf_op jit(solution)/shard_map/ppermute | solution.py:366
  15.4 0.9 %collective-permute-done.3.refs_7_ = bf16[12,64,128]{2,1,0:T(8,128)(2,1)S(1)} collective-permute-done((bf16[12,64,128]{2,1,0:T(8,128)(2,1)S(1)}, bf16[12,64,128]{2,1,0:T(8,128)(2,1)S(1)}, u32[]{:S(2)}, u32[]{:S(2)}) %collective-permute-start.3) | collective-permute-done | bytes 196640 | tf_op jit(solution)/shard_map/ppermute | solution.py:290
  16.4 1.3 %collective-permute-start.6 = (bf16[12,64,128]{2,1,0:T(8,128)(2,1)S(1)}, bf16[12,64,128]{2,1,0:T(8,128)(2,1)S(1)}, u32[]{:S(2)}, u32[]{:S(2)}) collective-permute-start(bf16[12,64,128]{2,1,0:T(8,128)(2,1)S(1)} %broadcast_select_fusion.6), channel_id=1, source_target_pairs={{0,4},{2,6},{4,0},{6,2},{8,12},{10,14},{12,8},{14,10},{16,20},{18,... | collective-permute-start | bytes 589832 | tf_op jit(solution)/shard_map/ppermute | solution.py:366
  17.7 0.0 collective-permute-start.5
  17.7 0.0 collective-permute-done.10.refs_1_
  17.7 4.3 %collective-permute-done.8.refs_8_ = bf16[15,64,128]{2,1,0:T(8,128)(2,1)S(1)} collective-permute-done((bf16[15,64,128]{2,1,0:T(8,128)(2,1)S(1)}, bf16[15,64,128]{2,1,0:T(8,128)(2,1)S(1)}, u32[]{:S(2)}, u32[]{:S(2)}) %collective-permute-start.8) | collective-permute-done | bytes 245792 | tf_op jit(solution)/shard_map/ppermute | solution.py:363
  22.0 1.1 %collective-permute-start.12 = (bf16[15,64,128]{2,1,0:T(8,128)(2,1)S(1)}, bf16[15,64,128]{2,1,0:T(8,128)(2,1)S(1)}, u32[]{:S(2)}, u32[]{:S(2)}) collective-permute-start(bf16[15,64,128]{2,1,0:T(8,128)(2,1)S(1)} %broadcast_select_fusion), channel_id=1, source_target_pairs={{0,4},{2,6},{4,0},{6,2},{8,12},{10,14},{12,8},{14,10},{16,20},{18,... | collective-permute-start | bytes 737288 | tf_op jit(solution)/shard_map/ppermute | solution.py:366
  23.1 0.0 collective-permute-start.11
  23.1 0.0 collective-permute-done.6.refs_2_
  23.1 0.7 %collective-permute-start.13 = (bf16[12,64,128]{2,1,0:T(8,128)(2,1)S(1)}, bf16[12,64,128]{2,1,0:T(8,128)(2,1)S(1)}, u32[]{:S(2)}, u32[]{:S(2)}) collective-permute-start(bf16[12,64,128]{2,1,0:T(8,128)(2,1)S(1)} %get-tuple-element.93), channel_id=1, source_target_pairs={{0,8},{2,10},{4,12},{6,14},{8,16},{10,18},{12,20},{14,22},{16,24},... | collective-permute-start | bytes 589832 | tf_op jit(solution)/shard_map/ppermute | solution.py:363
  23.8 0.8 %collective-permute-done.5.refs_9_ = bf16[12,64,128]{2,1,0:T(8,128)(2,1)S(1)} collective-permute-done((bf16[12,64,128]{2,1,0:T(8,128)(2,1)S(1)}, bf16[12,64,128]{2,1,0:T(8,128)(2,1)S(1)}, u32[]{:S(2)}, u32[]{:S(2)}) %collective-permute-start.5) | collective-permute-done | bytes 196640 | tf_op jit(solution)/shard_map/ppermute | solution.py:363
  24.5 2.4 %collective-permute-start.14 = (bf16[12,64,128]{2,1,0:T(8,128)(2,1)S(1)}, bf16[12,64,128]{2,1,0:T(8,128)(2,1)S(1)}, u32[]{:S(2)}, u32[]{:S(2)}) collective-permute-start(bf16[12,64,128]{2,1,0:T(8,128)(2,1)S(1)} %broadcast_select_fusion.5), channel_id=1, source_target_pairs={{0,4},{2,6},{4,0},{6,2},{8,12},{10,14},{12,8},{14,10},{16,20},{18,... | collective-permute-start | bytes 589832 | tf_op jit(solution)/shard_map/ppermute | solution.py:366
  27.0 2.4 %collective-permute-done.11.refs_2_ = bf16[12,64,128]{2,1,0:T(8,128)(2,1)S(1)} collective-permute-done((bf16[12,64,128]{2,1,0:T(8,128)(2,1)S(1)}, bf16[12,64,128]{2,1,0:T(8,128)(2,1)S(1)}, u32[]{:S(2)}, u32[]{:S(2)}) %collective-permute-start.11) | collective-permute-done | bytes 196640 | tf_op jit(solution)/shard_map/ppermute | solution.py:363
  29.4 0.0 collective-permute-start.7
  29.4 0.0 collective-permute-done.12.refs_3_
  29.4 1.4 %collective-permute-start.15 = (bf16[12,64,128]{2,1,0:T(8,128)(2,1)S(1)}, bf16[12,64,128]{2,1,0:T(8,128)(2,1)S(1)}, u32[]{:S(2)}, u32[]{:S(2)}) collective-permute-start(bf16[12,64,128]{2,1,0:T(8,128)(2,1)S(1)} %broadcast_select_fusion.4), channel_id=1, source_target_pairs={{0,4},{2,6},{4,0},{6,2},{8,12},{10,14},{12,8},{14,10},{16,20},{18,... | collective-permute-start | bytes 589832 | tf_op jit(solution)/shard_map/ppermute | solution.py:366
  30.9 2.1 %collective-permute-done.13.refs_3_ = bf16[12,64,128]{2,1,0:T(8,128)(2,1)S(1)} collective-permute-done((bf16[12,64,128]{2,1,0:T(8,128)(2,1)S(1)}, bf16[12,64,128]{2,1,0:T(8,128)(2,1)S(1)}, u32[]{:S(2)}, u32[]{:S(2)}) %collective-permute-start.13) | collective-permute-done | bytes 196640 | tf_op jit(solution)/shard_map/ppermute | solution.py:363
  33.0 0.0 collective-permute-start.17
  33.0 0.0 collective-permute-done.14.refs_4_
  33.0 2.1 %collective-permute-start.18 = (bf16[12,64,128]{2,1,0:T(8,128)(2,1)S(1)}, bf16[12,64,128]{2,1,0:T(8,128)(2,1)S(1)}, u32[]{:S(2)}, u32[]{:S(2)}) collective-permute-start(bf16[12,64,128]{2,1,0:T(8,128)(2,1)S(1)} %broadcast_select_fusion.2), channel_id=1, source_target_pairs={{0,4},{2,6},{4,0},{6,2},{8,12},{10,14},{12,8},{14,10},{16,20},{18,... | collective-permute-start | bytes 589832 | tf_op jit(solution)/shard_map/ppermute | solution.py:366
  35.1 0.0 collective-permute-done.2.mate_ref
  35.1 2.6 %cross.4 = (f32[2,2,4,128,128]{4,3,2,1,0:T(8,128)S(1)}, f32[2,2,4,128,128]{4,3,2,1,0:T(8,128)S(1)}) custom-call(s32[5]{0:T(128)S(1)} %convert_reduce_fusion.bounds_ref, f32[4]{0:T(128)S(1)} %multiply_rsqrt_fusion.norm_ref, bf16[4,128,1536]{2,1,0:T(8,128)(2,1)S(1)} %get-tuple-element.69.own_ref, bf16[4,128,1536]{2,1,0:T(8,128)(2,1)S(1)} %collective-permute-done.2.mate_ref, ...), custom_call_target="tpu_custom_call" | custom-call | flops 805306368 | tf_op jit(solution)/shard_map/cross/pallas_call | solution.py:322
  37.7 0.4 collective-permute-done.7.refs_0_
  38.1 0.0 collective-permute-done.15.refs_0_
  38.1 0.6 %collective-permute-start.16 = (bf16[12,64,128]{2,1,0:T(8,128)(2,1)S(1)}, bf16[12,64,128]{2,1,0:T(8,128)(2,1)S(1)}, u32[]{:S(2)}, u32[]{:S(2)}) collective-permute-start(bf16[12,64,128]{2,1,0:T(8,128)(2,1)S(1)} %broadcast_select_fusion.3), channel_id=1, source_target_pairs={{0,4},{2,6},{4,0},{6,2},{8,12},{10,14},{12,8},{14,10},{16,20},{18,... | collective-permute-start | bytes 589832 | tf_op jit(solution)/shard_map/ppermute | solution.py:366
  38.7 2.3 %near.1.refs_1_ = f32[2,4,128,128]{3,2,1,0:T(8,128)S(1)} custom-call(s32[5]{0:T(128)S(1)} %convert_reduce_fusion.bounds_ref, f32[4]{0:T(128)S(1)} %multiply_rsqrt_fusion.norm_ref, bf16[4,128,1536]{2,1,0:T(8,128)(2,1)S(1)} %get-tuple-element.69.own_ref, bf16[4,128,1536]{2,1,0:T(8,128)(2,1)S(1)} %collective-permute-done.2.mate_ref), custom_call_target="tpu_custom_call" | custom-call | flops 1000 | bytes 1000 | tf_op jit(solution)/shard_map/near/pallas_call | solution.py:339
  41.0 0.1 collective-permute-done.17.refs_1_
  41.1 0.0 collective-permute-done.18.refs_1_
  41.2 0.9 %collective-permute-start.19 = (bf16[12,64,128]{2,1,0:T(8,128)(2,1)S(1)}, bf16[12,64,128]{2,1,0:T(8,128)(2,1)S(1)}, u32[]{:S(2)}, u32[]{:S(2)}) collective-permute-start(bf16[12,64,128]{2,1,0:T(8,128)(2,1)S(1)} %broadcast_select_fusion.1), channel_id=1, source_target_pairs={{0,4},{2,6},{4,0},{6,2},{8,12},{10,14},{12,8},{14,10},{16,20},{18,... | collective-permute-start | bytes 589832 | tf_op jit(solution)/shard_map/ppermute | solution.py:396
  42.0 2.0 %cross.5 = (f32[2,2,4,128,128]{4,3,2,1,0:T(8,128)S(1)}, f32[2,2,4,128,128]{4,3,2,1,0:T(8,128)S(1)}) custom-call(s32[5]{0:T(128)S(1)} %convert_reduce_fusion.bounds_ref, f32[4]{0:T(128)S(1)} %multiply_rsqrt_fusion.norm_ref, bf16[4,128,1536]{2,1,0:T(8,128)(2,1)S(1)} %get-tuple-element.69.own_ref, bf16[4,128,1536]{2,1,0:T(8,128)(2,1)S(1)} %collective-permute-done.2.mate_ref, ...), custom_call_target="tpu_custom_call" | custom-call | flops 402653184 | tf_op jit(solution)/shard_map/cross/pallas_call | solution.py:322
  44.1 1.5 %cross.6 = (f32[2,2,4,128,128]{4,3,2,1,0:T(8,128)S(1)}, bf16[2,4,128,128]{3,2,1,0:T(8,128)(2,1)S(1)}) custom-call(s32[5]{0:T(128)S(1)} %convert_reduce_fusion.bounds_ref, f32[4]{0:T(128)S(1)} %multiply_rsqrt_fusion.norm_ref, bf16[4,128,1536]{2,1,0:T(8,128)(2,1)S(1)} %get-tuple-element.69.own_ref, bf16[4,128,1536]{2,1,0:T(8,128)(2,1)S(1)} %collective-permute-done.2.mate_ref, ...), custom_call_target="tpu_custom_call" | custom-call | flops 201326592 | tf_op jit(solution)/shard_map/cross/pallas_call | solution.py:322
  45.6 5.3 %collective-permute-start.21 = (bf16[2,4,128,128]{3,2,1,0:T(8,128)(2,1)S(1)}, bf16[2,4,128,128]{3,2,1,0:T(8,128)(2,1)S(1)}, u32[]{:S(2)}, u32[]{:S(2)}) collective-permute-start(bf16[2,4,128,128]{3,2,1,0:T(8,128)(2,1)S(1)} %get-tuple-element.117), channel_id=1, source_target_pairs={{0,2},{2,0},{4,6},{6,4},{8,10},{10,8},{12,14},{14,12},{16,18},{18,... | collective-permute-start | bytes 786440 | tf_op jit(solution)/shard_map/ppermute | solution.py:398
  50.9 0.8 %put.4.refs_1_ = f32[2,4,4,128,128]{4,3,2,1,0:T(8,128)} custom-call(f32[2,2,4,128,128]{4,3,2,1,0:T(8,128)S(1)} %get-tuple-element.114.refs_0_), custom_call_target="tpu_custom_call" | custom-call | flops 1000 | bytes 6291456 | tf_op jit(solution)/shard_map/put/pallas_call | solution.py:381
  51.8 0.0 collective-permute-done.16.refs_0_
  51.8 0.0 collective-permute-done.19.refs_1_
  51.8 1.5 %cross.7 = (f32[2,2,4,128,128]{4,3,2,1,0:T(8,128)S(1)}, bf16[2,4,128,128]{3,2,1,0:T(8,128)(2,1)S(1)}) custom-call(s32[5]{0:T(128)S(1)} %convert_reduce_fusion.bounds_ref, f32[4]{0:T(128)S(1)} %multiply_rsqrt_fusion.norm_ref, bf16[4,128,1536]{2,1,0:T(8,128)(2,1)S(1)} %get-tuple-element.69.own_ref, bf16[4,128,1536]{2,1,0:T(8,128)(2,1)S(1)} %collective-permute-done.2.mate_ref, ...), custom_call_target="tpu_custom_call" | custom-call | flops 201326592 | tf_op jit(solution)/shard_map/cross/pallas_call | solution.py:322
  53.3 0.4 collective-permute-start.20
  53.6 0.8 %put.5.refs_2_ = f32[2,4,4,128,128]{4,3,2,1,0:T(8,128)} custom-call(f32[2,2,4,128,128]{4,3,2,1,0:T(8,128)S(1)} %get-tuple-element.119.refs_0_, f32[2,4,4,128,128]{4,3,2,1,0:T(8,128)} %put.4.refs_1_), custom_call_target="tpu_custom_call", output_to_operand_aliasing={{}: (1, {})} | custom-call | flops 1000 | bytes 6291456 | tf_op jit(solution)/shard_map/put/pallas_call | solution.py:381
  54.5 0.0 collective-permute-done.21.refs_0_
  54.5 0.9 %put.6.refs_1_ = f32[2,4,4,128,128]{4,3,2,1,0:T(8,128)} custom-call(bf16[2,4,128,128]{3,2,1,0:T(8,128)(2,1)S(1)} %collective-permute-done.21.refs_0_, f32[2,4,128,128]{3,2,1,0:T(8,128)S(1)} %near.1.refs_1_, f32[2,4,4,128,128]{4,3,2,1,0:T(8,128)} %put.5.refs_2_), custom_call_target="tpu_custom_call", output_to_operand_aliasing={{}: (2, {})} | custom-call | flops 1000 | bytes 6291456 | tf_op jit(solution)/shard_map/put/pallas_call | solution.py:381
  55.4 0.0 collective-permute-done.20.refs_0_
  55.4 0.9 %put.7 = f32[2,4,4,128,128]{4,3,2,1,0:T(8,128)} custom-call(bf16[2,4,128,128]{3,2,1,0:T(8,128)(2,1)S(1)} %collective-permute-done.20.refs_0_, f32[2,4,4,128,128]{4,3,2,1,0:T(8,128)} %put.6.refs_1_), custom_call_target="tpu_custom_call", output_to_operand_aliasing={{}: (1, {})} | custom-call | flops 1000 | bytes 6291456 | tf_op jit(solution)/shard_map/put/pallas_call | solution.py:381
  (9 shorter events, 0.2 us)
Async XLA Ops:
  0.0 1.4 %copy-start = (bf16[2,48,64,128]{3,2,1,0:T(8,128)(2,1)S(1)}, bf16[2,48,64,128]{3,2,1,0:T(8,128)(2,1)}, u32[]{:S(2)}) copy-start(bf16[2,48,64,128]{3,2,1,0:T(8,128)(2,1)} %param.2) | copy-start | bytes 4718596
  1.4 7.2 %copy-start.1 = (bf16[2,48,64,128]{3,2,1,0:T(8,128)(2,1)S(1)}, bf16[2,48,64,128]{3,2,1,0:T(8,128)(2,1)}, u32[]{:S(2)}) copy-start(bf16[2,48,64,128]{3,2,1,0:T(8,128)(2,1)} %param.2) | copy-start | bytes 4718596
  1.8 6.9 %collective-permute-start = (f32[4,128]{1,0:T(4,128)S(1)}, f32[4,128]{1,0:T(4,128)S(1)}, u32[]{:S(2)}, u32[]{:S(2)}) collective-permute-start(f32[4,128]{1,0:T(4,128)S(1)} %get-tuple-element.66), channel_id=1, source_target_pairs={{0,1},{1,0},{2,3},{3,2},{4,5},{5,4},{6,7},{7,6},{8,9},{9,8},{10,11... | collective-permute-start | bytes 6152 | tf_op jit(solution)/shard_map/ppermute | solution.py:291
  3.9 5.3 %collective-permute-start.1 = (bf16[4,64,128]{2,1,0:T(8,128)(2,1)S(1)}, bf16[4,64,128]{2,1,0:T(8,128)(2,1)S(1)}, u32[]{:S(2)}, u32[]{:S(2)}) collective-permute-start(bf16[4,64,128]{2,1,0:T(8,128)(2,1)S(1)} %get-tuple-element.68), channel_id=1, source_target_pairs={{0,8},{2,10},{4,12},{6,14},{8,16},{10,18},{12,20},{14,22},{16,24},... | collective-permute-start | bytes 196616 | tf_op jit(solution)/shard_map/ppermute | solution.py:290
  5.2 7.7 %collective-permute-start.9 = (bf16[8,64,128]{2,1,0:T(8,128)(2,1)S(1)}, bf16[8,64,128]{2,1,0:T(8,128)(2,1)S(1)}, u32[]{:S(2)}, u32[]{:S(2)}) collective-permute-start(bf16[8,64,128]{2,1,0:T(8,128)(2,1)S(1)} %get-tuple-element.85), channel_id=1, source_target_pairs={{0,8},{2,10},{4,12},{6,14},{8,16},{10,18},{12,20},{14,22},{16,24},... | collective-permute-start | bytes 393224 | tf_op jit(solution)/shard_map/ppermute | solution.py:290
  6.5 9.9 %collective-permute-start.3 = (bf16[12,64,128]{2,1,0:T(8,128)(2,1)S(1)}, bf16[12,64,128]{2,1,0:T(8,128)(2,1)S(1)}, u32[]{:S(2)}, u32[]{:S(2)}) collective-permute-start(bf16[12,64,128]{2,1,0:T(8,128)(2,1)S(1)} %get-tuple-element.70), channel_id=1, source_target_pairs={{0,8},{2,10},{4,12},{6,14},{8,16},{10,18},{12,20},{14,22},{16,24},... | collective-permute-start | bytes 589832 | tf_op jit(solution)/shard_map/ppermute | solution.py:290
  9.2 25.9 %collective-permute-start.2 = (bf16[4,128,1536]{2,1,0:T(8,128)(2,1)S(1)}, bf16[4,128,1536]{2,1,0:T(8,128)(2,1)S(1)}, u32[]{:S(2)}, u32[]{:S(2)}) collective-permute-start(bf16[4,128,1536]{2,1,0:T(8,128)(2,1)S(1)} %get-tuple-element.69.own_ref), channel_id=1, source_target_pairs={{0,2},{2,0},{4,6},{6,4},{8,10},{10,8},{12,14},{14,12},{16,18},{18,... | collective-permute-start | bytes 4718600 | tf_op jit(solution)/shard_map/ppermute | solution.py:338
  11.6 3.8 %collective-permute-start.4 = (bf16[4,64,128]{2,1,0:T(8,128)(2,1)S(1)}, bf16[4,64,128]{2,1,0:T(8,128)(2,1)S(1)}, u32[]{:S(2)}, u32[]{:S(2)}) collective-permute-start(bf16[4,64,128]{2,1,0:T(8,128)(2,1)S(1)} %broadcast_select_fusion.8), channel_id=1, source_target_pairs={{0,4},{2,6},{4,0},{6,2},{8,12},{10,14},{12,8},{14,10},{16,20},{18,... | collective-permute-start | bytes 196616 | tf_op jit(solution)/shard_map/ppermute | solution.py:366
  12.9 9.1 %collective-permute-start.8 = (bf16[15,64,128]{2,1,0:T(8,128)(2,1)S(1)}, bf16[15,64,128]{2,1,0:T(8,128)(2,1)S(1)}, u32[]{:S(2)}, u32[]{:S(2)}) collective-permute-start(bf16[15,64,128]{2,1,0:T(8,128)(2,1)S(1)} %get-tuple-element.84), channel_id=1, source_target_pairs={{0,8},{2,10},{4,12},{6,14},{8,16},{10,18},{12,20},{14,22},{16,24},... | collective-permute-start | bytes 737288 | tf_op jit(solution)/shard_map/ppermute | solution.py:363
  13.0 4.7 %collective-permute-start.10 = (bf16[8,64,128]{2,1,0:T(8,128)(2,1)S(1)}, bf16[8,64,128]{2,1,0:T(8,128)(2,1)S(1)}, u32[]{:S(2)}, u32[]{:S(2)}) collective-permute-start(bf16[8,64,128]{2,1,0:T(8,128)(2,1)S(1)} %broadcast_select_fusion.7), channel_id=1, source_target_pairs={{0,4},{2,6},{4,0},{6,2},{8,12},{10,14},{12,8},{14,10},{16,20},{18,... | collective-permute-start | bytes 393224 | tf_op jit(solution)/shard_map/ppermute | solution.py:366
  16.4 6.7 %collective-permute-start.6 = (bf16[12,64,128]{2,1,0:T(8,128)(2,1)S(1)}, bf16[12,64,128]{2,1,0:T(8,128)(2,1)S(1)}, u32[]{:S(2)}, u32[]{:S(2)}) collective-permute-start(bf16[12,64,128]{2,1,0:T(8,128)(2,1)S(1)} %broadcast_select_fusion.6), channel_id=1, source_target_pairs={{0,4},{2,6},{4,0},{6,2},{8,12},{10,14},{12,8},{14,10},{16,20},{18,... | collective-permute-start | bytes 589832 | tf_op jit(solution)/shard_map/ppermute | solution.py:366
  17.7 6.8 %collective-permute-start.5 = (bf16[12,64,128]{2,1,0:T(8,128)(2,1)S(1)}, bf16[12,64,128]{2,1,0:T(8,128)(2,1)S(1)}, u32[]{:S(2)}, u32[]{:S(2)}) collective-permute-start(bf16[12,64,128]{2,1,0:T(8,128)(2,1)S(1)} %get-tuple-element.76), channel_id=1, source_target_pairs={{0,8},{2,10},{4,12},{6,14},{8,16},{10,18},{12,20},{14,22},{16,24},... | collective-permute-start | bytes 589832 | tf_op jit(solution)/shard_map/ppermute | solution.py:363
  22.0 7.4 %collective-permute-start.12 = (bf16[15,64,128]{2,1,0:T(8,128)(2,1)S(1)}, bf16[15,64,128]{2,1,0:T(8,128)(2,1)S(1)}, u32[]{:S(2)}, u32[]{:S(2)}) collective-permute-start(bf16[15,64,128]{2,1,0:T(8,128)(2,1)S(1)} %broadcast_select_fusion), channel_id=1, source_target_pairs={{0,4},{2,6},{4,0},{6,2},{8,12},{10,14},{12,8},{14,10},{16,20},{18,... | collective-permute-start | bytes 737288 | tf_op jit(solution)/shard_map/ppermute | solution.py:366
  23.1 6.3 %collective-permute-start.11 = (bf16[12,64,128]{2,1,0:T(8,128)(2,1)S(1)}, bf16[12,64,128]{2,1,0:T(8,128)(2,1)S(1)}, u32[]{:S(2)}, u32[]{:S(2)}) collective-permute-start(bf16[12,64,128]{2,1,0:T(8,128)(2,1)S(1)} %get-tuple-element.88), channel_id=1, source_target_pairs={{0,8},{2,10},{4,12},{6,14},{8,16},{10,18},{12,20},{14,22},{16,24},... | collective-permute-start | bytes 589832 | tf_op jit(solution)/shard_map/ppermute | solution.py:363
  23.1 9.9 %collective-permute-start.13 = (bf16[12,64,128]{2,1,0:T(8,128)(2,1)S(1)}, bf16[12,64,128]{2,1,0:T(8,128)(2,1)S(1)}, u32[]{:S(2)}, u32[]{:S(2)}) collective-permute-start(bf16[12,64,128]{2,1,0:T(8,128)(2,1)S(1)} %get-tuple-element.93), channel_id=1, source_target_pairs={{0,8},{2,10},{4,12},{6,14},{8,16},{10,18},{12,20},{14,22},{16,24},... | collective-permute-start | bytes 589832 | tf_op jit(solution)/shard_map/ppermute | solution.py:363
  24.5 8.4 %collective-permute-start.14 = (bf16[12,64,128]{2,1,0:T(8,128)(2,1)S(1)}, bf16[12,64,128]{2,1,0:T(8,128)(2,1)S(1)}, u32[]{:S(2)}, u32[]{:S(2)}) collective-permute-start(bf16[12,64,128]{2,1,0:T(8,128)(2,1)S(1)} %broadcast_select_fusion.5), channel_id=1, source_target_pairs={{0,4},{2,6},{4,0},{6,2},{8,12},{10,14},{12,8},{14,10},{16,20},{18,... | collective-permute-start | bytes 589832 | tf_op jit(solution)/shard_map/ppermute | solution.py:366
  29.4 8.7 %collective-permute-start.7 = (bf16[12,64,128]{2,1,0:T(8,128)(2,1)S(1)}, bf16[12,64,128]{2,1,0:T(8,128)(2,1)S(1)}, u32[]{:S(2)}, u32[]{:S(2)}) collective-permute-start(bf16[12,64,128]{2,1,0:T(8,128)(2,1)S(1)} %get-tuple-element.82), channel_id=1, source_target_pairs={{0,8},{2,10},{4,12},{6,14},{8,16},{10,18},{12,20},{14,22},{16,24},... | collective-permute-start | bytes 589832 | tf_op jit(solution)/shard_map/ppermute | solution.py:363
  29.4 8.6 %collective-permute-start.15 = (bf16[12,64,128]{2,1,0:T(8,128)(2,1)S(1)}, bf16[12,64,128]{2,1,0:T(8,128)(2,1)S(1)}, u32[]{:S(2)}, u32[]{:S(2)}) collective-permute-start(bf16[12,64,128]{2,1,0:T(8,128)(2,1)S(1)} %broadcast_select_fusion.4), channel_id=1, source_target_pairs={{0,4},{2,6},{4,0},{6,2},{8,12},{10,14},{12,8},{14,10},{16,20},{18,... | collective-permute-start | bytes 589832 | tf_op jit(solution)/shard_map/ppermute | solution.py:366
  33.0 8.2 %collective-permute-start.17 = (bf16[12,64,128]{2,1,0:T(8,128)(2,1)S(1)}, bf16[12,64,128]{2,1,0:T(8,128)(2,1)S(1)}, u32[]{:S(2)}, u32[]{:S(2)}) collective-permute-start(bf16[12,64,128]{2,1,0:T(8,128)(2,1)S(1)} %get-tuple-element.102), channel_id=1, source_target_pairs={{0,8},{2,10},{4,12},{6,14},{8,16},{10,18},{12,20},{14,22},{16,24},... | collective-permute-start | bytes 589832 | tf_op jit(solution)/shard_map/ppermute | solution.py:363
  33.0 8.1 %collective-permute-start.18 = (bf16[12,64,128]{2,1,0:T(8,128)(2,1)S(1)}, bf16[12,64,128]{2,1,0:T(8,128)(2,1)S(1)}, u32[]{:S(2)}, u32[]{:S(2)}) collective-permute-start(bf16[12,64,128]{2,1,0:T(8,128)(2,1)S(1)} %broadcast_select_fusion.2), channel_id=1, source_target_pairs={{0,4},{2,6},{4,0},{6,2},{8,12},{10,14},{12,8},{14,10},{16,20},{18,... | collective-permute-start | bytes 589832 | tf_op jit(solution)/shard_map/ppermute | solution.py:366
  38.1 13.7 %collective-permute-start.16 = (bf16[12,64,128]{2,1,0:T(8,128)(2,1)S(1)}, bf16[12,64,128]{2,1,0:T(8,128)(2,1)S(1)}, u32[]{:S(2)}, u32[]{:S(2)}) collective-permute-start(bf16[12,64,128]{2,1,0:T(8,128)(2,1)S(1)} %broadcast_select_fusion.3), channel_id=1, source_target_pairs={{0,4},{2,6},{4,0},{6,2},{8,12},{10,14},{12,8},{14,10},{16,20},{18,... | collective-permute-start | bytes 589832 | tf_op jit(solution)/shard_map/ppermute | solution.py:366
  41.2 10.6 %collective-permute-start.19 = (bf16[12,64,128]{2,1,0:T(8,128)(2,1)S(1)}, bf16[12,64,128]{2,1,0:T(8,128)(2,1)S(1)}, u32[]{:S(2)}, u32[]{:S(2)}) collective-permute-start(bf16[12,64,128]{2,1,0:T(8,128)(2,1)S(1)} %broadcast_select_fusion.1), channel_id=1, source_target_pairs={{0,4},{2,6},{4,0},{6,2},{8,12},{10,14},{12,8},{14,10},{16,20},{18,... | collective-permute-start | bytes 589832 | tf_op jit(solution)/shard_map/ppermute | solution.py:396
  45.6 8.9 %collective-permute-start.21 = (bf16[2,4,128,128]{3,2,1,0:T(8,128)(2,1)S(1)}, bf16[2,4,128,128]{3,2,1,0:T(8,128)(2,1)S(1)}, u32[]{:S(2)}, u32[]{:S(2)}) collective-permute-start(bf16[2,4,128,128]{3,2,1,0:T(8,128)(2,1)S(1)} %get-tuple-element.117), channel_id=1, source_target_pairs={{0,2},{2,0},{4,6},{6,4},{8,10},{10,8},{12,14},{14,12},{16,18},{18,... | collective-permute-start | bytes 786440 | tf_op jit(solution)/shard_map/ppermute | solution.py:398
  53.3 2.1 %collective-permute-start.20 = (bf16[2,4,128,128]{3,2,1,0:T(8,128)(2,1)S(1)}, bf16[2,4,128,128]{3,2,1,0:T(8,128)(2,1)S(1)}, u32[]{:S(2)}, u32[]{:S(2)}) collective-permute-start(bf16[2,4,128,128]{3,2,1,0:T(8,128)(2,1)S(1)} %get-tuple-element.116), channel_id=1, source_target_pairs={{0,2},{2,0},{4,6},{6,4},{8,10},{10,8},{12,14},{14,12},{16,18},{18,... | collective-permute-start | bytes 786440 | tf_op jit(solution)/shard_map/ppermute | solution.py:403

commit v9 on v8

--- a/solution.py
+++ b/solution.py
@@ -26,7 +26,7 @@
 LEFT_AFTER = -1
 OTHER_AFTER = 0
 NEAR_BEFORE = 8
-CROSS_BEFORE = (7, 9)
+CROSS_BEFORE = 7
 VMEM_LIMIT = 10 * 1024 * 1024
 
 
@@ -164,57 +164,72 @@
         each_band(bounds_ref, groups, bands, add)
 
 
-def cross_kernel(these, kinds, first, last, bounds_ref, norm_ref, own_ref, mate_ref, *refs):
-    count, start = len(these), sum(SIZES[: these[0]])
-    rights = [refs[k * count : (k + 1) * count] for k in range(kinds)]
-    refs = refs[kinds * count :]
+def cross_kernel(jobs, first, sent, bounds_ref, norm_ref, own_ref, mate_ref, *refs):
+    present = sorted({kind for kinds, _ in jobs for kind in kinds})
+    work = []
+    for kinds, these in jobs:
+        taken = []
+        for _ in kinds:
+            taken.append(refs[: len(these)])
+            refs = refs[len(these) :]
+        work.append((kinds, these, taken))
     if not first:
-        befores, refs = refs[:kinds], refs[kinds:]
-    sums = refs[:kinds]
-    width, channels = rights[0][0].shape[1:]
-    bands = sums[0].shape[2]
+        befores, refs = refs[: len(present)], refs[len(present) :]
+    sums = dict(zip(present, refs))
+    width, channels = work[0][2][0][0].shape[1:]
+    bands = refs[0].shape[2]
     half = own_ref.shape[2] // 2
-    lanes = slice(start * GROUP, sum(SIZES[: these[-1] + 1]) * GROUP)
-    turned = lanes.start >= half
-    shift = -half if turned else half
-    across = slice(lanes.start + shift, lanes.stop + shift)
-    for k in range(kinds):
-        sums[k][...] = jnp.zeros_like(sums[k]) if first else befores[k][...]
-
-    def column(right, here, held):
+    for index, kind in enumerate(present):
+        sums[kind][...] = jnp.zeros_like(refs[0]) if first else befores[index][...]
+
+    def column(right, these, here, held):
         scale = None
         if first:
             for term in range(TERMS):
                 part = right[RAW][SIZES[RAW] + term, here, :].astype(jnp.float32)
                 scale = part if scale is None else scale + part
         blocks = []
-        for index, ref in enumerate(right):
-            size = SIZES[these[index]]
+        for ref, number in zip(right, these):
+            size = SIZES[number]
             block = ref[:size, here, :]
-            if first and index < RAW:
+            if number < RAW:
                 block = (block.astype(jnp.float32) * scale[None]).astype(jnp.bfloat16)
             blocks.append((block * held[None]).reshape(size * GROUP, channels))
         return jnp.concatenate(blocks, axis=0)
 
-    def add(group, band, low, high):
-        begin = group * GROUP
-        here = pl.ds(begin if isinstance(group, int) else pl.multiple_of(begin, GROUP), GROUP)
-        held = inside(group, low, high, (GROUP, channels), 0)
-        left = jnp.concatenate(
-            [ref[group, :, part] for ref in (own_ref, mate_ref) for part in (lanes, across)], axis=0
-        )
-        right = jnp.concatenate([column(right, here, held) for right in rights], axis=1)
-        product = jnp.dot(left, right, preferred_element_type=jnp.float32) * norm_ref[band]
-        for k in range(kinds):
-            for owner in range(2):
-                for part in range(2):
-                    row = (2 * owner + part) * channels
-                    term = product[row : row + channels, k * channels : (k + 1) * channels]
-                    sums[k][part, owner, band] += -term if part and turned else term
-
-    each_band(bounds_ref, width // GROUP, bands, add)
-    if last:
-        refs[kinds][...] = sums[0][:, 1].astype(jnp.bfloat16)
+    def multiply(kinds, these, taken, owners):
+        start, stop = sum(SIZES[: these[0]]) * GROUP, sum(SIZES[: these[-1] + 1]) * GROUP
+        turned = start >= half
+        shift = -half if turned else half
+        parts = slice(start, stop), slice(start + shift, stop + shift)
+
+        def add(group, band, low, high):
+            begin = group * GROUP
+            here = pl.ds(begin if isinstance(group, int) else pl.multiple_of(begin, GROUP), GROUP)
+            held = inside(group, low, high, (GROUP, channels), 0)
+            left = jnp.concatenate(
+                [ref[group, :, part] for ref in (own_ref, mate_ref)[:owners] for part in parts], axis=0
+            )
+            right = jnp.concatenate([column(right, these, here, held) for right in taken], axis=1)
+            product = jnp.dot(left, right, preferred_element_type=jnp.float32) * norm_ref[band]
+            for k, kind in enumerate(kinds):
+                for owner in range(owners):
+                    for part in range(2):
+                        row = (2 * owner + part) * channels
+                        term = product[row : row + channels, k * channels : (k + 1) * channels]
+                        sums[kind][part, owner, band] += -term if part and turned else term
+
+        each_band(bounds_ref, width // GROUP, bands, add)
+
+    core = lax.axis_index("ch") % 2
+    for kinds, these, taken in work:
+        if kinds == (1,):
+            pl.when(core == 0)(functools.partial(multiply, kinds, these, taken, 1))
+            pl.when(core == 1)(functools.partial(multiply, kinds, these, taken, 2))
+        else:
+            multiply(kinds, these, taken, 2)
+    if sent is not None:
+        refs[-1][...] = sums[sent][:, 1].astype(jnp.bfloat16)
 
 
 def put_kernel(kind, *refs):
@@ -308,32 +323,27 @@
     near_shape = jax.ShapeDtypeStruct((2, band_width, channels, channels), jnp.float32)
     send_shape = jax.ShapeDtypeStruct((2, band_width, channels, channels), jnp.bfloat16)
 
-    sets = [range(sum(SETS[:s]), sum(SETS[: s + 1])) for s in range(len(SETS))]
+    sets = [tuple(range(sum(SETS[:s]), sum(SETS[: s + 1]))) for s in range(len(SETS))]
     ones, onward = {}, {}
-    sums = {}
-
-    def cross(these, flights, befores, last=False):
-        first = befores is None
+
+    def cross(jobs, befores=(), sent=None):
         operands = [bounds, norms, left, other]
-        for flight in flights:
-            operands += [flight[k] for k in these]
-        operands += [] if first else befores
-        kinds = len(flights)
+        for kinds, these in jobs:
+            for kind in kinds:
+                operands += [(ones, twos)[kind][k] for k in these]
+        operands += befores
+        count = len({kind for kinds, _ in jobs for kind in kinds})
+        products = sum(len(kinds) * SIZES[k] for kinds, these in jobs for k in these)
         return call(
-            functools.partial(
-                cross_kernel, tuple(these), kinds, first, last
-            ),
+            functools.partial(cross_kernel, jobs, not befores, sent),
             "cross",
-            (sum_shape,) * kinds + (send_shape,) * last,
+            (sum_shape,) * count + (send_shape,) * (sent is not None),
             [smem(), smem()] + [vmem()] * (len(operands) - 2),
-            (vmem(),) * (kinds + last),
-            8 * kinds * sum(SIZES[k] for k in these) * width * channels * channels,
+            (vmem(),) * (count + (sent is not None)),
+            8 * products * width * channels * channels,
             0 * nbytes,
         )(*operands)
 
-    for k in range(RAW, pieces):
-        if Z_AFTER[k] < 0:
-            twos[k] = lax.ppermute(mine[k], "ch", ahead)
     left, twos[OTHER_AFTER] = after(left, twos[OTHER_AFTER])
     other = lax.ppermute(left, "ch", mate)
     near = call(
@@ -349,10 +359,9 @@
     for k in range(pieces):
         if k == NEAR_BEFORE:
             twos[k], near = after(twos[k], near)
-        for s in range(len(SETS) - 1):
-            if CROSS_BEFORE[s] == k:
-                sums[s] = list(cross(sets[s], (ones, twos), sums.get(s - 1)))
-                twos[k], sums[s][0] = after(twos[k], sums[s][0])
+        if k == CROSS_BEFORE:
+            one_sum, two_sum = cross((((0, 1), sets[0]),))
+            twos[k], one_sum = after(twos[k], one_sum)
         if Y_AFTER[k] >= 0:
             twos[k], ones[Y_AFTER[k]] = after(twos[k], ones[Y_AFTER[k]])
         if CHAIN and k > 0:
@@ -365,15 +374,12 @@
         if k < pieces - 1:
             ones[k] = lax.ppermute(onward[k], "ch", beside)
     final = pieces - 1
-    for s in range(len(SETS) - 1):
-        if s not in sums:
-            onward[final], twos[sets[s][0]] = after(onward[final], twos[sets[s][0]])
-            if NEAR_BEFORE == pieces:
-                twos[sets[s][0]], near = after(twos[sets[s][0]], near)
-            if LAST_TIE:
-                ones[final - 1], twos[sets[s][0]] = after(ones[final - 1], twos[sets[s][0]])
-            sums[s] = list(cross(sets[s], (ones, twos), sums.get(s - 1)))
-    one_sum, two_sum = sums[len(SETS) - 2]
+    middle = sets[1][0]
+    onward[final], twos[middle] = after(onward[final], twos[middle])
+    if NEAR_BEFORE == pieces:
+        twos[middle], near = after(twos[middle], near)
+    if LAST_TIE:
+        ones[final - 1], twos[middle] = after(ones[final - 1], twos[middle])
 
     def put(kind, out, *values):
         aliased = out is not None
@@ -394,12 +400,14 @@
         )(*operands)
 
     ones[final] = lax.ppermute(onward[final], "ch", beside)
-    two_sum, two_sent = cross(sets[-1], (twos,), [two_sum], True)
+    one_sum, two_sum, two_sent = cross(
+        (((0,), sets[1]), ((1,), sets[1] + sets[2])), (one_sum, two_sum), 1
+    )
     two_got = lax.ppermute(two_sent, "ch", mate)
     out = put("two", None, two_sum)
     if PUT_TIE:
         one_sum, out = after(one_sum, out)
-    one_sum, one_sent = cross(sets[-1], (ones,), [one_sum], True)
+    one_sum, one_sent = cross((((0,), sets[2]),), (one_sum,), 0)
     one_got = lax.ppermute(one_sent, "ch", mate)
     out = put("one", out, one_sum)
     out = put("near", out, two_got, near)

time: 56.5 us -> 56.4 us (level)
    ppermute x1, starting transfers between devices: 0.36 us -> 1.43 us  [shards(): one_got = lax.ppermute(one_sent, 'ch', mate)]
    ppermute x1, starting transfers between devices: 5.34 us -> 4.37 us  [shards(): two_got = lax.ppermute(two_sent, 'ch', mate)]
    pallas_call x4 -> x3, Pallas kernels: 7.54 us -> 7.45 us  [cross(): call(functools.partial(cross_kernel, jobs, not befores, sent), 'cross', (...]
where the time goes in v9:
time: 56.4 us; the launch traced here: 56.2 us
  starting transfers between devices  26.5 us (47%)
  Pallas kernels  14.1 us (25%)
  waiting for transfers between devices  13 us (23%)
  local copies, waits for them, and re-layouts  1.41 us (2%)
  other arithmetic  1.04 us (2%)
    ppermute x8, starting transfers between devices, shards(): ones[k] = lax.ppermute(onward[k], 'ch', beside)  10.8 us
    ppermute x6, waiting for transfers between devices, shards(): twos[later] = lax.ppermute(mine[later], 'ch', ahead)  10.1 us
    pallas_call x3, Pallas kernels, cross(): call(functools.partial(cross_kernel, jobs, not befores, sent), 'cross', (...  7.45 us
    ppermute x1, starting transfers between devices, shards(): two_got = lax.ppermute(two_sent, 'ch', mate)  4.37 us
    ppermute x3, starting transfers between devices, shards(): twos = {k: lax.ppermute(early[k], 'ch', ahead) for k in range(RAW)}  3.89 us
    pallas_call x4, Pallas kernels, put(): call(functools.partial(put_kernel, kind), 'put', out_shape, [vmem()] * le...  3.43 us
    ppermute x1, starting transfers between devices, shards(): other = lax.ppermute(left, 'ch', mate)  2.42 us
    pallas_call x1, Pallas kernels, shards(): call(near_kernel, 'near', near_shape, [smem(), smem(), vmem(), vmem()], v...  2.29 us
  transfers between devices with their start and end apart: 22, of which 8 were waited for; matrix products, arithmetic and copies ran while one was open for 2% of the time, Pallas kernels for 23%

profile of v9, /device:TPU:1, one launch (start us, length us, event | category | flops | bytes accessed | tf_op | source)
XLA Modules:
  0.0 56.2 jit_solution(6226078754628137051)
XLA Ops:
  0.0 0.0 copy-start
  0.0 1.4 %copy-done = bf16[2,48,64,128]{3,2,1,0:T(8,128)(2,1)S(1)} copy-done((bf16[2,48,64,128]{3,2,1,0:T(8,128)(2,1)S(1)}, bf16[2,48,64,128]{3,2,1,0:T(8,128)(2,1)}, u32[]{:S(2)}) %copy-start) | copy-done | bytes 1572888
  1.4 0.0 copy-start.1
  1.4 0.4 power.1
  1.8 2.1 %collective-permute-start = (f32[4,128]{1,0:T(4,128)S(1)}, f32[4,128]{1,0:T(4,128)S(1)}, u32[]{:S(2)}, u32[]{:S(2)}) collective-permute-start(f32[4,128]{1,0:T(4,128)S(1)} %get-tuple-element.65), channel_id=1, source_target_pairs={{0,1},{1,0},{2,3},{3,2},{4,5},{5,4},{6,7},{7,6},{8,9},{9,8},{10,11... | collective-permute-start | bytes 6152 | tf_op jit(solution)/shard_map/ppermute | solution.py:306
  3.9 1.3 %collective-permute-start.1 = (bf16[4,64,128]{2,1,0:T(8,128)(2,1)S(1)}, bf16[4,64,128]{2,1,0:T(8,128)(2,1)S(1)}, u32[]{:S(2)}, u32[]{:S(2)}) collective-permute-start(bf16[4,64,128]{2,1,0:T(8,128)(2,1)S(1)} %get-tuple-element.67), channel_id=1, source_target_pairs={{0,8},{2,10},{4,12},{6,14},{8,16},{10,18},{12,20},{14,22},{16,24},... | collective-permute-start | bytes 196616 | tf_op jit(solution)/shard_map/ppermute | solution.py:305
  5.2 1.3 %collective-permute-start.9 = (bf16[8,64,128]{2,1,0:T(8,128)(2,1)S(1)}, bf16[8,64,128]{2,1,0:T(8,128)(2,1)S(1)}, u32[]{:S(2)}, u32[]{:S(2)}) collective-permute-start(bf16[8,64,128]{2,1,0:T(8,128)(2,1)S(1)} %get-tuple-element.84), channel_id=1, source_target_pairs={{0,8},{2,10},{4,12},{6,14},{8,16},{10,18},{12,20},{14,22},{16,24},... | collective-permute-start | bytes 393224 | tf_op jit(solution)/shard_map/ppermute | solution.py:305
  6.5 1.3 %collective-permute-start.3 = (bf16[12,64,128]{2,1,0:T(8,128)(2,1)S(1)}, bf16[12,64,128]{2,1,0:T(8,128)(2,1)S(1)}, u32[]{:S(2)}, u32[]{:S(2)}) collective-permute-start(bf16[12,64,128]{2,1,0:T(8,128)(2,1)S(1)} %get-tuple-element.69), channel_id=1, source_target_pairs={{0,8},{2,10},{4,12},{6,14},{8,16},{10,18},{12,20},{14,22},{16,24},... | collective-permute-start | bytes 589832 | tf_op jit(solution)/shard_map/ppermute | solution.py:305
  7.8 0.7 %broadcast_subtract_fusion = s32[64]{0:T(128)S(1)} fusion(s32[64]{0:T(128)} %param.3, s32[]{:T(128)S(6)} %mul.6), kind=kLoop, calls=%fused_computation.12 | loop fusion | flops 64 | bytes 516 | tf_op jit(solution)/shard_map/sub | solution.py:299
  8.4 0.1 convert_reduce_fusion.bounds_ref
  8.6 0.1 multiply_rsqrt_fusion.norm_ref
  8.6 0.0 collective-permute-done.halo_ref
  8.6 0.0 copy-done.1
  8.6 0.5 left.1
  9.2 0.0 collective-permute-done.1.refs_5_
  9.2 2.4 %collective-permute-start.2 = (bf16[4,128,1536]{2,1,0:T(8,128)(2,1)S(1)}, bf16[4,128,1536]{2,1,0:T(8,128)(2,1)S(1)}, u32[]{:S(2)}, u32[]{:S(2)}) collective-permute-start(bf16[4,128,1536]{2,1,0:T(8,128)(2,1)S(1)} %get-tuple-element.68.own_ref), channel_id=1, source_target_pairs={{0,2},{2,0},{4,6},{6,4},{8,10},{10,8},{12,14},{14,12},{16,18},{18,... | collective-permute-start | bytes 4718600 | tf_op jit(solution)/shard_map/ppermute | solution.py:348
  11.6 1.3 %collective-permute-start.4 = (bf16[4,64,128]{2,1,0:T(8,128)(2,1)S(1)}, bf16[4,64,128]{2,1,0:T(8,128)(2,1)S(1)}, u32[]{:S(2)}, u32[]{:S(2)}) collective-permute-start(bf16[4,64,128]{2,1,0:T(8,128)(2,1)S(1)} %broadcast_select_fusion.8), channel_id=1, source_target_pairs={{0,4},{2,6},{4,0},{6,2},{8,12},{10,14},{12,8},{14,10},{16,20},{18,... | collective-permute-start | bytes 196616 | tf_op jit(solution)/shard_map/ppermute | solution.py:375
  12.9 0.0 collective-permute-start.8
  12.9 0.0 collective-permute-done.9.refs_6_
  13.0 0.5 collective-permute-start.10
  13.5 1.9 %collective-permute-done.4.refs_0_ = bf16[4,64,128]{2,1,0:T(8,128)(2,1)S(1)} collective-permute-done((bf16[4,64,128]{2,1,0:T(8,128)(2,1)S(1)}, bf16[4,64,128]{2,1,0:T(8,128)(2,1)S(1)}, u32[]{:S(2)}, u32[]{:S(2)}) %collective-permute-start.4) | collective-permute-done | bytes 65568 | tf_op jit(solution)/shard_map/ppermute | solution.py:375
  15.4 0.9 %collective-permute-done.3.refs_7_ = bf16[12,64,128]{2,1,0:T(8,128)(2,1)S(1)} collective-permute-done((bf16[12,64,128]{2,1,0:T(8,128)(2,1)S(1)}, bf16[12,64,128]{2,1,0:T(8,128)(2,1)S(1)}, u32[]{:S(2)}, u32[]{:S(2)}) %collective-permute-start.3) | collective-permute-done | bytes 196640 | tf_op jit(solution)/shard_map/ppermute | solution.py:305
  16.4 1.3 %collective-permute-start.6 = (bf16[12,64,128]{2,1,0:T(8,128)(2,1)S(1)}, bf16[12,64,128]{2,1,0:T(8,128)(2,1)S(1)}, u32[]{:S(2)}, u32[]{:S(2)}) collective-permute-start(bf16[12,64,128]{2,1,0:T(8,128)(2,1)S(1)} %broadcast_select_fusion.6), channel_id=1, source_target_pairs={{0,4},{2,6},{4,0},{6,2},{8,12},{10,14},{12,8},{14,10},{16,20},{18,... | collective-permute-start | bytes 589832 | tf_op jit(solution)/shard_map/ppermute | solution.py:375
  17.7 0.0 collective-permute-start.5
  17.7 0.0 collective-permute-done.10.refs_1_
  17.7 4.3 %collective-permute-done.8.refs_8_ = bf16[15,64,128]{2,1,0:T(8,128)(2,1)S(1)} collective-permute-done((bf16[15,64,128]{2,1,0:T(8,128)(2,1)S(1)}, bf16[15,64,128]{2,1,0:T(8,128)(2,1)S(1)}, u32[]{:S(2)}, u32[]{:S(2)}) %collective-permute-start.8) | collective-permute-done | bytes 245792 | tf_op jit(solution)/shard_map/ppermute | solution.py:372
  22.0 1.1 %collective-permute-start.12 = (bf16[15,64,128]{2,1,0:T(8,128)(2,1)S(1)}, bf16[15,64,128]{2,1,0:T(8,128)(2,1)S(1)}, u32[]{:S(2)}, u32[]{:S(2)}) collective-permute-start(bf16[15,64,128]{2,1,0:T(8,128)(2,1)S(1)} %broadcast_select_fusion), channel_id=1, source_target_pairs={{0,4},{2,6},{4,0},{6,2},{8,12},{10,14},{12,8},{14,10},{16,20},{18,... | collective-permute-start | bytes 737288 | tf_op jit(solution)/shard_map/ppermute | solution.py:375
  23.1 0.0 collective-permute-start.11
  23.1 0.0 collective-permute-done.6.refs_2_
  23.1 0.7 %collective-permute-start.13 = (bf16[12,64,128]{2,1,0:T(8,128)(2,1)S(1)}, bf16[12,64,128]{2,1,0:T(8,128)(2,1)S(1)}, u32[]{:S(2)}, u32[]{:S(2)}) collective-permute-start(bf16[12,64,128]{2,1,0:T(8,128)(2,1)S(1)} %get-tuple-element.92), channel_id=1, source_target_pairs={{0,8},{2,10},{4,12},{6,14},{8,16},{10,18},{12,20},{14,22},{16,24},... | collective-permute-start | bytes 589832 | tf_op jit(solution)/shard_map/ppermute | solution.py:372
  23.8 0.8 %collective-permute-done.5.refs_9_ = bf16[12,64,128]{2,1,0:T(8,128)(2,1)S(1)} collective-permute-done((bf16[12,64,128]{2,1,0:T(8,128)(2,1)S(1)}, bf16[12,64,128]{2,1,0:T(8,128)(2,1)S(1)}, u32[]{:S(2)}, u32[]{:S(2)}) %collective-permute-start.5) | collective-permute-done | bytes 196640 | tf_op jit(solution)/shard_map/ppermute | solution.py:372
  24.5 2.4 %collective-permute-start.14 = (bf16[12,64,128]{2,1,0:T(8,128)(2,1)S(1)}, bf16[12,64,128]{2,1,0:T(8,128)(2,1)S(1)}, u32[]{:S(2)}, u32[]{:S(2)}) collective-permute-start(bf16[12,64,128]{2,1,0:T(8,128)(2,1)S(1)} %broadcast_select_fusion.5), channel_id=1, source_target_pairs={{0,4},{2,6},{4,0},{6,2},{8,12},{10,14},{12,8},{14,10},{16,20},{18,... | collective-permute-start | bytes 589832 | tf_op jit(solution)/shard_map/ppermute | solution.py:375
  27.0 2.4 %collective-permute-done.11.refs_2_ = bf16[12,64,128]{2,1,0:T(8,128)(2,1)S(1)} collective-permute-done((bf16[12,64,128]{2,1,0:T(8,128)(2,1)S(1)}, bf16[12,64,128]{2,1,0:T(8,128)(2,1)S(1)}, u32[]{:S(2)}, u32[]{:S(2)}) %collective-permute-start.11) | collective-permute-done | bytes 196640 | tf_op jit(solution)/shard_map/ppermute | solution.py:372
  29.4 0.0 collective-permute-start.7
  29.4 0.0 collective-permute-done.12.refs_3_
  29.4 1.4 %collective-permute-start.15 = (bf16[12,64,128]{2,1,0:T(8,128)(2,1)S(1)}, bf16[12,64,128]{2,1,0:T(8,128)(2,1)S(1)}, u32[]{:S(2)}, u32[]{:S(2)}) collective-permute-start(bf16[12,64,128]{2,1,0:T(8,128)(2,1)S(1)} %broadcast_select_fusion.4), channel_id=1, source_target_pairs={{0,4},{2,6},{4,0},{6,2},{8,12},{10,14},{12,8},{14,10},{16,20},{18,... | collective-permute-start | bytes 589832 | tf_op jit(solution)/shard_map/ppermute | solution.py:375
  30.9 2.1 %collective-permute-done.13.refs_3_ = bf16[12,64,128]{2,1,0:T(8,128)(2,1)S(1)} collective-permute-done((bf16[12,64,128]{2,1,0:T(8,128)(2,1)S(1)}, bf16[12,64,128]{2,1,0:T(8,128)(2,1)S(1)}, u32[]{:S(2)}, u32[]{:S(2)}) %collective-permute-start.13) | collective-permute-done | bytes 196640 | tf_op jit(solution)/shard_map/ppermute | solution.py:372
  33.0 0.0 collective-permute-start.17
  33.0 0.0 collective-permute-done.14.refs_4_
  33.0 2.1 %collective-permute-start.18 = (bf16[12,64,128]{2,1,0:T(8,128)(2,1)S(1)}, bf16[12,64,128]{2,1,0:T(8,128)(2,1)S(1)}, u32[]{:S(2)}, u32[]{:S(2)}) collective-permute-start(bf16[12,64,128]{2,1,0:T(8,128)(2,1)S(1)} %broadcast_select_fusion.2), channel_id=1, source_target_pairs={{0,4},{2,6},{4,0},{6,2},{8,12},{10,14},{12,8},{14,10},{16,20},{18,... | collective-permute-start | bytes 589832 | tf_op jit(solution)/shard_map/ppermute | solution.py:375
  35.1 0.0 collective-permute-done.2.mate_ref
  35.1 2.6 %cross.3 = (f32[2,2,4,128,128]{4,3,2,1,0:T(8,128)S(1)}, f32[2,2,4,128,128]{4,3,2,1,0:T(8,128)S(1)}) custom-call(s32[5]{0:T(128)S(1)} %convert_reduce_fusion.bounds_ref, f32[4]{0:T(128)S(1)} %multiply_rsqrt_fusion.norm_ref, bf16[4,128,1536]{2,1,0:T(8,128)(2,1)S(1)} %get-tuple-element.68.own_ref, bf16[4,128,1536]{2,1,0:T(8,128)(2,1)S(1)} %collective-permute-done.2.mate_ref, ...), custom_call_target="tpu_custom_call" | custom-call | flops 805306368 | tf_op jit(solution)/shard_map/cross/pallas_call | solution.py:337
  37.7 0.4 collective-permute-done.7.refs_4_
  38.1 0.0 collective-permute-done.15.refs_0_
  38.1 0.6 %collective-permute-start.16 = (bf16[12,64,128]{2,1,0:T(8,128)(2,1)S(1)}, bf16[12,64,128]{2,1,0:T(8,128)(2,1)S(1)}, u32[]{:S(2)}, u32[]{:S(2)}) collective-permute-start(bf16[12,64,128]{2,1,0:T(8,128)(2,1)S(1)} %broadcast_select_fusion.3), channel_id=1, source_target_pairs={{0,4},{2,6},{4,0},{6,2},{8,12},{10,14},{12,8},{14,10},{16,20},{18,... | collective-permute-start | bytes 589832 | tf_op jit(solution)/shard_map/ppermute | solution.py:375
  38.7 2.3 %near.1.refs_1_ = f32[2,4,128,128]{3,2,1,0:T(8,128)S(1)} custom-call(s32[5]{0:T(128)S(1)} %convert_reduce_fusion.bounds_ref, f32[4]{0:T(128)S(1)} %multiply_rsqrt_fusion.norm_ref, bf16[4,128,1536]{2,1,0:T(8,128)(2,1)S(1)} %get-tuple-element.68.own_ref, bf16[4,128,1536]{2,1,0:T(8,128)(2,1)S(1)} %collective-permute-done.2.mate_ref), custom_call_target="tpu_custom_call" | custom-call | flops 1000 | bytes 1000 | tf_op jit(solution)/shard_map/near/pallas_call | solution.py:349
  41.0 0.1 collective-permute-done.17.refs_5_
  41.1 0.0 collective-permute-done.18.refs_1_
  41.2 0.9 %collective-permute-start.19 = (bf16[12,64,128]{2,1,0:T(8,128)(2,1)S(1)}, bf16[12,64,128]{2,1,0:T(8,128)(2,1)S(1)}, u32[]{:S(2)}, u32[]{:S(2)}) collective-permute-start(bf16[12,64,128]{2,1,0:T(8,128)(2,1)S(1)} %broadcast_select_fusion.1), channel_id=1, source_target_pairs={{0,4},{2,6},{4,0},{6,2},{8,12},{10,14},{12,8},{14,10},{16,20},{18,... | collective-permute-start | bytes 589832 | tf_op jit(solution)/shard_map/ppermute | solution.py:402
  42.0 3.4 %cross.4 = (f32[2,2,4,128,128]{4,3,2,1,0:T(8,128)S(1)}, f32[2,2,4,128,128]{4,3,2,1,0:T(8,128)S(1)}, bf16[2,4,128,128]{3,2,1,0:T(8,128)(2,1)S(1)}) custom-call(s32[5]{0:T(128)S(1)} %convert_reduce_fusion.bounds_ref, f32[4]{0:T(128)S(1)} %multiply_rsqrt_fusion.norm_ref, bf16[4,128,1536]{2,1,0:T(8,128)(2,1)S(1)} %get-tuple-element.68.own_ref, ...), custom_call_target="tpu_custom_call" | custom-call | flops 603979776 | tf_op jit(solution)/shard_map/cross/pallas_call | solution.py:337
  45.5 4.4 %collective-permute-start.21 = (bf16[2,4,128,128]{3,2,1,0:T(8,128)(2,1)S(1)}, bf16[2,4,128,128]{3,2,1,0:T(8,128)(2,1)S(1)}, u32[]{:S(2)}, u32[]{:S(2)}) collective-permute-start(bf16[2,4,128,128]{3,2,1,0:T(8,128)(2,1)S(1)} %get-tuple-element.115), channel_id=1, source_target_pairs={{0,2},{2,0},{4,6},{6,4},{8,10},{10,8},{12,14},{14,12},{16,18},{18,... | collective-permute-start | bytes 786440 | tf_op jit(solution)/shard_map/ppermute | solution.py:406
  49.8 0.8 %put.4.refs_1_ = f32[2,4,4,128,128]{4,3,2,1,0:T(8,128)} custom-call(f32[2,2,4,128,128]{4,3,2,1,0:T(8,128)S(1)} %get-tuple-element.112.refs_0_), custom_call_target="tpu_custom_call" | custom-call | flops 1000 | bytes 6291456 | tf_op jit(solution)/shard_map/put/pallas_call | solution.py:387
  50.7 0.0 collective-permute-done.16.refs_0_
  50.7 0.0 collective-permute-done.19.refs_1_
  50.7 1.5 %cross.5 = (f32[2,2,4,128,128]{4,3,2,1,0:T(8,128)S(1)}, bf16[2,4,128,128]{3,2,1,0:T(8,128)(2,1)S(1)}) custom-call(s32[5]{0:T(128)S(1)} %convert_reduce_fusion.bounds_ref, f32[4]{0:T(128)S(1)} %multiply_rsqrt_fusion.norm_ref, bf16[4,128,1536]{2,1,0:T(8,128)(2,1)S(1)} %get-tuple-element.68.own_ref, bf16[4,128,1536]{2,1,0:T(8,128)(2,1)S(1)} %collective-permute-done.2.mate_ref, ...), custom_call_target="tpu_custom_call" | custom-call | flops 201326592 | tf_op jit(solution)/shard_map/cross/pallas_call | solution.py:337
  52.2 1.4 %collective-permute-start.20 = (bf16[2,4,128,128]{3,2,1,0:T(8,128)(2,1)S(1)}, bf16[2,4,128,128]{3,2,1,0:T(8,128)(2,1)S(1)}, u32[]{:S(2)}, u32[]{:S(2)}) collective-permute-start(bf16[2,4,128,128]{3,2,1,0:T(8,128)(2,1)S(1)} %get-tuple-element.114), channel_id=1, source_target_pairs={{0,2},{2,0},{4,6},{6,4},{8,10},{10,8},{12,14},{14,12},{16,18},{18,... | collective-permute-start | bytes 786440 | tf_op jit(solution)/shard_map/ppermute | solution.py:411
  53.6 0.8 %put.5.refs_2_ = f32[2,4,4,128,128]{4,3,2,1,0:T(8,128)} custom-call(f32[2,2,4,128,128]{4,3,2,1,0:T(8,128)S(1)} %get-tuple-element.117.refs_0_, f32[2,4,4,128,128]{4,3,2,1,0:T(8,128)} %put.4.refs_1_), custom_call_target="tpu_custom_call", output_to_operand_aliasing={{}: (1, {})} | custom-call | flops 1000 | bytes 6291456 | tf_op jit(solution)/shard_map/put/pallas_call | solution.py:387
  54.5 0.0 collective-permute-done.21.refs_0_
  54.5 0.9 %put.6.refs_1_ = f32[2,4,4,128,128]{4,3,2,1,0:T(8,128)} custom-call(bf16[2,4,128,128]{3,2,1,0:T(8,128)(2,1)S(1)} %collective-permute-done.21.refs_0_, f32[2,4,128,128]{3,2,1,0:T(8,128)S(1)} %near.1.refs_1_, f32[2,4,4,128,128]{4,3,2,1,0:T(8,128)} %put.5.refs_2_), custom_call_target="tpu_custom_call", output_to_operand_aliasing={{}: (2, {})} | custom-call | flops 1000 | bytes 6291456 | tf_op jit(solution)/shard_map/put/pallas_call | solution.py:387
  55.4 0.0 collective-permute-done.20.refs_0_
  55.4 0.9 %put.7 = f32[2,4,4,128,128]{4,3,2,1,0:T(8,128)} custom-call(bf16[2,4,128,128]{3,2,1,0:T(8,128)(2,1)S(1)} %collective-permute-done.20.refs_0_, f32[2,4,4,128,128]{4,3,2,1,0:T(8,128)} %put.6.refs_1_), custom_call_target="tpu_custom_call", output_to_operand_aliasing={{}: (1, {})} | custom-call | flops 1000 | bytes 6291456 | tf_op jit(solution)/shard_map/put/pallas_call | solution.py:387
  (9 shorter events, 0.2 us)
Async XLA Ops:
  0.0 1.4 %copy-start = (bf16[2,48,64,128]{3,2,1,0:T(8,128)(2,1)S(1)}, bf16[2,48,64,128]{3,2,1,0:T(8,128)(2,1)}, u32[]{:S(2)}) copy-start(bf16[2,48,64,128]{3,2,1,0:T(8,128)(2,1)} %param.2) | copy-start | bytes 4718596
  1.4 7.2 %copy-start.1 = (bf16[2,48,64,128]{3,2,1,0:T(8,128)(2,1)S(1)}, bf16[2,48,64,128]{3,2,1,0:T(8,128)(2,1)}, u32[]{:S(2)}) copy-start(bf16[2,48,64,128]{3,2,1,0:T(8,128)(2,1)} %param.2) | copy-start | bytes 4718596
  1.8 6.9 %collective-permute-start = (f32[4,128]{1,0:T(4,128)S(1)}, f32[4,128]{1,0:T(4,128)S(1)}, u32[]{:S(2)}, u32[]{:S(2)}) collective-permute-start(f32[4,128]{1,0:T(4,128)S(1)} %get-tuple-element.65), channel_id=1, source_target_pairs={{0,1},{1,0},{2,3},{3,2},{4,5},{5,4},{6,7},{7,6},{8,9},{9,8},{10,11... | collective-permute-start | bytes 6152 | tf_op jit(solution)/shard_map/ppermute | solution.py:306
  3.9 5.3 %collective-permute-start.1 = (bf16[4,64,128]{2,1,0:T(8,128)(2,1)S(1)}, bf16[4,64,128]{2,1,0:T(8,128)(2,1)S(1)}, u32[]{:S(2)}, u32[]{:S(2)}) collective-permute-start(bf16[4,64,128]{2,1,0:T(8,128)(2,1)S(1)} %get-tuple-element.67), channel_id=1, source_target_pairs={{0,8},{2,10},{4,12},{6,14},{8,16},{10,18},{12,20},{14,22},{16,24},... | collective-permute-start | bytes 196616 | tf_op jit(solution)/shard_map/ppermute | solution.py:305
  5.2 7.7 %collective-permute-start.9 = (bf16[8,64,128]{2,1,0:T(8,128)(2,1)S(1)}, bf16[8,64,128]{2,1,0:T(8,128)(2,1)S(1)}, u32[]{:S(2)}, u32[]{:S(2)}) collective-permute-start(bf16[8,64,128]{2,1,0:T(8,128)(2,1)S(1)} %get-tuple-element.84), channel_id=1, source_target_pairs={{0,8},{2,10},{4,12},{6,14},{8,16},{10,18},{12,20},{14,22},{16,24},... | collective-permute-start | bytes 393224 | tf_op jit(solution)/shard_map/ppermute | solution.py:305
  6.5 9.9 %collective-permute-start.3 = (bf16[12,64,128]{2,1,0:T(8,128)(2,1)S(1)}, bf16[12,64,128]{2,1,0:T(8,128)(2,1)S(1)}, u32[]{:S(2)}, u32[]{:S(2)}) collective-permute-start(bf16[12,64,128]{2,1,0:T(8,128)(2,1)S(1)} %get-tuple-element.69), channel_id=1, source_target_pairs={{0,8},{2,10},{4,12},{6,14},{8,16},{10,18},{12,20},{14,22},{16,24},... | collective-permute-start | bytes 589832 | tf_op jit(solution)/shard_map/ppermute | solution.py:305
  9.2 25.9 %collective-permute-start.2 = (bf16[4,128,1536]{2,1,0:T(8,128)(2,1)S(1)}, bf16[4,128,1536]{2,1,0:T(8,128)(2,1)S(1)}, u32[]{:S(2)}, u32[]{:S(2)}) collective-permute-start(bf16[4,128,1536]{2,1,0:T(8,128)(2,1)S(1)} %get-tuple-element.68.own_ref), channel_id=1, source_target_pairs={{0,2},{2,0},{4,6},{6,4},{8,10},{10,8},{12,14},{14,12},{16,18},{18,... | collective-permute-start | bytes 4718600 | tf_op jit(solution)/shard_map/ppermute | solution.py:348
  11.6 3.8 %collective-permute-start.4 = (bf16[4,64,128]{2,1,0:T(8,128)(2,1)S(1)}, bf16[4,64,128]{2,1,0:T(8,128)(2,1)S(1)}, u32[]{:S(2)}, u32[]{:S(2)}) collective-permute-start(bf16[4,64,128]{2,1,0:T(8,128)(2,1)S(1)} %broadcast_select_fusion.8), channel_id=1, source_target_pairs={{0,4},{2,6},{4,0},{6,2},{8,12},{10,14},{12,8},{14,10},{16,20},{18,... | collective-permute-start | bytes 196616 | tf_op jit(solution)/shard_map/ppermute | solution.py:375
  12.9 9.1 %collective-permute-start.8 = (bf16[15,64,128]{2,1,0:T(8,128)(2,1)S(1)}, bf16[15,64,128]{2,1,0:T(8,128)(2,1)S(1)}, u32[]{:S(2)}, u32[]{:S(2)}) collective-permute-start(bf16[15,64,128]{2,1,0:T(8,128)(2,1)S(1)} %get-tuple-element.83), channel_id=1, source_target_pairs={{0,8},{2,10},{4,12},{6,14},{8,16},{10,18},{12,20},{14,22},{16,24},... | collective-permute-start | bytes 737288 | tf_op jit(solution)/shard_map/ppermute | solution.py:372
  13.0 4.7 %collective-permute-start.10 = (bf16[8,64,128]{2,1,0:T(8,128)(2,1)S(1)}, bf16[8,64,128]{2,1,0:T(8,128)(2,1)S(1)}, u32[]{:S(2)}, u32[]{:S(2)}) collective-permute-start(bf16[8,64,128]{2,1,0:T(8,128)(2,1)S(1)} %broadcast_select_fusion.7), channel_id=1, source_target_pairs={{0,4},{2,6},{4,0},{6,2},{8,12},{10,14},{12,8},{14,10},{16,20},{18,... | collective-permute-start | bytes 393224 | tf_op jit(solution)/shard_map/ppermute | solution.py:375
  16.4 6.7 %collective-permute-start.6 = (bf16[12,64,128]{2,1,0:T(8,128)(2,1)S(1)}, bf16[12,64,128]{2,1,0:T(8,128)(2,1)S(1)}, u32[]{:S(2)}, u32[]{:S(2)}) collective-permute-start(bf16[12,64,128]{2,1,0:T(8,128)(2,1)S(1)} %broadcast_select_fusion.6), channel_id=1, source_target_pairs={{0,4},{2,6},{4,0},{6,2},{8,12},{10,14},{12,8},{14,10},{16,20},{18,... | collective-permute-start | bytes 589832 | tf_op jit(solution)/shard_map/ppermute | solution.py:375
  17.7 6.8 %collective-permute-start.5 = (bf16[12,64,128]{2,1,0:T(8,128)(2,1)S(1)}, bf16[12,64,128]{2,1,0:T(8,128)(2,1)S(1)}, u32[]{:S(2)}, u32[]{:S(2)}) collective-permute-start(bf16[12,64,128]{2,1,0:T(8,128)(2,1)S(1)} %get-tuple-element.75), channel_id=1, source_target_pairs={{0,8},{2,10},{4,12},{6,14},{8,16},{10,18},{12,20},{14,22},{16,24},... | collective-permute-start | bytes 589832 | tf_op jit(solution)/shard_map/ppermute | solution.py:372
  22.0 7.4 %collective-permute-start.12 = (bf16[15,64,128]{2,1,0:T(8,128)(2,1)S(1)}, bf16[15,64,128]{2,1,0:T(8,128)(2,1)S(1)}, u32[]{:S(2)}, u32[]{:S(2)}) collective-permute-start(bf16[15,64,128]{2,1,0:T(8,128)(2,1)S(1)} %broadcast_select_fusion), channel_id=1, source_target_pairs={{0,4},{2,6},{4,0},{6,2},{8,12},{10,14},{12,8},{14,10},{16,20},{18,... | collective-permute-start | bytes 737288 | tf_op jit(solution)/shard_map/ppermute | solution.py:375
  23.1 6.3 %collective-permute-start.11 = (bf16[12,64,128]{2,1,0:T(8,128)(2,1)S(1)}, bf16[12,64,128]{2,1,0:T(8,128)(2,1)S(1)}, u32[]{:S(2)}, u32[]{:S(2)}) collective-permute-start(bf16[12,64,128]{2,1,0:T(8,128)(2,1)S(1)} %get-tuple-element.87), channel_id=1, source_target_pairs={{0,8},{2,10},{4,12},{6,14},{8,16},{10,18},{12,20},{14,22},{16,24},... | collective-permute-start | bytes 589832 | tf_op jit(solution)/shard_map/ppermute | solution.py:372
  23.1 9.9 %collective-permute-start.13 = (bf16[12,64,128]{2,1,0:T(8,128)(2,1)S(1)}, bf16[12,64,128]{2,1,0:T(8,128)(2,1)S(1)}, u32[]{:S(2)}, u32[]{:S(2)}) collective-permute-start(bf16[12,64,128]{2,1,0:T(8,128)(2,1)S(1)} %get-tuple-element.92), channel_id=1, source_target_pairs={{0,8},{2,10},{4,12},{6,14},{8,16},{10,18},{12,20},{14,22},{16,24},... | collective-permute-start | bytes 589832 | tf_op jit(solution)/shard_map/ppermute | solution.py:372
  24.5 8.4 %collective-permute-start.14 = (bf16[12,64,128]{2,1,0:T(8,128)(2,1)S(1)}, bf16[12,64,128]{2,1,0:T(8,128)(2,1)S(1)}, u32[]{:S(2)}, u32[]{:S(2)}) collective-permute-start(bf16[12,64,128]{2,1,0:T(8,128)(2,1)S(1)} %broadcast_select_fusion.5), channel_id=1, source_target_pairs={{0,4},{2,6},{4,0},{6,2},{8,12},{10,14},{12,8},{14,10},{16,20},{18,... | collective-permute-start | bytes 589832 | tf_op jit(solution)/shard_map/ppermute | solution.py:375
  29.4 8.7 %collective-permute-start.7 = (bf16[12,64,128]{2,1,0:T(8,128)(2,1)S(1)}, bf16[12,64,128]{2,1,0:T(8,128)(2,1)S(1)}, u32[]{:S(2)}, u32[]{:S(2)}) collective-permute-start(bf16[12,64,128]{2,1,0:T(8,128)(2,1)S(1)} %get-tuple-element.81), channel_id=1, source_target_pairs={{0,8},{2,10},{4,12},{6,14},{8,16},{10,18},{12,20},{14,22},{16,24},... | collective-permute-start | bytes 589832 | tf_op jit(solution)/shard_map/ppermute | solution.py:372
  29.4 8.6 %collective-permute-start.15 = (bf16[12,64,128]{2,1,0:T(8,128)(2,1)S(1)}, bf16[12,64,128]{2,1,0:T(8,128)(2,1)S(1)}, u32[]{:S(2)}, u32[]{:S(2)}) collective-permute-start(bf16[12,64,128]{2,1,0:T(8,128)(2,1)S(1)} %broadcast_select_fusion.4), channel_id=1, source_target_pairs={{0,4},{2,6},{4,0},{6,2},{8,12},{10,14},{12,8},{14,10},{16,20},{18,... | collective-permute-start | bytes 589832 | tf_op jit(solution)/shard_map/ppermute | solution.py:375
  33.0 8.2 %collective-permute-start.17 = (bf16[12,64,128]{2,1,0:T(8,128)(2,1)S(1)}, bf16[12,64,128]{2,1,0:T(8,128)(2,1)S(1)}, u32[]{:S(2)}, u32[]{:S(2)}) collective-permute-start(bf16[12,64,128]{2,1,0:T(8,128)(2,1)S(1)} %get-tuple-element.101), channel_id=1, source_target_pairs={{0,8},{2,10},{4,12},{6,14},{8,16},{10,18},{12,20},{14,22},{16,24},... | collective-permute-start | bytes 589832 | tf_op jit(solution)/shard_map/ppermute | solution.py:372
  33.0 8.1 %collective-permute-start.18 = (bf16[12,64,128]{2,1,0:T(8,128)(2,1)S(1)}, bf16[12,64,128]{2,1,0:T(8,128)(2,1)S(1)}, u32[]{:S(2)}, u32[]{:S(2)}) collective-permute-start(bf16[12,64,128]{2,1,0:T(8,128)(2,1)S(1)} %broadcast_select_fusion.2), channel_id=1, source_target_pairs={{0,4},{2,6},{4,0},{6,2},{8,12},{10,14},{12,8},{14,10},{16,20},{18,... | collective-permute-start | bytes 589832 | tf_op jit(solution)/shard_map/ppermute | solution.py:375
  38.1 12.6 %collective-permute-start.16 = (bf16[12,64,128]{2,1,0:T(8,128)(2,1)S(1)}, bf16[12,64,128]{2,1,0:T(8,128)(2,1)S(1)}, u32[]{:S(2)}, u32[]{:S(2)}) collective-permute-start(bf16[12,64,128]{2,1,0:T(8,128)(2,1)S(1)} %broadcast_select_fusion.3), channel_id=1, source_target_pairs={{0,4},{2,6},{4,0},{6,2},{8,12},{10,14},{12,8},{14,10},{16,20},{18,... | collective-permute-start | bytes 589832 | tf_op jit(solution)/shard_map/ppermute | solution.py:375
  41.2 9.5 %collective-permute-start.19 = (bf16[12,64,128]{2,1,0:T(8,128)(2,1)S(1)}, bf16[12,64,128]{2,1,0:T(8,128)(2,1)S(1)}, u32[]{:S(2)}, u32[]{:S(2)}) collective-permute-start(bf16[12,64,128]{2,1,0:T(8,128)(2,1)S(1)} %broadcast_select_fusion.1), channel_id=1, source_target_pairs={{0,4},{2,6},{4,0},{6,2},{8,12},{10,14},{12,8},{14,10},{16,20},{18,... | collective-permute-start | bytes 589832 | tf_op jit(solution)/shard_map/ppermute | solution.py:402
  45.5 9.0 %collective-permute-start.21 = (bf16[2,4,128,128]{3,2,1,0:T(8,128)(2,1)S(1)}, bf16[2,4,128,128]{3,2,1,0:T(8,128)(2,1)S(1)}, u32[]{:S(2)}, u32[]{:S(2)}) collective-permute-start(bf16[2,4,128,128]{3,2,1,0:T(8,128)(2,1)S(1)} %get-tuple-element.115), channel_id=1, source_target_pairs={{0,2},{2,0},{4,6},{6,4},{8,10},{10,8},{12,14},{14,12},{16,18},{18,... | collective-permute-start | bytes 786440 | tf_op jit(solution)/shard_map/ppermute | solution.py:406
  52.2 3.2 %collective-permute-start.20 = (bf16[2,4,128,128]{3,2,1,0:T(8,128)(2,1)S(1)}, bf16[2,4,128,128]{3,2,1,0:T(8,128)(2,1)S(1)}, u32[]{:S(2)}, u32[]{:S(2)}) collective-permute-start(bf16[2,4,128,128]{3,2,1,0:T(8,128)(2,1)S(1)} %get-tuple-element.114), channel_id=1, source_target_pairs={{0,2},{2,0},{4,6},{6,4},{8,10},{10,8},{12,14},{14,12},{16,18},{18,... | collective-permute-start | bytes 786440 | tf_op jit(solution)/shard_map/ppermute | solution.py:411

commit v10 on v9

--- a/solution.py
+++ b/solution.py
@@ -17,7 +17,8 @@
 BLOCK = 24
 RAW = 3
 TERMS = 3
-Z_AFTER = (-1, -1, -1, 0, 2, 2, 3, 4, 5)
+Z_AFTER = (-1, -1, -1, 0, 2, 2, 3, 5, 6)
+Z_BEHIND = (0,0,0,0,0,0,0,1,0)
 Y_AFTER = (-1, -1, 0, 1, 2, 3, 4, 5, 6)
 LAST_TIE = 0
 PUT_TIE = 1
@@ -367,10 +368,14 @@
         if CHAIN and k > 0:
             twos[k], onward[k - 1] = after(twos[k], onward[k - 1])
         for later in range(pieces):
-            if Z_AFTER[later] == k:
+            if Z_AFTER[later] == k and not Z_BEHIND[later]:
                 twos[k], mine[later] = after(twos[k], mine[later])
                 twos[later] = lax.ppermute(mine[later], "ch", ahead)
         onward[k] = jnp.where(odd_chip, twos[k], mine[k])
+        for later in range(pieces):
+            if Z_AFTER[later] == k and Z_BEHIND[later]:
+                onward[k], mine[later] = after(onward[k], mine[later])
+                twos[later] = lax.ppermute(mine[later], "ch", ahead)
         if k < pieces - 1:
             ones[k] = lax.ppermute(onward[k], "ch", beside)
     final = pieces - 1

time: 56.4 us -> 55.9 us (level)
  starting transfers between devices: 26.5 us -> 25.5 us
  waiting for transfers between devices: 13 us -> 13.6 us
    ppermute x6, starting transfers between devices: 0.67 us -> 2.24 us  [shards(): twos[later] = lax.ppermute(mine[later], 'ch', ahead)]
    ppermute x8, starting transfers between devices: 10.8 us -> 9.2 us  [shards(): ones[k] = lax.ppermute(onward[k], 'ch', beside)]
    ppermute x1, starting transfers between devices: 0.89 us -> 0.08 us  [shards(): ones[final] = lax.ppermute(onward[final], 'ch', beside)]
    ppermute x1, starting transfers between devices: 1.43 us -> 0.75 us  [shards(): one_got = lax.ppermute(one_sent, 'ch', mate)]
    ppermute x6, waiting for transfers between devices: 10.1 us -> 10.7 us  [shards(): twos[later] = lax.ppermute(mine[later], 'ch', ahead)]
where the time goes in v10:
time: 55.9 us; the launch traced here: 55.8 us
  starting transfers between devices  25.5 us (46%)
  Pallas kernels  14.1 us (25%)
  waiting for transfers between devices  13.6 us (24%)
  local copies, waits for them, and re-layouts  1.41 us (3%)
  other arithmetic  1.04 us (2%)
    ppermute x6, waiting for transfers between devices, shards(): twos[later] = lax.ppermute(mine[later], 'ch', ahead)  10.7 us
    ppermute x8, starting transfers between devices, shards(): ones[k] = lax.ppermute(onward[k], 'ch', beside)  9.2 us
    pallas_call x3, Pallas kernels, cross(): call(functools.partial(cross_kernel, jobs, not befores, sent), 'cross', (...  7.45 us
    ppermute x1, starting transfers between devices, shards(): two_got = lax.ppermute(two_sent, 'ch', mate)  4.8 us
    ppermute x3, starting transfers between devices, shards(): twos = {k: lax.ppermute(early[k], 'ch', ahead) for k in range(RAW)}  3.89 us
    pallas_call x4, Pallas kernels, put(): call(functools.partial(put_kernel, kind), 'put', out_shape, [vmem()] * le...  3.43 us
    ppermute x1, starting transfers between devices, shards(): other = lax.ppermute(left, 'ch', mate)  2.42 us
    pallas_call x1, Pallas kernels, shards(): call(near_kernel, 'near', near_shape, [smem(), smem(), vmem(), vmem()], v...  2.29 us
  transfers between devices with their start and end apart: 22, of which 8 were waited for; matrix products, arithmetic and copies ran while one was open for 2% of the time, Pallas kernels for 23%

profile of v10, /device:TPU:1, one launch (start us, length us, event | category | flops | bytes accessed | tf_op | source)
XLA Modules:
  0.0 55.8 jit_solution(7867428970559901278)
XLA Ops:
  0.0 0.0 copy-start
  0.0 1.4 %copy-done = bf16[2,48,64,128]{3,2,1,0:T(8,128)(2,1)S(1)} copy-done((bf16[2,48,64,128]{3,2,1,0:T(8,128)(2,1)S(1)}, bf16[2,48,64,128]{3,2,1,0:T(8,128)(2,1)}, u32[]{:S(2)}) %copy-start) | copy-done | bytes 1572888
  1.4 0.0 copy-start.1
  1.4 0.4 power.1
  1.8 2.1 %collective-permute-start = (f32[4,128]{1,0:T(4,128)S(1)}, f32[4,128]{1,0:T(4,128)S(1)}, u32[]{:S(2)}, u32[]{:S(2)}) collective-permute-start(f32[4,128]{1,0:T(4,128)S(1)} %get-tuple-element.65), channel_id=1, source_target_pairs={{0,1},{1,0},{2,3},{3,2},{4,5},{5,4},{6,7},{7,6},{8,9},{9,8},{10,11... | collective-permute-start | bytes 6152 | tf_op jit(solution)/shard_map/ppermute | solution.py:307
  3.9 1.3 %collective-permute-start.1 = (bf16[4,64,128]{2,1,0:T(8,128)(2,1)S(1)}, bf16[4,64,128]{2,1,0:T(8,128)(2,1)S(1)}, u32[]{:S(2)}, u32[]{:S(2)}) collective-permute-start(bf16[4,64,128]{2,1,0:T(8,128)(2,1)S(1)} %get-tuple-element.67), channel_id=1, source_target_pairs={{0,8},{2,10},{4,12},{6,14},{8,16},{10,18},{12,20},{14,22},{16,24},... | collective-permute-start | bytes 196616 | tf_op jit(solution)/shard_map/ppermute | solution.py:306
  5.2 1.3 %collective-permute-start.7 = (bf16[8,64,128]{2,1,0:T(8,128)(2,1)S(1)}, bf16[8,64,128]{2,1,0:T(8,128)(2,1)S(1)}, u32[]{:S(2)}, u32[]{:S(2)}) collective-permute-start(bf16[8,64,128]{2,1,0:T(8,128)(2,1)S(1)} %get-tuple-element.79), channel_id=1, source_target_pairs={{0,8},{2,10},{4,12},{6,14},{8,16},{10,18},{12,20},{14,22},{16,24},... | collective-permute-start | bytes 393224 | tf_op jit(solution)/shard_map/ppermute | solution.py:306
  6.5 1.3 %collective-permute-start.3 = (bf16[12,64,128]{2,1,0:T(8,128)(2,1)S(1)}, bf16[12,64,128]{2,1,0:T(8,128)(2,1)S(1)}, u32[]{:S(2)}, u32[]{:S(2)}) collective-permute-start(bf16[12,64,128]{2,1,0:T(8,128)(2,1)S(1)} %get-tuple-element.69), channel_id=1, source_target_pairs={{0,8},{2,10},{4,12},{6,14},{8,16},{10,18},{12,20},{14,22},{16,24},... | collective-permute-start | bytes 589832 | tf_op jit(solution)/shard_map/ppermute | solution.py:306
  7.8 0.7 %broadcast_subtract_fusion = s32[64]{0:T(128)S(1)} fusion(s32[64]{0:T(128)} %param.3, s32[]{:T(128)S(6)} %mul.6), kind=kLoop, calls=%fused_computation.12 | loop fusion | flops 64 | bytes 516 | tf_op jit(solution)/shard_map/sub | solution.py:300
  8.4 0.1 convert_reduce_fusion.bounds_ref
  8.6 0.1 multiply_rsqrt_fusion.norm_ref
  8.6 0.0 collective-permute-done.halo_ref
  8.6 0.0 copy-done.1
  8.6 0.5 left.1
  9.2 0.0 collective-permute-done.1.refs_5_
  9.2 2.4 %collective-permute-start.2 = (bf16[4,128,1536]{2,1,0:T(8,128)(2,1)S(1)}, bf16[4,128,1536]{2,1,0:T(8,128)(2,1)S(1)}, u32[]{:S(2)}, u32[]{:S(2)}) collective-permute-start(bf16[4,128,1536]{2,1,0:T(8,128)(2,1)S(1)} %get-tuple-element.68.own_ref), channel_id=1, source_target_pairs={{0,2},{2,0},{4,6},{6,4},{8,10},{10,8},{12,14},{14,12},{16,18},{18,... | collective-permute-start | bytes 4718600 | tf_op jit(solution)/shard_map/ppermute | solution.py:349
  11.6 1.3 %collective-permute-start.4 = (bf16[4,64,128]{2,1,0:T(8,128)(2,1)S(1)}, bf16[4,64,128]{2,1,0:T(8,128)(2,1)S(1)}, u32[]{:S(2)}, u32[]{:S(2)}) collective-permute-start(bf16[4,64,128]{2,1,0:T(8,128)(2,1)S(1)} %broadcast_select_fusion.8), channel_id=1, source_target_pairs={{0,4},{2,6},{4,0},{6,2},{8,12},{10,14},{12,8},{14,10},{16,20},{18,... | collective-permute-start | bytes 196616 | tf_op jit(solution)/shard_map/ppermute | solution.py:380
  12.9 0.0 collective-permute-start.6
  12.9 0.0 collective-permute-done.7.refs_6_
  13.0 0.5 collective-permute-start.8
  13.5 1.9 %collective-permute-done.4.refs_0_ = bf16[4,64,128]{2,1,0:T(8,128)(2,1)S(1)} collective-permute-done((bf16[4,64,128]{2,1,0:T(8,128)(2,1)S(1)}, bf16[4,64,128]{2,1,0:T(8,128)(2,1)S(1)}, u32[]{:S(2)}, u32[]{:S(2)}) %collective-permute-start.4) | collective-permute-done | bytes 65568 | tf_op jit(solution)/shard_map/ppermute | solution.py:380
  15.4 0.9 %collective-permute-done.3.refs_7_ = bf16[12,64,128]{2,1,0:T(8,128)(2,1)S(1)} collective-permute-done((bf16[12,64,128]{2,1,0:T(8,128)(2,1)S(1)}, bf16[12,64,128]{2,1,0:T(8,128)(2,1)S(1)}, u32[]{:S(2)}, u32[]{:S(2)}) %collective-permute-start.3) | collective-permute-done | bytes 196640 | tf_op jit(solution)/shard_map/ppermute | solution.py:306
  16.4 1.3 %collective-permute-start.12 = (bf16[12,64,128]{2,1,0:T(8,128)(2,1)S(1)}, bf16[12,64,128]{2,1,0:T(8,128)(2,1)S(1)}, u32[]{:S(2)}, u32[]{:S(2)}) collective-permute-start(bf16[12,64,128]{2,1,0:T(8,128)(2,1)S(1)} %broadcast_select_fusion.5), channel_id=1, source_target_pairs={{0,4},{2,6},{4,0},{6,2},{8,12},{10,14},{12,8},{14,10},{16,20},{18,... | collective-permute-start | bytes 589832 | tf_op jit(solution)/shard_map/ppermute | solution.py:380
  17.7 0.0 collective-permute-start.11
  17.7 0.0 collective-permute-done.8.refs_1_
  17.7 4.3 %collective-permute-done.6.refs_8_ = bf16[15,64,128]{2,1,0:T(8,128)(2,1)S(1)} collective-permute-done((bf16[15,64,128]{2,1,0:T(8,128)(2,1)S(1)}, bf16[15,64,128]{2,1,0:T(8,128)(2,1)S(1)}, u32[]{:S(2)}, u32[]{:S(2)}) %collective-permute-start.6) | collective-permute-done | bytes 245792 | tf_op jit(solution)/shard_map/ppermute | solution.py:373
  22.0 1.1 %collective-permute-start.9 = (bf16[15,64,128]{2,1,0:T(8,128)(2,1)S(1)}, bf16[15,64,128]{2,1,0:T(8,128)(2,1)S(1)}, u32[]{:S(2)}, u32[]{:S(2)}) collective-permute-start(bf16[15,64,128]{2,1,0:T(8,128)(2,1)S(1)} %broadcast_select_fusion), channel_id=1, source_target_pairs={{0,4},{2,6},{4,0},{6,2},{8,12},{10,14},{12,8},{14,10},{16,20},{18,... | collective-permute-start | bytes 737288 | tf_op jit(solution)/shard_map/ppermute | solution.py:380
  23.1 0.0 collective-permute-start.5
  23.1 0.0 collective-permute-done.12.refs_2_
  23.1 0.7 %collective-permute-start.13 = (bf16[12,64,128]{2,1,0:T(8,128)(2,1)S(1)}, bf16[12,64,128]{2,1,0:T(8,128)(2,1)S(1)}, u32[]{:S(2)}, u32[]{:S(2)}) collective-permute-start(bf16[12,64,128]{2,1,0:T(8,128)(2,1)S(1)} %get-tuple-element.92), channel_id=1, source_target_pairs={{0,8},{2,10},{4,12},{6,14},{8,16},{10,18},{12,20},{14,22},{16,24},... | collective-permute-start | bytes 589832 | tf_op jit(solution)/shard_map/ppermute | solution.py:373
  23.8 0.8 %collective-permute-done.11.refs_9_ = bf16[12,64,128]{2,1,0:T(8,128)(2,1)S(1)} collective-permute-done((bf16[12,64,128]{2,1,0:T(8,128)(2,1)S(1)}, bf16[12,64,128]{2,1,0:T(8,128)(2,1)S(1)}, u32[]{:S(2)}, u32[]{:S(2)}) %collective-permute-start.11) | collective-permute-done | bytes 196640 | tf_op jit(solution)/shard_map/ppermute | solution.py:373
  24.5 2.4 %collective-permute-start.14 = (bf16[12,64,128]{2,1,0:T(8,128)(2,1)S(1)}, bf16[12,64,128]{2,1,0:T(8,128)(2,1)S(1)}, u32[]{:S(2)}, u32[]{:S(2)}) collective-permute-start(bf16[12,64,128]{2,1,0:T(8,128)(2,1)S(1)} %broadcast_select_fusion.4), channel_id=1, source_target_pairs={{0,4},{2,6},{4,0},{6,2},{8,12},{10,14},{12,8},{14,10},{16,20},{18,... | collective-permute-start | bytes 589832 | tf_op jit(solution)/shard_map/ppermute | solution.py:380
  27.0 2.4 %collective-permute-done.5.refs_2_ = bf16[12,64,128]{2,1,0:T(8,128)(2,1)S(1)} collective-permute-done((bf16[12,64,128]{2,1,0:T(8,128)(2,1)S(1)}, bf16[12,64,128]{2,1,0:T(8,128)(2,1)S(1)}, u32[]{:S(2)}, u32[]{:S(2)}) %collective-permute-start.5) | collective-permute-done | bytes 196640 | tf_op jit(solution)/shard_map/ppermute | solution.py:373
  29.4 0.0 collective-permute-done.9.refs_3_
  29.4 0.6 %collective-permute-start.15 = (bf16[12,64,128]{2,1,0:T(8,128)(2,1)S(1)}, bf16[12,64,128]{2,1,0:T(8,128)(2,1)S(1)}, u32[]{:S(2)}, u32[]{:S(2)}) collective-permute-start(bf16[12,64,128]{2,1,0:T(8,128)(2,1)S(1)} %broadcast_select_fusion.6), channel_id=1, source_target_pairs={{0,4},{2,6},{4,0},{6,2},{8,12},{10,14},{12,8},{14,10},{16,20},{18,... | collective-permute-start | bytes 589832 | tf_op jit(solution)/shard_map/ppermute | solution.py:380
  30.0 0.8 %collective-permute-start.10 = (bf16[12,64,128]{2,1,0:T(8,128)(2,1)S(1)}, bf16[12,64,128]{2,1,0:T(8,128)(2,1)S(1)}, u32[]{:S(2)}, u32[]{:S(2)}) collective-permute-start(bf16[12,64,128]{2,1,0:T(8,128)(2,1)S(1)} %get-tuple-element.85), channel_id=1, source_target_pairs={{0,8},{2,10},{4,12},{6,14},{8,16},{10,18},{12,20},{14,22},{16,24},... | collective-permute-start | bytes 589832 | tf_op jit(solution)/shard_map/ppermute | solution.py:378
  30.9 2.1 %collective-permute-done.13.refs_3_ = bf16[12,64,128]{2,1,0:T(8,128)(2,1)S(1)} collective-permute-done((bf16[12,64,128]{2,1,0:T(8,128)(2,1)S(1)}, bf16[12,64,128]{2,1,0:T(8,128)(2,1)S(1)}, u32[]{:S(2)}, u32[]{:S(2)}) %collective-permute-start.13) | collective-permute-done | bytes 196640 | tf_op jit(solution)/shard_map/ppermute | solution.py:373
  33.0 0.0 collective-permute-done.14.refs_4_
  33.0 1.4 %collective-permute-start.18 = (bf16[12,64,128]{2,1,0:T(8,128)(2,1)S(1)}, bf16[12,64,128]{2,1,0:T(8,128)(2,1)S(1)}, u32[]{:S(2)}, u32[]{:S(2)}) collective-permute-start(bf16[12,64,128]{2,1,0:T(8,128)(2,1)S(1)} %broadcast_select_fusion.2), channel_id=1, source_target_pairs={{0,4},{2,6},{4,0},{6,2},{8,12},{10,14},{12,8},{14,10},{16,20},{18,... | collective-permute-start | bytes 589832 | tf_op jit(solution)/shard_map/ppermute | solution.py:380
  34.4 0.7 %collective-permute-start.17 = (bf16[12,64,128]{2,1,0:T(8,128)(2,1)S(1)}, bf16[12,64,128]{2,1,0:T(8,128)(2,1)S(1)}, u32[]{:S(2)}, u32[]{:S(2)}) collective-permute-start(bf16[12,64,128]{2,1,0:T(8,128)(2,1)S(1)} %get-tuple-element.101), channel_id=1, source_target_pairs={{0,8},{2,10},{4,12},{6,14},{8,16},{10,18},{12,20},{14,22},{16,24},... | collective-permute-start | bytes 589832 | tf_op jit(solution)/shard_map/ppermute | solution.py:373
  35.1 0.0 collective-permute-done.2.mate_ref
  35.1 2.6 %cross.3 = (f32[2,2,4,128,128]{4,3,2,1,0:T(8,128)S(1)}, f32[2,2,4,128,128]{4,3,2,1,0:T(8,128)S(1)}) custom-call(s32[5]{0:T(128)S(1)} %convert_reduce_fusion.bounds_ref, f32[4]{0:T(128)S(1)} %multiply_rsqrt_fusion.norm_ref, bf16[4,128,1536]{2,1,0:T(8,128)(2,1)S(1)} %get-tuple-element.68.own_ref, bf16[4,128,1536]{2,1,0:T(8,128)(2,1)S(1)} %collective-permute-done.2.mate_ref, ...), custom_call_target="tpu_custom_call" | custom-call | flops 805306368 | tf_op jit(solution)/shard_map/cross/pallas_call | solution.py:338
  37.7 0.2 collective-permute-done.10.refs_4_
  37.8 0.0 collective-permute-done.15.refs_0_
  37.9 0.6 %collective-permute-start.16 = (bf16[12,64,128]{2,1,0:T(8,128)(2,1)S(1)}, bf16[12,64,128]{2,1,0:T(8,128)(2,1)S(1)}, u32[]{:S(2)}, u32[]{:S(2)}) collective-permute-start(bf16[12,64,128]{2,1,0:T(8,128)(2,1)S(1)} %broadcast_select_fusion.3), channel_id=1, source_target_pairs={{0,4},{2,6},{4,0},{6,2},{8,12},{10,14},{12,8},{14,10},{16,20},{18,... | collective-permute-start | bytes 589832 | tf_op jit(solution)/shard_map/ppermute | solution.py:380
  38.5 2.3 %near.1.refs_1_ = f32[2,4,128,128]{3,2,1,0:T(8,128)S(1)} custom-call(s32[5]{0:T(128)S(1)} %convert_reduce_fusion.bounds_ref, f32[4]{0:T(128)S(1)} %multiply_rsqrt_fusion.norm_ref, bf16[4,128,1536]{2,1,0:T(8,128)(2,1)S(1)} %get-tuple-element.68.own_ref, bf16[4,128,1536]{2,1,0:T(8,128)(2,1)S(1)} %collective-permute-done.2.mate_ref), custom_call_target="tpu_custom_call" | custom-call | flops 1000 | bytes 1000 | tf_op jit(solution)/shard_map/near/pallas_call | solution.py:350
  40.8 0.9 %collective-permute-done.17.refs_5_ = bf16[12,64,128]{2,1,0:T(8,128)(2,1)S(1)} collective-permute-done((bf16[12,64,128]{2,1,0:T(8,128)(2,1)S(1)}, bf16[12,64,128]{2,1,0:T(8,128)(2,1)S(1)}, u32[]{:S(2)}, u32[]{:S(2)}) %collective-permute-start.17) | collective-permute-done | bytes 196640 | tf_op jit(solution)/shard_map/ppermute | solution.py:373
  41.7 0.0 collective-permute-done.18.refs_1_
  41.7 0.1 collective-permute-start.19
  41.8 3.4 %cross.4 = (f32[2,2,4,128,128]{4,3,2,1,0:T(8,128)S(1)}, f32[2,2,4,128,128]{4,3,2,1,0:T(8,128)S(1)}, bf16[2,4,128,128]{3,2,1,0:T(8,128)(2,1)S(1)}) custom-call(s32[5]{0:T(128)S(1)} %convert_reduce_fusion.bounds_ref, f32[4]{0:T(128)S(1)} %multiply_rsqrt_fusion.norm_ref, bf16[4,128,1536]{2,1,0:T(8,128)(2,1)S(1)} %get-tuple-element.68.own_ref, ...), custom_call_target="tpu_custom_call" | custom-call | flops 603979776 | tf_op jit(solution)/shard_map/cross/pallas_call | solution.py:338
  45.2 4.8 %collective-permute-start.21 = (bf16[2,4,128,128]{3,2,1,0:T(8,128)(2,1)S(1)}, bf16[2,4,128,128]{3,2,1,0:T(8,128)(2,1)S(1)}, u32[]{:S(2)}, u32[]{:S(2)}) collective-permute-start(bf16[2,4,128,128]{3,2,1,0:T(8,128)(2,1)S(1)} %get-tuple-element.115), channel_id=1, source_target_pairs={{0,2},{2,0},{4,6},{6,4},{8,10},{10,8},{12,14},{14,12},{16,18},{18,... | collective-permute-start | bytes 786440 | tf_op jit(solution)/shard_map/ppermute | solution.py:411
  50.0 0.8 %put.4.refs_1_ = f32[2,4,4,128,128]{4,3,2,1,0:T(8,128)} custom-call(f32[2,2,4,128,128]{4,3,2,1,0:T(8,128)S(1)} %get-tuple-element.112.refs_0_), custom_call_target="tpu_custom_call" | custom-call | flops 1000 | bytes 6291456 | tf_op jit(solution)/shard_map/put/pallas_call | solution.py:392
  50.9 0.0 collective-permute-done.16.refs_0_
  50.9 0.0 collective-permute-done.19.refs_1_
  50.9 1.5 %cross.5 = (f32[2,2,4,128,128]{4,3,2,1,0:T(8,128)S(1)}, bf16[2,4,128,128]{3,2,1,0:T(8,128)(2,1)S(1)}) custom-call(s32[5]{0:T(128)S(1)} %convert_reduce_fusion.bounds_ref, f32[4]{0:T(128)S(1)} %multiply_rsqrt_fusion.norm_ref, bf16[4,128,1536]{2,1,0:T(8,128)(2,1)S(1)} %get-tuple-element.68.own_ref, bf16[4,128,1536]{2,1,0:T(8,128)(2,1)S(1)} %collective-permute-done.2.mate_ref, ...), custom_call_target="tpu_custom_call" | custom-call | flops 201326592 | tf_op jit(solution)/shard_map/cross/pallas_call | solution.py:338
  52.4 0.7 %collective-permute-start.20 = (bf16[2,4,128,128]{3,2,1,0:T(8,128)(2,1)S(1)}, bf16[2,4,128,128]{3,2,1,0:T(8,128)(2,1)S(1)}, u32[]{:S(2)}, u32[]{:S(2)}) collective-permute-start(bf16[2,4,128,128]{3,2,1,0:T(8,128)(2,1)S(1)} %get-tuple-element.114), channel_id=1, source_target_pairs={{0,2},{2,0},{4,6},{6,4},{8,10},{10,8},{12,14},{14,12},{16,18},{18,... | collective-permute-start | bytes 786440 | tf_op jit(solution)/shard_map/ppermute | solution.py:416
  53.1 0.8 %put.5.refs_2_ = f32[2,4,4,128,128]{4,3,2,1,0:T(8,128)} custom-call(f32[2,2,4,128,128]{4,3,2,1,0:T(8,128)S(1)} %get-tuple-element.117.refs_0_, f32[2,4,4,128,128]{4,3,2,1,0:T(8,128)} %put.4.refs_1_), custom_call_target="tpu_custom_call", output_to_operand_aliasing={{}: (1, {})} | custom-call | flops 1000 | bytes 6291456 | tf_op jit(solution)/shard_map/put/pallas_call | solution.py:392
  54.0 0.0 collective-permute-done.21.refs_0_
  54.0 0.9 %put.6.refs_1_ = f32[2,4,4,128,128]{4,3,2,1,0:T(8,128)} custom-call(bf16[2,4,128,128]{3,2,1,0:T(8,128)(2,1)S(1)} %collective-permute-done.21.refs_0_, f32[2,4,128,128]{3,2,1,0:T(8,128)S(1)} %near.1.refs_1_, f32[2,4,4,128,128]{4,3,2,1,0:T(8,128)} %put.5.refs_2_), custom_call_target="tpu_custom_call", output_to_operand_aliasing={{}: (2, {})} | custom-call | flops 1000 | bytes 6291456 | tf_op jit(solution)/shard_map/put/pallas_call | solution.py:392
  54.9 0.0 collective-permute-done.20.refs_0_
  54.9 0.9 %put.7 = f32[2,4,4,128,128]{4,3,2,1,0:T(8,128)} custom-call(bf16[2,4,128,128]{3,2,1,0:T(8,128)(2,1)S(1)} %collective-permute-done.20.refs_0_, f32[2,4,4,128,128]{4,3,2,1,0:T(8,128)} %put.6.refs_1_), custom_call_target="tpu_custom_call", output_to_operand_aliasing={{}: (1, {})} | custom-call | flops 1000 | bytes 6291456 | tf_op jit(solution)/shard_map/put/pallas_call | solution.py:392
  (9 shorter events, 0.2 us)
Async XLA Ops:
  0.0 1.4 %copy-start = (bf16[2,48,64,128]{3,2,1,0:T(8,128)(2,1)S(1)}, bf16[2,48,64,128]{3,2,1,0:T(8,128)(2,1)}, u32[]{:S(2)}) copy-start(bf16[2,48,64,128]{3,2,1,0:T(8,128)(2,1)} %param.2) | copy-start | bytes 4718596
  1.4 7.2 %copy-start.1 = (bf16[2,48,64,128]{3,2,1,0:T(8,128)(2,1)S(1)}, bf16[2,48,64,128]{3,2,1,0:T(8,128)(2,1)}, u32[]{:S(2)}) copy-start(bf16[2,48,64,128]{3,2,1,0:T(8,128)(2,1)} %param.2) | copy-start | bytes 4718596
  1.8 6.9 %collective-permute-start = (f32[4,128]{1,0:T(4,128)S(1)}, f32[4,128]{1,0:T(4,128)S(1)}, u32[]{:S(2)}, u32[]{:S(2)}) collective-permute-start(f32[4,128]{1,0:T(4,128)S(1)} %get-tuple-element.65), channel_id=1, source_target_pairs={{0,1},{1,0},{2,3},{3,2},{4,5},{5,4},{6,7},{7,6},{8,9},{9,8},{10,11... | collective-permute-start | bytes 6152 | tf_op jit(solution)/shard_map/ppermute | solution.py:307
  3.9 5.3 %collective-permute-start.1 = (bf16[4,64,128]{2,1,0:T(8,128)(2,1)S(1)}, bf16[4,64,128]{2,1,0:T(8,128)(2,1)S(1)}, u32[]{:S(2)}, u32[]{:S(2)}) collective-permute-start(bf16[4,64,128]{2,1,0:T(8,128)(2,1)S(1)} %get-tuple-element.67), channel_id=1, source_target_pairs={{0,8},{2,10},{4,12},{6,14},{8,16},{10,18},{12,20},{14,22},{16,24},... | collective-permute-start | bytes 196616 | tf_op jit(solution)/shard_map/ppermute | solution.py:306
  5.2 7.7 %collective-permute-start.7 = (bf16[8,64,128]{2,1,0:T(8,128)(2,1)S(1)}, bf16[8,64,128]{2,1,0:T(8,128)(2,1)S(1)}, u32[]{:S(2)}, u32[]{:S(2)}) collective-permute-start(bf16[8,64,128]{2,1,0:T(8,128)(2,1)S(1)} %get-tuple-element.79), channel_id=1, source_target_pairs={{0,8},{2,10},{4,12},{6,14},{8,16},{10,18},{12,20},{14,22},{16,24},... | collective-permute-start | bytes 393224 | tf_op jit(solution)/shard_map/ppermute | solution.py:306
  6.5 9.9 %collective-permute-start.3 = (bf16[12,64,128]{2,1,0:T(8,128)(2,1)S(1)}, bf16[12,64,128]{2,1,0:T(8,128)(2,1)S(1)}, u32[]{:S(2)}, u32[]{:S(2)}) collective-permute-start(bf16[12,64,128]{2,1,0:T(8,128)(2,1)S(1)} %get-tuple-element.69), channel_id=1, source_target_pairs={{0,8},{2,10},{4,12},{6,14},{8,16},{10,18},{12,20},{14,22},{16,24},... | collective-permute-start | bytes 589832 | tf_op jit(solution)/shard_map/ppermute | solution.py:306
  9.2 25.9 %collective-permute-start.2 = (bf16[4,128,1536]{2,1,0:T(8,128)(2,1)S(1)}, bf16[4,128,1536]{2,1,0:T(8,128)(2,1)S(1)}, u32[]{:S(2)}, u32[]{:S(2)}) collective-permute-start(bf16[4,128,1536]{2,1,0:T(8,128)(2,1)S(1)} %get-tuple-element.68.own_ref), channel_id=1, source_target_pairs={{0,2},{2,0},{4,6},{6,4},{8,10},{10,8},{12,14},{14,12},{16,18},{18,... | collective-permute-start | bytes 4718600 | tf_op jit(solution)/shard_map/ppermute | solution.py:349
  11.6 3.8 %collective-permute-start.4 = (bf16[4,64,128]{2,1,0:T(8,128)(2,1)S(1)}, bf16[4,64,128]{2,1,0:T(8,128)(2,1)S(1)}, u32[]{:S(2)}, u32[]{:S(2)}) collective-permute-start(bf16[4,64,128]{2,1,0:T(8,128)(2,1)S(1)} %broadcast_select_fusion.8), channel_id=1, source_target_pairs={{0,4},{2,6},{4,0},{6,2},{8,12},{10,14},{12,8},{14,10},{16,20},{18,... | collective-permute-start | bytes 196616 | tf_op jit(solution)/shard_map/ppermute | solution.py:380
  12.9 9.1 %collective-permute-start.6 = (bf16[15,64,128]{2,1,0:T(8,128)(2,1)S(1)}, bf16[15,64,128]{2,1,0:T(8,128)(2,1)S(1)}, u32[]{:S(2)}, u32[]{:S(2)}) collective-permute-start(bf16[15,64,128]{2,1,0:T(8,128)(2,1)S(1)} %get-tuple-element.78), channel_id=1, source_target_pairs={{0,8},{2,10},{4,12},{6,14},{8,16},{10,18},{12,20},{14,22},{16,24},... | collective-permute-start | bytes 737288 | tf_op jit(solution)/shard_map/ppermute | solution.py:373
  13.0 4.7 %collective-permute-start.8 = (bf16[8,64,128]{2,1,0:T(8,128)(2,1)S(1)}, bf16[8,64,128]{2,1,0:T(8,128)(2,1)S(1)}, u32[]{:S(2)}, u32[]{:S(2)}) collective-permute-start(bf16[8,64,128]{2,1,0:T(8,128)(2,1)S(1)} %broadcast_select_fusion.7), channel_id=1, source_target_pairs={{0,4},{2,6},{4,0},{6,2},{8,12},{10,14},{12,8},{14,10},{16,20},{18,... | collective-permute-start | bytes 393224 | tf_op jit(solution)/shard_map/ppermute | solution.py:380
  16.4 6.7 %collective-permute-start.12 = (bf16[12,64,128]{2,1,0:T(8,128)(2,1)S(1)}, bf16[12,64,128]{2,1,0:T(8,128)(2,1)S(1)}, u32[]{:S(2)}, u32[]{:S(2)}) collective-permute-start(bf16[12,64,128]{2,1,0:T(8,128)(2,1)S(1)} %broadcast_select_fusion.5), channel_id=1, source_target_pairs={{0,4},{2,6},{4,0},{6,2},{8,12},{10,14},{12,8},{14,10},{16,20},{18,... | collective-permute-start | bytes 589832 | tf_op jit(solution)/shard_map/ppermute | solution.py:380
  17.7 6.8 %collective-permute-start.11 = (bf16[12,64,128]{2,1,0:T(8,128)(2,1)S(1)}, bf16[12,64,128]{2,1,0:T(8,128)(2,1)S(1)}, u32[]{:S(2)}, u32[]{:S(2)}) collective-permute-start(bf16[12,64,128]{2,1,0:T(8,128)(2,1)S(1)} %get-tuple-element.88), channel_id=1, source_target_pairs={{0,8},{2,10},{4,12},{6,14},{8,16},{10,18},{12,20},{14,22},{16,24},... | collective-permute-start | bytes 589832 | tf_op jit(solution)/shard_map/ppermute | solution.py:373
  22.0 7.4 %collective-permute-start.9 = (bf16[15,64,128]{2,1,0:T(8,128)(2,1)S(1)}, bf16[15,64,128]{2,1,0:T(8,128)(2,1)S(1)}, u32[]{:S(2)}, u32[]{:S(2)}) collective-permute-start(bf16[15,64,128]{2,1,0:T(8,128)(2,1)S(1)} %broadcast_select_fusion), channel_id=1, source_target_pairs={{0,4},{2,6},{4,0},{6,2},{8,12},{10,14},{12,8},{14,10},{16,20},{18,... | collective-permute-start | bytes 737288 | tf_op jit(solution)/shard_map/ppermute | solution.py:380
  23.1 6.3 %collective-permute-start.5 = (bf16[12,64,128]{2,1,0:T(8,128)(2,1)S(1)}, bf16[12,64,128]{2,1,0:T(8,128)(2,1)S(1)}, u32[]{:S(2)}, u32[]{:S(2)}) collective-permute-start(bf16[12,64,128]{2,1,0:T(8,128)(2,1)S(1)} %get-tuple-element.77), channel_id=1, source_target_pairs={{0,8},{2,10},{4,12},{6,14},{8,16},{10,18},{12,20},{14,22},{16,24},... | collective-permute-start | bytes 589832 | tf_op jit(solution)/shard_map/ppermute | solution.py:373
  23.1 9.9 %collective-permute-start.13 = (bf16[12,64,128]{2,1,0:T(8,128)(2,1)S(1)}, bf16[12,64,128]{2,1,0:T(8,128)(2,1)S(1)}, u32[]{:S(2)}, u32[]{:S(2)}) collective-permute-start(bf16[12,64,128]{2,1,0:T(8,128)(2,1)S(1)} %get-tuple-element.92), channel_id=1, source_target_pairs={{0,8},{2,10},{4,12},{6,14},{8,16},{10,18},{12,20},{14,22},{16,24},... | collective-permute-start | bytes 589832 | tf_op jit(solution)/shard_map/ppermute | solution.py:373
  24.5 8.4 %collective-permute-start.14 = (bf16[12,64,128]{2,1,0:T(8,128)(2,1)S(1)}, bf16[12,64,128]{2,1,0:T(8,128)(2,1)S(1)}, u32[]{:S(2)}, u32[]{:S(2)}) collective-permute-start(bf16[12,64,128]{2,1,0:T(8,128)(2,1)S(1)} %broadcast_select_fusion.4), channel_id=1, source_target_pairs={{0,4},{2,6},{4,0},{6,2},{8,12},{10,14},{12,8},{14,10},{16,20},{18,... | collective-permute-start | bytes 589832 | tf_op jit(solution)/shard_map/ppermute | solution.py:380
  29.4 8.4 %collective-permute-start.15 = (bf16[12,64,128]{2,1,0:T(8,128)(2,1)S(1)}, bf16[12,64,128]{2,1,0:T(8,128)(2,1)S(1)}, u32[]{:S(2)}, u32[]{:S(2)}) collective-permute-start(bf16[12,64,128]{2,1,0:T(8,128)(2,1)S(1)} %broadcast_select_fusion.6), channel_id=1, source_target_pairs={{0,4},{2,6},{4,0},{6,2},{8,12},{10,14},{12,8},{14,10},{16,20},{18,... | collective-permute-start | bytes 589832 | tf_op jit(solution)/shard_map/ppermute | solution.py:380
  30.0 7.8 %collective-permute-start.10 = (bf16[12,64,128]{2,1,0:T(8,128)(2,1)S(1)}, bf16[12,64,128]{2,1,0:T(8,128)(2,1)S(1)}, u32[]{:S(2)}, u32[]{:S(2)}) collective-permute-start(bf16[12,64,128]{2,1,0:T(8,128)(2,1)S(1)} %get-tuple-element.85), channel_id=1, source_target_pairs={{0,8},{2,10},{4,12},{6,14},{8,16},{10,18},{12,20},{14,22},{16,24},... | collective-permute-start | bytes 589832 | tf_op jit(solution)/shard_map/ppermute | solution.py:378
  33.0 8.7 %collective-permute-start.18 = (bf16[12,64,128]{2,1,0:T(8,128)(2,1)S(1)}, bf16[12,64,128]{2,1,0:T(8,128)(2,1)S(1)}, u32[]{:S(2)}, u32[]{:S(2)}) collective-permute-start(bf16[12,64,128]{2,1,0:T(8,128)(2,1)S(1)} %broadcast_select_fusion.2), channel_id=1, source_target_pairs={{0,4},{2,6},{4,0},{6,2},{8,12},{10,14},{12,8},{14,10},{16,20},{18,... | collective-permute-start | bytes 589832 | tf_op jit(solution)/shard_map/ppermute | solution.py:380
  34.4 7.3 %collective-permute-start.17 = (bf16[12,64,128]{2,1,0:T(8,128)(2,1)S(1)}, bf16[12,64,128]{2,1,0:T(8,128)(2,1)S(1)}, u32[]{:S(2)}, u32[]{:S(2)}) collective-permute-start(bf16[12,64,128]{2,1,0:T(8,128)(2,1)S(1)} %get-tuple-element.101), channel_id=1, source_target_pairs={{0,8},{2,10},{4,12},{6,14},{8,16},{10,18},{12,20},{14,22},{16,24},... | collective-permute-start | bytes 589832 | tf_op jit(solution)/shard_map/ppermute | solution.py:373
  37.9 13.0 %collective-permute-start.16 = (bf16[12,64,128]{2,1,0:T(8,128)(2,1)S(1)}, bf16[12,64,128]{2,1,0:T(8,128)(2,1)S(1)}, u32[]{:S(2)}, u32[]{:S(2)}) collective-permute-start(bf16[12,64,128]{2,1,0:T(8,128)(2,1)S(1)} %broadcast_select_fusion.3), channel_id=1, source_target_pairs={{0,4},{2,6},{4,0},{6,2},{8,12},{10,14},{12,8},{14,10},{16,20},{18,... | collective-permute-start | bytes 589832 | tf_op jit(solution)/shard_map/ppermute | solution.py:380
  41.7 9.2 %collective-permute-start.19 = (bf16[12,64,128]{2,1,0:T(8,128)(2,1)S(1)}, bf16[12,64,128]{2,1,0:T(8,128)(2,1)S(1)}, u32[]{:S(2)}, u32[]{:S(2)}) collective-permute-start(bf16[12,64,128]{2,1,0:T(8,128)(2,1)S(1)} %broadcast_select_fusion.1), channel_id=1, source_target_pairs={{0,4},{2,6},{4,0},{6,2},{8,12},{10,14},{12,8},{14,10},{16,20},{18,... | collective-permute-start | bytes 589832 | tf_op jit(solution)/shard_map/ppermute | solution.py:407
  45.2 8.8 %collective-permute-start.21 = (bf16[2,4,128,128]{3,2,1,0:T(8,128)(2,1)S(1)}, bf16[2,4,128,128]{3,2,1,0:T(8,128)(2,1)S(1)}, u32[]{:S(2)}, u32[]{:S(2)}) collective-permute-start(bf16[2,4,128,128]{3,2,1,0:T(8,128)(2,1)S(1)} %get-tuple-element.115), channel_id=1, source_target_pairs={{0,2},{2,0},{4,6},{6,4},{8,10},{10,8},{12,14},{14,12},{16,18},{18,... | collective-permute-start | bytes 786440 | tf_op jit(solution)/shard_map/ppermute | solution.py:411
  52.4 2.5 %collective-permute-start.20 = (bf16[2,4,128,128]{3,2,1,0:T(8,128)(2,1)S(1)}, bf16[2,4,128,128]{3,2,1,0:T(8,128)(2,1)S(1)}, u32[]{:S(2)}, u32[]{:S(2)}) collective-permute-start(bf16[2,4,128,128]{3,2,1,0:T(8,128)(2,1)S(1)} %get-tuple-element.114), channel_id=1, source_target_pairs={{0,2},{2,0},{4,6},{6,4},{8,10},{10,8},{12,14},{14,12},{16,18},{18,... | collective-permute-start | bytes 786440 | tf_op jit(solution)/shard_map/ppermute | solution.py:416

commit v11 on v10

--- a/solution.py
+++ b/solution.py
@@ -15,15 +15,16 @@
 GROUP = 16
 SIZES = (4,8,12,12,12,12,12,12,12)
 BLOCK = 24
-RAW = 3
+RAW = 4
 TERMS = 3
-Z_AFTER = (-1, -1, -1, 0, 2, 2, 3, 5, 6)
+Z_AFTER = (-1, -1, -1, -1, 2, 2, 3, 5, 6)
 Z_BEHIND = (0,0,0,0,0,0,0,1,0)
 Y_AFTER = (-1, -1, 0, 1, 2, 3, 4, 5, 6)
 LAST_TIE = 0
 PUT_TIE = 1
 CHAIN = 0
 SETS = (5, 2, 2)
+EDGE_AFTER = 0
 LEFT_AFTER = -1
 OTHER_AFTER = 0
 NEAR_BEFORE = 8
@@ -233,28 +234,29 @@
         refs[-1][...] = sums[sent][:, 1].astype(jnp.bfloat16)
 
 
-def put_kernel(kind, *refs):
-    value_ref, refs = refs[0], refs[1:]
+def put_kernel(kinds, *refs):
+    out_ref, wide, sems = refs[-3:]
     core = lax.axis_index("ch") % 2
-    if kind == "near":
-        near_ref, refs = refs[0], refs[1:]
-    out_ref, wide, sems = refs[-3:]
-    turn = {"one": 1, "two": 3, "far": 2 * core, "near": 2 - 2 * core}[kind]
+    turns = {"one": 1, "two": 3, "far": 2 * core, "near": 2 - 2 * core}
     copies = []
-    for part in range(2):
-        for band in range(out_ref.shape[2]):
-            if kind in ("one", "two"):
-                source = value_ref.at[part, 0, band]
-            else:
-                value = value_ref[part, band].astype(jnp.float32)
-                if kind == "near":
-                    value = jnp.where(core == 0, value, near_ref[part, band])
-                wide[part, band] = value
-                source = wide.at[part, band]
-            copies.append(
-                pltpu.make_async_copy(source, out_ref.at[part, turn, band], sems.at[part, band])
-            )
-            copies[-1].start()
+    for kind in kinds:
+        value_ref, refs = refs[0], refs[1:]
+        if kind == "near":
+            near_ref, refs = refs[0], refs[1:]
+        for part in range(2):
+            for band in range(out_ref.shape[2]):
+                if kind in ("one", "two"):
+                    source = value_ref.at[part, 0, band]
+                else:
+                    value = value_ref[part, band].astype(jnp.float32)
+                    if kind == "near":
+                        value = jnp.where(core == 0, value, near_ref[part, band])
+                    wide[part, band] = value
+                    source = wide.at[part, band]
+                turn = turns[kind]
+                sem = sems.at[kinds.index(kind), part, band]
+                copies.append(pltpu.make_async_copy(source, out_ref.at[part, turn, band], sem))
+                copies[-1].start()
     for copy in copies:
         copy.wait()
 
@@ -304,6 +306,8 @@
     power, norms = after(power, norms)
 
     twos = {k: lax.ppermute(early[k], "ch", ahead) for k in range(RAW)}
+    if EDGE_AFTER >= 0:
+        twos[EDGE_AFTER], edge = after(twos[EDGE_AFTER], edge)
     halo = lax.ppermute(edge, "fq", [(0, 1), (1, 0)])
     if LEFT_AFTER >= 0:
         twos[LEFT_AFTER], halo = after(twos[LEFT_AFTER], halo)
@@ -386,11 +390,11 @@
     if LAST_TIE:
         ones[final - 1], twos[middle] = after(ones[final - 1], twos[middle])
 
-    def put(kind, out, *values):
+    def put(kinds, out, *values):
         aliased = out is not None
         operands = [*values, out] if aliased else list(values)
         return call(
-            functools.partial(put_kernel, kind),
+            functools.partial(put_kernel, kinds),
             "put",
             out_shape,
             [vmem()] * len(values) + [hbm()] * aliased,
@@ -400,7 +404,7 @@
             input_output_aliases={len(values): 0} if aliased else {},
             scratch_shapes=[
                 pltpu.VMEM(near_shape.shape, jnp.float32),
-                pltpu.SemaphoreType.DMA((2, band_width)),
+                pltpu.SemaphoreType.DMA((len(kinds), 2, band_width)),
             ],
         )(*operands)
 
@@ -409,14 +413,13 @@
         (((0,), sets[1]), ((1,), sets[1] + sets[2])), (one_sum, two_sum), 1
     )
     two_got = lax.ppermute(two_sent, "ch", mate)
-    out = put("two", None, two_sum)
+    out = put(("two",), None, two_sum)
     if PUT_TIE:
         one_sum, out = after(one_sum, out)
     one_sum, one_sent = cross((((0,), sets[2]),), (one_sum,), 0)
     one_got = lax.ppermute(one_sent, "ch", mate)
-    out = put("one", out, one_sum)
-    out = put("near", out, two_got, near)
-    return put("far", out, one_got)
+    out = put(("one", "near"), out, one_sum, two_got, near)
+    return put(("far",), out, one_got)
 
 
 def solution(mesh):

time: 55.9 us -> 58.3 us (1.043)
  waiting for transfers between devices: 13.6 us -> 16.7 us
  Pallas kernels: 14.1 us -> 13.4 us
    ppermute x8, waiting for transfers between devices: 1.96 us -> 3.95 us  [shards(): ones[k] = lax.ppermute(onward[k], 'ch', beside)]
    ppermute x1, waiting for transfers between devices: 0.01 us -> 1.44 us  [shards(): halo = lax.ppermute(edge, 'fq', [(0, 1), (1, 0)])]
    ppermute x8, starting transfers between devices: 9.2 us -> 8.04 us  [shards(): ones[k] = lax.ppermute(onward[k], 'ch', beside)]
    ppermute x3 -> x4, starting transfers between devices: 3.89 us -> 4.84 us  [shards(): twos = {k: lax.ppermute(early[k], 'ch', ahead) for k in range(RAW)}]
    ppermute x1, starting transfers between devices: 2.11 us -> 1.21 us  [shards(): halo = lax.ppermute(edge, 'fq', [(0, 1), (1, 0)])]
    ppermute x3 -> x4, waiting for transfers between devices: 0.95 us -> 0.25 us  [shards(): twos = {k: lax.ppermute(early[k], 'ch', ahead) for k in range(RAW)}]
    pallas_call x4 -> x3, Pallas kernels: 3.43 us -> 2.79 us  [put(): call(functools.partial(put_kernel, kinds), 'put', out_shape, [vmem()] * l...]
    ppermute x6 -> x5, waiting for transfers between devices: 10.7 us -> 10.9 us  [shards(): twos[later] = lax.ppermute(mine[later], 'ch', ahead)]
  transfers between devices with their start and end apart: 22 -> 22, of which waited for: 8 -> 10; matrix products, arithmetic and copies ran while one was open for 2% -> 2% of each run, Pallas kernels for 23% -> 21%
where the time goes in v11:
time: 58.3 us; the launch traced here: 57.9 us
  starting transfers between devices  25.2 us (43%)
  waiting for transfers between devices  16.7 us (29%)
  Pallas kernels  13.4 us (23%)
  local copies, waits for them, and re-layouts  1.41 us (2%)
  other arithmetic  1.04 us (2%)
    ppermute x5, waiting for transfers between devices, shards(): twos[later] = lax.ppermute(mine[later], 'ch', ahead)  10.9 us
    ppermute x8, starting transfers between devices, shards(): ones[k] = lax.ppermute(onward[k], 'ch', beside)  8.04 us
    pallas_call x3, Pallas kernels, cross(): call(functools.partial(cross_kernel, jobs, not befores, sent), 'cross', (...  7.47 us
    ppermute x1, starting transfers between devices, shards(): two_got = lax.ppermute(two_sent, 'ch', mate)  5.3 us
    ppermute x4, starting transfers between devices, shards(): twos = {k: lax.ppermute(early[k], 'ch', ahead) for k in range(RAW)}  4.84 us
    ppermute x8, waiting for transfers between devices, shards(): ones[k] = lax.ppermute(onward[k], 'ch', beside)  3.95 us
    ppermute x1, starting transfers between devices, shards(): other = lax.ppermute(left, 'ch', mate)  2.88 us
    pallas_call x3, Pallas kernels, put(): call(functools.partial(put_kernel, kinds), 'put', out_shape, [vmem()] * l...  2.79 us
  transfers between devices with their start and end apart: 22, of which 10 were waited for; matrix products, arithmetic and copies ran while one was open for 2% of the time, Pallas kernels for 21%

profile of v11, /device:TPU:1, one launch (start us, length us, event | category | flops | bytes accessed | tf_op | source)
XLA Modules:
  0.0 57.9 jit_solution(16546124507490011738)
XLA Ops:
  0.0 0.0 copy-start
  0.0 1.4 %copy-done = bf16[2,48,64,128]{3,2,1,0:T(8,128)(2,1)S(1)} copy-done((bf16[2,48,64,128]{3,2,1,0:T(8,128)(2,1)S(1)}, bf16[2,48,64,128]{3,2,1,0:T(8,128)(2,1)}, u32[]{:S(2)}) %copy-start) | copy-done | bytes 1572888
  1.4 0.0 copy-start.1
  1.4 0.4 power.1
  1.8 2.2 %collective-permute-start = (bf16[4,64,128]{2,1,0:T(8,128)(2,1)S(1)}, bf16[4,64,128]{2,1,0:T(8,128)(2,1)S(1)}, u32[]{:S(2)}, u32[]{:S(2)}) collective-permute-start(bf16[4,64,128]{2,1,0:T(8,128)(2,1)S(1)} %get-tuple-element.65), channel_id=1, source_target_pairs={{0,8},{2,10},{4,12},{6,14},{8,16},{10,18},{12,20},{14,22},{16,24},... | collective-permute-start | bytes 196616 | tf_op jit(solution)/shard_map/ppermute | solution.py:308
  4.0 1.3 %collective-permute-start.7 = (bf16[8,64,128]{2,1,0:T(8,128)(2,1)S(1)}, bf16[8,64,128]{2,1,0:T(8,128)(2,1)S(1)}, u32[]{:S(2)}, u32[]{:S(2)}) collective-permute-start(bf16[8,64,128]{2,1,0:T(8,128)(2,1)S(1)} %get-tuple-element.79), channel_id=1, source_target_pairs={{0,8},{2,10},{4,12},{6,14},{8,16},{10,18},{12,20},{14,22},{16,24},... | collective-permute-start | bytes 393224 | tf_op jit(solution)/shard_map/ppermute | solution.py:308
  5.3 1.3 %collective-permute-start.3 = (bf16[12,64,128]{2,1,0:T(8,128)(2,1)S(1)}, bf16[12,64,128]{2,1,0:T(8,128)(2,1)S(1)}, u32[]{:S(2)}, u32[]{:S(2)}) collective-permute-start(bf16[12,64,128]{2,1,0:T(8,128)(2,1)S(1)} %get-tuple-element.71), channel_id=1, source_target_pairs={{0,8},{2,10},{4,12},{6,14},{8,16},{10,18},{12,20},{14,22},{16,24},... | collective-permute-start | bytes 589832 | tf_op jit(solution)/shard_map/ppermute | solution.py:308
  6.6 0.1 collective-permute-start.6
  6.6 0.7 %broadcast_subtract_fusion = s32[64]{0:T(128)S(1)} fusion(s32[64]{0:T(128)} %param.3, s32[]{:T(128)S(6)} %mul.6), kind=kLoop, calls=%fused_computation.12 | loop fusion | flops 64 | bytes 516 | tf_op jit(solution)/shard_map/sub | solution.py:302
  7.3 0.1 convert_reduce_fusion.bounds_ref
  7.4 0.2 collective-permute-done.refs_5_
  7.7 1.2 %collective-permute-start.1 = (f32[4,128]{1,0:T(4,128)S(1)}, f32[4,128]{1,0:T(4,128)S(1)}, u32[]{:S(2)}, u32[]{:S(2)}) collective-permute-start(f32[4,128]{1,0:T(4,128)S(1)} %get-tuple-element.67), channel_id=1, source_target_pairs={{0,1},{1,0},{2,3},{3,2},{4,5},{5,4},{6,7},{7,6},{8,9},{9,8},{10,11... | collective-permute-start | bytes 6152 | tf_op jit(solution)/shard_map/ppermute | solution.py:311
  8.9 0.1 multiply_rsqrt_fusion.norm_ref
  8.9 1.4 %collective-permute-done.1.halo_ref = f32[4,128]{1,0:T(4,128)S(1)} collective-permute-done((f32[4,128]{1,0:T(4,128)S(1)}, f32[4,128]{1,0:T(4,128)S(1)}, u32[]{:S(2)}, u32[]{:S(2)}) %collective-permute-start.1) | collective-permute-done | bytes 2080 | tf_op jit(solution)/shard_map/ppermute | solution.py:311
  10.4 0.0 copy-done.1
  10.4 0.5 left.1
  10.9 2.9 %collective-permute-start.2 = (bf16[4,128,1536]{2,1,0:T(8,128)(2,1)S(1)}, bf16[4,128,1536]{2,1,0:T(8,128)(2,1)S(1)}, u32[]{:S(2)}, u32[]{:S(2)}) collective-permute-start(bf16[4,128,1536]{2,1,0:T(8,128)(2,1)S(1)} %get-tuple-element.70.own_ref), channel_id=1, source_target_pairs={{0,2},{2,0},{4,6},{6,4},{8,10},{10,8},{12,14},{14,12},{16,18},{18,... | collective-permute-start | bytes 4718600 | tf_op jit(solution)/shard_map/ppermute | solution.py:353
  13.8 1.6 %collective-permute-start.4 = (bf16[4,64,128]{2,1,0:T(8,128)(2,1)S(1)}, bf16[4,64,128]{2,1,0:T(8,128)(2,1)S(1)}, u32[]{:S(2)}, u32[]{:S(2)}) collective-permute-start(bf16[4,64,128]{2,1,0:T(8,128)(2,1)S(1)} %broadcast_select_fusion.8), channel_id=1, source_target_pairs={{0,4},{2,6},{4,0},{6,2},{8,12},{10,14},{12,8},{14,10},{16,20},{18,... | collective-permute-start | bytes 196616 | tf_op jit(solution)/shard_map/ppermute | solution.py:384
  15.5 0.0 collective-permute-done.7.refs_6_
  15.5 0.1 collective-permute-start.8
  15.6 2.3 %collective-permute-done.4.refs_0_ = bf16[4,64,128]{2,1,0:T(8,128)(2,1)S(1)} collective-permute-done((bf16[4,64,128]{2,1,0:T(8,128)(2,1)S(1)}, bf16[4,64,128]{2,1,0:T(8,128)(2,1)S(1)}, u32[]{:S(2)}, u32[]{:S(2)}) %collective-permute-start.4) | collective-permute-done | bytes 65568 | tf_op jit(solution)/shard_map/ppermute | solution.py:384
  17.8 0.0 collective-permute-done.3.refs_7_
  17.8 0.6 collective-permute-start.11
  18.4 1.3 %collective-permute-start.12 = (bf16[12,64,128]{2,1,0:T(8,128)(2,1)S(1)}, bf16[12,64,128]{2,1,0:T(8,128)(2,1)S(1)}, u32[]{:S(2)}, u32[]{:S(2)}) collective-permute-start(bf16[12,64,128]{2,1,0:T(8,128)(2,1)S(1)} %broadcast_select_fusion.4), channel_id=1, source_target_pairs={{0,4},{2,6},{4,0},{6,2},{8,12},{10,14},{12,8},{14,10},{16,20},{18,... | collective-permute-start | bytes 589832 | tf_op jit(solution)/shard_map/ppermute | solution.py:384
  19.7 0.0 collective-permute-done.6.refs_8_
  19.8 1.3 %collective-permute-start.5 = (bf16[12,64,128]{2,1,0:T(8,128)(2,1)S(1)}, bf16[12,64,128]{2,1,0:T(8,128)(2,1)S(1)}, u32[]{:S(2)}, u32[]{:S(2)}) collective-permute-start(bf16[12,64,128]{2,1,0:T(8,128)(2,1)S(1)} %get-tuple-element.77), channel_id=1, source_target_pairs={{0,8},{2,10},{4,12},{6,14},{8,16},{10,18},{12,20},{14,22},{16,24},... | collective-permute-start | bytes 589832 | tf_op jit(solution)/shard_map/ppermute | solution.py:377
  21.1 0.0 collective-permute-done.8.refs_1_
  21.1 1.0 %collective-permute-start.9 = (bf16[12,64,128]{2,1,0:T(8,128)(2,1)S(1)}, bf16[12,64,128]{2,1,0:T(8,128)(2,1)S(1)}, u32[]{:S(2)}, u32[]{:S(2)}) collective-permute-start(bf16[12,64,128]{2,1,0:T(8,128)(2,1)S(1)} %broadcast_select_fusion.6), channel_id=1, source_target_pairs={{0,4},{2,6},{4,0},{6,2},{8,12},{10,14},{12,8},{14,10},{16,20},{18,... | collective-permute-start | bytes 589832 | tf_op jit(solution)/shard_map/ppermute | solution.py:384
  22.1 1.7 %collective-permute-done.12.refs_2_ = bf16[12,64,128]{2,1,0:T(8,128)(2,1)S(1)} collective-permute-done((bf16[12,64,128]{2,1,0:T(8,128)(2,1)S(1)}, bf16[12,64,128]{2,1,0:T(8,128)(2,1)S(1)}, u32[]{:S(2)}, u32[]{:S(2)}) %collective-permute-start.12) | collective-permute-done | bytes 196640 | tf_op jit(solution)/shard_map/ppermute | solution.py:384
  23.7 2.7 %collective-permute-done.11.refs_9_ = bf16[15,64,128]{2,1,0:T(8,128)(2,1)S(1)} collective-permute-done((bf16[15,64,128]{2,1,0:T(8,128)(2,1)S(1)}, bf16[15,64,128]{2,1,0:T(8,128)(2,1)S(1)}, u32[]{:S(2)}, u32[]{:S(2)}) %collective-permute-start.11) | collective-permute-done | bytes 245792 | tf_op jit(solution)/shard_map/ppermute | solution.py:377
  26.5 0.8 %collective-permute-start.14 = (bf16[15,64,128]{2,1,0:T(8,128)(2,1)S(1)}, bf16[15,64,128]{2,1,0:T(8,128)(2,1)S(1)}, u32[]{:S(2)}, u32[]{:S(2)}) collective-permute-start(bf16[15,64,128]{2,1,0:T(8,128)(2,1)S(1)} %broadcast_select_fusion), channel_id=1, source_target_pairs={{0,4},{2,6},{4,0},{6,2},{8,12},{10,14},{12,8},{14,10},{16,20},{18,... | collective-permute-start | bytes 737288 | tf_op jit(solution)/shard_map/ppermute | solution.py:384
  27.3 0.0 collective-permute-start.13
  27.3 3.4 %collective-permute-done.5.refs_2_ = bf16[12,64,128]{2,1,0:T(8,128)(2,1)S(1)} collective-permute-done((bf16[12,64,128]{2,1,0:T(8,128)(2,1)S(1)}, bf16[12,64,128]{2,1,0:T(8,128)(2,1)S(1)}, u32[]{:S(2)}, u32[]{:S(2)}) %collective-permute-start.5) | collective-permute-done | bytes 196640 | tf_op jit(solution)/shard_map/ppermute | solution.py:377
  30.7 0.0 collective-permute-done.9.refs_3_
  30.7 0.8 %collective-permute-start.15 = (bf16[12,64,128]{2,1,0:T(8,128)(2,1)S(1)}, bf16[12,64,128]{2,1,0:T(8,128)(2,1)S(1)}, u32[]{:S(2)}, u32[]{:S(2)}) collective-permute-start(bf16[12,64,128]{2,1,0:T(8,128)(2,1)S(1)} %broadcast_select_fusion.5), channel_id=1, source_target_pairs={{0,4},{2,6},{4,0},{6,2},{8,12},{10,14},{12,8},{14,10},{16,20},{18,... | collective-permute-start | bytes 589832 | tf_op jit(solution)/shard_map/ppermute | solution.py:384
  31.5 0.0 collective-permute-start.10
  31.5 2.1 %collective-permute-done.13.refs_3_ = bf16[12,64,128]{2,1,0:T(8,128)(2,1)S(1)} collective-permute-done((bf16[12,64,128]{2,1,0:T(8,128)(2,1)S(1)}, bf16[12,64,128]{2,1,0:T(8,128)(2,1)S(1)}, u32[]{:S(2)}, u32[]{:S(2)}) %collective-permute-start.13) | collective-permute-done | bytes 196640 | tf_op jit(solution)/shard_map/ppermute | solution.py:377
  33.6 0.0 collective-permute-done.14.refs_4_
  33.7 1.4 %collective-permute-start.18 = (bf16[12,64,128]{2,1,0:T(8,128)(2,1)S(1)}, bf16[12,64,128]{2,1,0:T(8,128)(2,1)S(1)}, u32[]{:S(2)}, u32[]{:S(2)}) collective-permute-start(bf16[12,64,128]{2,1,0:T(8,128)(2,1)S(1)} %broadcast_select_fusion.2), channel_id=1, source_target_pairs={{0,4},{2,6},{4,0},{6,2},{8,12},{10,14},{12,8},{14,10},{16,20},{18,... | collective-permute-start | bytes 589832 | tf_op jit(solution)/shard_map/ppermute | solution.py:384
  35.1 0.5 collective-permute-start.17
  35.5 0.0 collective-permute-done.2.mate_ref
  35.5 2.6 %cross.3 = (f32[2,2,4,128,128]{4,3,2,1,0:T(8,128)S(1)}, f32[2,2,4,128,128]{4,3,2,1,0:T(8,128)S(1)}) custom-call(s32[5]{0:T(128)S(1)} %convert_reduce_fusion.bounds_ref, f32[4]{0:T(128)S(1)} %multiply_rsqrt_fusion.norm_ref, bf16[4,128,1536]{2,1,0:T(8,128)(2,1)S(1)} %get-tuple-element.70.own_ref, bf16[4,128,1536]{2,1,0:T(8,128)(2,1)S(1)} %collective-permute-done.2.mate_ref, ...), custom_call_target="tpu_custom_call" | custom-call | flops 805306368 | tf_op jit(solution)/shard_map/cross/pallas_call | solution.py:342
  38.1 1.8 %collective-permute-done.10.refs_4_ = bf16[12,64,128]{2,1,0:T(8,128)(2,1)S(1)} collective-permute-done((bf16[12,64,128]{2,1,0:T(8,128)(2,1)S(1)}, bf16[12,64,128]{2,1,0:T(8,128)(2,1)S(1)}, u32[]{:S(2)}, u32[]{:S(2)}) %collective-permute-start.10) | collective-permute-done | bytes 196640 | tf_op jit(solution)/shard_map/ppermute | solution.py:382
  40.0 0.0 collective-permute-done.15.refs_0_
  40.0 1.0 %collective-permute-start.16 = (bf16[12,64,128]{2,1,0:T(8,128)(2,1)S(1)}, bf16[12,64,128]{2,1,0:T(8,128)(2,1)S(1)}, u32[]{:S(2)}, u32[]{:S(2)}) collective-permute-start(bf16[12,64,128]{2,1,0:T(8,128)(2,1)S(1)} %broadcast_select_fusion.3), channel_id=1, source_target_pairs={{0,4},{2,6},{4,0},{6,2},{8,12},{10,14},{12,8},{14,10},{16,20},{18,... | collective-permute-start | bytes 589832 | tf_op jit(solution)/shard_map/ppermute | solution.py:384
  41.0 2.3 %near.1.refs_2_ = f32[2,4,128,128]{3,2,1,0:T(8,128)S(1)} custom-call(s32[5]{0:T(128)S(1)} %convert_reduce_fusion.bounds_ref, f32[4]{0:T(128)S(1)} %multiply_rsqrt_fusion.norm_ref, bf16[4,128,1536]{2,1,0:T(8,128)(2,1)S(1)} %get-tuple-element.70.own_ref, bf16[4,128,1536]{2,1,0:T(8,128)(2,1)S(1)} %collective-permute-done.2.mate_ref), custom_call_target="tpu_custom_call" | custom-call | flops 1000 | bytes 1000 | tf_op jit(solution)/shard_map/near/pallas_call | solution.py:354
  43.3 0.9 %collective-permute-done.17.refs_5_ = bf16[12,64,128]{2,1,0:T(8,128)(2,1)S(1)} collective-permute-done((bf16[12,64,128]{2,1,0:T(8,128)(2,1)S(1)}, bf16[12,64,128]{2,1,0:T(8,128)(2,1)S(1)}, u32[]{:S(2)}, u32[]{:S(2)}) %collective-permute-start.17) | collective-permute-done | bytes 196640 | tf_op jit(solution)/shard_map/ppermute | solution.py:377
  44.2 0.0 collective-permute-done.18.refs_1_
  44.2 0.2 collective-permute-start.19
  44.4 3.4 %cross.4 = (f32[2,2,4,128,128]{4,3,2,1,0:T(8,128)S(1)}, f32[2,2,4,128,128]{4,3,2,1,0:T(8,128)S(1)}, bf16[2,4,128,128]{3,2,1,0:T(8,128)(2,1)S(1)}) custom-call(s32[5]{0:T(128)S(1)} %convert_reduce_fusion.bounds_ref, f32[4]{0:T(128)S(1)} %multiply_rsqrt_fusion.norm_ref, bf16[4,128,1536]{2,1,0:T(8,128)(2,1)S(1)} %get-tuple-element.70.own_ref, ...), custom_call_target="tpu_custom_call" | custom-call | flops 603979776 | tf_op jit(solution)/shard_map/cross/pallas_call | solution.py:342
  47.8 5.3 %collective-permute-start.21 = (bf16[2,4,128,128]{3,2,1,0:T(8,128)(2,1)S(1)}, bf16[2,4,128,128]{3,2,1,0:T(8,128)(2,1)S(1)}, u32[]{:S(2)}, u32[]{:S(2)}) collective-permute-start(bf16[2,4,128,128]{3,2,1,0:T(8,128)(2,1)S(1)} %get-tuple-element.116), channel_id=1, source_target_pairs={{0,2},{2,0},{4,6},{6,4},{8,10},{10,8},{12,14},{14,12},{16,18},{18,... | collective-permute-start | bytes 786440 | tf_op jit(solution)/shard_map/ppermute | solution.py:415
  53.1 0.8 %put.3.refs_3_ = f32[2,4,4,128,128]{4,3,2,1,0:T(8,128)} custom-call(f32[2,2,4,128,128]{4,3,2,1,0:T(8,128)S(1)} %get-tuple-element.112.refs_0_), custom_call_target="tpu_custom_call" | custom-call | flops 1000 | bytes 6291456 | tf_op jit(solution)/shard_map/put/pallas_call | solution.py:396
  54.0 0.0 collective-permute-done.16.refs_0_
  54.0 0.0 collective-permute-done.19.refs_1_
  54.0 1.5 %cross.5 = (f32[2,2,4,128,128]{4,3,2,1,0:T(8,128)S(1)}, bf16[2,4,128,128]{3,2,1,0:T(8,128)(2,1)S(1)}) custom-call(s32[5]{0:T(128)S(1)} %convert_reduce_fusion.bounds_ref, f32[4]{0:T(128)S(1)} %multiply_rsqrt_fusion.norm_ref, bf16[4,128,1536]{2,1,0:T(8,128)(2,1)S(1)} %get-tuple-element.70.own_ref, bf16[4,128,1536]{2,1,0:T(8,128)(2,1)S(1)} %collective-permute-done.2.mate_ref, ...), custom_call_target="tpu_custom_call" | custom-call | flops 201326592 | tf_op jit(solution)/shard_map/cross/pallas_call | solution.py:342
  55.5 0.4 collective-permute-start.20
  55.9 0.0 collective-permute-done.21.refs_1_
  55.9 1.1 %put.4.refs_1_ = f32[2,4,4,128,128]{4,3,2,1,0:T(8,128)} custom-call(f32[2,2,4,128,128]{4,3,2,1,0:T(8,128)S(1)} %get-tuple-element.115.refs_0_, bf16[2,4,128,128]{3,2,1,0:T(8,128)(2,1)S(1)} %collective-permute-done.21.refs_1_, f32[2,4,128,128]{3,2,1,0:T(8,128)S(1)} %near.1.refs_2_, f32[2,4,4,128,128]{4,3,2,1,0:T(8,128)} %put.3.refs_3_), custom_call_target="tpu_custom_call", output_to_operand_aliasing={{}: (3, {})} | custom-call | flops 1000 | bytes 6291456 | tf_op jit(solution)/shard_map/put/pallas_call | solution.py:396
  57.0 0.1 collective-permute-done.20.refs_0_
  57.1 0.9 %put.5 = f32[2,4,4,128,128]{4,3,2,1,0:T(8,128)} custom-call(bf16[2,4,128,128]{3,2,1,0:T(8,128)(2,1)S(1)} %collective-permute-done.20.refs_0_, f32[2,4,4,128,128]{4,3,2,1,0:T(8,128)} %put.4.refs_1_), custom_call_target="tpu_custom_call", output_to_operand_aliasing={{}: (1, {})} | custom-call | flops 1000 | bytes 6291456 | tf_op jit(solution)/shard_map/put/pallas_call | solution.py:396
  (9 shorter events, 0.2 us)
Async XLA Ops:
  0.0 1.4 %copy-start = (bf16[2,48,64,128]{3,2,1,0:T(8,128)(2,1)S(1)}, bf16[2,48,64,128]{3,2,1,0:T(8,128)(2,1)}, u32[]{:S(2)}) copy-start(bf16[2,48,64,128]{3,2,1,0:T(8,128)(2,1)} %param.2) | copy-start | bytes 4718596
  1.4 9.0 %copy-start.1 = (bf16[2,48,64,128]{3,2,1,0:T(8,128)(2,1)S(1)}, bf16[2,48,64,128]{3,2,1,0:T(8,128)(2,1)}, u32[]{:S(2)}) copy-start(bf16[2,48,64,128]{3,2,1,0:T(8,128)(2,1)} %param.2) | copy-start | bytes 4718596
  1.8 5.9 %collective-permute-start = (bf16[4,64,128]{2,1,0:T(8,128)(2,1)S(1)}, bf16[4,64,128]{2,1,0:T(8,128)(2,1)S(1)}, u32[]{:S(2)}, u32[]{:S(2)}) collective-permute-start(bf16[4,64,128]{2,1,0:T(8,128)(2,1)S(1)} %get-tuple-element.65), channel_id=1, source_target_pairs={{0,8},{2,10},{4,12},{6,14},{8,16},{10,18},{12,20},{14,22},{16,24},... | collective-permute-start | bytes 196616 | tf_op jit(solution)/shard_map/ppermute | solution.py:308
  4.0 11.5 %collective-permute-start.7 = (bf16[8,64,128]{2,1,0:T(8,128)(2,1)S(1)}, bf16[8,64,128]{2,1,0:T(8,128)(2,1)S(1)}, u32[]{:S(2)}, u32[]{:S(2)}) collective-permute-start(bf16[8,64,128]{2,1,0:T(8,128)(2,1)S(1)} %get-tuple-element.79), channel_id=1, source_target_pairs={{0,8},{2,10},{4,12},{6,14},{8,16},{10,18},{12,20},{14,22},{16,24},... | collective-permute-start | bytes 393224 | tf_op jit(solution)/shard_map/ppermute | solution.py:308
  5.3 12.6 %collective-permute-start.3 = (bf16[12,64,128]{2,1,0:T(8,128)(2,1)S(1)}, bf16[12,64,128]{2,1,0:T(8,128)(2,1)S(1)}, u32[]{:S(2)}, u32[]{:S(2)}) collective-permute-start(bf16[12,64,128]{2,1,0:T(8,128)(2,1)S(1)} %get-tuple-element.71), channel_id=1, source_target_pairs={{0,8},{2,10},{4,12},{6,14},{8,16},{10,18},{12,20},{14,22},{16,24},... | collective-permute-start | bytes 589832 | tf_op jit(solution)/shard_map/ppermute | solution.py:308
  6.6 13.2 %collective-permute-start.6 = (bf16[12,64,128]{2,1,0:T(8,128)(2,1)S(1)}, bf16[12,64,128]{2,1,0:T(8,128)(2,1)S(1)}, u32[]{:S(2)}, u32[]{:S(2)}) collective-permute-start(bf16[12,64,128]{2,1,0:T(8,128)(2,1)S(1)} %get-tuple-element.78), channel_id=1, source_target_pairs={{0,8},{2,10},{4,12},{6,14},{8,16},{10,18},{12,20},{14,22},{16,24},... | collective-permute-start | bytes 589832 | tf_op jit(solution)/shard_map/ppermute | solution.py:308
  7.7 2.7 %collective-permute-start.1 = (f32[4,128]{1,0:T(4,128)S(1)}, f32[4,128]{1,0:T(4,128)S(1)}, u32[]{:S(2)}, u32[]{:S(2)}) collective-permute-start(f32[4,128]{1,0:T(4,128)S(1)} %get-tuple-element.67), channel_id=1, source_target_pairs={{0,1},{1,0},{2,3},{3,2},{4,5},{5,4},{6,7},{7,6},{8,9},{9,8},{10,11... | collective-permute-start | bytes 6152 | tf_op jit(solution)/shard_map/ppermute | solution.py:311
  10.9 24.6 %collective-permute-start.2 = (bf16[4,128,1536]{2,1,0:T(8,128)(2,1)S(1)}, bf16[4,128,1536]{2,1,0:T(8,128)(2,1)S(1)}, u32[]{:S(2)}, u32[]{:S(2)}) collective-permute-start(bf16[4,128,1536]{2,1,0:T(8,128)(2,1)S(1)} %get-tuple-element.70.own_ref), channel_id=1, source_target_pairs={{0,2},{2,0},{4,6},{6,4},{8,10},{10,8},{12,14},{14,12},{16,18},{18,... | collective-permute-start | bytes 4718600 | tf_op jit(solution)/shard_map/ppermute | solution.py:353
  13.8 4.0 %collective-permute-start.4 = (bf16[4,64,128]{2,1,0:T(8,128)(2,1)S(1)}, bf16[4,64,128]{2,1,0:T(8,128)(2,1)S(1)}, u32[]{:S(2)}, u32[]{:S(2)}) collective-permute-start(bf16[4,64,128]{2,1,0:T(8,128)(2,1)S(1)} %broadcast_select_fusion.8), channel_id=1, source_target_pairs={{0,4},{2,6},{4,0},{6,2},{8,12},{10,14},{12,8},{14,10},{16,20},{18,... | collective-permute-start | bytes 196616 | tf_op jit(solution)/shard_map/ppermute | solution.py:384
  15.5 5.6 %collective-permute-start.8 = (bf16[8,64,128]{2,1,0:T(8,128)(2,1)S(1)}, bf16[8,64,128]{2,1,0:T(8,128)(2,1)S(1)}, u32[]{:S(2)}, u32[]{:S(2)}) collective-permute-start(bf16[8,64,128]{2,1,0:T(8,128)(2,1)S(1)} %broadcast_select_fusion.7), channel_id=1, source_target_pairs={{0,4},{2,6},{4,0},{6,2},{8,12},{10,14},{12,8},{14,10},{16,20},{18,... | collective-permute-start | bytes 393224 | tf_op jit(solution)/shard_map/ppermute | solution.py:384
  17.8 8.6 %collective-permute-start.11 = (bf16[15,64,128]{2,1,0:T(8,128)(2,1)S(1)}, bf16[15,64,128]{2,1,0:T(8,128)(2,1)S(1)}, u32[]{:S(2)}, u32[]{:S(2)}) collective-permute-start(bf16[15,64,128]{2,1,0:T(8,128)(2,1)S(1)} %get-tuple-element.88), channel_id=1, source_target_pairs={{0,8},{2,10},{4,12},{6,14},{8,16},{10,18},{12,20},{14,22},{16,24},... | collective-permute-start | bytes 737288 | tf_op jit(solution)/shard_map/ppermute | solution.py:377
  18.4 5.3 %collective-permute-start.12 = (bf16[12,64,128]{2,1,0:T(8,128)(2,1)S(1)}, bf16[12,64,128]{2,1,0:T(8,128)(2,1)S(1)}, u32[]{:S(2)}, u32[]{:S(2)}) collective-permute-start(bf16[12,64,128]{2,1,0:T(8,128)(2,1)S(1)} %broadcast_select_fusion.4), channel_id=1, source_target_pairs={{0,4},{2,6},{4,0},{6,2},{8,12},{10,14},{12,8},{14,10},{16,20},{18,... | collective-permute-start | bytes 589832 | tf_op jit(solution)/shard_map/ppermute | solution.py:384
  19.8 10.9 %collective-permute-start.5 = (bf16[12,64,128]{2,1,0:T(8,128)(2,1)S(1)}, bf16[12,64,128]{2,1,0:T(8,128)(2,1)S(1)}, u32[]{:S(2)}, u32[]{:S(2)}) collective-permute-start(bf16[12,64,128]{2,1,0:T(8,128)(2,1)S(1)} %get-tuple-element.77), channel_id=1, source_target_pairs={{0,8},{2,10},{4,12},{6,14},{8,16},{10,18},{12,20},{14,22},{16,24},... | collective-permute-start | bytes 589832 | tf_op jit(solution)/shard_map/ppermute | solution.py:377
  21.1 9.6 %collective-permute-start.9 = (bf16[12,64,128]{2,1,0:T(8,128)(2,1)S(1)}, bf16[12,64,128]{2,1,0:T(8,128)(2,1)S(1)}, u32[]{:S(2)}, u32[]{:S(2)}) collective-permute-start(bf16[12,64,128]{2,1,0:T(8,128)(2,1)S(1)} %broadcast_select_fusion.6), channel_id=1, source_target_pairs={{0,4},{2,6},{4,0},{6,2},{8,12},{10,14},{12,8},{14,10},{16,20},{18,... | collective-permute-start | bytes 589832 | tf_op jit(solution)/shard_map/ppermute | solution.py:384
  26.5 7.1 %collective-permute-start.14 = (bf16[15,64,128]{2,1,0:T(8,128)(2,1)S(1)}, bf16[15,64,128]{2,1,0:T(8,128)(2,1)S(1)}, u32[]{:S(2)}, u32[]{:S(2)}) collective-permute-start(bf16[15,64,128]{2,1,0:T(8,128)(2,1)S(1)} %broadcast_select_fusion), channel_id=1, source_target_pairs={{0,4},{2,6},{4,0},{6,2},{8,12},{10,14},{12,8},{14,10},{16,20},{18,... | collective-permute-start | bytes 737288 | tf_op jit(solution)/shard_map/ppermute | solution.py:384
  27.3 6.3 %collective-permute-start.13 = (bf16[12,64,128]{2,1,0:T(8,128)(2,1)S(1)}, bf16[12,64,128]{2,1,0:T(8,128)(2,1)S(1)}, u32[]{:S(2)}, u32[]{:S(2)}) collective-permute-start(bf16[12,64,128]{2,1,0:T(8,128)(2,1)S(1)} %get-tuple-element.92), channel_id=1, source_target_pairs={{0,8},{2,10},{4,12},{6,14},{8,16},{10,18},{12,20},{14,22},{16,24},... | collective-permute-start | bytes 589832 | tf_op jit(solution)/shard_map/ppermute | solution.py:377
  30.7 9.2 %collective-permute-start.15 = (bf16[12,64,128]{2,1,0:T(8,128)(2,1)S(1)}, bf16[12,64,128]{2,1,0:T(8,128)(2,1)S(1)}, u32[]{:S(2)}, u32[]{:S(2)}) collective-permute-start(bf16[12,64,128]{2,1,0:T(8,128)(2,1)S(1)} %broadcast_select_fusion.5), channel_id=1, source_target_pairs={{0,4},{2,6},{4,0},{6,2},{8,12},{10,14},{12,8},{14,10},{16,20},{18,... | collective-permute-start | bytes 589832 | tf_op jit(solution)/shard_map/ppermute | solution.py:384
  31.5 8.4 %collective-permute-start.10 = (bf16[12,64,128]{2,1,0:T(8,128)(2,1)S(1)}, bf16[12,64,128]{2,1,0:T(8,128)(2,1)S(1)}, u32[]{:S(2)}, u32[]{:S(2)}) collective-permute-start(bf16[12,64,128]{2,1,0:T(8,128)(2,1)S(1)} %get-tuple-element.85), channel_id=1, source_target_pairs={{0,8},{2,10},{4,12},{6,14},{8,16},{10,18},{12,20},{14,22},{16,24},... | collective-permute-start | bytes 589832 | tf_op jit(solution)/shard_map/ppermute | solution.py:382
  33.7 10.5 %collective-permute-start.18 = (bf16[12,64,128]{2,1,0:T(8,128)(2,1)S(1)}, bf16[12,64,128]{2,1,0:T(8,128)(2,1)S(1)}, u32[]{:S(2)}, u32[]{:S(2)}) collective-permute-start(bf16[12,64,128]{2,1,0:T(8,128)(2,1)S(1)} %broadcast_select_fusion.2), channel_id=1, source_target_pairs={{0,4},{2,6},{4,0},{6,2},{8,12},{10,14},{12,8},{14,10},{16,20},{18,... | collective-permute-start | bytes 589832 | tf_op jit(solution)/shard_map/ppermute | solution.py:384
  35.1 9.1 %collective-permute-start.17 = (bf16[12,64,128]{2,1,0:T(8,128)(2,1)S(1)}, bf16[12,64,128]{2,1,0:T(8,128)(2,1)S(1)}, u32[]{:S(2)}, u32[]{:S(2)}) collective-permute-start(bf16[12,64,128]{2,1,0:T(8,128)(2,1)S(1)} %get-tuple-element.101), channel_id=1, source_target_pairs={{0,8},{2,10},{4,12},{6,14},{8,16},{10,18},{12,20},{14,22},{16,24},... | collective-permute-start | bytes 589832 | tf_op jit(solution)/shard_map/ppermute | solution.py:377
  40.0 14.0 %collective-permute-start.16 = (bf16[12,64,128]{2,1,0:T(8,128)(2,1)S(1)}, bf16[12,64,128]{2,1,0:T(8,128)(2,1)S(1)}, u32[]{:S(2)}, u32[]{:S(2)}) collective-permute-start(bf16[12,64,128]{2,1,0:T(8,128)(2,1)S(1)} %broadcast_select_fusion.3), channel_id=1, source_target_pairs={{0,4},{2,6},{4,0},{6,2},{8,12},{10,14},{12,8},{14,10},{16,20},{18,... | collective-permute-start | bytes 589832 | tf_op jit(solution)/shard_map/ppermute | solution.py:384
  44.2 9.8 %collective-permute-start.19 = (bf16[12,64,128]{2,1,0:T(8,128)(2,1)S(1)}, bf16[12,64,128]{2,1,0:T(8,128)(2,1)S(1)}, u32[]{:S(2)}, u32[]{:S(2)}) collective-permute-start(bf16[12,64,128]{2,1,0:T(8,128)(2,1)S(1)} %broadcast_select_fusion.1), channel_id=1, source_target_pairs={{0,4},{2,6},{4,0},{6,2},{8,12},{10,14},{12,8},{14,10},{16,20},{18,... | collective-permute-start | bytes 589832 | tf_op jit(solution)/shard_map/ppermute | solution.py:411
  47.8 8.0 %collective-permute-start.21 = (bf16[2,4,128,128]{3,2,1,0:T(8,128)(2,1)S(1)}, bf16[2,4,128,128]{3,2,1,0:T(8,128)(2,1)S(1)}, u32[]{:S(2)}, u32[]{:S(2)}) collective-permute-start(bf16[2,4,128,128]{3,2,1,0:T(8,128)(2,1)S(1)} %get-tuple-element.116), channel_id=1, source_target_pairs={{0,2},{2,0},{4,6},{6,4},{8,10},{10,8},{12,14},{14,12},{16,18},{18,... | collective-permute-start | bytes 786440 | tf_op jit(solution)/shard_map/ppermute | solution.py:415
  55.5 1.6 %collective-permute-start.20 = (bf16[2,4,128,128]{3,2,1,0:T(8,128)(2,1)S(1)}, bf16[2,4,128,128]{3,2,1,0:T(8,128)(2,1)S(1)}, u32[]{:S(2)}, u32[]{:S(2)}) collective-permute-start(bf16[2,4,128,128]{3,2,1,0:T(8,128)(2,1)S(1)} %get-tuple-element.114), channel_id=1, source_target_pairs={{0,2},{2,0},{4,6},{6,4},{8,10},{10,8},{12,14},{14,12},{16,18},{18,... | collective-permute-start | bytes 786440 | tf_op jit(solution)/shard_map/ppermute | solution.py:420

commit v12 on v11

--- a/solution.py
+++ b/solution.py
@@ -15,16 +15,16 @@
 GROUP = 16
 SIZES = (4,8,12,12,12,12,12,12,12)
 BLOCK = 24
-RAW = 4
+RAW = 3
 TERMS = 3
-Z_AFTER = (-1, -1, -1, -1, 2, 2, 3, 5, 6)
+Z_AFTER = (-1, -1, -1, 0, 2, 2, 3, 5, 6)
 Z_BEHIND = (0,0,0,0,0,0,0,1,0)
 Y_AFTER = (-1, -1, 0, 1, 2, 3, 4, 5, 6)
 LAST_TIE = 0
 PUT_TIE = 1
 CHAIN = 0
 SETS = (5, 2, 2)
-EDGE_AFTER = 0
+EDGE_AFTER = -1
 LEFT_AFTER = -1
 OTHER_AFTER = 0
 NEAR_BEFORE = 8

time: 58.3 us -> 55.6 us (0.954)
  waiting for transfers between devices: 16.7 us -> 13.6 us
    ppermute x8, waiting for transfers between devices: 3.95 us -> 1.96 us  [shards(): ones[k] = lax.ppermute(onward[k], 'ch', beside)]
    ppermute x1, waiting for transfers between devices: 1.44 us -> 0.01 us  [shards(): halo = lax.ppermute(edge, 'fq', [(0, 1), (1, 0)])]
    ppermute x8, starting transfers between devices: 8.04 us -> 9.2 us  [shards(): ones[k] = lax.ppermute(onward[k], 'ch', beside)]
    ppermute x4 -> x3, starting transfers between devices: 4.84 us -> 3.89 us  [shards(): twos = {k: lax.ppermute(early[k], 'ch', ahead) for k in range(RAW)}]
    ppermute x1, starting transfers between devices: 1.21 us -> 2.11 us  [shards(): halo = lax.ppermute(edge, 'fq', [(0, 1), (1, 0)])]
    ppermute x4 -> x3, waiting for transfers between devices: 0.25 us -> 0.95 us  [shards(): twos = {k: lax.ppermute(early[k], 'ch', ahead) for k in range(RAW)}]
    ppermute x5 -> x6, waiting for transfers between devices: 10.9 us -> 10.7 us  [shards(): twos[later] = lax.ppermute(mine[later], 'ch', ahead)]
    ppermute x5 -> x6, starting transfers between devices: 2.35 us -> 2.24 us  [shards(): twos[later] = lax.ppermute(mine[later], 'ch', ahead)]
  transfers between devices with their start and end apart: 22 -> 22, of which waited for: 10 -> 9; matrix products, arithmetic and copies ran while one was open for 2% -> 2% of each run, Pallas kernels for 21% -> 22%
where the time goes in v12:
time: 55.6 us; the launch traced here: 55.2 us
  starting transfers between devices  25.5 us (46%)
  waiting for transfers between devices  13.6 us (24%)
  Pallas kernels  13.4 us (24%)
  local copies, waits for them, and re-layouts  1.41 us (3%)
  other arithmetic  1.04 us (2%)
    ppermute x6, waiting for transfers between devices, shards(): twos[later] = lax.ppermute(mine[later], 'ch', ahead)  10.7 us
    ppermute x8, starting transfers between devices, shards(): ones[k] = lax.ppermute(onward[k], 'ch', beside)  9.2 us
    pallas_call x3, Pallas kernels, cross(): call(functools.partial(cross_kernel, jobs, not befores, sent), 'cross', (...  7.45 us
    ppermute x1, starting transfers between devices, shards(): two_got = lax.ppermute(two_sent, 'ch', mate)  4.79 us
    ppermute x3, starting transfers between devices, shards(): twos = {k: lax.ppermute(early[k], 'ch', ahead) for k in range(RAW)}  3.89 us
    pallas_call x3, Pallas kernels, put(): call(functools.partial(put_kernel, kinds), 'put', out_shape, [vmem()] * l...  2.79 us
    ppermute x1, starting transfers between devices, shards(): other = lax.ppermute(left, 'ch', mate)  2.42 us
    pallas_call x1, Pallas kernels, shards(): call(near_kernel, 'near', near_shape, [smem(), smem(), vmem(), vmem()], v...  2.29 us
  transfers between devices with their start and end apart: 22, of which 9 were waited for; matrix products, arithmetic and copies ran while one was open for 2% of the time, Pallas kernels for 22%

profile of v12, /device:TPU:1, one launch (start us, length us, event | category | flops | bytes accessed | tf_op | source)
XLA Modules:
  0.0 55.2 jit_solution(13145695811400964858)
XLA Ops:
  0.0 0.0 copy-start
  0.0 1.4 %copy-done = bf16[2,48,64,128]{3,2,1,0:T(8,128)(2,1)S(1)} copy-done((bf16[2,48,64,128]{3,2,1,0:T(8,128)(2,1)S(1)}, bf16[2,48,64,128]{3,2,1,0:T(8,128)(2,1)}, u32[]{:S(2)}) %copy-start) | copy-done | bytes 1572888
  1.4 0.0 copy-start.1
  1.4 0.4 power.1
  1.8 2.1 %collective-permute-start = (f32[4,128]{1,0:T(4,128)S(1)}, f32[4,128]{1,0:T(4,128)S(1)}, u32[]{:S(2)}, u32[]{:S(2)}) collective-permute-start(f32[4,128]{1,0:T(4,128)S(1)} %get-tuple-element.65), channel_id=1, source_target_pairs={{0,1},{1,0},{2,3},{3,2},{4,5},{5,4},{6,7},{7,6},{8,9},{9,8},{10,11... | collective-permute-start | bytes 6152 | tf_op jit(solution)/shard_map/ppermute | solution.py:311
  3.9 1.3 %collective-permute-start.1 = (bf16[4,64,128]{2,1,0:T(8,128)(2,1)S(1)}, bf16[4,64,128]{2,1,0:T(8,128)(2,1)S(1)}, u32[]{:S(2)}, u32[]{:S(2)}) collective-permute-start(bf16[4,64,128]{2,1,0:T(8,128)(2,1)S(1)} %get-tuple-element.67), channel_id=1, source_target_pairs={{0,8},{2,10},{4,12},{6,14},{8,16},{10,18},{12,20},{14,22},{16,24},... | collective-permute-start | bytes 196616 | tf_op jit(solution)/shard_map/ppermute | solution.py:308
  5.2 1.3 %collective-permute-start.7 = (bf16[8,64,128]{2,1,0:T(8,128)(2,1)S(1)}, bf16[8,64,128]{2,1,0:T(8,128)(2,1)S(1)}, u32[]{:S(2)}, u32[]{:S(2)}) collective-permute-start(bf16[8,64,128]{2,1,0:T(8,128)(2,1)S(1)} %get-tuple-element.79), channel_id=1, source_target_pairs={{0,8},{2,10},{4,12},{6,14},{8,16},{10,18},{12,20},{14,22},{16,24},... | collective-permute-start | bytes 393224 | tf_op jit(solution)/shard_map/ppermute | solution.py:308
  6.5 1.3 %collective-permute-start.3 = (bf16[12,64,128]{2,1,0:T(8,128)(2,1)S(1)}, bf16[12,64,128]{2,1,0:T(8,128)(2,1)S(1)}, u32[]{:S(2)}, u32[]{:S(2)}) collective-permute-start(bf16[12,64,128]{2,1,0:T(8,128)(2,1)S(1)} %get-tuple-element.69), channel_id=1, source_target_pairs={{0,8},{2,10},{4,12},{6,14},{8,16},{10,18},{12,20},{14,22},{16,24},... | collective-permute-start | bytes 589832 | tf_op jit(solution)/shard_map/ppermute | solution.py:308
  7.8 0.7 %broadcast_subtract_fusion = s32[64]{0:T(128)S(1)} fusion(s32[64]{0:T(128)} %param.3, s32[]{:T(128)S(6)} %mul.6), kind=kLoop, calls=%fused_computation.12 | loop fusion | flops 64 | bytes 516 | tf_op jit(solution)/shard_map/sub | solution.py:302
  8.4 0.1 convert_reduce_fusion.bounds_ref
  8.6 0.1 multiply_rsqrt_fusion.norm_ref
  8.6 0.0 collective-permute-done.halo_ref
  8.6 0.0 copy-done.1
  8.6 0.5 left.1
  9.2 0.0 collective-permute-done.1.refs_5_
  9.2 2.4 %collective-permute-start.2 = (bf16[4,128,1536]{2,1,0:T(8,128)(2,1)S(1)}, bf16[4,128,1536]{2,1,0:T(8,128)(2,1)S(1)}, u32[]{:S(2)}, u32[]{:S(2)}) collective-permute-start(bf16[4,128,1536]{2,1,0:T(8,128)(2,1)S(1)} %get-tuple-element.68.own_ref), channel_id=1, source_target_pairs={{0,2},{2,0},{4,6},{6,4},{8,10},{10,8},{12,14},{14,12},{16,18},{18,... | collective-permute-start | bytes 4718600 | tf_op jit(solution)/shard_map/ppermute | solution.py:353
  11.6 1.3 %collective-permute-start.4 = (bf16[4,64,128]{2,1,0:T(8,128)(2,1)S(1)}, bf16[4,64,128]{2,1,0:T(8,128)(2,1)S(1)}, u32[]{:S(2)}, u32[]{:S(2)}) collective-permute-start(bf16[4,64,128]{2,1,0:T(8,128)(2,1)S(1)} %broadcast_select_fusion.8), channel_id=1, source_target_pairs={{0,4},{2,6},{4,0},{6,2},{8,12},{10,14},{12,8},{14,10},{16,20},{18,... | collective-permute-start | bytes 196616 | tf_op jit(solution)/shard_map/ppermute | solution.py:384
  12.9 0.0 collective-permute-start.6
  12.9 0.0 collective-permute-done.7.refs_6_
  13.0 0.5 collective-permute-start.8
  13.5 1.9 %collective-permute-done.4.refs_0_ = bf16[4,64,128]{2,1,0:T(8,128)(2,1)S(1)} collective-permute-done((bf16[4,64,128]{2,1,0:T(8,128)(2,1)S(1)}, bf16[4,64,128]{2,1,0:T(8,128)(2,1)S(1)}, u32[]{:S(2)}, u32[]{:S(2)}) %collective-permute-start.4) | collective-permute-done | bytes 65568 | tf_op jit(solution)/shard_map/ppermute | solution.py:384
  15.4 0.9 %collective-permute-done.3.refs_7_ = bf16[12,64,128]{2,1,0:T(8,128)(2,1)S(1)} collective-permute-done((bf16[12,64,128]{2,1,0:T(8,128)(2,1)S(1)}, bf16[12,64,128]{2,1,0:T(8,128)(2,1)S(1)}, u32[]{:S(2)}, u32[]{:S(2)}) %collective-permute-start.3) | collective-permute-done | bytes 196640 | tf_op jit(solution)/shard_map/ppermute | solution.py:308
  16.4 1.3 %collective-permute-start.12 = (bf16[12,64,128]{2,1,0:T(8,128)(2,1)S(1)}, bf16[12,64,128]{2,1,0:T(8,128)(2,1)S(1)}, u32[]{:S(2)}, u32[]{:S(2)}) collective-permute-start(bf16[12,64,128]{2,1,0:T(8,128)(2,1)S(1)} %broadcast_select_fusion.5), channel_id=1, source_target_pairs={{0,4},{2,6},{4,0},{6,2},{8,12},{10,14},{12,8},{14,10},{16,20},{18,... | collective-permute-start | bytes 589832 | tf_op jit(solution)/shard_map/ppermute | solution.py:384
  17.7 0.0 collective-permute-start.11
  17.7 0.0 collective-permute-done.8.refs_1_
  17.7 4.3 %collective-permute-done.6.refs_8_ = bf16[15,64,128]{2,1,0:T(8,128)(2,1)S(1)} collective-permute-done((bf16[15,64,128]{2,1,0:T(8,128)(2,1)S(1)}, bf16[15,64,128]{2,1,0:T(8,128)(2,1)S(1)}, u32[]{:S(2)}, u32[]{:S(2)}) %collective-permute-start.6) | collective-permute-done | bytes 245792 | tf_op jit(solution)/shard_map/ppermute | solution.py:377
  22.0 1.1 %collective-permute-start.9 = (bf16[15,64,128]{2,1,0:T(8,128)(2,1)S(1)}, bf16[15,64,128]{2,1,0:T(8,128)(2,1)S(1)}, u32[]{:S(2)}, u32[]{:S(2)}) collective-permute-start(bf16[15,64,128]{2,1,0:T(8,128)(2,1)S(1)} %broadcast_select_fusion), channel_id=1, source_target_pairs={{0,4},{2,6},{4,0},{6,2},{8,12},{10,14},{12,8},{14,10},{16,20},{18,... | collective-permute-start | bytes 737288 | tf_op jit(solution)/shard_map/ppermute | solution.py:384
  23.1 0.0 collective-permute-start.5
  23.1 0.0 collective-permute-done.12.refs_2_
  23.1 0.7 %collective-permute-start.13 = (bf16[12,64,128]{2,1,0:T(8,128)(2,1)S(1)}, bf16[12,64,128]{2,1,0:T(8,128)(2,1)S(1)}, u32[]{:S(2)}, u32[]{:S(2)}) collective-permute-start(bf16[12,64,128]{2,1,0:T(8,128)(2,1)S(1)} %get-tuple-element.92), channel_id=1, source_target_pairs={{0,8},{2,10},{4,12},{6,14},{8,16},{10,18},{12,20},{14,22},{16,24},... | collective-permute-start | bytes 589832 | tf_op jit(solution)/shard_map/ppermute | solution.py:377
  23.8 0.8 %collective-permute-done.11.refs_9_ = bf16[12,64,128]{2,1,0:T(8,128)(2,1)S(1)} collective-permute-done((bf16[12,64,128]{2,1,0:T(8,128)(2,1)S(1)}, bf16[12,64,128]{2,1,0:T(8,128)(2,1)S(1)}, u32[]{:S(2)}, u32[]{:S(2)}) %collective-permute-start.11) | collective-permute-done | bytes 196640 | tf_op jit(solution)/shard_map/ppermute | solution.py:377
  24.5 2.4 %collective-permute-start.14 = (bf16[12,64,128]{2,1,0:T(8,128)(2,1)S(1)}, bf16[12,64,128]{2,1,0:T(8,128)(2,1)S(1)}, u32[]{:S(2)}, u32[]{:S(2)}) collective-permute-start(bf16[12,64,128]{2,1,0:T(8,128)(2,1)S(1)} %broadcast_select_fusion.4), channel_id=1, source_target_pairs={{0,4},{2,6},{4,0},{6,2},{8,12},{10,14},{12,8},{14,10},{16,20},{18,... | collective-permute-start | bytes 589832 | tf_op jit(solution)/shard_map/ppermute | solution.py:384
  27.0 2.4 %collective-permute-done.5.refs_2_ = bf16[12,64,128]{2,1,0:T(8,128)(2,1)S(1)} collective-permute-done((bf16[12,64,128]{2,1,0:T(8,128)(2,1)S(1)}, bf16[12,64,128]{2,1,0:T(8,128)(2,1)S(1)}, u32[]{:S(2)}, u32[]{:S(2)}) %collective-permute-start.5) | collective-permute-done | bytes 196640 | tf_op jit(solution)/shard_map/ppermute | solution.py:377
  29.4 0.0 collective-permute-done.9.refs_3_
  29.4 0.6 %collective-permute-start.15 = (bf16[12,64,128]{2,1,0:T(8,128)(2,1)S(1)}, bf16[12,64,128]{2,1,0:T(8,128)(2,1)S(1)}, u32[]{:S(2)}, u32[]{:S(2)}) collective-permute-start(bf16[12,64,128]{2,1,0:T(8,128)(2,1)S(1)} %broadcast_select_fusion.6), channel_id=1, source_target_pairs={{0,4},{2,6},{4,0},{6,2},{8,12},{10,14},{12,8},{14,10},{16,20},{18,... | collective-permute-start | bytes 589832 | tf_op jit(solution)/shard_map/ppermute | solution.py:384
  30.0 0.8 %collective-permute-start.10 = (bf16[12,64,128]{2,1,0:T(8,128)(2,1)S(1)}, bf16[12,64,128]{2,1,0:T(8,128)(2,1)S(1)}, u32[]{:S(2)}, u32[]{:S(2)}) collective-permute-start(bf16[12,64,128]{2,1,0:T(8,128)(2,1)S(1)} %get-tuple-element.85), channel_id=1, source_target_pairs={{0,8},{2,10},{4,12},{6,14},{8,16},{10,18},{12,20},{14,22},{16,24},... | collective-permute-start | bytes 589832 | tf_op jit(solution)/shard_map/ppermute | solution.py:382
  30.9 2.1 %collective-permute-done.13.refs_3_ = bf16[12,64,128]{2,1,0:T(8,128)(2,1)S(1)} collective-permute-done((bf16[12,64,128]{2,1,0:T(8,128)(2,1)S(1)}, bf16[12,64,128]{2,1,0:T(8,128)(2,1)S(1)}, u32[]{:S(2)}, u32[]{:S(2)}) %collective-permute-start.13) | collective-permute-done | bytes 196640 | tf_op jit(solution)/shard_map/ppermute | solution.py:377
  33.0 0.0 collective-permute-done.14.refs_4_
  33.0 1.4 %collective-permute-start.18 = (bf16[12,64,128]{2,1,0:T(8,128)(2,1)S(1)}, bf16[12,64,128]{2,1,0:T(8,128)(2,1)S(1)}, u32[]{:S(2)}, u32[]{:S(2)}) collective-permute-start(bf16[12,64,128]{2,1,0:T(8,128)(2,1)S(1)} %broadcast_select_fusion.2), channel_id=1, source_target_pairs={{0,4},{2,6},{4,0},{6,2},{8,12},{10,14},{12,8},{14,10},{16,20},{18,... | collective-permute-start | bytes 589832 | tf_op jit(solution)/shard_map/ppermute | solution.py:384
  34.4 0.7 %collective-permute-start.17 = (bf16[12,64,128]{2,1,0:T(8,128)(2,1)S(1)}, bf16[12,64,128]{2,1,0:T(8,128)(2,1)S(1)}, u32[]{:S(2)}, u32[]{:S(2)}) collective-permute-start(bf16[12,64,128]{2,1,0:T(8,128)(2,1)S(1)} %get-tuple-element.101), channel_id=1, source_target_pairs={{0,8},{2,10},{4,12},{6,14},{8,16},{10,18},{12,20},{14,22},{16,24},... | collective-permute-start | bytes 589832 | tf_op jit(solution)/shard_map/ppermute | solution.py:377
  35.1 0.0 collective-permute-done.2.mate_ref
  35.1 2.6 %cross.3 = (f32[2,2,4,128,128]{4,3,2,1,0:T(8,128)S(1)}, f32[2,2,4,128,128]{4,3,2,1,0:T(8,128)S(1)}) custom-call(s32[5]{0:T(128)S(1)} %convert_reduce_fusion.bounds_ref, f32[4]{0:T(128)S(1)} %multiply_rsqrt_fusion.norm_ref, bf16[4,128,1536]{2,1,0:T(8,128)(2,1)S(1)} %get-tuple-element.68.own_ref, bf16[4,128,1536]{2,1,0:T(8,128)(2,1)S(1)} %collective-permute-done.2.mate_ref, ...), custom_call_target="tpu_custom_call" | custom-call | flops 805306368 | tf_op jit(solution)/shard_map/cross/pallas_call | solution.py:342
  37.7 0.2 collective-permute-done.10.refs_4_
  37.8 0.0 collective-permute-done.15.refs_0_
  37.9 0.6 %collective-permute-start.16 = (bf16[12,64,128]{2,1,0:T(8,128)(2,1)S(1)}, bf16[12,64,128]{2,1,0:T(8,128)(2,1)S(1)}, u32[]{:S(2)}, u32[]{:S(2)}) collective-permute-start(bf16[12,64,128]{2,1,0:T(8,128)(2,1)S(1)} %broadcast_select_fusion.3), channel_id=1, source_target_pairs={{0,4},{2,6},{4,0},{6,2},{8,12},{10,14},{12,8},{14,10},{16,20},{18,... | collective-permute-start | bytes 589832 | tf_op jit(solution)/shard_map/ppermute | solution.py:384
  38.5 2.3 %near.1.refs_2_ = f32[2,4,128,128]{3,2,1,0:T(8,128)S(1)} custom-call(s32[5]{0:T(128)S(1)} %convert_reduce_fusion.bounds_ref, f32[4]{0:T(128)S(1)} %multiply_rsqrt_fusion.norm_ref, bf16[4,128,1536]{2,1,0:T(8,128)(2,1)S(1)} %get-tuple-element.68.own_ref, bf16[4,128,1536]{2,1,0:T(8,128)(2,1)S(1)} %collective-permute-done.2.mate_ref), custom_call_target="tpu_custom_call" | custom-call | flops 1000 | bytes 1000 | tf_op jit(solution)/shard_map/near/pallas_call | solution.py:354
  40.8 0.9 %collective-permute-done.17.refs_5_ = bf16[12,64,128]{2,1,0:T(8,128)(2,1)S(1)} collective-permute-done((bf16[12,64,128]{2,1,0:T(8,128)(2,1)S(1)}, bf16[12,64,128]{2,1,0:T(8,128)(2,1)S(1)}, u32[]{:S(2)}, u32[]{:S(2)}) %collective-permute-start.17) | collective-permute-done | bytes 196640 | tf_op jit(solution)/shard_map/ppermute | solution.py:377
  41.7 0.0 collective-permute-done.18.refs_1_
  41.7 0.1 collective-permute-start.19
  41.8 3.4 %cross.4 = (f32[2,2,4,128,128]{4,3,2,1,0:T(8,128)S(1)}, f32[2,2,4,128,128]{4,3,2,1,0:T(8,128)S(1)}, bf16[2,4,128,128]{3,2,1,0:T(8,128)(2,1)S(1)}) custom-call(s32[5]{0:T(128)S(1)} %convert_reduce_fusion.bounds_ref, f32[4]{0:T(128)S(1)} %multiply_rsqrt_fusion.norm_ref, bf16[4,128,1536]{2,1,0:T(8,128)(2,1)S(1)} %get-tuple-element.68.own_ref, ...), custom_call_target="tpu_custom_call" | custom-call | flops 603979776 | tf_op jit(solution)/shard_map/cross/pallas_call | solution.py:342
  45.2 4.8 %collective-permute-start.21 = (bf16[2,4,128,128]{3,2,1,0:T(8,128)(2,1)S(1)}, bf16[2,4,128,128]{3,2,1,0:T(8,128)(2,1)S(1)}, u32[]{:S(2)}, u32[]{:S(2)}) collective-permute-start(bf16[2,4,128,128]{3,2,1,0:T(8,128)(2,1)S(1)} %get-tuple-element.116), channel_id=1, source_target_pairs={{0,2},{2,0},{4,6},{6,4},{8,10},{10,8},{12,14},{14,12},{16,18},{18,... | collective-permute-start | bytes 786440 | tf_op jit(solution)/shard_map/ppermute | solution.py:415
  50.0 0.8 %put.3.refs_3_ = f32[2,4,4,128,128]{4,3,2,1,0:T(8,128)} custom-call(f32[2,2,4,128,128]{4,3,2,1,0:T(8,128)S(1)} %get-tuple-element.112.refs_0_), custom_call_target="tpu_custom_call" | custom-call | flops 1000 | bytes 6291456 | tf_op jit(solution)/shard_map/put/pallas_call | solution.py:396
  50.9 0.0 collective-permute-done.16.refs_0_
  50.9 0.0 collective-permute-done.19.refs_1_
  50.9 1.5 %cross.5 = (f32[2,2,4,128,128]{4,3,2,1,0:T(8,128)S(1)}, bf16[2,4,128,128]{3,2,1,0:T(8,128)(2,1)S(1)}) custom-call(s32[5]{0:T(128)S(1)} %convert_reduce_fusion.bounds_ref, f32[4]{0:T(128)S(1)} %multiply_rsqrt_fusion.norm_ref, bf16[4,128,1536]{2,1,0:T(8,128)(2,1)S(1)} %get-tuple-element.68.own_ref, bf16[4,128,1536]{2,1,0:T(8,128)(2,1)S(1)} %collective-permute-done.2.mate_ref, ...), custom_call_target="tpu_custom_call" | custom-call | flops 201326592 | tf_op jit(solution)/shard_map/cross/pallas_call | solution.py:342
  52.4 0.8 %collective-permute-start.20 = (bf16[2,4,128,128]{3,2,1,0:T(8,128)(2,1)S(1)}, bf16[2,4,128,128]{3,2,1,0:T(8,128)(2,1)S(1)}, u32[]{:S(2)}, u32[]{:S(2)}) collective-permute-start(bf16[2,4,128,128]{3,2,1,0:T(8,128)(2,1)S(1)} %get-tuple-element.114), channel_id=1, source_target_pairs={{0,2},{2,0},{4,6},{6,4},{8,10},{10,8},{12,14},{14,12},{16,18},{18,... | collective-permute-start | bytes 786440 | tf_op jit(solution)/shard_map/ppermute | solution.py:420
  53.1 0.0 collective-permute-done.21.refs_1_
  53.1 1.1 %put.4.refs_1_ = f32[2,4,4,128,128]{4,3,2,1,0:T(8,128)} custom-call(f32[2,2,4,128,128]{4,3,2,1,0:T(8,128)S(1)} %get-tuple-element.115.refs_0_, bf16[2,4,128,128]{3,2,1,0:T(8,128)(2,1)S(1)} %collective-permute-done.21.refs_1_, f32[2,4,128,128]{3,2,1,0:T(8,128)S(1)} %near.1.refs_2_, f32[2,4,4,128,128]{4,3,2,1,0:T(8,128)} %put.3.refs_3_), custom_call_target="tpu_custom_call", output_to_operand_aliasing={{}: (3, {})} | custom-call | flops 1000 | bytes 6291456 | tf_op jit(solution)/shard_map/put/pallas_call | solution.py:396
  54.2 0.1 collective-permute-done.20.refs_0_
  54.3 0.9 %put.5 = f32[2,4,4,128,128]{4,3,2,1,0:T(8,128)} custom-call(bf16[2,4,128,128]{3,2,1,0:T(8,128)(2,1)S(1)} %collective-permute-done.20.refs_0_, f32[2,4,4,128,128]{4,3,2,1,0:T(8,128)} %put.4.refs_1_), custom_call_target="tpu_custom_call", output_to_operand_aliasing={{}: (1, {})} | custom-call | flops 1000 | bytes 6291456 | tf_op jit(solution)/shard_map/put/pallas_call | solution.py:396
  (9 shorter events, 0.2 us)
Async XLA Ops:
  0.0 1.4 %copy-start = (bf16[2,48,64,128]{3,2,1,0:T(8,128)(2,1)S(1)}, bf16[2,48,64,128]{3,2,1,0:T(8,128)(2,1)}, u32[]{:S(2)}) copy-start(bf16[2,48,64,128]{3,2,1,0:T(8,128)(2,1)} %param.2) | copy-start | bytes 4718596
  1.4 7.2 %copy-start.1 = (bf16[2,48,64,128]{3,2,1,0:T(8,128)(2,1)S(1)}, bf16[2,48,64,128]{3,2,1,0:T(8,128)(2,1)}, u32[]{:S(2)}) copy-start(bf16[2,48,64,128]{3,2,1,0:T(8,128)(2,1)} %param.2) | copy-start | bytes 4718596
  1.8 6.9 %collective-permute-start = (f32[4,128]{1,0:T(4,128)S(1)}, f32[4,128]{1,0:T(4,128)S(1)}, u32[]{:S(2)}, u32[]{:S(2)}) collective-permute-start(f32[4,128]{1,0:T(4,128)S(1)} %get-tuple-element.65), channel_id=1, source_target_pairs={{0,1},{1,0},{2,3},{3,2},{4,5},{5,4},{6,7},{7,6},{8,9},{9,8},{10,11... | collective-permute-start | bytes 6152 | tf_op jit(solution)/shard_map/ppermute | solution.py:311
  3.9 5.3 %collective-permute-start.1 = (bf16[4,64,128]{2,1,0:T(8,128)(2,1)S(1)}, bf16[4,64,128]{2,1,0:T(8,128)(2,1)S(1)}, u32[]{:S(2)}, u32[]{:S(2)}) collective-permute-start(bf16[4,64,128]{2,1,0:T(8,128)(2,1)S(1)} %get-tuple-element.67), channel_id=1, source_target_pairs={{0,8},{2,10},{4,12},{6,14},{8,16},{10,18},{12,20},{14,22},{16,24},... | collective-permute-start | bytes 196616 | tf_op jit(solution)/shard_map/ppermute | solution.py:308
  5.2 7.7 %collective-permute-start.7 = (bf16[8,64,128]{2,1,0:T(8,128)(2,1)S(1)}, bf16[8,64,128]{2,1,0:T(8,128)(2,1)S(1)}, u32[]{:S(2)}, u32[]{:S(2)}) collective-permute-start(bf16[8,64,128]{2,1,0:T(8,128)(2,1)S(1)} %get-tuple-element.79), channel_id=1, source_target_pairs={{0,8},{2,10},{4,12},{6,14},{8,16},{10,18},{12,20},{14,22},{16,24},... | collective-permute-start | bytes 393224 | tf_op jit(solution)/shard_map/ppermute | solution.py:308
  6.5 9.9 %collective-permute-start.3 = (bf16[12,64,128]{2,1,0:T(8,128)(2,1)S(1)}, bf16[12,64,128]{2,1,0:T(8,128)(2,1)S(1)}, u32[]{:S(2)}, u32[]{:S(2)}) collective-permute-start(bf16[12,64,128]{2,1,0:T(8,128)(2,1)S(1)} %get-tuple-element.69), channel_id=1, source_target_pairs={{0,8},{2,10},{4,12},{6,14},{8,16},{10,18},{12,20},{14,22},{16,24},... | collective-permute-start | bytes 589832 | tf_op jit(solution)/shard_map/ppermute | solution.py:308
  9.2 25.9 %collective-permute-start.2 = (bf16[4,128,1536]{2,1,0:T(8,128)(2,1)S(1)}, bf16[4,128,1536]{2,1,0:T(8,128)(2,1)S(1)}, u32[]{:S(2)}, u32[]{:S(2)}) collective-permute-start(bf16[4,128,1536]{2,1,0:T(8,128)(2,1)S(1)} %get-tuple-element.68.own_ref), channel_id=1, source_target_pairs={{0,2},{2,0},{4,6},{6,4},{8,10},{10,8},{12,14},{14,12},{16,18},{18,... | collective-permute-start | bytes 4718600 | tf_op jit(solution)/shard_map/ppermute | solution.py:353
  11.6 3.8 %collective-permute-start.4 = (bf16[4,64,128]{2,1,0:T(8,128)(2,1)S(1)}, bf16[4,64,128]{2,1,0:T(8,128)(2,1)S(1)}, u32[]{:S(2)}, u32[]{:S(2)}) collective-permute-start(bf16[4,64,128]{2,1,0:T(8,128)(2,1)S(1)} %broadcast_select_fusion.8), channel_id=1, source_target_pairs={{0,4},{2,6},{4,0},{6,2},{8,12},{10,14},{12,8},{14,10},{16,20},{18,... | collective-permute-start | bytes 196616 | tf_op jit(solution)/shard_map/ppermute | solution.py:384
  12.9 9.1 %collective-permute-start.6 = (bf16[15,64,128]{2,1,0:T(8,128)(2,1)S(1)}, bf16[15,64,128]{2,1,0:T(8,128)(2,1)S(1)}, u32[]{:S(2)}, u32[]{:S(2)}) collective-permute-start(bf16[15,64,128]{2,1,0:T(8,128)(2,1)S(1)} %get-tuple-element.78), channel_id=1, source_target_pairs={{0,8},{2,10},{4,12},{6,14},{8,16},{10,18},{12,20},{14,22},{16,24},... | collective-permute-start | bytes 737288 | tf_op jit(solution)/shard_map/ppermute | solution.py:377
  13.0 4.7 %collective-permute-start.8 = (bf16[8,64,128]{2,1,0:T(8,128)(2,1)S(1)}, bf16[8,64,128]{2,1,0:T(8,128)(2,1)S(1)}, u32[]{:S(2)}, u32[]{:S(2)}) collective-permute-start(bf16[8,64,128]{2,1,0:T(8,128)(2,1)S(1)} %broadcast_select_fusion.7), channel_id=1, source_target_pairs={{0,4},{2,6},{4,0},{6,2},{8,12},{10,14},{12,8},{14,10},{16,20},{18,... | collective-permute-start | bytes 393224 | tf_op jit(solution)/shard_map/ppermute | solution.py:384
  16.4 6.7 %collective-permute-start.12 = (bf16[12,64,128]{2,1,0:T(8,128)(2,1)S(1)}, bf16[12,64,128]{2,1,0:T(8,128)(2,1)S(1)}, u32[]{:S(2)}, u32[]{:S(2)}) collective-permute-start(bf16[12,64,128]{2,1,0:T(8,128)(2,1)S(1)} %broadcast_select_fusion.5), channel_id=1, source_target_pairs={{0,4},{2,6},{4,0},{6,2},{8,12},{10,14},{12,8},{14,10},{16,20},{18,... | collective-permute-start | bytes 589832 | tf_op jit(solution)/shard_map/ppermute | solution.py:384
  17.7 6.8 %collective-permute-start.11 = (bf16[12,64,128]{2,1,0:T(8,128)(2,1)S(1)}, bf16[12,64,128]{2,1,0:T(8,128)(2,1)S(1)}, u32[]{:S(2)}, u32[]{:S(2)}) collective-permute-start(bf16[12,64,128]{2,1,0:T(8,128)(2,1)S(1)} %get-tuple-element.88), channel_id=1, source_target_pairs={{0,8},{2,10},{4,12},{6,14},{8,16},{10,18},{12,20},{14,22},{16,24},... | collective-permute-start | bytes 589832 | tf_op jit(solution)/shard_map/ppermute | solution.py:377
  22.0 7.4 %collective-permute-start.9 = (bf16[15,64,128]{2,1,0:T(8,128)(2,1)S(1)}, bf16[15,64,128]{2,1,0:T(8,128)(2,1)S(1)}, u32[]{:S(2)}, u32[]{:S(2)}) collective-permute-start(bf16[15,64,128]{2,1,0:T(8,128)(2,1)S(1)} %broadcast_select_fusion), channel_id=1, source_target_pairs={{0,4},{2,6},{4,0},{6,2},{8,12},{10,14},{12,8},{14,10},{16,20},{18,... | collective-permute-start | bytes 737288 | tf_op jit(solution)/shard_map/ppermute | solution.py:384
  23.1 6.3 %collective-permute-start.5 = (bf16[12,64,128]{2,1,0:T(8,128)(2,1)S(1)}, bf16[12,64,128]{2,1,0:T(8,128)(2,1)S(1)}, u32[]{:S(2)}, u32[]{:S(2)}) collective-permute-start(bf16[12,64,128]{2,1,0:T(8,128)(2,1)S(1)} %get-tuple-element.77), channel_id=1, source_target_pairs={{0,8},{2,10},{4,12},{6,14},{8,16},{10,18},{12,20},{14,22},{16,24},... | collective-permute-start | bytes 589832 | tf_op jit(solution)/shard_map/ppermute | solution.py:377
  23.1 9.9 %collective-permute-start.13 = (bf16[12,64,128]{2,1,0:T(8,128)(2,1)S(1)}, bf16[12,64,128]{2,1,0:T(8,128)(2,1)S(1)}, u32[]{:S(2)}, u32[]{:S(2)}) collective-permute-start(bf16[12,64,128]{2,1,0:T(8,128)(2,1)S(1)} %get-tuple-element.92), channel_id=1, source_target_pairs={{0,8},{2,10},{4,12},{6,14},{8,16},{10,18},{12,20},{14,22},{16,24},... | collective-permute-start | bytes 589832 | tf_op jit(solution)/shard_map/ppermute | solution.py:377
  24.5 8.4 %collective-permute-start.14 = (bf16[12,64,128]{2,1,0:T(8,128)(2,1)S(1)}, bf16[12,64,128]{2,1,0:T(8,128)(2,1)S(1)}, u32[]{:S(2)}, u32[]{:S(2)}) collective-permute-start(bf16[12,64,128]{2,1,0:T(8,128)(2,1)S(1)} %broadcast_select_fusion.4), channel_id=1, source_target_pairs={{0,4},{2,6},{4,0},{6,2},{8,12},{10,14},{12,8},{14,10},{16,20},{18,... | collective-permute-start | bytes 589832 | tf_op jit(solution)/shard_map/ppermute | solution.py:384
  29.4 8.4 %collective-permute-start.15 = (bf16[12,64,128]{2,1,0:T(8,128)(2,1)S(1)}, bf16[12,64,128]{2,1,0:T(8,128)(2,1)S(1)}, u32[]{:S(2)}, u32[]{:S(2)}) collective-permute-start(bf16[12,64,128]{2,1,0:T(8,128)(2,1)S(1)} %broadcast_select_fusion.6), channel_id=1, source_target_pairs={{0,4},{2,6},{4,0},{6,2},{8,12},{10,14},{12,8},{14,10},{16,20},{18,... | collective-permute-start | bytes 589832 | tf_op jit(solution)/shard_map/ppermute | solution.py:384
  30.0 7.8 %collective-permute-start.10 = (bf16[12,64,128]{2,1,0:T(8,128)(2,1)S(1)}, bf16[12,64,128]{2,1,0:T(8,128)(2,1)S(1)}, u32[]{:S(2)}, u32[]{:S(2)}) collective-permute-start(bf16[12,64,128]{2,1,0:T(8,128)(2,1)S(1)} %get-tuple-element.85), channel_id=1, source_target_pairs={{0,8},{2,10},{4,12},{6,14},{8,16},{10,18},{12,20},{14,22},{16,24},... | collective-permute-start | bytes 589832 | tf_op jit(solution)/shard_map/ppermute | solution.py:382
  33.0 8.7 %collective-permute-start.18 = (bf16[12,64,128]{2,1,0:T(8,128)(2,1)S(1)}, bf16[12,64,128]{2,1,0:T(8,128)(2,1)S(1)}, u32[]{:S(2)}, u32[]{:S(2)}) collective-permute-start(bf16[12,64,128]{2,1,0:T(8,128)(2,1)S(1)} %broadcast_select_fusion.2), channel_id=1, source_target_pairs={{0,4},{2,6},{4,0},{6,2},{8,12},{10,14},{12,8},{14,10},{16,20},{18,... | collective-permute-start | bytes 589832 | tf_op jit(solution)/shard_map/ppermute | solution.py:384
  34.4 7.3 %collective-permute-start.17 = (bf16[12,64,128]{2,1,0:T(8,128)(2,1)S(1)}, bf16[12,64,128]{2,1,0:T(8,128)(2,1)S(1)}, u32[]{:S(2)}, u32[]{:S(2)}) collective-permute-start(bf16[12,64,128]{2,1,0:T(8,128)(2,1)S(1)} %get-tuple-element.101), channel_id=1, source_target_pairs={{0,8},{2,10},{4,12},{6,14},{8,16},{10,18},{12,20},{14,22},{16,24},... | collective-permute-start | bytes 589832 | tf_op jit(solution)/shard_map/ppermute | solution.py:377
  37.9 13.0 %collective-permute-start.16 = (bf16[12,64,128]{2,1,0:T(8,128)(2,1)S(1)}, bf16[12,64,128]{2,1,0:T(8,128)(2,1)S(1)}, u32[]{:S(2)}, u32[]{:S(2)}) collective-permute-start(bf16[12,64,128]{2,1,0:T(8,128)(2,1)S(1)} %broadcast_select_fusion.3), channel_id=1, source_target_pairs={{0,4},{2,6},{4,0},{6,2},{8,12},{10,14},{12,8},{14,10},{16,20},{18,... | collective-permute-start | bytes 589832 | tf_op jit(solution)/shard_map/ppermute | solution.py:384
  41.7 9.2 %collective-permute-start.19 = (bf16[12,64,128]{2,1,0:T(8,128)(2,1)S(1)}, bf16[12,64,128]{2,1,0:T(8,128)(2,1)S(1)}, u32[]{:S(2)}, u32[]{:S(2)}) collective-permute-start(bf16[12,64,128]{2,1,0:T(8,128)(2,1)S(1)} %broadcast_select_fusion.1), channel_id=1, source_target_pairs={{0,4},{2,6},{4,0},{6,2},{8,12},{10,14},{12,8},{14,10},{16,20},{18,... | collective-permute-start | bytes 589832 | tf_op jit(solution)/shard_map/ppermute | solution.py:411
  45.2 7.9 %collective-permute-start.21 = (bf16[2,4,128,128]{3,2,1,0:T(8,128)(2,1)S(1)}, bf16[2,4,128,128]{3,2,1,0:T(8,128)(2,1)S(1)}, u32[]{:S(2)}, u32[]{:S(2)}) collective-permute-start(bf16[2,4,128,128]{3,2,1,0:T(8,128)(2,1)S(1)} %get-tuple-element.116), channel_id=1, source_target_pairs={{0,2},{2,0},{4,6},{6,4},{8,10},{10,8},{12,14},{14,12},{16,18},{18,... | collective-permute-start | bytes 786440 | tf_op jit(solution)/shard_map/ppermute | solution.py:415
  52.4 1.9 %collective-permute-start.20 = (bf16[2,4,128,128]{3,2,1,0:T(8,128)(2,1)S(1)}, bf16[2,4,128,128]{3,2,1,0:T(8,128)(2,1)S(1)}, u32[]{:S(2)}, u32[]{:S(2)}) collective-permute-start(bf16[2,4,128,128]{3,2,1,0:T(8,128)(2,1)S(1)} %get-tuple-element.114), channel_id=1, source_target_pairs={{0,2},{2,0},{4,6},{6,4},{8,10},{10,8},{12,14},{14,12},{16,18},{18,... | collective-permute-start | bytes 786440 | tf_op jit(solution)/shard_map/ppermute | solution.py:420

commit v13 on v11

--- a/solution.py
+++ b/solution.py
@@ -18,13 +18,13 @@
 RAW = 4
 TERMS = 3
 Z_AFTER = (-1, -1, -1, -1, 2, 2, 3, 5, 6)
-Z_BEHIND = (0,0,0,0,0,0,0,1,0)
+Z_BEHIND = (0, 0, 0, 0, 0, 1, 0, 1, 0)
 Y_AFTER = (-1, -1, 0, 1, 2, 3, 4, 5, 6)
 LAST_TIE = 0
 PUT_TIE = 1
 CHAIN = 0
 SETS = (5, 2, 2)
-EDGE_AFTER = 0
+EDGE_AFTER = -1
 LEFT_AFTER = -1
 OTHER_AFTER = 0
 NEAR_BEFORE = 8

time: 58.3 us -> 58.1 us (level)
    ppermute x4, waiting for transfers between devices: 0.25 us -> 3.83 us  [shards(): twos = {k: lax.ppermute(early[k], 'ch', ahead) for k in range(RAW)}]
    ppermute x8, waiting for transfers between devices: 3.95 us -> 1.96 us  [shards(): ones[k] = lax.ppermute(onward[k], 'ch', beside)]
    ppermute x1, waiting for transfers between devices: 1.44 us -> 0.01 us  [shards(): halo = lax.ppermute(edge, 'fq', [(0, 1), (1, 0)])]
    ppermute x5, starting transfers between devices: 2.35 us -> 1.16 us  [shards(): twos[later] = lax.ppermute(mine[later], 'ch', ahead)]
    ppermute x4, starting transfers between devices: 4.84 us -> 3.94 us  [shards(): twos = {k: lax.ppermute(early[k], 'ch', ahead) for k in range(RAW)}]
    ppermute x1, starting transfers between devices: 1.21 us -> 2.11 us  [shards(): halo = lax.ppermute(edge, 'fq', [(0, 1), (1, 0)])]
    ppermute x8, starting transfers between devices: 8.04 us -> 8.63 us  [shards(): ones[k] = lax.ppermute(onward[k], 'ch', beside)]
  transfers between devices with their start and end apart: 22 -> 22, of which waited for: 10 -> 9; matrix products, arithmetic and copies ran while one was open for 2% -> 2% of each run, Pallas kernels for 21% -> 21%
where the time goes in v13:
time: 58.1 us; the launch traced here: 57.6 us
  starting transfers between devices  24.8 us (43%)
  waiting for transfers between devices  16.7 us (29%)
  Pallas kernels  13.5 us (23%)
  local copies, waits for them, and re-layouts  1.41 us (2%)
  other arithmetic  1.04 us (2%)
    ppermute x5, waiting for transfers between devices, shards(): twos[later] = lax.ppermute(mine[later], 'ch', ahead)  10.8 us
    ppermute x8, starting transfers between devices, shards(): ones[k] = lax.ppermute(onward[k], 'ch', beside)  8.63 us
    pallas_call x3, Pallas kernels, cross(): call(functools.partial(cross_kernel, jobs, not befores, sent), 'cross', (...  7.52 us
    ppermute x1, starting transfers between devices, shards(): two_got = lax.ppermute(two_sent, 'ch', mate)  5.49 us
    ppermute x4, starting transfers between devices, shards(): twos = {k: lax.ppermute(early[k], 'ch', ahead) for k in range(RAW)}  3.94 us
    ppermute x4, waiting for transfers between devices, shards(): twos = {k: lax.ppermute(early[k], 'ch', ahead) for k in range(RAW)}  3.83 us
    pallas_call x3, Pallas kernels, put(): call(functools.partial(put_kernel, kinds), 'put', out_shape, [vmem()] * l...  2.79 us
    ppermute x1, starting transfers between devices, shards(): other = lax.ppermute(left, 'ch', mate)  2.38 us
  transfers between devices with their start and end apart: 22, of which 9 were waited for; matrix products, arithmetic and copies ran while one was open for 2% of the time, Pallas kernels for 21%

profile of v13, /device:TPU:1, one launch (start us, length us, event | category | flops | bytes accessed | tf_op | source)
XLA Modules:
  0.0 57.6 jit_solution(12277784850841060186)
XLA Ops:
  0.0 0.0 copy-start
  0.0 1.4 %copy-done = bf16[2,48,64,128]{3,2,1,0:T(8,128)(2,1)S(1)} copy-done((bf16[2,48,64,128]{3,2,1,0:T(8,128)(2,1)S(1)}, bf16[2,48,64,128]{3,2,1,0:T(8,128)(2,1)}, u32[]{:S(2)}) %copy-start) | copy-done | bytes 1572888
  1.4 0.0 copy-start.1
  1.4 0.4 power.1
  1.8 2.1 %collective-permute-start = (f32[4,128]{1,0:T(4,128)S(1)}, f32[4,128]{1,0:T(4,128)S(1)}, u32[]{:S(2)}, u32[]{:S(2)}) collective-permute-start(f32[4,128]{1,0:T(4,128)S(1)} %get-tuple-element.63), channel_id=1, source_target_pairs={{0,1},{1,0},{2,3},{3,2},{4,5},{5,4},{6,7},{7,6},{8,9},{9,8},{10,11... | collective-permute-start | bytes 6152 | tf_op jit(solution)/shard_map/ppermute | solution.py:311
  3.9 1.3 %collective-permute-start.1 = (bf16[4,64,128]{2,1,0:T(8,128)(2,1)S(1)}, bf16[4,64,128]{2,1,0:T(8,128)(2,1)S(1)}, u32[]{:S(2)}, u32[]{:S(2)}) collective-permute-start(bf16[4,64,128]{2,1,0:T(8,128)(2,1)S(1)} %get-tuple-element.65), channel_id=1, source_target_pairs={{0,8},{2,10},{4,12},{6,14},{8,16},{10,18},{12,20},{14,22},{16,24},... | collective-permute-start | bytes 196616 | tf_op jit(solution)/shard_map/ppermute | solution.py:308
  5.2 1.3 %collective-permute-start.7 = (bf16[8,64,128]{2,1,0:T(8,128)(2,1)S(1)}, bf16[8,64,128]{2,1,0:T(8,128)(2,1)S(1)}, u32[]{:S(2)}, u32[]{:S(2)}) collective-permute-start(bf16[8,64,128]{2,1,0:T(8,128)(2,1)S(1)} %get-tuple-element.75), channel_id=1, source_target_pairs={{0,8},{2,10},{4,12},{6,14},{8,16},{10,18},{12,20},{14,22},{16,24},... | collective-permute-start | bytes 393224 | tf_op jit(solution)/shard_map/ppermute | solution.py:308
  6.5 1.3 %collective-permute-start.3 = (bf16[12,64,128]{2,1,0:T(8,128)(2,1)S(1)}, bf16[12,64,128]{2,1,0:T(8,128)(2,1)S(1)}, u32[]{:S(2)}, u32[]{:S(2)}) collective-permute-start(bf16[12,64,128]{2,1,0:T(8,128)(2,1)S(1)} %get-tuple-element.67), channel_id=1, source_target_pairs={{0,8},{2,10},{4,12},{6,14},{8,16},{10,18},{12,20},{14,22},{16,24},... | collective-permute-start | bytes 589832 | tf_op jit(solution)/shard_map/ppermute | solution.py:308
  7.8 0.0 collective-permute-start.6
  7.8 0.7 %broadcast_subtract_fusion = s32[64]{0:T(128)S(1)} fusion(s32[64]{0:T(128)} %param.3, s32[]{:T(128)S(6)} %mul.6), kind=kLoop, calls=%fused_computation.12 | loop fusion | flops 64 | bytes 516 | tf_op jit(solution)/shard_map/sub | solution.py:302
  8.5 0.1 convert_reduce_fusion.bounds_ref
  8.6 0.1 multiply_rsqrt_fusion.norm_ref
  8.7 0.0 collective-permute-done.halo_ref
  8.7 0.0 copy-done.1
  8.7 0.5 left.1
  9.2 0.0 collective-permute-done.1.refs_5_
  9.2 2.4 %collective-permute-start.2 = (bf16[4,128,1536]{2,1,0:T(8,128)(2,1)S(1)}, bf16[4,128,1536]{2,1,0:T(8,128)(2,1)S(1)}, u32[]{:S(2)}, u32[]{:S(2)}) collective-permute-start(bf16[4,128,1536]{2,1,0:T(8,128)(2,1)S(1)} %get-tuple-element.66.own_ref), channel_id=1, source_target_pairs={{0,2},{2,0},{4,6},{6,4},{8,10},{10,8},{12,14},{14,12},{16,18},{18,... | collective-permute-start | bytes 4718600 | tf_op jit(solution)/shard_map/ppermute | solution.py:353
  11.6 1.3 %collective-permute-start.4 = (bf16[4,64,128]{2,1,0:T(8,128)(2,1)S(1)}, bf16[4,64,128]{2,1,0:T(8,128)(2,1)S(1)}, u32[]{:S(2)}, u32[]{:S(2)}) collective-permute-start(bf16[4,64,128]{2,1,0:T(8,128)(2,1)S(1)} %broadcast_select_fusion.8), channel_id=1, source_target_pairs={{0,4},{2,6},{4,0},{6,2},{8,12},{10,14},{12,8},{14,10},{16,20},{18,... | collective-permute-start | bytes 196616 | tf_op jit(solution)/shard_map/ppermute | solution.py:384
  12.9 0.0 collective-permute-done.7.refs_6_
  13.0 0.5 collective-permute-start.8
  13.5 1.9 %collective-permute-done.4.refs_0_ = bf16[4,64,128]{2,1,0:T(8,128)(2,1)S(1)} collective-permute-done((bf16[4,64,128]{2,1,0:T(8,128)(2,1)S(1)}, bf16[4,64,128]{2,1,0:T(8,128)(2,1)S(1)}, u32[]{:S(2)}, u32[]{:S(2)}) %collective-permute-start.4) | collective-permute-done | bytes 65568 | tf_op jit(solution)/shard_map/ppermute | solution.py:384
  15.4 0.9 %collective-permute-done.3.refs_7_ = bf16[12,64,128]{2,1,0:T(8,128)(2,1)S(1)} collective-permute-done((bf16[12,64,128]{2,1,0:T(8,128)(2,1)S(1)}, bf16[12,64,128]{2,1,0:T(8,128)(2,1)S(1)}, u32[]{:S(2)}, u32[]{:S(2)}) %collective-permute-start.3) | collective-permute-done | bytes 196640 | tf_op jit(solution)/shard_map/ppermute | solution.py:308
  16.4 0.0 collective-permute-start.11
  16.4 1.3 %collective-permute-start.12 = (bf16[12,64,128]{2,1,0:T(8,128)(2,1)S(1)}, bf16[12,64,128]{2,1,0:T(8,128)(2,1)S(1)}, u32[]{:S(2)}, u32[]{:S(2)}) collective-permute-start(bf16[12,64,128]{2,1,0:T(8,128)(2,1)S(1)} %broadcast_select_fusion.6), channel_id=1, source_target_pairs={{0,4},{2,6},{4,0},{6,2},{8,12},{10,14},{12,8},{14,10},{16,20},{18,... | collective-permute-start | bytes 589832 | tf_op jit(solution)/shard_map/ppermute | solution.py:384
  17.7 2.9 %collective-permute-done.6.refs_8_ = bf16[12,64,128]{2,1,0:T(8,128)(2,1)S(1)} collective-permute-done((bf16[12,64,128]{2,1,0:T(8,128)(2,1)S(1)}, bf16[12,64,128]{2,1,0:T(8,128)(2,1)S(1)}, u32[]{:S(2)}, u32[]{:S(2)}) %collective-permute-start.6) | collective-permute-done | bytes 196640 | tf_op jit(solution)/shard_map/ppermute | solution.py:308
  20.6 0.0 collective-permute-start.5
  20.6 0.0 collective-permute-done.8.refs_1_
  20.6 1.3 %collective-permute-start.9 = (bf16[12,64,128]{2,1,0:T(8,128)(2,1)S(1)}, bf16[12,64,128]{2,1,0:T(8,128)(2,1)S(1)}, u32[]{:S(2)}, u32[]{:S(2)}) collective-permute-start(bf16[12,64,128]{2,1,0:T(8,128)(2,1)S(1)} %broadcast_select_fusion.5), channel_id=1, source_target_pairs={{0,4},{2,6},{4,0},{6,2},{8,12},{10,14},{12,8},{14,10},{16,20},{18,... | collective-permute-start | bytes 589832 | tf_op jit(solution)/shard_map/ppermute | solution.py:384
  21.9 0.0 collective-permute-done.12.refs_2_
  21.9 2.7 %collective-permute-done.11.refs_9_ = bf16[15,64,128]{2,1,0:T(8,128)(2,1)S(1)} collective-permute-done((bf16[15,64,128]{2,1,0:T(8,128)(2,1)S(1)}, bf16[15,64,128]{2,1,0:T(8,128)(2,1)S(1)}, u32[]{:S(2)}, u32[]{:S(2)}) %collective-permute-start.11) | collective-permute-done | bytes 245792 | tf_op jit(solution)/shard_map/ppermute | solution.py:377
  24.7 1.3 %collective-permute-start.14 = (bf16[15,64,128]{2,1,0:T(8,128)(2,1)S(1)}, bf16[15,64,128]{2,1,0:T(8,128)(2,1)S(1)}, u32[]{:S(2)}, u32[]{:S(2)}) collective-permute-start(bf16[15,64,128]{2,1,0:T(8,128)(2,1)S(1)} %broadcast_select_fusion), channel_id=1, source_target_pairs={{0,4},{2,6},{4,0},{6,2},{8,12},{10,14},{12,8},{14,10},{16,20},{18,... | collective-permute-start | bytes 737288 | tf_op jit(solution)/shard_map/ppermute | solution.py:384
  26.0 0.7 %collective-permute-start.13 = (bf16[12,64,128]{2,1,0:T(8,128)(2,1)S(1)}, bf16[12,64,128]{2,1,0:T(8,128)(2,1)S(1)}, u32[]{:S(2)}, u32[]{:S(2)}) collective-permute-start(bf16[12,64,128]{2,1,0:T(8,128)(2,1)S(1)} %get-tuple-element.88), channel_id=1, source_target_pairs={{0,8},{2,10},{4,12},{6,14},{8,16},{10,18},{12,20},{14,22},{16,24},... | collective-permute-start | bytes 589832 | tf_op jit(solution)/shard_map/ppermute | solution.py:377
  26.7 2.6 %collective-permute-done.5.refs_2_ = bf16[12,64,128]{2,1,0:T(8,128)(2,1)S(1)} collective-permute-done((bf16[12,64,128]{2,1,0:T(8,128)(2,1)S(1)}, bf16[12,64,128]{2,1,0:T(8,128)(2,1)S(1)}, u32[]{:S(2)}, u32[]{:S(2)}) %collective-permute-start.5) | collective-permute-done | bytes 196640 | tf_op jit(solution)/shard_map/ppermute | solution.py:382
  29.3 0.0 collective-permute-done.9.refs_3_
  29.4 1.3 %collective-permute-start.15 = (bf16[12,64,128]{2,1,0:T(8,128)(2,1)S(1)}, bf16[12,64,128]{2,1,0:T(8,128)(2,1)S(1)}, u32[]{:S(2)}, u32[]{:S(2)}) collective-permute-start(bf16[12,64,128]{2,1,0:T(8,128)(2,1)S(1)} %broadcast_select_fusion.4), channel_id=1, source_target_pairs={{0,4},{2,6},{4,0},{6,2},{8,12},{10,14},{12,8},{14,10},{16,20},{18,... | collective-permute-start | bytes 589832 | tf_op jit(solution)/shard_map/ppermute | solution.py:384
  30.7 0.2 collective-permute-start.10
  30.9 2.0 %collective-permute-done.13.refs_3_ = bf16[12,64,128]{2,1,0:T(8,128)(2,1)S(1)} collective-permute-done((bf16[12,64,128]{2,1,0:T(8,128)(2,1)S(1)}, bf16[12,64,128]{2,1,0:T(8,128)(2,1)S(1)}, u32[]{:S(2)}, u32[]{:S(2)}) %collective-permute-start.13) | collective-permute-done | bytes 196640 | tf_op jit(solution)/shard_map/ppermute | solution.py:377
  32.9 0.0 collective-permute-done.14.refs_4_
  33.0 1.3 %collective-permute-start.18 = (bf16[12,64,128]{2,1,0:T(8,128)(2,1)S(1)}, bf16[12,64,128]{2,1,0:T(8,128)(2,1)S(1)}, u32[]{:S(2)}, u32[]{:S(2)}) collective-permute-start(bf16[12,64,128]{2,1,0:T(8,128)(2,1)S(1)} %broadcast_select_fusion.2), channel_id=1, source_target_pairs={{0,4},{2,6},{4,0},{6,2},{8,12},{10,14},{12,8},{14,10},{16,20},{18,... | collective-permute-start | bytes 589832 | tf_op jit(solution)/shard_map/ppermute | solution.py:384
  34.3 0.2 collective-permute-start.17
  34.5 0.0 collective-permute-done.2.mate_ref
  34.5 2.6 %cross.3 = (f32[2,2,4,128,128]{4,3,2,1,0:T(8,128)S(1)}, f32[2,2,4,128,128]{4,3,2,1,0:T(8,128)S(1)}) custom-call(s32[5]{0:T(128)S(1)} %convert_reduce_fusion.bounds_ref, f32[4]{0:T(128)S(1)} %multiply_rsqrt_fusion.norm_ref, bf16[4,128,1536]{2,1,0:T(8,128)(2,1)S(1)} %get-tuple-element.66.own_ref, bf16[4,128,1536]{2,1,0:T(8,128)(2,1)S(1)} %collective-permute-done.2.mate_ref, ...), custom_call_target="tpu_custom_call" | custom-call | flops 805306368 | tf_op jit(solution)/shard_map/cross/pallas_call | solution.py:342
  37.1 1.8 %collective-permute-done.10.refs_4_ = bf16[12,64,128]{2,1,0:T(8,128)(2,1)S(1)} collective-permute-done((bf16[12,64,128]{2,1,0:T(8,128)(2,1)S(1)}, bf16[12,64,128]{2,1,0:T(8,128)(2,1)S(1)}, u32[]{:S(2)}, u32[]{:S(2)}) %collective-permute-start.10) | collective-permute-done | bytes 196640 | tf_op jit(solution)/shard_map/ppermute | solution.py:382
  39.0 0.0 collective-permute-done.15.refs_0_
  39.0 0.3 collective-permute-start.16
  39.3 2.3 %near.1.refs_2_ = f32[2,4,128,128]{3,2,1,0:T(8,128)S(1)} custom-call(s32[5]{0:T(128)S(1)} %convert_reduce_fusion.bounds_ref, f32[4]{0:T(128)S(1)} %multiply_rsqrt_fusion.norm_ref, bf16[4,128,1536]{2,1,0:T(8,128)(2,1)S(1)} %get-tuple-element.66.own_ref, bf16[4,128,1536]{2,1,0:T(8,128)(2,1)S(1)} %collective-permute-done.2.mate_ref), custom_call_target="tpu_custom_call" | custom-call | flops 1000 | bytes 1000 | tf_op jit(solution)/shard_map/near/pallas_call | solution.py:354
  41.6 1.6 %collective-permute-done.17.refs_5_ = bf16[12,64,128]{2,1,0:T(8,128)(2,1)S(1)} collective-permute-done((bf16[12,64,128]{2,1,0:T(8,128)(2,1)S(1)}, bf16[12,64,128]{2,1,0:T(8,128)(2,1)S(1)}, u32[]{:S(2)}, u32[]{:S(2)}) %collective-permute-start.17) | collective-permute-done | bytes 196640 | tf_op jit(solution)/shard_map/ppermute | solution.py:377
  43.2 0.0 collective-permute-done.18.refs_1_
  43.2 0.3 collective-permute-start.19
  43.5 3.4 %cross.4 = (f32[2,2,4,128,128]{4,3,2,1,0:T(8,128)S(1)}, f32[2,2,4,128,128]{4,3,2,1,0:T(8,128)S(1)}, bf16[2,4,128,128]{3,2,1,0:T(8,128)(2,1)S(1)}) custom-call(s32[5]{0:T(128)S(1)} %convert_reduce_fusion.bounds_ref, f32[4]{0:T(128)S(1)} %multiply_rsqrt_fusion.norm_ref, bf16[4,128,1536]{2,1,0:T(8,128)(2,1)S(1)} %get-tuple-element.66.own_ref, ...), custom_call_target="tpu_custom_call" | custom-call | flops 603979776 | tf_op jit(solution)/shard_map/cross/pallas_call | solution.py:342
  46.9 5.5 %collective-permute-start.21 = (bf16[2,4,128,128]{3,2,1,0:T(8,128)(2,1)S(1)}, bf16[2,4,128,128]{3,2,1,0:T(8,128)(2,1)S(1)}, u32[]{:S(2)}, u32[]{:S(2)}) collective-permute-start(bf16[2,4,128,128]{3,2,1,0:T(8,128)(2,1)S(1)} %get-tuple-element.112), channel_id=1, source_target_pairs={{0,2},{2,0},{4,6},{6,4},{8,10},{10,8},{12,14},{14,12},{16,18},{18,... | collective-permute-start | bytes 786440 | tf_op jit(solution)/shard_map/ppermute | solution.py:415
  52.4 0.8 %put.3.refs_3_ = f32[2,4,4,128,128]{4,3,2,1,0:T(8,128)} custom-call(f32[2,2,4,128,128]{4,3,2,1,0:T(8,128)S(1)} %get-tuple-element.108.refs_0_), custom_call_target="tpu_custom_call" | custom-call | flops 1000 | bytes 6291456 | tf_op jit(solution)/shard_map/put/pallas_call | solution.py:396
  53.3 0.0 collective-permute-done.16.refs_0_
  53.3 0.0 collective-permute-done.19.refs_1_
  53.3 1.5 %cross.5 = (f32[2,2,4,128,128]{4,3,2,1,0:T(8,128)S(1)}, bf16[2,4,128,128]{3,2,1,0:T(8,128)(2,1)S(1)}) custom-call(s32[5]{0:T(128)S(1)} %convert_reduce_fusion.bounds_ref, f32[4]{0:T(128)S(1)} %multiply_rsqrt_fusion.norm_ref, bf16[4,128,1536]{2,1,0:T(8,128)(2,1)S(1)} %get-tuple-element.66.own_ref, bf16[4,128,1536]{2,1,0:T(8,128)(2,1)S(1)} %collective-permute-done.2.mate_ref, ...), custom_call_target="tpu_custom_call" | custom-call | flops 201326592 | tf_op jit(solution)/shard_map/cross/pallas_call | solution.py:342
  54.8 0.8 %collective-permute-start.20 = (bf16[2,4,128,128]{3,2,1,0:T(8,128)(2,1)S(1)}, bf16[2,4,128,128]{3,2,1,0:T(8,128)(2,1)S(1)}, u32[]{:S(2)}, u32[]{:S(2)}) collective-permute-start(bf16[2,4,128,128]{3,2,1,0:T(8,128)(2,1)S(1)} %get-tuple-element.110), channel_id=1, source_target_pairs={{0,2},{2,0},{4,6},{6,4},{8,10},{10,8},{12,14},{14,12},{16,18},{18,... | collective-permute-start | bytes 786440 | tf_op jit(solution)/shard_map/ppermute | solution.py:420
  55.6 0.0 collective-permute-done.21.refs_1_
  55.6 1.1 %put.4.refs_1_ = f32[2,4,4,128,128]{4,3,2,1,0:T(8,128)} custom-call(f32[2,2,4,128,128]{4,3,2,1,0:T(8,128)S(1)} %get-tuple-element.111.refs_0_, bf16[2,4,128,128]{3,2,1,0:T(8,128)(2,1)S(1)} %collective-permute-done.21.refs_1_, f32[2,4,128,128]{3,2,1,0:T(8,128)S(1)} %near.1.refs_2_, f32[2,4,4,128,128]{4,3,2,1,0:T(8,128)} %put.3.refs_3_), custom_call_target="tpu_custom_call", output_to_operand_aliasing={{}: (3, {})} | custom-call | flops 1000 | bytes 6291456 | tf_op jit(solution)/shard_map/put/pallas_call | solution.py:396
  56.7 0.1 collective-permute-done.20.refs_0_
  56.8 0.9 %put.5 = f32[2,4,4,128,128]{4,3,2,1,0:T(8,128)} custom-call(bf16[2,4,128,128]{3,2,1,0:T(8,128)(2,1)S(1)} %collective-permute-done.20.refs_0_, f32[2,4,4,128,128]{4,3,2,1,0:T(8,128)} %put.4.refs_1_), custom_call_target="tpu_custom_call", output_to_operand_aliasing={{}: (1, {})} | custom-call | flops 1000 | bytes 6291456 | tf_op jit(solution)/shard_map/put/pallas_call | solution.py:396
  (9 shorter events, 0.2 us)
Async XLA Ops:
  0.0 1.4 %copy-start = (bf16[2,48,64,128]{3,2,1,0:T(8,128)(2,1)S(1)}, bf16[2,48,64,128]{3,2,1,0:T(8,128)(2,1)}, u32[]{:S(2)}) copy-start(bf16[2,48,64,128]{3,2,1,0:T(8,128)(2,1)} %param.2) | copy-start | bytes 4718596
  1.4 7.3 %copy-start.1 = (bf16[2,48,64,128]{3,2,1,0:T(8,128)(2,1)S(1)}, bf16[2,48,64,128]{3,2,1,0:T(8,128)(2,1)}, u32[]{:S(2)}) copy-start(bf16[2,48,64,128]{3,2,1,0:T(8,128)(2,1)} %param.2) | copy-start | bytes 4718596
  1.8 6.9 %collective-permute-start = (f32[4,128]{1,0:T(4,128)S(1)}, f32[4,128]{1,0:T(4,128)S(1)}, u32[]{:S(2)}, u32[]{:S(2)}) collective-permute-start(f32[4,128]{1,0:T(4,128)S(1)} %get-tuple-element.63), channel_id=1, source_target_pairs={{0,1},{1,0},{2,3},{3,2},{4,5},{5,4},{6,7},{7,6},{8,9},{9,8},{10,11... | collective-permute-start | bytes 6152 | tf_op jit(solution)/shard_map/ppermute | solution.py:311
  3.9 5.3 %collective-permute-start.1 = (bf16[4,64,128]{2,1,0:T(8,128)(2,1)S(1)}, bf16[4,64,128]{2,1,0:T(8,128)(2,1)S(1)}, u32[]{:S(2)}, u32[]{:S(2)}) collective-permute-start(bf16[4,64,128]{2,1,0:T(8,128)(2,1)S(1)} %get-tuple-element.65), channel_id=1, source_target_pairs={{0,8},{2,10},{4,12},{6,14},{8,16},{10,18},{12,20},{14,22},{16,24},... | collective-permute-start | bytes 196616 | tf_op jit(solution)/shard_map/ppermute | solution.py:308
  5.2 7.7 %collective-permute-start.7 = (bf16[8,64,128]{2,1,0:T(8,128)(2,1)S(1)}, bf16[8,64,128]{2,1,0:T(8,128)(2,1)S(1)}, u32[]{:S(2)}, u32[]{:S(2)}) collective-permute-start(bf16[8,64,128]{2,1,0:T(8,128)(2,1)S(1)} %get-tuple-element.75), channel_id=1, source_target_pairs={{0,8},{2,10},{4,12},{6,14},{8,16},{10,18},{12,20},{14,22},{16,24},... | collective-permute-start | bytes 393224 | tf_op jit(solution)/shard_map/ppermute | solution.py:308
  6.5 9.9 %collective-permute-start.3 = (bf16[12,64,128]{2,1,0:T(8,128)(2,1)S(1)}, bf16[12,64,128]{2,1,0:T(8,128)(2,1)S(1)}, u32[]{:S(2)}, u32[]{:S(2)}) collective-permute-start(bf16[12,64,128]{2,1,0:T(8,128)(2,1)S(1)} %get-tuple-element.67), channel_id=1, source_target_pairs={{0,8},{2,10},{4,12},{6,14},{8,16},{10,18},{12,20},{14,22},{16,24},... | collective-permute-start | bytes 589832 | tf_op jit(solution)/shard_map/ppermute | solution.py:308
  7.8 12.8 %collective-permute-start.6 = (bf16[12,64,128]{2,1,0:T(8,128)(2,1)S(1)}, bf16[12,64,128]{2,1,0:T(8,128)(2,1)S(1)}, u32[]{:S(2)}, u32[]{:S(2)}) collective-permute-start(bf16[12,64,128]{2,1,0:T(8,128)(2,1)S(1)} %get-tuple-element.74), channel_id=1, source_target_pairs={{0,8},{2,10},{4,12},{6,14},{8,16},{10,18},{12,20},{14,22},{16,24},... | collective-permute-start | bytes 589832 | tf_op jit(solution)/shard_map/ppermute | solution.py:308
  9.2 25.2 %collective-permute-start.2 = (bf16[4,128,1536]{2,1,0:T(8,128)(2,1)S(1)}, bf16[4,128,1536]{2,1,0:T(8,128)(2,1)S(1)}, u32[]{:S(2)}, u32[]{:S(2)}) collective-permute-start(bf16[4,128,1536]{2,1,0:T(8,128)(2,1)S(1)} %get-tuple-element.66.own_ref), channel_id=1, source_target_pairs={{0,2},{2,0},{4,6},{6,4},{8,10},{10,8},{12,14},{14,12},{16,18},{18,... | collective-permute-start | bytes 4718600 | tf_op jit(solution)/shard_map/ppermute | solution.py:353
  11.6 3.8 %collective-permute-start.4 = (bf16[4,64,128]{2,1,0:T(8,128)(2,1)S(1)}, bf16[4,64,128]{2,1,0:T(8,128)(2,1)S(1)}, u32[]{:S(2)}, u32[]{:S(2)}) collective-permute-start(bf16[4,64,128]{2,1,0:T(8,128)(2,1)S(1)} %broadcast_select_fusion.8), channel_id=1, source_target_pairs={{0,4},{2,6},{4,0},{6,2},{8,12},{10,14},{12,8},{14,10},{16,20},{18,... | collective-permute-start | bytes 196616 | tf_op jit(solution)/shard_map/ppermute | solution.py:384
  13.0 7.6 %collective-permute-start.8 = (bf16[8,64,128]{2,1,0:T(8,128)(2,1)S(1)}, bf16[8,64,128]{2,1,0:T(8,128)(2,1)S(1)}, u32[]{:S(2)}, u32[]{:S(2)}) collective-permute-start(bf16[8,64,128]{2,1,0:T(8,128)(2,1)S(1)} %broadcast_select_fusion.7), channel_id=1, source_target_pairs={{0,4},{2,6},{4,0},{6,2},{8,12},{10,14},{12,8},{14,10},{16,20},{18,... | collective-permute-start | bytes 393224 | tf_op jit(solution)/shard_map/ppermute | solution.py:384
  16.4 8.3 %collective-permute-start.11 = (bf16[15,64,128]{2,1,0:T(8,128)(2,1)S(1)}, bf16[15,64,128]{2,1,0:T(8,128)(2,1)S(1)}, u32[]{:S(2)}, u32[]{:S(2)}) collective-permute-start(bf16[15,64,128]{2,1,0:T(8,128)(2,1)S(1)} %get-tuple-element.84), channel_id=1, source_target_pairs={{0,8},{2,10},{4,12},{6,14},{8,16},{10,18},{12,20},{14,22},{16,24},... | collective-permute-start | bytes 737288 | tf_op jit(solution)/shard_map/ppermute | solution.py:377
  16.4 5.5 %collective-permute-start.12 = (bf16[12,64,128]{2,1,0:T(8,128)(2,1)S(1)}, bf16[12,64,128]{2,1,0:T(8,128)(2,1)S(1)}, u32[]{:S(2)}, u32[]{:S(2)}) collective-permute-start(bf16[12,64,128]{2,1,0:T(8,128)(2,1)S(1)} %broadcast_select_fusion.6), channel_id=1, source_target_pairs={{0,4},{2,6},{4,0},{6,2},{8,12},{10,14},{12,8},{14,10},{16,20},{18,... | collective-permute-start | bytes 589832 | tf_op jit(solution)/shard_map/ppermute | solution.py:384
  20.6 8.7 %collective-permute-start.5 = (bf16[12,64,128]{2,1,0:T(8,128)(2,1)S(1)}, bf16[12,64,128]{2,1,0:T(8,128)(2,1)S(1)}, u32[]{:S(2)}, u32[]{:S(2)}) collective-permute-start(bf16[12,64,128]{2,1,0:T(8,128)(2,1)S(1)} %get-tuple-element.73), channel_id=1, source_target_pairs={{0,8},{2,10},{4,12},{6,14},{8,16},{10,18},{12,20},{14,22},{16,24},... | collective-permute-start | bytes 589832 | tf_op jit(solution)/shard_map/ppermute | solution.py:382
  20.6 8.7 %collective-permute-start.9 = (bf16[12,64,128]{2,1,0:T(8,128)(2,1)S(1)}, bf16[12,64,128]{2,1,0:T(8,128)(2,1)S(1)}, u32[]{:S(2)}, u32[]{:S(2)}) collective-permute-start(bf16[12,64,128]{2,1,0:T(8,128)(2,1)S(1)} %broadcast_select_fusion.5), channel_id=1, source_target_pairs={{0,4},{2,6},{4,0},{6,2},{8,12},{10,14},{12,8},{14,10},{16,20},{18,... | collective-permute-start | bytes 589832 | tf_op jit(solution)/shard_map/ppermute | solution.py:384
  24.7 8.3 %collective-permute-start.14 = (bf16[15,64,128]{2,1,0:T(8,128)(2,1)S(1)}, bf16[15,64,128]{2,1,0:T(8,128)(2,1)S(1)}, u32[]{:S(2)}, u32[]{:S(2)}) collective-permute-start(bf16[15,64,128]{2,1,0:T(8,128)(2,1)S(1)} %broadcast_select_fusion), channel_id=1, source_target_pairs={{0,4},{2,6},{4,0},{6,2},{8,12},{10,14},{12,8},{14,10},{16,20},{18,... | collective-permute-start | bytes 737288 | tf_op jit(solution)/shard_map/ppermute | solution.py:384
  26.0 7.0 %collective-permute-start.13 = (bf16[12,64,128]{2,1,0:T(8,128)(2,1)S(1)}, bf16[12,64,128]{2,1,0:T(8,128)(2,1)S(1)}, u32[]{:S(2)}, u32[]{:S(2)}) collective-permute-start(bf16[12,64,128]{2,1,0:T(8,128)(2,1)S(1)} %get-tuple-element.88), channel_id=1, source_target_pairs={{0,8},{2,10},{4,12},{6,14},{8,16},{10,18},{12,20},{14,22},{16,24},... | collective-permute-start | bytes 589832 | tf_op jit(solution)/shard_map/ppermute | solution.py:377
  29.4 9.6 %collective-permute-start.15 = (bf16[12,64,128]{2,1,0:T(8,128)(2,1)S(1)}, bf16[12,64,128]{2,1,0:T(8,128)(2,1)S(1)}, u32[]{:S(2)}, u32[]{:S(2)}) collective-permute-start(bf16[12,64,128]{2,1,0:T(8,128)(2,1)S(1)} %broadcast_select_fusion.4), channel_id=1, source_target_pairs={{0,4},{2,6},{4,0},{6,2},{8,12},{10,14},{12,8},{14,10},{16,20},{18,... | collective-permute-start | bytes 589832 | tf_op jit(solution)/shard_map/ppermute | solution.py:384
  30.7 8.3 %collective-permute-start.10 = (bf16[12,64,128]{2,1,0:T(8,128)(2,1)S(1)}, bf16[12,64,128]{2,1,0:T(8,128)(2,1)S(1)}, u32[]{:S(2)}, u32[]{:S(2)}) collective-permute-start(bf16[12,64,128]{2,1,0:T(8,128)(2,1)S(1)} %get-tuple-element.81), channel_id=1, source_target_pairs={{0,8},{2,10},{4,12},{6,14},{8,16},{10,18},{12,20},{14,22},{16,24},... | collective-permute-start | bytes 589832 | tf_op jit(solution)/shard_map/ppermute | solution.py:382
  33.0 10.2 %collective-permute-start.18 = (bf16[12,64,128]{2,1,0:T(8,128)(2,1)S(1)}, bf16[12,64,128]{2,1,0:T(8,128)(2,1)S(1)}, u32[]{:S(2)}, u32[]{:S(2)}) collective-permute-start(bf16[12,64,128]{2,1,0:T(8,128)(2,1)S(1)} %broadcast_select_fusion.2), channel_id=1, source_target_pairs={{0,4},{2,6},{4,0},{6,2},{8,12},{10,14},{12,8},{14,10},{16,20},{18,... | collective-permute-start | bytes 589832 | tf_op jit(solution)/shard_map/ppermute | solution.py:384
  34.3 8.9 %collective-permute-start.17 = (bf16[12,64,128]{2,1,0:T(8,128)(2,1)S(1)}, bf16[12,64,128]{2,1,0:T(8,128)(2,1)S(1)}, u32[]{:S(2)}, u32[]{:S(2)}) collective-permute-start(bf16[12,64,128]{2,1,0:T(8,128)(2,1)S(1)} %get-tuple-element.97), channel_id=1, source_target_pairs={{0,8},{2,10},{4,12},{6,14},{8,16},{10,18},{12,20},{14,22},{16,24},... | collective-permute-start | bytes 589832 | tf_op jit(solution)/shard_map/ppermute | solution.py:377
  39.0 14.3 %collective-permute-start.16 = (bf16[12,64,128]{2,1,0:T(8,128)(2,1)S(1)}, bf16[12,64,128]{2,1,0:T(8,128)(2,1)S(1)}, u32[]{:S(2)}, u32[]{:S(2)}) collective-permute-start(bf16[12,64,128]{2,1,0:T(8,128)(2,1)S(1)} %broadcast_select_fusion.3), channel_id=1, source_target_pairs={{0,4},{2,6},{4,0},{6,2},{8,12},{10,14},{12,8},{14,10},{16,20},{18,... | collective-permute-start | bytes 589832 | tf_op jit(solution)/shard_map/ppermute | solution.py:384
  43.2 10.1 %collective-permute-start.19 = (bf16[12,64,128]{2,1,0:T(8,128)(2,1)S(1)}, bf16[12,64,128]{2,1,0:T(8,128)(2,1)S(1)}, u32[]{:S(2)}, u32[]{:S(2)}) collective-permute-start(bf16[12,64,128]{2,1,0:T(8,128)(2,1)S(1)} %broadcast_select_fusion.1), channel_id=1, source_target_pairs={{0,4},{2,6},{4,0},{6,2},{8,12},{10,14},{12,8},{14,10},{16,20},{18,... | collective-permute-start | bytes 589832 | tf_op jit(solution)/shard_map/ppermute | solution.py:411
  46.9 8.7 %collective-permute-start.21 = (bf16[2,4,128,128]{3,2,1,0:T(8,128)(2,1)S(1)}, bf16[2,4,128,128]{3,2,1,0:T(8,128)(2,1)S(1)}, u32[]{:S(2)}, u32[]{:S(2)}) collective-permute-start(bf16[2,4,128,128]{3,2,1,0:T(8,128)(2,1)S(1)} %get-tuple-element.112), channel_id=1, source_target_pairs={{0,2},{2,0},{4,6},{6,4},{8,10},{10,8},{12,14},{14,12},{16,18},{18,... | collective-permute-start | bytes 786440 | tf_op jit(solution)/shard_map/ppermute | solution.py:415
  54.8 2.0 %collective-permute-start.20 = (bf16[2,4,128,128]{3,2,1,0:T(8,128)(2,1)S(1)}, bf16[2,4,128,128]{3,2,1,0:T(8,128)(2,1)S(1)}, u32[]{:S(2)}, u32[]{:S(2)}) collective-permute-start(bf16[2,4,128,128]{3,2,1,0:T(8,128)(2,1)S(1)} %get-tuple-element.110), channel_id=1, source_target_pairs={{0,2},{2,0},{4,6},{6,4},{8,10},{10,8},{12,14},{14,12},{16,18},{18,... | collective-permute-start | bytes 786440 | tf_op jit(solution)/shard_map/ppermute | solution.py:420

commit v14 on v12

--- a/solution.py
+++ b/solution.py
@@ -17,12 +17,12 @@
 BLOCK = 24
 RAW = 3
 TERMS = 3
-Z_AFTER = (-1, -1, -1, 0, 2, 2, 3, 5, 6)
-Z_BEHIND = (0,0,0,0,0,0,0,1,0)
+Z_AFTER = (-1, -1, -1, 0, 1, 2, 3, 5, 6)
+Z_BEHIND = (0, 0, 0, 0, 0, 0, 0, 1, 0)
 Y_AFTER = (-1, -1, 0, 1, 2, 3, 4, 5, 6)
 LAST_TIE = 0
 PUT_TIE = 1
-CHAIN = 0
+CHAIN = 1
 SETS = (5, 2, 2)
 EDGE_AFTER = -1
 LEFT_AFTER = -1

time: 55.6 us -> 57.6 us (1.036)
  waiting for transfers between devices: 13.6 us -> 19.4 us
  starting transfers between devices: 25.5 us -> 21.7 us
    ppermute x6, waiting for transfers between devices: 10.7 us -> 16.4 us  [shards(): twos[later] = lax.ppermute(mine[later], 'ch', ahead)]
    ppermute x6, starting transfers between devices: 2.24 us -> 0.07 us  [shards(): twos[later] = lax.ppermute(mine[later], 'ch', ahead)]
    ppermute x8, starting transfers between devices: 9.2 us -> 7.97 us  [shards(): ones[k] = lax.ppermute(onward[k], 'ch', beside)]
    ppermute x1, starting transfers between devices: 4.79 us -> 3.92 us  [shards(): two_got = lax.ppermute(two_sent, 'ch', mate)]
  transfers between devices with their start and end apart: 22 -> 22, of which waited for: 9 -> 9; matrix products, arithmetic and copies ran while one was open for 2% -> 2% of each run, Pallas kernels for 22% -> 21%
where the time goes in v14:
time: 57.6 us; the launch traced here: 57.1 us
  starting transfers between devices  21.7 us (38%)
  waiting for transfers between devices  19.4 us (34%)
  Pallas kernels  13.5 us (23%)
  local copies, waits for them, and re-layouts  1.41 us (2%)
  other arithmetic  1.04 us (2%)
    ppermute x6, waiting for transfers between devices, shards(): twos[later] = lax.ppermute(mine[later], 'ch', ahead)  16.4 us
    ppermute x8, starting transfers between devices, shards(): ones[k] = lax.ppermute(onward[k], 'ch', beside)  7.97 us
    pallas_call x3, Pallas kernels, cross(): call(functools.partial(cross_kernel, jobs, not befores, sent), 'cross', (...  7.5 us
    ppermute x1, starting transfers between devices, shards(): two_got = lax.ppermute(two_sent, 'ch', mate)  3.92 us
    ppermute x3, starting transfers between devices, shards(): twos = {k: lax.ppermute(early[k], 'ch', ahead) for k in range(RAW)}  3.89 us
    pallas_call x3, Pallas kernels, put(): call(functools.partial(put_kernel, kinds), 'put', out_shape, [vmem()] * l...  2.79 us
    ppermute x1, starting transfers between devices, shards(): other = lax.ppermute(left, 'ch', mate)  2.42 us
    pallas_call x1, Pallas kernels, shards(): call(near_kernel, 'near', near_shape, [smem(), smem(), vmem(), vmem()], v...  2.3 us
  transfers between devices with their start and end apart: 22, of which 9 were waited for; matrix products, arithmetic and copies ran while one was open for 2% of the time, Pallas kernels for 21%

profile of v14, /device:TPU:1, one launch (start us, length us, event | category | flops | bytes accessed | tf_op | source)
XLA Modules:
  0.0 57.1 jit_solution(1762516412191074884)
XLA Ops:
  0.0 0.0 copy-start
  0.0 1.4 %copy-done = bf16[2,48,64,128]{3,2,1,0:T(8,128)(2,1)S(1)} copy-done((bf16[2,48,64,128]{3,2,1,0:T(8,128)(2,1)S(1)}, bf16[2,48,64,128]{3,2,1,0:T(8,128)(2,1)}, u32[]{:S(2)}) %copy-start) | copy-done | bytes 1572888
  1.4 0.0 copy-start.1
  1.4 0.4 power.1
  1.8 2.1 %collective-permute-start = (f32[4,128]{1,0:T(4,128)S(1)}, f32[4,128]{1,0:T(4,128)S(1)}, u32[]{:S(2)}, u32[]{:S(2)}) collective-permute-start(f32[4,128]{1,0:T(4,128)S(1)} %get-tuple-element.73), channel_id=1, source_target_pairs={{0,1},{1,0},{2,3},{3,2},{4,5},{5,4},{6,7},{7,6},{8,9},{9,8},{10,11... | collective-permute-start | bytes 6152 | tf_op jit(solution)/shard_map/ppermute | solution.py:311
  3.9 1.3 %collective-permute-start.1 = (bf16[4,64,128]{2,1,0:T(8,128)(2,1)S(1)}, bf16[4,64,128]{2,1,0:T(8,128)(2,1)S(1)}, u32[]{:S(2)}, u32[]{:S(2)}) collective-permute-start(bf16[4,64,128]{2,1,0:T(8,128)(2,1)S(1)} %get-tuple-element.75), channel_id=1, source_target_pairs={{0,8},{2,10},{4,12},{6,14},{8,16},{10,18},{12,20},{14,22},{16,24},... | collective-permute-start | bytes 196616 | tf_op jit(solution)/shard_map/ppermute | solution.py:308
  5.2 1.3 %collective-permute-start.5 = (bf16[8,64,128]{2,1,0:T(8,128)(2,1)S(1)}, bf16[8,64,128]{2,1,0:T(8,128)(2,1)S(1)}, u32[]{:S(2)}, u32[]{:S(2)}) collective-permute-start(bf16[8,64,128]{2,1,0:T(8,128)(2,1)S(1)} %get-tuple-element.82), channel_id=1, source_target_pairs={{0,8},{2,10},{4,12},{6,14},{8,16},{10,18},{12,20},{14,22},{16,24},... | collective-permute-start | bytes 393224 | tf_op jit(solution)/shard_map/ppermute | solution.py:308
  6.5 1.3 %collective-permute-start.3 = (bf16[12,64,128]{2,1,0:T(8,128)(2,1)S(1)}, bf16[12,64,128]{2,1,0:T(8,128)(2,1)S(1)}, u32[]{:S(2)}, u32[]{:S(2)}) collective-permute-start(bf16[12,64,128]{2,1,0:T(8,128)(2,1)S(1)} %get-tuple-element.77), channel_id=1, source_target_pairs={{0,8},{2,10},{4,12},{6,14},{8,16},{10,18},{12,20},{14,22},{16,24},... | collective-permute-start | bytes 589832 | tf_op jit(solution)/shard_map/ppermute | solution.py:308
  7.8 0.7 %broadcast_subtract_fusion = s32[64]{0:T(128)S(1)} fusion(s32[64]{0:T(128)} %param.3, s32[]{:T(128)S(6)} %mul.6), kind=kLoop, calls=%fused_computation.12 | loop fusion | flops 64 | bytes 516 | tf_op jit(solution)/shard_map/sub | solution.py:302
  8.4 0.1 convert_reduce_fusion.bounds_ref
  8.6 0.1 multiply_rsqrt_fusion.norm_ref
  8.6 0.0 collective-permute-done.halo_ref
  8.6 0.0 copy-done.1
  8.6 0.5 left.1
  9.2 0.0 collective-permute-done.1.refs_5_
  9.2 2.4 %collective-permute-start.2 = (bf16[4,128,1536]{2,1,0:T(8,128)(2,1)S(1)}, bf16[4,128,1536]{2,1,0:T(8,128)(2,1)S(1)}, u32[]{:S(2)}, u32[]{:S(2)}) collective-permute-start(bf16[4,128,1536]{2,1,0:T(8,128)(2,1)S(1)} %get-tuple-element.76.own_ref), channel_id=1, source_target_pairs={{0,2},{2,0},{4,6},{6,4},{8,10},{10,8},{12,14},{14,12},{16,18},{18,... | collective-permute-start | bytes 4718600 | tf_op jit(solution)/shard_map/ppermute | solution.py:353
  11.6 1.3 %collective-permute-start.4 = (bf16[4,64,128]{2,1,0:T(8,128)(2,1)S(1)}, bf16[4,64,128]{2,1,0:T(8,128)(2,1)S(1)}, u32[]{:S(2)}, u32[]{:S(2)}) collective-permute-start(bf16[4,64,128]{2,1,0:T(8,128)(2,1)S(1)} %broadcast_select_fusion.8), channel_id=1, source_target_pairs={{0,4},{2,6},{4,0},{6,2},{8,12},{10,14},{12,8},{14,10},{16,20},{18,... | collective-permute-start | bytes 196616 | tf_op jit(solution)/shard_map/ppermute | solution.py:384
  12.9 0.0 collective-permute-start.7
  12.9 0.0 collective-permute-done.5.refs_6_
  13.0 0.5 collective-permute-start.8
  13.5 1.9 %collective-permute-done.4.refs_0_ = bf16[4,64,128]{2,1,0:T(8,128)(2,1)S(1)} collective-permute-done((bf16[4,64,128]{2,1,0:T(8,128)(2,1)S(1)}, bf16[4,64,128]{2,1,0:T(8,128)(2,1)S(1)}, u32[]{:S(2)}, u32[]{:S(2)}) %collective-permute-start.4) | collective-permute-done | bytes 65568 | tf_op jit(solution)/shard_map/ppermute | solution.py:384
  15.4 0.0 collective-permute-start.10
  15.4 0.9 %collective-permute-done.3.refs_7_ = bf16[12,64,128]{2,1,0:T(8,128)(2,1)S(1)} collective-permute-done((bf16[12,64,128]{2,1,0:T(8,128)(2,1)S(1)}, bf16[12,64,128]{2,1,0:T(8,128)(2,1)S(1)}, u32[]{:S(2)}, u32[]{:S(2)}) %collective-permute-start.3) | collective-permute-done | bytes 196640 | tf_op jit(solution)/shard_map/ppermute | solution.py:308
  16.4 1.3 %collective-permute-start.11 = (bf16[12,64,128]{2,1,0:T(8,128)(2,1)S(1)}, bf16[12,64,128]{2,1,0:T(8,128)(2,1)S(1)}, u32[]{:S(2)}, u32[]{:S(2)}) collective-permute-start(bf16[12,64,128]{2,1,0:T(8,128)(2,1)S(1)} %broadcast_select_fusion.6), channel_id=1, source_target_pairs={{0,4},{2,6},{4,0},{6,2},{8,12},{10,14},{12,8},{14,10},{16,20},{18,... | collective-permute-start | bytes 589832 | tf_op jit(solution)/shard_map/ppermute | solution.py:384
  17.7 0.0 collective-permute-done.8.refs_1_
  17.7 4.3 %collective-permute-done.7.refs_8_ = bf16[15,64,128]{2,1,0:T(8,128)(2,1)S(1)} collective-permute-done((bf16[15,64,128]{2,1,0:T(8,128)(2,1)S(1)}, bf16[15,64,128]{2,1,0:T(8,128)(2,1)S(1)}, u32[]{:S(2)}, u32[]{:S(2)}) %collective-permute-start.7) | collective-permute-done | bytes 245792 | tf_op jit(solution)/shard_map/ppermute | solution.py:377
  22.0 1.1 %collective-permute-start.9 = (bf16[15,64,128]{2,1,0:T(8,128)(2,1)S(1)}, bf16[15,64,128]{2,1,0:T(8,128)(2,1)S(1)}, u32[]{:S(2)}, u32[]{:S(2)}) collective-permute-start(bf16[15,64,128]{2,1,0:T(8,128)(2,1)S(1)} %broadcast_select_fusion), channel_id=1, source_target_pairs={{0,4},{2,6},{4,0},{6,2},{8,12},{10,14},{12,8},{14,10},{16,20},{18,... | collective-permute-start | bytes 737288 | tf_op jit(solution)/shard_map/ppermute | solution.py:384
  23.1 0.0 collective-permute-start.6
  23.1 3.1 %collective-permute-done.10.refs_9_ = bf16[12,64,128]{2,1,0:T(8,128)(2,1)S(1)} collective-permute-done((bf16[12,64,128]{2,1,0:T(8,128)(2,1)S(1)}, bf16[12,64,128]{2,1,0:T(8,128)(2,1)S(1)}, u32[]{:S(2)}, u32[]{:S(2)}) %collective-permute-start.10) | collective-permute-done | bytes 196640 | tf_op jit(solution)/shard_map/ppermute | solution.py:377
  26.2 0.0 collective-permute-start.13
  26.2 0.0 collective-permute-done.11.refs_2_
  26.2 1.1 %collective-permute-start.14 = (bf16[12,64,128]{2,1,0:T(8,128)(2,1)S(1)}, bf16[12,64,128]{2,1,0:T(8,128)(2,1)S(1)}, u32[]{:S(2)}, u32[]{:S(2)}) collective-permute-start(bf16[12,64,128]{2,1,0:T(8,128)(2,1)S(1)} %broadcast_select_fusion.5), channel_id=1, source_target_pairs={{0,4},{2,6},{4,0},{6,2},{8,12},{10,14},{12,8},{14,10},{16,20},{18,... | collective-permute-start | bytes 589832 | tf_op jit(solution)/shard_map/ppermute | solution.py:384
  27.3 2.1 %collective-permute-done.6.refs_2_ = bf16[12,64,128]{2,1,0:T(8,128)(2,1)S(1)} collective-permute-done((bf16[12,64,128]{2,1,0:T(8,128)(2,1)S(1)}, bf16[12,64,128]{2,1,0:T(8,128)(2,1)S(1)}, u32[]{:S(2)}, u32[]{:S(2)}) %collective-permute-start.6) | collective-permute-done | bytes 196640 | tf_op jit(solution)/shard_map/ppermute | solution.py:377
  29.4 0.0 collective-permute-done.9.refs_3_
  29.4 0.1 collective-permute-start.12
  29.5 1.4 %collective-permute-start.15 = (bf16[12,64,128]{2,1,0:T(8,128)(2,1)S(1)}, bf16[12,64,128]{2,1,0:T(8,128)(2,1)S(1)}, u32[]{:S(2)}, u32[]{:S(2)}) collective-permute-start(bf16[12,64,128]{2,1,0:T(8,128)(2,1)S(1)} %broadcast_select_fusion.4), channel_id=1, source_target_pairs={{0,4},{2,6},{4,0},{6,2},{8,12},{10,14},{12,8},{14,10},{16,20},{18,... | collective-permute-start | bytes 589832 | tf_op jit(solution)/shard_map/ppermute | solution.py:384
  30.9 4.1 %collective-permute-done.13.refs_3_ = bf16[12,64,128]{2,1,0:T(8,128)(2,1)S(1)} collective-permute-done((bf16[12,64,128]{2,1,0:T(8,128)(2,1)S(1)}, bf16[12,64,128]{2,1,0:T(8,128)(2,1)S(1)}, u32[]{:S(2)}, u32[]{:S(2)}) %collective-permute-start.13) | collective-permute-done | bytes 196640 | tf_op jit(solution)/shard_map/ppermute | solution.py:377
  34.9 0.0 collective-permute-done.14.refs_4_
  35.0 1.1 %collective-permute-start.18 = (bf16[12,64,128]{2,1,0:T(8,128)(2,1)S(1)}, bf16[12,64,128]{2,1,0:T(8,128)(2,1)S(1)}, u32[]{:S(2)}, u32[]{:S(2)}) collective-permute-start(bf16[12,64,128]{2,1,0:T(8,128)(2,1)S(1)} %broadcast_select_fusion.3), channel_id=1, source_target_pairs={{0,4},{2,6},{4,0},{6,2},{8,12},{10,14},{12,8},{14,10},{16,20},{18,... | collective-permute-start | bytes 589832 | tf_op jit(solution)/shard_map/ppermute | solution.py:384
  36.0 0.0 collective-permute-start.17
  36.0 0.0 collective-permute-done.2.mate_ref
  36.0 2.6 %cross.3 = (f32[2,2,4,128,128]{4,3,2,1,0:T(8,128)S(1)}, f32[2,2,4,128,128]{4,3,2,1,0:T(8,128)S(1)}) custom-call(s32[5]{0:T(128)S(1)} %convert_reduce_fusion.bounds_ref, f32[4]{0:T(128)S(1)} %multiply_rsqrt_fusion.norm_ref, bf16[4,128,1536]{2,1,0:T(8,128)(2,1)S(1)} %get-tuple-element.76.own_ref, bf16[4,128,1536]{2,1,0:T(8,128)(2,1)S(1)} %collective-permute-done.2.mate_ref, ...), custom_call_target="tpu_custom_call" | custom-call | flops 805306368 | tf_op jit(solution)/shard_map/cross/pallas_call | solution.py:342
  38.6 0.3 collective-permute-done.12.refs_4_
  38.9 0.0 collective-permute-done.15.refs_0_
  38.9 0.3 collective-permute-start.16
  39.2 2.3 %near.1.refs_2_ = f32[2,4,128,128]{3,2,1,0:T(8,128)S(1)} custom-call(s32[5]{0:T(128)S(1)} %convert_reduce_fusion.bounds_ref, f32[4]{0:T(128)S(1)} %multiply_rsqrt_fusion.norm_ref, bf16[4,128,1536]{2,1,0:T(8,128)(2,1)S(1)} %get-tuple-element.76.own_ref, bf16[4,128,1536]{2,1,0:T(8,128)(2,1)S(1)} %collective-permute-done.2.mate_ref), custom_call_target="tpu_custom_call" | custom-call | flops 1000 | bytes 1000 | tf_op jit(solution)/shard_map/near/pallas_call | solution.py:354
  41.5 2.5 %collective-permute-done.17.refs_5_ = bf16[12,64,128]{2,1,0:T(8,128)(2,1)S(1)} collective-permute-done((bf16[12,64,128]{2,1,0:T(8,128)(2,1)S(1)}, bf16[12,64,128]{2,1,0:T(8,128)(2,1)S(1)}, u32[]{:S(2)}, u32[]{:S(2)}) %collective-permute-start.17) | collective-permute-done | bytes 196640 | tf_op jit(solution)/shard_map/ppermute | solution.py:377
  44.0 0.0 collective-permute-done.18.refs_1_
  44.1 0.1 collective-permute-start.19
  44.2 3.4 %cross.4 = (f32[2,2,4,128,128]{4,3,2,1,0:T(8,128)S(1)}, f32[2,2,4,128,128]{4,3,2,1,0:T(8,128)S(1)}, bf16[2,4,128,128]{3,2,1,0:T(8,128)(2,1)S(1)}) custom-call(s32[5]{0:T(128)S(1)} %convert_reduce_fusion.bounds_ref, f32[4]{0:T(128)S(1)} %multiply_rsqrt_fusion.norm_ref, bf16[4,128,1536]{2,1,0:T(8,128)(2,1)S(1)} %get-tuple-element.76.own_ref, ...), custom_call_target="tpu_custom_call" | custom-call | flops 603979776 | tf_op jit(solution)/shard_map/cross/pallas_call | solution.py:342
  47.6 3.9 %collective-permute-start.21 = (bf16[2,4,128,128]{3,2,1,0:T(8,128)(2,1)S(1)}, bf16[2,4,128,128]{3,2,1,0:T(8,128)(2,1)S(1)}, u32[]{:S(2)}, u32[]{:S(2)}) collective-permute-start(bf16[2,4,128,128]{3,2,1,0:T(8,128)(2,1)S(1)} %get-tuple-element.132), channel_id=1, source_target_pairs={{0,2},{2,0},{4,6},{6,4},{8,10},{10,8},{12,14},{14,12},{16,18},{18,... | collective-permute-start | bytes 786440 | tf_op jit(solution)/shard_map/ppermute | solution.py:415
  51.5 0.8 %put.3.refs_3_ = f32[2,4,4,128,128]{4,3,2,1,0:T(8,128)} custom-call(f32[2,2,4,128,128]{4,3,2,1,0:T(8,128)S(1)} %get-tuple-element.128.refs_0_), custom_call_target="tpu_custom_call" | custom-call | flops 1000 | bytes 6291456 | tf_op jit(solution)/shard_map/put/pallas_call | solution.py:396
  52.4 0.0 collective-permute-done.16.refs_0_
  52.4 0.0 collective-permute-done.19.refs_1_
  52.4 1.5 %cross.5 = (f32[2,2,4,128,128]{4,3,2,1,0:T(8,128)S(1)}, bf16[2,4,128,128]{3,2,1,0:T(8,128)(2,1)S(1)}) custom-call(s32[5]{0:T(128)S(1)} %convert_reduce_fusion.bounds_ref, f32[4]{0:T(128)S(1)} %multiply_rsqrt_fusion.norm_ref, bf16[4,128,1536]{2,1,0:T(8,128)(2,1)S(1)} %get-tuple-element.76.own_ref, bf16[4,128,1536]{2,1,0:T(8,128)(2,1)S(1)} %collective-permute-done.2.mate_ref, ...), custom_call_target="tpu_custom_call" | custom-call | flops 201326592 | tf_op jit(solution)/shard_map/cross/pallas_call | solution.py:342
  53.9 1.2 %collective-permute-start.20 = (bf16[2,4,128,128]{3,2,1,0:T(8,128)(2,1)S(1)}, bf16[2,4,128,128]{3,2,1,0:T(8,128)(2,1)S(1)}, u32[]{:S(2)}, u32[]{:S(2)}) collective-permute-start(bf16[2,4,128,128]{3,2,1,0:T(8,128)(2,1)S(1)} %get-tuple-element.130), channel_id=1, source_target_pairs={{0,2},{2,0},{4,6},{6,4},{8,10},{10,8},{12,14},{14,12},{16,18},{18,... | collective-permute-start | bytes 786440 | tf_op jit(solution)/shard_map/ppermute | solution.py:420
  55.1 0.0 collective-permute-done.21.refs_1_
  55.1 1.1 %put.4.refs_1_ = f32[2,4,4,128,128]{4,3,2,1,0:T(8,128)} custom-call(f32[2,2,4,128,128]{4,3,2,1,0:T(8,128)S(1)} %get-tuple-element.131.refs_0_, bf16[2,4,128,128]{3,2,1,0:T(8,128)(2,1)S(1)} %collective-permute-done.21.refs_1_, f32[2,4,128,128]{3,2,1,0:T(8,128)S(1)} %near.1.refs_2_, f32[2,4,4,128,128]{4,3,2,1,0:T(8,128)} %put.3.refs_3_), custom_call_target="tpu_custom_call", output_to_operand_aliasing={{}: (3, {})} | custom-call | flops 1000 | bytes 6291456 | tf_op jit(solution)/shard_map/put/pallas_call | solution.py:396
  56.2 0.1 collective-permute-done.20.refs_0_
  56.3 0.9 %put.5 = f32[2,4,4,128,128]{4,3,2,1,0:T(8,128)} custom-call(bf16[2,4,128,128]{3,2,1,0:T(8,128)(2,1)S(1)} %collective-permute-done.20.refs_0_, f32[2,4,4,128,128]{4,3,2,1,0:T(8,128)} %put.4.refs_1_), custom_call_target="tpu_custom_call", output_to_operand_aliasing={{}: (1, {})} | custom-call | flops 1000 | bytes 6291456 | tf_op jit(solution)/shard_map/put/pallas_call | solution.py:396
  (9 shorter events, 0.2 us)
Async XLA Ops:
  0.0 1.4 %copy-start = (bf16[2,48,64,128]{3,2,1,0:T(8,128)(2,1)S(1)}, bf16[2,48,64,128]{3,2,1,0:T(8,128)(2,1)}, u32[]{:S(2)}) copy-start(bf16[2,48,64,128]{3,2,1,0:T(8,128)(2,1)} %param.2) | copy-start | bytes 4718596
  1.4 7.2 %copy-start.1 = (bf16[2,48,64,128]{3,2,1,0:T(8,128)(2,1)S(1)}, bf16[2,48,64,128]{3,2,1,0:T(8,128)(2,1)}, u32[]{:S(2)}) copy-start(bf16[2,48,64,128]{3,2,1,0:T(8,128)(2,1)} %param.2) | copy-start | bytes 4718596
  1.8 6.9 %collective-permute-start = (f32[4,128]{1,0:T(4,128)S(1)}, f32[4,128]{1,0:T(4,128)S(1)}, u32[]{:S(2)}, u32[]{:S(2)}) collective-permute-start(f32[4,128]{1,0:T(4,128)S(1)} %get-tuple-element.73), channel_id=1, source_target_pairs={{0,1},{1,0},{2,3},{3,2},{4,5},{5,4},{6,7},{7,6},{8,9},{9,8},{10,11... | collective-permute-start | bytes 6152 | tf_op jit(solution)/shard_map/ppermute | solution.py:311
  3.9 5.3 %collective-permute-start.1 = (bf16[4,64,128]{2,1,0:T(8,128)(2,1)S(1)}, bf16[4,64,128]{2,1,0:T(8,128)(2,1)S(1)}, u32[]{:S(2)}, u32[]{:S(2)}) collective-permute-start(bf16[4,64,128]{2,1,0:T(8,128)(2,1)S(1)} %get-tuple-element.75), channel_id=1, source_target_pairs={{0,8},{2,10},{4,12},{6,14},{8,16},{10,18},{12,20},{14,22},{16,24},... | collective-permute-start | bytes 196616 | tf_op jit(solution)/shard_map/ppermute | solution.py:308
  5.2 7.7 %collective-permute-start.5 = (bf16[8,64,128]{2,1,0:T(8,128)(2,1)S(1)}, bf16[8,64,128]{2,1,0:T(8,128)(2,1)S(1)}, u32[]{:S(2)}, u32[]{:S(2)}) collective-permute-start(bf16[8,64,128]{2,1,0:T(8,128)(2,1)S(1)} %get-tuple-element.82), channel_id=1, source_target_pairs={{0,8},{2,10},{4,12},{6,14},{8,16},{10,18},{12,20},{14,22},{16,24},... | collective-permute-start | bytes 393224 | tf_op jit(solution)/shard_map/ppermute | solution.py:308
  6.5 9.9 %collective-permute-start.3 = (bf16[12,64,128]{2,1,0:T(8,128)(2,1)S(1)}, bf16[12,64,128]{2,1,0:T(8,128)(2,1)S(1)}, u32[]{:S(2)}, u32[]{:S(2)}) collective-permute-start(bf16[12,64,128]{2,1,0:T(8,128)(2,1)S(1)} %get-tuple-element.77), channel_id=1, source_target_pairs={{0,8},{2,10},{4,12},{6,14},{8,16},{10,18},{12,20},{14,22},{16,24},... | collective-permute-start | bytes 589832 | tf_op jit(solution)/shard_map/ppermute | solution.py:308
  9.2 26.9 %collective-permute-start.2 = (bf16[4,128,1536]{2,1,0:T(8,128)(2,1)S(1)}, bf16[4,128,1536]{2,1,0:T(8,128)(2,1)S(1)}, u32[]{:S(2)}, u32[]{:S(2)}) collective-permute-start(bf16[4,128,1536]{2,1,0:T(8,128)(2,1)S(1)} %get-tuple-element.76.own_ref), channel_id=1, source_target_pairs={{0,2},{2,0},{4,6},{6,4},{8,10},{10,8},{12,14},{14,12},{16,18},{18,... | collective-permute-start | bytes 4718600 | tf_op jit(solution)/shard_map/ppermute | solution.py:353
  11.6 3.8 %collective-permute-start.4 = (bf16[4,64,128]{2,1,0:T(8,128)(2,1)S(1)}, bf16[4,64,128]{2,1,0:T(8,128)(2,1)S(1)}, u32[]{:S(2)}, u32[]{:S(2)}) collective-permute-start(bf16[4,64,128]{2,1,0:T(8,128)(2,1)S(1)} %broadcast_select_fusion.8), channel_id=1, source_target_pairs={{0,4},{2,6},{4,0},{6,2},{8,12},{10,14},{12,8},{14,10},{16,20},{18,... | collective-permute-start | bytes 196616 | tf_op jit(solution)/shard_map/ppermute | solution.py:384
  12.9 9.1 %collective-permute-start.7 = (bf16[15,64,128]{2,1,0:T(8,128)(2,1)S(1)}, bf16[15,64,128]{2,1,0:T(8,128)(2,1)S(1)}, u32[]{:S(2)}, u32[]{:S(2)}) collective-permute-start(bf16[15,64,128]{2,1,0:T(8,128)(2,1)S(1)} %get-tuple-element.89), channel_id=1, source_target_pairs={{0,8},{2,10},{4,12},{6,14},{8,16},{10,18},{12,20},{14,22},{16,24},... | collective-permute-start | bytes 737288 | tf_op jit(solution)/shard_map/ppermute | solution.py:377
  13.0 4.7 %collective-permute-start.8 = (bf16[8,64,128]{2,1,0:T(8,128)(2,1)S(1)}, bf16[8,64,128]{2,1,0:T(8,128)(2,1)S(1)}, u32[]{:S(2)}, u32[]{:S(2)}) collective-permute-start(bf16[8,64,128]{2,1,0:T(8,128)(2,1)S(1)} %broadcast_select_fusion.7), channel_id=1, source_target_pairs={{0,4},{2,6},{4,0},{6,2},{8,12},{10,14},{12,8},{14,10},{16,20},{18,... | collective-permute-start | bytes 393224 | tf_op jit(solution)/shard_map/ppermute | solution.py:384
  15.4 10.8 %collective-permute-start.10 = (bf16[12,64,128]{2,1,0:T(8,128)(2,1)S(1)}, bf16[12,64,128]{2,1,0:T(8,128)(2,1)S(1)}, u32[]{:S(2)}, u32[]{:S(2)}) collective-permute-start(bf16[12,64,128]{2,1,0:T(8,128)(2,1)S(1)} %get-tuple-element.96), channel_id=1, source_target_pairs={{0,8},{2,10},{4,12},{6,14},{8,16},{10,18},{12,20},{14,22},{16,24},... | collective-permute-start | bytes 589832 | tf_op jit(solution)/shard_map/ppermute | solution.py:377
  16.4 9.8 %collective-permute-start.11 = (bf16[12,64,128]{2,1,0:T(8,128)(2,1)S(1)}, bf16[12,64,128]{2,1,0:T(8,128)(2,1)S(1)}, u32[]{:S(2)}, u32[]{:S(2)}) collective-permute-start(bf16[12,64,128]{2,1,0:T(8,128)(2,1)S(1)} %broadcast_select_fusion.6), channel_id=1, source_target_pairs={{0,4},{2,6},{4,0},{6,2},{8,12},{10,14},{12,8},{14,10},{16,20},{18,... | collective-permute-start | bytes 589832 | tf_op jit(solution)/shard_map/ppermute | solution.py:384
  22.0 7.4 %collective-permute-start.9 = (bf16[15,64,128]{2,1,0:T(8,128)(2,1)S(1)}, bf16[15,64,128]{2,1,0:T(8,128)(2,1)S(1)}, u32[]{:S(2)}, u32[]{:S(2)}) collective-permute-start(bf16[15,64,128]{2,1,0:T(8,128)(2,1)S(1)} %broadcast_select_fusion), channel_id=1, source_target_pairs={{0,4},{2,6},{4,0},{6,2},{8,12},{10,14},{12,8},{14,10},{16,20},{18,... | collective-permute-start | bytes 737288 | tf_op jit(solution)/shard_map/ppermute | solution.py:384
  23.1 6.3 %collective-permute-start.6 = (bf16[12,64,128]{2,1,0:T(8,128)(2,1)S(1)}, bf16[12,64,128]{2,1,0:T(8,128)(2,1)S(1)}, u32[]{:S(2)}, u32[]{:S(2)}) collective-permute-start(bf16[12,64,128]{2,1,0:T(8,128)(2,1)S(1)} %get-tuple-element.88), channel_id=1, source_target_pairs={{0,8},{2,10},{4,12},{6,14},{8,16},{10,18},{12,20},{14,22},{16,24},... | collective-permute-start | bytes 589832 | tf_op jit(solution)/shard_map/ppermute | solution.py:377
  26.2 8.7 %collective-permute-start.13 = (bf16[12,64,128]{2,1,0:T(8,128)(2,1)S(1)}, bf16[12,64,128]{2,1,0:T(8,128)(2,1)S(1)}, u32[]{:S(2)}, u32[]{:S(2)}) collective-permute-start(bf16[12,64,128]{2,1,0:T(8,128)(2,1)S(1)} %get-tuple-element.106), channel_id=1, source_target_pairs={{0,8},{2,10},{4,12},{6,14},{8,16},{10,18},{12,20},{14,22},{16,24},... | collective-permute-start | bytes 589832 | tf_op jit(solution)/shard_map/ppermute | solution.py:377
  26.2 8.7 %collective-permute-start.14 = (bf16[12,64,128]{2,1,0:T(8,128)(2,1)S(1)}, bf16[12,64,128]{2,1,0:T(8,128)(2,1)S(1)}, u32[]{:S(2)}, u32[]{:S(2)}) collective-permute-start(bf16[12,64,128]{2,1,0:T(8,128)(2,1)S(1)} %broadcast_select_fusion.5), channel_id=1, source_target_pairs={{0,4},{2,6},{4,0},{6,2},{8,12},{10,14},{12,8},{14,10},{16,20},{18,... | collective-permute-start | bytes 589832 | tf_op jit(solution)/shard_map/ppermute | solution.py:384
  29.4 9.5 %collective-permute-start.12 = (bf16[12,64,128]{2,1,0:T(8,128)(2,1)S(1)}, bf16[12,64,128]{2,1,0:T(8,128)(2,1)S(1)}, u32[]{:S(2)}, u32[]{:S(2)}) collective-permute-start(bf16[12,64,128]{2,1,0:T(8,128)(2,1)S(1)} %get-tuple-element.101), channel_id=1, source_target_pairs={{0,8},{2,10},{4,12},{6,14},{8,16},{10,18},{12,20},{14,22},{16,24},... | collective-permute-start | bytes 589832 | tf_op jit(solution)/shard_map/ppermute | solution.py:382
  29.5 9.4 %collective-permute-start.15 = (bf16[12,64,128]{2,1,0:T(8,128)(2,1)S(1)}, bf16[12,64,128]{2,1,0:T(8,128)(2,1)S(1)}, u32[]{:S(2)}, u32[]{:S(2)}) collective-permute-start(bf16[12,64,128]{2,1,0:T(8,128)(2,1)S(1)} %broadcast_select_fusion.4), channel_id=1, source_target_pairs={{0,4},{2,6},{4,0},{6,2},{8,12},{10,14},{12,8},{14,10},{16,20},{18,... | collective-permute-start | bytes 589832 | tf_op jit(solution)/shard_map/ppermute | solution.py:384
  35.0 9.1 %collective-permute-start.18 = (bf16[12,64,128]{2,1,0:T(8,128)(2,1)S(1)}, bf16[12,64,128]{2,1,0:T(8,128)(2,1)S(1)}, u32[]{:S(2)}, u32[]{:S(2)}) collective-permute-start(bf16[12,64,128]{2,1,0:T(8,128)(2,1)S(1)} %broadcast_select_fusion.3), channel_id=1, source_target_pairs={{0,4},{2,6},{4,0},{6,2},{8,12},{10,14},{12,8},{14,10},{16,20},{18,... | collective-permute-start | bytes 589832 | tf_op jit(solution)/shard_map/ppermute | solution.py:384
  36.0 8.0 %collective-permute-start.17 = (bf16[12,64,128]{2,1,0:T(8,128)(2,1)S(1)}, bf16[12,64,128]{2,1,0:T(8,128)(2,1)S(1)}, u32[]{:S(2)}, u32[]{:S(2)}) collective-permute-start(bf16[12,64,128]{2,1,0:T(8,128)(2,1)S(1)} %get-tuple-element.117), channel_id=1, source_target_pairs={{0,8},{2,10},{4,12},{6,14},{8,16},{10,18},{12,20},{14,22},{16,24},... | collective-permute-start | bytes 589832 | tf_op jit(solution)/shard_map/ppermute | solution.py:377
  38.9 13.5 %collective-permute-start.16 = (bf16[12,64,128]{2,1,0:T(8,128)(2,1)S(1)}, bf16[12,64,128]{2,1,0:T(8,128)(2,1)S(1)}, u32[]{:S(2)}, u32[]{:S(2)}) collective-permute-start(bf16[12,64,128]{2,1,0:T(8,128)(2,1)S(1)} %broadcast_select_fusion.2), channel_id=1, source_target_pairs={{0,4},{2,6},{4,0},{6,2},{8,12},{10,14},{12,8},{14,10},{16,20},{18,... | collective-permute-start | bytes 589832 | tf_op jit(solution)/shard_map/ppermute | solution.py:384
  44.1 8.3 %collective-permute-start.19 = (bf16[12,64,128]{2,1,0:T(8,128)(2,1)S(1)}, bf16[12,64,128]{2,1,0:T(8,128)(2,1)S(1)}, u32[]{:S(2)}, u32[]{:S(2)}) collective-permute-start(bf16[12,64,128]{2,1,0:T(8,128)(2,1)S(1)} %broadcast_select_fusion.1), channel_id=1, source_target_pairs={{0,4},{2,6},{4,0},{6,2},{8,12},{10,14},{12,8},{14,10},{16,20},{18,... | collective-permute-start | bytes 589832 | tf_op jit(solution)/shard_map/ppermute | solution.py:411
  47.6 7.5 %collective-permute-start.21 = (bf16[2,4,128,128]{3,2,1,0:T(8,128)(2,1)S(1)}, bf16[2,4,128,128]{3,2,1,0:T(8,128)(2,1)S(1)}, u32[]{:S(2)}, u32[]{:S(2)}) collective-permute-start(bf16[2,4,128,128]{3,2,1,0:T(8,128)(2,1)S(1)} %get-tuple-element.132), channel_id=1, source_target_pairs={{0,2},{2,0},{4,6},{6,4},{8,10},{10,8},{12,14},{14,12},{16,18},{18,... | collective-permute-start | bytes 786440 | tf_op jit(solution)/shard_map/ppermute | solution.py:415
  53.9 2.4 %collective-permute-start.20 = (bf16[2,4,128,128]{3,2,1,0:T(8,128)(2,1)S(1)}, bf16[2,4,128,128]{3,2,1,0:T(8,128)(2,1)S(1)}, u32[]{:S(2)}, u32[]{:S(2)}) collective-permute-start(bf16[2,4,128,128]{3,2,1,0:T(8,128)(2,1)S(1)} %get-tuple-element.130), channel_id=1, source_target_pairs={{0,2},{2,0},{4,6},{6,4},{8,10},{10,8},{12,14},{14,12},{16,18},{18,... | collective-permute-start | bytes 786440 | tf_op jit(solution)/shard_map/ppermute | solution.py:420
